TPU v7x, 32 devices: a whole 2x2x4 slice. The times are simulated.
32 devices in a mesh: groups: 2 (over x), dom: 16 (over z, y, core).
Axes of the slice: x: 2, y: 2, z: 4, core: 2. Of those that a mesh axis runs over, the one named last changes fastest.
Arguments:
- particle_fourier: float32 [3072, 1024], P(('groups', 'dom')), parts along dimension 0, may hold values from -90 to 90, as said below
- defocus: float32 [3072], P(('groups', 'dom')), parts along dimension 0, may hold values from 20 to 80
- particle_offset: int32 [3072, 2], P(('groups', 'dom')), parts along dimension 0, may hold values from -4 to 4
- prior_rotation: int32 [3072], P(('groups', 'dom')), parts along dimension 0, may hold values from 0 to 15
- group_id: int32 [3072], P(('groups', 'dom')), parts along dimension 0, may hold values from 0 to 127, never falling along the last dimension, each value on 1 to 24 neighbouring positions
- live_count: int32 [32], P(('groups', 'dom')), parts along dimension 0, may hold values from 24 to 96, as said below
- noise_power: float32 [256, 512], P('groups'), parts along dimension 0, may hold values from 0.5 to 2
- signal_power: float32 [1024], P('groups'), parts along dimension 0, may hold values from 0.5 to 4
- class_refs: float32 [64, 16, 1024], P(('groups', 'dom')), parts along dimension 0, may hold values from -0.5 to 0.5
Outputs:
- expected_shift: float32 [3072, 2], P(('groups', 'dom')), parts along dimension 0
- new_refs: float32 [64, 16, 1024], P(('groups', 'dom')), parts along dimension 0
There are 2 independent parts, one for each index of `groups`. A program takes and returns all parts, laid end to end along the dimension named above; each array names one. Nothing has to cross between parts.
Inputs may be any that keep to these rules, and one draw needn't show every extreme that they name: `particle_fourier`: drawn alike for all particles. `live_count`: devices of even index along dom hold at most 96 live slots, and one of them exactly 96; devices of odd index at most 48, and one of them exactly that many. Live slots come first on each device.
All inputs are finite; a program needn't handle non-finite values.
Results may differ from a plain program's by a relative error of at most 0.0003.
Values sent between devices are 32-bit elements; how exact they have to be, the bound alone decides.
No kernel may reach another device: no remote copies, remote signals or barrier semaphores. Data moves between devices by JAX's collectives and lax.ppermute only.
A program may use at most 128 MiB of HBM per device.

v0:
```python
import math

import jax
import jax.numpy as jnp
from jax import lax
from jax.sharding import PartitionSpec as P

ROT = 16
SIDE = 3
BOX = 128
FY = 32
SHIFTS = 9


prior_strength = 2.0


def from_behind(block, axis, distance):
    devices = range(lax.axis_size(axis))
    route = [(i - distance, i) for i in devices if i - distance in devices]
    return lax.ppermute(block, axis, route)


def shift_grid():
    shift_id = jnp.arange(SIDE * SIDE, dtype=jnp.int32)
    grid_x = (shift_id // SIDE - SIDE // 2).astype(jnp.float32)
    grid_y = (shift_id % SIDE - SIDE // 2).astype(jnp.float32)
    return (grid_x, grid_y)


def spectra(fourier, focus, offsets, noise_rows):
    half_width = fourier.shape[1] // 2
    coeff = jnp.arange(half_width, dtype=jnp.int32)
    freq_x = (coeff // FY).astype(jnp.float32)
    freq_y = (coeff % FY - FY // 2).astype(jnp.float32)
    phase_chi = focus[:, None] * ((freq_x * freq_x + freq_y * freq_y) / 1024.0)[None, :]
    ctf = -(0.995 * jnp.sin(phase_chi) + 0.1 * jnp.cos(phase_chi))
    scaled = ctf / noise_rows
    ctf_power = ctf * scaled
    real_part = fourier[:, :half_width]
    imag_part = fourier[:, half_width:]
    grid_x, grid_y = shift_grid()
    total_x = offsets[:, 0].astype(jnp.float32)[:, None] + grid_x[None, :]
    total_y = offsets[:, 1].astype(jnp.float32)[:, None] + grid_y[None, :]
    angles = (
        2.0
        * math.pi
        / BOX
        * (
            freq_x[None, None, :] * total_x[:, :, None]
            + freq_y[None, None, :] * total_y[:, :, None]
        )
    )
    cosine = jnp.cos(angles)
    sine = jnp.sin(angles)
    shifted_real = scaled[:, None, :] * (
        real_part[:, None, :] * cosine - imag_part[:, None, :] * sine
    )
    shifted_imag = scaled[:, None, :] * (
        real_part[:, None, :] * sine + imag_part[:, None, :] * cosine
    )
    return (jnp.concatenate([shifted_real, shifted_imag], axis=2), ctf_power)


def block_scores(shifted_rows, ctf_power, prior_rows, ref_rows):
    particles_here = ctf_power.shape[0]
    half_width = ctf_power.shape[1]
    hypotheses = ref_rows.shape[0]
    cross = jnp.einsum("rf,kf->rk", shifted_rows, ref_rows, precision=lax.Precision.HIGHEST)
    power = (
        ref_rows[:, :half_width] * ref_rows[:, :half_width]
        + ref_rows[:, half_width:] * ref_rows[:, half_width:]
    )
    quadratic = jnp.einsum("pf,kf->pk", ctf_power, power, precision=lax.Precision.HIGHEST)
    rotation = jnp.arange(hypotheses, dtype=jnp.int32) % ROT
    distance = (rotation[None, :] - prior_rows[:, None]).astype(jnp.float32)
    prior_term = prior_strength * jnp.cos(2.0 * math.pi / ROT * distance)
    return (
        cross.reshape(particles_here, SHIFTS, hypotheses)
        - 0.5 * quadratic[:, None, :]
        + prior_term[:, None, :]
    )


def posterior(scores):
    highest = jnp.max(scores, axis=(1, 2), keepdims=True)
    normaliser = jnp.sum(jnp.exp(scores - highest), axis=(1, 2), keepdims=True)
    weights = jnp.exp(scores - highest - jnp.log(normaliser))
    over_shifts = jnp.sum(weights, axis=2)
    grid_x, grid_y = shift_grid()
    shift_mean = jnp.stack(
        [
            jnp.sum(over_shifts * grid_x[None, :], axis=1),
            jnp.sum(over_shifts * grid_y[None, :], axis=1),
        ],
        axis=-1,
    )
    return (weights, shift_mean)


def on_device(
    particle_fourier,
    defocus,
    particle_offset,
    prior_rotation,
    group_id,
    live_count,
    noise_power,
    signal_power,
    class_refs,
):
    slot_count = particle_fourier.shape[0]
    kept_rows = 3 * slot_count // 4
    half_rows = slot_count // 2
    place_idx = lax.axis_index("dom")
    is_odd = place_idx % 2 == 1
    live_here = live_count[0]
    arrived = from_behind(
        (
            particle_fourier[kept_rows:],
            defocus[kept_rows:],
            particle_offset[kept_rows:],
            prior_rotation[kept_rows:],
            group_id[kept_rows:],
            live_count,
        ),
        "dom",
        1,
    )

    def merged(own, received):
        return jnp.where(
            is_odd, jnp.concatenate([own[:half_rows], received], axis=0), own[:kept_rows]
        )

    spectrum = merged(particle_fourier, arrived[0])
    focus_rows = merged(defocus, arrived[1])
    offset_rows = merged(particle_offset, arrived[2])
    prior_rows = merged(prior_rotation, arrived[3])
    group_rows = merged(group_id, arrived[4])
    slot_ids = jnp.arange(kept_rows, dtype=jnp.int32)
    live_odd = jnp.where(
        slot_ids < half_rows, slot_ids < live_here, slot_ids - half_rows + kept_rows < arrived[5][0]
    )
    live_rows = jnp.where(is_odd, live_odd, slot_ids < live_here).astype(jnp.float32)
    group_total = noise_power.shape[0]
    onehot = (group_rows[:, None] == jnp.arange(group_total, dtype=jnp.int32)[None, :]).astype(
        jnp.float32
    )
    noise_rows = jnp.dot(onehot, noise_power, precision=lax.Precision.HIGHEST)
    shifted, ctf_power = spectra(spectrum, focus_rows, offset_rows, noise_rows)
    particles_here = spectrum.shape[0]
    shifted_rows = shifted.reshape(particles_here * SHIFTS, spectrum.shape[1])
    block_cols = class_refs.shape[0] * class_refs.shape[1]
    piece = lax.all_gather(class_refs, "dom", axis=0, tiled=True)
    ref_rows = piece.reshape(-1, piece.shape[2])
    fresh = block_scores(shifted_rows, ctf_power, prior_rows, ref_rows)
    weights, shift_mean = posterior(fresh)
    shift_mean = shift_mean * live_rows[:, None]
    masked = weights * live_rows[:, None, None]
    summed_shifts = jnp.sum(masked, axis=1)
    half_width = ctf_power.shape[1]
    columns = masked.reshape(particles_here * SHIFTS, block_cols * lax.axis_size("dom"))
    data_part = jnp.einsum("rk,rf->kf", columns, shifted_rows, precision=lax.Precision.HIGHEST)
    weight_part = jnp.einsum("pk,pf->kf", summed_shifts, ctf_power, precision=lax.Precision.HIGHEST)
    data_part, weight_part = (data_part, weight_part)
    summed = lax.psum_scatter(
        jnp.concatenate([data_part, weight_part], axis=1), "dom", scatter_dimension=0, tiled=True
    )
    data_sum = summed[:, : 2 * half_width]
    weight_sum = summed[:, 2 * half_width :]
    inverse = 1.0 / signal_power
    denominator = weight_sum + inverse[None, :]
    updated = data_sum / jnp.concatenate([denominator, denominator], axis=1)
    new_refs = updated.reshape(class_refs.shape)
    returned_rows = from_behind(shift_mean[half_rows:], "dom", -1)
    odd_result = jnp.concatenate(
        [shift_mean[:half_rows], jnp.zeros((slot_count - half_rows, 2), jnp.float32)], axis=0
    )
    even_result = jnp.concatenate([shift_mean, returned_rows], axis=0)
    expected = jnp.where(is_odd, odd_result, even_result)
    return (expected, new_refs)


def solution(mesh):
    in_specs = (
        P(("groups", "dom"), None),
        P(("groups", "dom")),
        P(("groups", "dom"), None),
        P(("groups", "dom")),
        P(("groups", "dom")),
        P(("groups", "dom")),
        P("groups", None),
        P("groups"),
        P(("groups", "dom"), None, None),
    )
    out_specs = (P(("groups", "dom"), None), P(("groups", "dom"), None, None))
    return jax.shard_map(
        on_device, mesh=mesh, in_specs=in_specs, out_specs=out_specs, check_vma=False
    )
```

profile of v0, /device:TPU:0, one launch (start us, length us, event | category | flops | bytes accessed | tf_op | source)
XLA Modules:
  0.0 148.3 jit_solution(36546337253125742)
XLA Ops:
  7.2 0.0 copy-start
  7.2 0.0 copy-start.2
  7.2 0.0 copy-start.1
  7.2 0.0 slice-start
  7.2 0.0 all-gather.2.cloned.1.call-start
  7.3 0.7 all-gather.2.cloned.1.call-update
  7.9 0.0 reduce-scatter.2.cloned.1.call-start
  8.0 0.7 slice.78
  8.7 2.3 %collective-permute-start = (f32[24]{0:T(128)S(1)}, f32[24]{0:T(128)S(1)}, u32[]{:S(2)}, u32[]{:S(2)}) collective-permute-start(f32[24]{0:T(128)S(1)} %slice.78), channel_id=1, source_target_pairs={{0,1},{1,2},{2,3},{3,4},{4,5},{5,6},{6,7},{7,8},{8,9},{9,10},{10,1... | collective-permute-start | bytes 296 | tf_op jit(solution)/shard_map/ppermute | solution.py:21
  11.1 0.7 slice.81
  11.8 4.5 %collective-permute-start.1 = (s32[24]{0:T(128)S(1)}, s32[24]{0:T(128)S(1)}, u32[]{:S(2)}, u32[]{:S(2)}) collective-permute-start(s32[24]{0:T(128)S(1)} %slice.81), channel_id=1, source_target_pairs={{0,1},{1,2},{2,3},{3,4},{4,5},{5,6},{6,7},{7,8},{8,9},{9,10},{10,1... | collective-permute-start | bytes 296 | tf_op jit(solution)/shard_map/ppermute | solution.py:21
  16.3 0.8 slice.88
  17.1 1.9 %collective-permute-start.3 = (s32[24,2]{0,1:T(2,128)S(1)}, s32[24,2]{0,1:T(2,128)S(1)}, u32[]{:S(2)}, u32[]{:S(2)}) collective-permute-start(s32[24,2]{0,1:T(2,128)S(1)} %slice.88), channel_id=1, source_target_pairs={{0,1},{1,2},{2,3},{3,4},{4,5},{5,6},{6,7},{7,8},{8,9},{9,10},{10,1... | collective-permute-start | bytes 584 | tf_op jit(solution)/shard_map/ppermute | solution.py:21
  19.0 0.9 slice.84
  19.9 3.5 %collective-permute-start.2 = (f32[24,1024]{1,0:T(8,128)S(1)}, f32[24,1024]{1,0:T(8,128)S(1)}, u32[]{:S(2)}, u32[]{:S(2)}) collective-permute-start(f32[24,1024]{1,0:T(8,128)S(1)} %slice.84), channel_id=1, source_target_pairs={{0,1},{1,2},{2,3},{3,4},{4,5},{5,6},{6,7},{7,8},{8,9},{9,10},{10,1... | collective-permute-start | bytes 294920 | tf_op jit(solution)/shard_map/ppermute | solution.py:21
  23.4 2.5 %collective-permute-start.5 = (s32[1]{0:T(128)}, s32[1]{0:T(128)}, u32[]{:S(2)}, u32[]{:S(2)}) collective-permute-start(s32[1]{0:T(128)} %param.14), channel_id=1, source_target_pairs={{0,1},{1,2},{2,3},{3,4},{4,5},{5,6},{6,7},{7,8},{8,9},{9,10},{10,1... | collective-permute-start | bytes 20 | tf_op jit(solution)/shard_map/ppermute | solution.py:21
  26.6 0.7 slice.96
  27.4 0.0 collective-permute-done.5
  27.4 3.0 %collective-permute-start.4 = (s32[24]{0:T(128)S(1)}, s32[24]{0:T(128)S(1)}, u32[]{:S(2)}, u32[]{:S(2)}) collective-permute-start(s32[24]{0:T(128)S(1)} %slice.96), channel_id=1, source_target_pairs={{0,1},{1,2},{2,3},{3,4},{4,5},{5,6},{6,7},{7,8},{8,9},{9,10},{10,1... | collective-permute-start | bytes 296 | tf_op jit(solution)/shard_map/ppermute | solution.py:21
  30.4 0.7 fusion.36
  31.1 0.0 collective-permute-done
  31.1 0.8 broadcast_select_fusion.2
  31.9 0.0 collective-permute-done.1
  31.9 0.8 broadcast_select_fusion.1
  32.7 0.0 collective-permute-done.4
  32.7 0.8 broadcast_select_fusion
  33.5 0.0 copy-done
  33.5 0.7 convolution_divide_fusion
  34.2 0.6 cosine_multiply_fusion
  34.8 0.0 collective-permute-done.3
  34.8 0.0 copy-done.2
  34.8 0.1 add_select_fusion.2
  34.9 0.1 broadcast_add_fusion
  34.9 0.0 collective-permute-done.2
  35.0 0.0 copy-done.1
  35.0 0.0 slice-done
  35.0 5.2 %subtract_multiply_fusion = (f32[72,9,512]{2,0,1:T(8,128)S(1)}, f32[72,9,512]{2,0,1:T(8,128)S(1)}) fusion(f32[72,512]{1,0:T(8,128)S(1)} %get-tuple-element.9, f32[72,9]{0,1:T(8,128)S(1)} %get-tuple-element.14, f32[512]{0:T(512)S(1)} %get-tuple-element.17, f32[72,9]{0,1:T(8,128)S(1)} %get-tuple-element.15, f32[512]{0:T(512)S(1)} %get-tuple-element.16, ...), kind=kLoop, calls=%fused_computation.10 | loop fusion | flops 3981312 | bytes 3105856 | tf_op jit(solution)/shard_map/mul | solution.py:56
  40.3 14.3 %all-gather.2.cloned.1.call-done = f32[32,16,1024]{2,1,0:T(8,128)} async-done(((f32[2,16,1024]{2,1,0:T(8,128)}), f32[32,16,1024]{2,1,0:T(8,128)}) %all-gather.2.cloned.1.call-update) | async-done | bytes 2097168 | tf_op jit(solution)/shard_map/all_gather | solution.py:155
  54.6 3.3 %convolution_multiply_fusion = f32[72,512]{1,0:T(8,128)S(1)} fusion(f32[512,1024]{1,0:T(8,128)} %bitcast.23, f32[72,512]{1,0:T(8,128)S(1)} %convolution_divide_fusion, f32[512]{0:T(512)S(1)} %add_multiply_fusion.2, f32[72]{0:T(128)S(1)} %broadcast_select_fusion.2), kind=kOutput, calls=%fused_computation.16 | convolution fusion | flops 227536896 | bytes 2394400 | tf_op jit(solution)/shard_map/pf,kf->pk/dot_general | solution.py:74
  57.8 6.3 %fusion.48 = (f32[72]{0:T(128)S(1)}, f32[72,9,512]{2,0,1:T(8,128)S(1)}) fusion(f32[72,512]{1,0:T(8,128)S(1)} %cosine_multiply_fusion, f32[72,512]{1,0:T(8,128)S(1)} %convolution_multiply_fusion, f32[512,1024,1]{1,0,2:T(8,128)} %bitcast.24, f32[72,9,512]{2,0,1:T(8,128)S(1)} %get-tuple-element.7, f32[72,9,512]{2,0,1:T(8,128)S(1)} %get-tuple-element.6), kind=kOutput, calls=%fused_computation.90 | convolution fusion | flops 4078522368 | bytes 6373664 | tf_op jit(solution)/shard_map/rf,kf->rk/dot_general | solution.py:69
  64.2 0.4 exponential_reduce_fusion
  64.5 5.3 %fusion.2 = f32[512,1024]{1,0:T(8,128)S(1)} fusion(f32[72,9,512]{2,0,1:T(8,128)S(1)} %get-tuple-element.7, f32[72,9,512]{2,0,1:T(8,128)S(1)} %get-tuple-element.6, f32[72,9,512]{2,0,1:T(8,128)S(1)} %get-tuple-element.13, f32[72]{0:T(128)S(1)} %fusion.36, f32[72]{0:T(128)S(1)} %log.8, f32[72]{0:T(128)S(1)} %get-tuple-element.12), kind=kOutput, calls=%fused_computation.4 | convolution fusion | flops 4078522368 | bytes 6079328 | tf_op jit(solution)/shard_map/rk,rf->kf/dot_general | solution.py:164
  69.9 0.5 multiply_reduce_fusion
  70.4 1.6 %fusion.19 = f32[512,512]{1,0:T(8,128)S(1)} fusion(f32[72,512]{1,0:T(8,128)S(1)} %get-tuple-element.2, f32[72,512]{1,0:T(8,128)S(1)} %convolution_divide_fusion, f32[512]{0:T(512)S(1)} %add_multiply_fusion.2, f32[72]{0:T(128)S(1)} %broadcast_select_fusion.2), kind=kOutput, calls=%fused_computation.37 | convolution fusion | flops 226713600 | bytes 1345824 | tf_op jit(solution)/shard_map/pk,pf->kf/dot_general | solution.py:165
  71.9 1.9 %pad_maximum_fusion = f32[512,1536]{1,0:T(8,128)} fusion(f32[512,512]{1,0:T(8,128)S(1)} %fusion.19, f32[512,1024]{1,0:T(8,128)S(1)} %fusion.2), kind=kLoop, calls=%fused_computation | loop fusion | flops 786432 | bytes 6291456 | tf_op jit(solution)/shard_map/concatenate | solution.py:168
  73.9 0.0 copy-start.3
  73.9 0.0 reduce-scatter.2.cloned.1.call-update
  73.9 0.1 multiply_reduce_fusion.2
  74.0 0.1 slice.99
  74.1 1.3 collective-permute-start.6
  75.4 0.0 copy-done.3
  75.4 1.7 %collective-permute-done.6 = f32[24,2]{0,1:T(2,128)S(1)} collective-permute-done((f32[24,2]{0,1:T(2,128)S(1)}, f32[24,2]{0,1:T(2,128)S(1)}, u32[]{:S(2)}, u32[]{:S(2)}) %collective-permute-start.6) | collective-permute-done | bytes 224 | tf_op jit(solution)/shard_map/ppermute | solution.py:21
  77.1 0.6 maximum_select_fusion.1
  77.7 61.3 %reduce-scatter.2.cloned.1.call-done = f32[32,1536]{1,0:T(8,128)} async-done(((f32[512,1536]{1,0:T(8,128)}), f32[32,1536]{1,0:T(8,128)}) %reduce-scatter.2.cloned.1.call-update) | async-done | bytes 196624 | tf_op jit(solution)/shard_map/reduce_scatter | solution.py:167
  139.0 0.8 slice_add_fusion
  139.9 1.6 %slice_divide_fusion = f32[32,1024]{1,0:T(8,128)} fusion(f32[32,1536]{1,0:T(8,128)} %reduce-scatter.2.cloned.1.call-done, f32[32,512]{1,0:T(8,128)S(1)} %slice_add_fusion), kind=kLoop, calls=%fused_computation.34 | loop fusion | flops 65536 | bytes 327680 | tf_op jit(solution)/shard_map/div | solution.py:174
  (11 shorter events, 0.1 us)
Async XLA Ops:
  7.2 26.4 %copy-start = (f32[128,512]{1,0:T(8,128)S(1)}, f32[128,512]{1,0:T(8,128)}, u32[]{:S(2)}) copy-start(f32[128,512]{1,0:T(8,128)} %param.15) | copy-start | bytes 786436
  7.2 27.6 %copy-start.2 = (s32[96,2]{0,1:T(2,128)S(1)}, s32[96,2]{0,1:T(2,128)}, u32[]{:S(2)}) copy-start(s32[96,2]{0,1:T(2,128)} %param.11) | copy-start | bytes 2308
  7.2 27.8 %copy-start.1 = (f32[96,1024]{1,0:T(8,128)S(1)}, f32[96,1024]{1,0:T(8,128)}, u32[]{:S(2)}) copy-start(f32[96,1024]{1,0:T(8,128)} %param.9) | copy-start | bytes 1179652
  7.2 27.8 %slice-start = ((f32[96,1024]{1,0:T(8,128)}), f32[48,1024]{1,0:T(8,128)S(1)}, s32[]{:S(2)}) async-start(f32[96,1024]{1,0:T(8,128)} %param.9), calls=%async_computation.3 | async-start | bytes 393216 | tf_op jit(solution)/shard_map/slice | solution.py:133
  7.2 47.3 %all-gather.2.cloned.1.call-start = ((), (), s32[]{:S(2)}) async-start(), calls=%async_computation.1 | async-start | bytes 2228224 | tf_op jit(solution)/shard_map/all_gather | solution.py:155
  7.9 131.1 %reduce-scatter.2.cloned.1.call-start = ((), (), s32[]{:S(2)}) async-start(), calls=%async_computation.2 | async-start | bytes 3342336 | tf_op jit(solution)/shard_map/reduce_scatter | solution.py:167
  8.7 22.4 %collective-permute-start = (f32[24]{0:T(128)S(1)}, f32[24]{0:T(128)S(1)}, u32[]{:S(2)}, u32[]{:S(2)}) collective-permute-start(f32[24]{0:T(128)S(1)} %slice.78), channel_id=1, source_target_pairs={{0,1},{1,2},{2,3},{3,4},{4,5},{5,6},{6,7},{7,8},{8,9},{9,10},{10,1... | collective-permute-start | bytes 296 | tf_op jit(solution)/shard_map/ppermute | solution.py:21
  11.8 20.1 %collective-permute-start.1 = (s32[24]{0:T(128)S(1)}, s32[24]{0:T(128)S(1)}, u32[]{:S(2)}, u32[]{:S(2)}) collective-permute-start(s32[24]{0:T(128)S(1)} %slice.81), channel_id=1, source_target_pairs={{0,1},{1,2},{2,3},{3,4},{4,5},{5,6},{6,7},{7,8},{8,9},{9,10},{10,1... | collective-permute-start | bytes 296 | tf_op jit(solution)/shard_map/ppermute | solution.py:21
  17.1 17.7 %collective-permute-start.3 = (s32[24,2]{0,1:T(2,128)S(1)}, s32[24,2]{0,1:T(2,128)S(1)}, u32[]{:S(2)}, u32[]{:S(2)}) collective-permute-start(s32[24,2]{0,1:T(2,128)S(1)} %slice.88), channel_id=1, source_target_pairs={{0,1},{1,2},{2,3},{3,4},{4,5},{5,6},{6,7},{7,8},{8,9},{9,10},{10,1... | collective-permute-start | bytes 584 | tf_op jit(solution)/shard_map/ppermute | solution.py:21
  19.9 15.0 %collective-permute-start.2 = (f32[24,1024]{1,0:T(8,128)S(1)}, f32[24,1024]{1,0:T(8,128)S(1)}, u32[]{:S(2)}, u32[]{:S(2)}) collective-permute-start(f32[24,1024]{1,0:T(8,128)S(1)} %slice.84), channel_id=1, source_target_pairs={{0,1},{1,2},{2,3},{3,4},{4,5},{5,6},{6,7},{7,8},{8,9},{9,10},{10,1... | collective-permute-start | bytes 294920 | tf_op jit(solution)/shard_map/ppermute | solution.py:21
  23.4 3.9 %collective-permute-start.5 = (s32[1]{0:T(128)}, s32[1]{0:T(128)}, u32[]{:S(2)}, u32[]{:S(2)}) collective-permute-start(s32[1]{0:T(128)} %param.14), channel_id=1, source_target_pairs={{0,1},{1,2},{2,3},{3,4},{4,5},{5,6},{6,7},{7,8},{8,9},{9,10},{10,1... | collective-permute-start | bytes 20 | tf_op jit(solution)/shard_map/ppermute | solution.py:21
  27.4 5.3 %collective-permute-start.4 = (s32[24]{0:T(128)S(1)}, s32[24]{0:T(128)S(1)}, u32[]{:S(2)}, u32[]{:S(2)}) collective-permute-start(s32[24]{0:T(128)S(1)} %slice.96), channel_id=1, source_target_pairs={{0,1},{1,2},{2,3},{3,4},{4,5},{5,6},{6,7},{7,8},{8,9},{9,10},{10,1... | collective-permute-start | bytes 296 | tf_op jit(solution)/shard_map/ppermute | solution.py:21
  73.9 1.5 %copy-start.3 = (f32[512]{0:T(512)S(1)}, f32[512]{0:T(512)}, u32[]{:S(2)}) copy-start(f32[512]{0:T(512)} %param.16) | copy-start | bytes 6148
  74.1 3.0 %collective-permute-start.6 = (f32[24,2]{0,1:T(2,128)S(1)}, f32[24,2]{0,1:T(2,128)S(1)}, u32[]{:S(2)}, u32[]{:S(2)}) collective-permute-start(f32[24,2]{0,1:T(2,128)S(1)} %slice.99), channel_id=1, source_target_pairs={{1,0},{2,1},{3,2},{4,3},{5,4},{6,5},{7,6},{8,7},{9,8},{10,9},{11,1... | collective-permute-start | bytes 584 | tf_op jit(solution)/shard_map/ppermute | solution.py:21
Sparse Core Ops, SparseCore 0:
  10.2 44.3 all-gather.1
  74.0 64.9 reduce-scatter.1
where the time goes:
time: 149 us; the launch traced here: 148 us
  waiting for transfers between devices  78 us (52%)
  starting transfers between devices  19.1 us (13%)
  matrix products  17.2 us (12%)
  other arithmetic  15.1 us (10%)
  between operations  14.9 us (10%)
  local copies, waits for them, and re-layouts  3.98 us (3%)
    reduce_scatter x1, waiting for transfers between devices, on_device(): lax.psum_scatter(jnp.concatenate([data_part, weight_part], axis=1), 'dom'...  61.3 us
    ppermute x7, starting transfers between devices, from_behind(): return lax.ppermute(block, axis, route)  19.1 us
    all_gather x1, waiting for transfers between devices, on_device(): piece = lax.all_gather(class_refs, 'dom', axis=0, tiled=True)  14.3 us
    dot_general x1, matrix products, block_scores(): jnp.einsum('rf,kf->rk', shifted_rows, ref_rows, precision=lax.Precision.H...  6.33 us
    dot_general x1, matrix products, on_device(): jnp.einsum('rk,rf->kf', columns, shifted_rows, precision=lax.Precision.HI...  5.34 us
    mul x1, other arithmetic, spectra(): scaled[:, None, :]  5.24 us
    dot_general x1, matrix products, block_scores(): jnp.einsum('pf,kf->pk', ctf_power, power, precision=lax.Precision.HIGHEST)  3.27 us
  transfers between devices with their start and end apart: 9, of which 3 were waited for; matrix products, arithmetic and copies ran while one was open for 10% of the time, Pallas kernels for 0%

commit v1 on v0

v1 whole, which is shorter than its diff:
```python
import math

import jax
import jax.numpy as jnp
from jax import lax
from jax.experimental import pallas as pl
from jax.experimental.pallas import tpu as pltpu
from jax.sharding import PartitionSpec as P

ROT = 16
SIDE = 3
BOX = 128
FY = 32
SHIFTS = 9
TEAM = 4
PRIOR = 2.0
CTF_SIZE = math.hypot(0.995, 0.1)
CTF_TURN = math.atan2(0.1, 0.995)
SINE = (
    9.99999976e-01,
    -1.66666476e-01,
    8.33289854e-03,
    -1.98008185e-04,
    2.59032780e-06,
)
TWO_PI = 2.0 * math.pi
PI_A = 3.140625
PI_B = 0.0009670257568359375
PI_C = math.pi - PI_A - PI_B
HIGHEST = lax.Precision.HIGHEST
GRID = tuple((t // SIDE - SIDE // 2, t % SIDE - SIDE // 2) for t in range(SHIFTS))
LIMIT = 56 * 1024 * 1024


def half_turn_sine(x):
    s = x * x
    p = SINE[4]
    for c in SINE[3::-1]:
        p = p * s + c
    return x * p


def turn_cos(turns):
    t = jnp.abs(turns - jnp.round(turns))
    return half_turn_sine(TWO_PI * (0.25 - t))


def turn_sin(turns):
    return turn_cos(turns - 0.25)


def freq_rows(width, rows):
    f = lax.broadcasted_iota(jnp.int32, (rows, width), 1)
    kx = (f // FY).astype(jnp.float32)
    ky = (f % FY - FY // 2).astype(jnp.float32)
    return kx, ky


def dot_nt(a, b):
    return lax.dot_general(
        a, b, (((1,), (1,)), ((), ())), precision=HIGHEST, preferred_element_type=jnp.float32
    )


def dot_nn(a, b):
    return lax.dot_general(
        a, b, (((1,), (0,)), ((), ())), precision=HIGHEST, preferred_element_type=jnp.float32
    )


def grid_phases(width):
    kx, ky = freq_rows(width, 1)
    out = []
    for t, (gx, gy) in enumerate(GRID):
        if t < SHIFTS // 2:
            m = (kx * gx + ky * gy) * (1.0 / BOX)
            out.append((turn_cos(m), turn_sin(m)))
    return out


def phase_of(phases, t):
    mid = SHIFTS // 2
    if t < mid:
        return phases[t]
    c, s = phases[SHIFTS - 1 - t]
    return c, -s


def score_kernel(blocks, slots, own, cnb, ynb, cynb, *rest):
    refs = rest[:blocks]
    noise, e_out, y_out, power_out, stats_out, raw, scal, sems = rest[blocks:]
    half = slots // 2
    group = slots + half
    live_rows = 2 * group
    width = own.shape[1]
    freq = width // 2
    me = lax.axis_index("dom")
    core = me % 2
    yy = (me // 2) % 2

    sources = ((own, 0, 0), (cnb, 0, 1), (ynb, 1, 0), (cynb, 1, 1))
    copies = []
    for n, (src, dy, dc) in enumerate(sources):
        y_s = (yy + dy) % 2
        c_s = (core + dc) % 2
        at = pl.multiple_of(y_s * group + c_s * slots, 8)
        low = pltpu.make_async_copy(
            src.at[pl.ds(0, half)], raw.at[pl.ds(at, half)], sems.at[n]
        )
        high = pltpu.make_async_copy(
            src.at[pl.ds(half, half)], raw.at[pl.ds(at + half, half)], sems.at[4 + n]
        )
        facts = pltpu.make_async_copy(
            src.at[pl.ds(slots, 8), pl.ds(0, 128)], scal.at[2 * y_s + c_s], sems.at[8 + n]
        )
        facts.start()
        low.start()

        @pl.when(c_s == 0)
        def _(high=high):
            high.start()

        copies.append((low, high, facts, c_s))

    inverse = 1.0 / noise[...]
    for low, high, facts, c_s in copies:
        facts.wait()

    lane = lax.broadcasted_iota(jnp.int32, (8, 128), 1)
    a, b, c, d = scal[0], scal[1], scal[2], scal[3]
    b96 = pltpu.roll(b, 96, 1)
    d112 = pltpu.roll(d, 112, 1)
    tiles = (
        jnp.where(lane < 96, a, b96),
        jnp.where(lane < 16, b96, jnp.where(lane < 112, pltpu.roll(c, 16, 1), d112)),
        jnp.where(lane < 32, d112, 0.0),
    )
    row_facts = jnp.concatenate(tiles, axis=1)[:, :live_rows]
    col_facts = jnp.concatenate(
        [jnp.concatenate([t, jnp.zeros((120, 128), jnp.float32)], axis=0).T for t in tiles], axis=0
    )[:live_rows]
    focus = col_facts[:, 0:1]
    off_x = col_facts[:, 1:2]
    off_y = col_facts[:, 2:3]
    group_col = col_facts[:, 4:5]

    total = noise.shape[0]
    onehot = (
        group_col == lax.broadcasted_iota(jnp.int32, (live_rows, total), 1).astype(jnp.float32)
    ).astype(jnp.float32)
    noise_rows = dot_nn(onehot, inverse)

    kx, ky = freq_rows(freq, 1)
    chi = focus * ((kx * kx + ky * ky) * (1.0 / 1024.0))
    k = jnp.round(chi * (1.0 / math.pi))
    rest_angle = ((chi - k * PI_A) - k * PI_B) - k * PI_C
    shifted_angle = rest_angle + CTF_TURN
    over = shifted_angle > (0.5 * math.pi)
    folded = jnp.where(over, math.pi - shifted_angle, shifted_angle)
    parity = 0.5 * k
    sign = (parity - jnp.floor(parity)) * (4.0 * CTF_SIZE) - CTF_SIZE
    ctf = half_turn_sine(folded) * sign
    scaled = ctf * noise_rows
    power = ctf * scaled
    power_out[...] = power

    kx0, ky0 = freq_rows(128, 1)
    m = (kx0 * off_x + ky0 * off_y) * (1.0 / BOX)
    pc, ps = turn_cos(m), turn_sin(m)
    step = off_x * ((128 // FY) / BOX) + jnp.zeros((live_rows, 128), jnp.float32)
    sc, ss = turn_cos(step), turn_sin(step)
    cos_parts, sin_parts = [], []
    for _ in range(freq // 128):
        cos_parts.append(pc)
        sin_parts.append(ps)
        pc, ps = pc * sc - ps * ss, ps * sc + pc * ss
    cosine = jnp.concatenate(cos_parts, axis=1) * scaled
    sine = jnp.concatenate(sin_parts, axis=1) * scaled

    for low, high, facts, c_s in copies:
        low.wait()

        @pl.when(c_s == 0)
        def _(high=high):
            high.wait()

    xr = raw[:, :freq]
    xi = raw[:, freq:]
    y_out[:, :freq] = xr * cosine - xi * sine
    y_out[:, freq:] = xr * sine + xi * cosine

    per = refs[0].shape[0]
    r = (lax.broadcasted_iota(jnp.int32, (per, live_rows), 0) % ROT).astype(jnp.float32)
    prior = PRIOR * turn_cos((r - row_facts[3:4, :]) * (1.0 / ROT))
    phases = grid_phases(freq)
    y = y_out[...]
    high = None
    for n in range(blocks):
        rr = refs[n][:, :freq]
        ri = refs[n][:, freq:]
        quad = dot_nt(rr * rr + ri * ri, power)
        base = prior - 0.5 * quad
        rows = []
        for t in range(SHIFTS):
            if t == SHIFTS // 2:
                rows.append(refs[n][...])
            else:
                cg, sg = phase_of(phases, t)
                rows.append(jnp.concatenate([rr * cg + ri * sg, ri * cg - rr * sg], axis=1))
        score = dot_nt(jnp.concatenate(rows, axis=0), y)
        score = score.reshape(SHIFTS, per, live_rows) + base[None]
        e_out[n] = score
        top = jnp.max(score, axis=0)
        high = top if high is None else jnp.maximum(high, top)
    high = jnp.max(high, axis=0, keepdims=True)
    sums = [jnp.zeros((per, live_rows), jnp.float32) for _ in range(SHIFTS)]
    for n in range(blocks):
        for t in range(SHIFTS):
            e = jnp.exp(e_out[n, t] - high)
            e_out[n, t] = e
            sums[t] = sums[t] + e
    sums = [jnp.sum(s, axis=0, keepdims=True) for s in sums]
    mass = sum(sums)
    mean_x = sum(s * float(gx) for s, (gx, gy) in zip(sums, GRID) if gx)
    mean_y = sum(s * float(gy) for s, (gx, gy) in zip(sums, GRID) if gy)
    stats_out[...] = jnp.zeros_like(stats_out)
    stats_out[0:1, :live_rows] = high
    stats_out[1:2, :live_rows] = mass
    stats_out[2:3, :live_rows] = mean_x
    stats_out[3:4, :live_rows] = mean_y
    stats_out[4:5, :live_rows] = row_facts[5:6, :]


def sum_kernel(stats_own, stats_all, e_ref, y_ref, power_ref, part_out, shift_out):
    live_rows, width = y_ref.shape
    freq = width // 2
    mine = stats_own[:, :live_rows]
    team = [stats_all[n][:, :live_rows] for n in range(TEAM)]
    top = team[0][0:1]
    for s in team[1:]:
        top = jnp.maximum(top, s[0:1])
    gains = [jnp.exp(s[0:1] - top) for s in team]
    mass = sum(g * s[1:2] for g, s in zip(gains, team))
    live = mine[4:5] / mass
    own_gain = jnp.exp(mine[0:1] - top) * live
    shift_out[...] = jnp.zeros_like(shift_out)
    shift_out[0:1, :live_rows] = sum(g * s[2:3] for g, s in zip(gains, team)) * live
    shift_out[1:2, :live_rows] = sum(g * s[3:4] for g, s in zip(gains, team)) * live
    per = e_ref.shape[1]
    w = e_ref[...] * own_gain[None]
    flat = dot_nn(w.reshape(SHIFTS * per, live_rows), y_ref[...])
    phases = grid_phases(freq)
    mid = SHIFTS // 2
    re = flat[mid * per : (mid + 1) * per, :freq]
    im = flat[mid * per : (mid + 1) * per, freq:]
    for t in range(SHIFTS):
        if t == mid:
            continue
        cg, sg = phase_of(phases, t)
        ar = flat[t * per : (t + 1) * per, :freq]
        ai = flat[t * per : (t + 1) * per, freq:]
        re = re + (ar * cg - ai * sg)
        im = im + (ar * sg + ai * cg)
    part_out[:, :freq] = re
    part_out[:, freq:width] = im
    part_out[:, width:] = dot_nn(jnp.sum(w, axis=0), power_ref[...])


def final_kernel(own, others, signal, out):
    width = out.shape[1]
    freq = width // 2
    total = own[...]
    for n in range(others.shape[0]):
        total = total + others[n]
    denominator = total[:, width:] + 1.0 / signal[...]
    out[:, :freq] = total[:, :freq] / denominator
    out[:, freq:] = total[:, freq:width] / denominator


def params():
    return pltpu.CompilerParams(vmem_limit_bytes=LIMIT)


def crossed(block, mask):
    size = lax.axis_size("dom")
    return lax.ppermute(block, "dom", [(i, i ^ mask) for i in range(size)])


def on_device(
    particle_fourier,
    defocus,
    particle_offset,
    prior_rotation,
    group_id,
    live_count,
    noise_power,
    signal_power,
    class_refs,
):
    slots, width = particle_fourier.shape
    freq = width // 2
    live_rows = 3 * slots
    size = lax.axis_size("dom")
    blocks = size // TEAM
    refs_own = class_refs.reshape(-1, width)
    per = refs_own.shape[0]

    live = (jnp.arange(slots, dtype=jnp.int32) < live_count[0]).astype(jnp.float32)
    facts = jnp.stack(
        [
            defocus,
            particle_offset[:, 0].astype(jnp.float32),
            particle_offset[:, 1].astype(jnp.float32),
            prior_rotation.astype(jnp.float32),
            group_id.astype(jnp.float32),
            live,
        ]
    )
    facts = jnp.pad(facts, ((0, 2), (0, width - slots)))
    packed = jnp.concatenate([particle_fourier, facts], axis=0)
    ynb = crossed(packed, 2)
    cnb = crossed(packed, 1)
    refs = [refs_own] + [crossed(refs_own, TEAM * n) for n in range(1, blocks)]
    cynb = crossed(ynb, 1)

    anywhere = pl.BlockSpec(memory_space=pl.ANY)
    vmem = pl.BlockSpec(memory_space=pltpu.VMEM)
    f32 = jnp.float32
    e_all, y, power, stats = pl.pallas_call(
        lambda *a: score_kernel(blocks, slots, *a),
        out_shape=(
            jax.ShapeDtypeStruct((blocks, SHIFTS, per, live_rows), f32),
            jax.ShapeDtypeStruct((live_rows, width), f32),
            jax.ShapeDtypeStruct((live_rows, freq), f32),
            jax.ShapeDtypeStruct((8, 384), f32),
        ),
        in_specs=[anywhere] * 4 + [vmem] * (blocks + 1),
        out_specs=(vmem,) * 4,
        scratch_shapes=[
            pltpu.VMEM((live_rows, width), f32),
            pltpu.VMEM((4, 8, 128), f32),
            pltpu.SemaphoreType.DMA((12,)),
        ],
        compiler_params=params(),
        name="scores",
    )(packed, cnb, ynb, cynb, *refs, noise_power)

    teams = [[TEAM * n + j for j in range(TEAM)] for n in range(blocks)]
    stats_all = lax.all_to_all(
        jnp.broadcast_to(stats[None], (TEAM, 8, 384)),
        "dom",
        0,
        0,
        axis_index_groups=teams,
        tiled=True,
    )

    def sums(n):
        return pl.pallas_call(
            sum_kernel,
            grid=(1,),
            out_shape=(
                jax.ShapeDtypeStruct((per, width + freq), f32),
                jax.ShapeDtypeStruct((8, 384), f32),
            ),
            in_specs=[
                pl.BlockSpec((8, 384), lambda i: (0, 0)),
                pl.BlockSpec((TEAM, 8, 384), lambda i: (0, 0, 0)),
                pl.BlockSpec((None, SHIFTS, per, live_rows), lambda i: (n, 0, 0, 0)),
                pl.BlockSpec((live_rows, width), lambda i: (0, 0)),
                pl.BlockSpec((live_rows, freq), lambda i: (0, 0)),
            ],
            out_specs=(
                pl.BlockSpec((per, width + freq), lambda i: (0, 0)),
                pl.BlockSpec((8, 384), lambda i: (0, 0)),
            ),
            compiler_params=params(),
            name="sums",
        )(stats, stats_all, e_all, y, power)

    arrived = []
    for n in sorted(range(1, blocks), key=lambda n: -n):
        part, _ = sums(n)
        arrived.append(crossed(part, TEAM * n))
    own_part, shift_rows = sums(0)

    refs_new = pl.pallas_call(
        final_kernel,
        out_shape=jax.ShapeDtypeStruct((per, width), f32),
        in_specs=[vmem] * 3,
        out_specs=vmem,
        compiler_params=params(),
        name="update",
    )(own_part, jnp.stack(arrived), signal_power.reshape(1, freq))

    me = lax.axis_index("dom")
    half = slots // 2
    at = (me // 2) % 2 * (slots + half) + me % 2 * slots
    at = jnp.minimum(at, live_rows - half)
    low = lax.dynamic_slice(shift_rows, (0, at), (2, half))
    high = lax.dynamic_slice(shift_rows, (0, at + half), (2, half))
    high = jnp.where(me % 2 == 0, high, 0.0)
    expected = jnp.concatenate([low, high], axis=1).T
    return (expected, refs_new.reshape(class_refs.shape))


def solution(mesh):
    in_specs = (
        P(("groups", "dom"), None),
        P(("groups", "dom")),
        P(("groups", "dom"), None),
        P(("groups", "dom")),
        P(("groups", "dom")),
        P(("groups", "dom")),
        P("groups", None),
        P("groups"),
        P(("groups", "dom"), None, None),
    )
    out_specs = (P(("groups", "dom"), None), P(("groups", "dom"), None, None))
    return jax.shard_map(
        on_device, mesh=mesh, in_specs=in_specs, out_specs=out_specs, check_vma=False
    )
```

time: 149 us -> 90.4 us (0.61)
  waiting for transfers between devices: 78 us -> 28.1 us
  Pallas kernels: 0 us -> 35.9 us
  matrix products: 17.2 us -> 0 us
  between operations: 14.9 us -> 1.43 us
  other arithmetic: 15.1 us -> 4.84 us
  starting transfers between devices: 19.1 us -> 15.3 us
    reduce_scatter x1 -> x0, waiting for transfers between devices: 61.3 us -> none  [on_device(): lax.psum_scatter(jnp.concatenate([data_part, weight_part], axis=1), 'dom'...]
    pallas_call x0 -> x6, Pallas kernels: none -> 35.9 us  [the longest x4 19.1 us: sums(): pl.pallas_call(sum_kernel, grid=(1,), out_shape=(jax.ShapeDtypeStruct((pe...]
    ppermute x7 -> x9, waiting for transfers between devices: 1.73 us -> 24.2 us  [crossed(): return lax.ppermute(block, 'dom', [(i, i ^ mask) for i in range(size)])]
    dot_general x5 -> x0, matrix products: 17.2 us -> none  [the longest x1 6.33 us: block_scores(): jnp.einsum('rf,kf->rk', shifted_rows, ref_rows, precision=lax.Precision.H...]
    all_gather x1 -> x0, waiting for transfers between devices: 14.3 us -> none  [on_device(): piece = lax.all_gather(class_refs, 'dom', axis=0, tiled=True)]
    ppermute x7 -> x9, starting transfers between devices: 19.1 us -> 11.8 us  [crossed(): return lax.ppermute(block, 'dom', [(i, i ^ mask) for i in range(size)])]
    mul x3 -> x0, other arithmetic: 5.83 us -> none  [the longest x1 5.24 us: spectra(): scaled[:, None, :]]
    all_to_all x0 -> x1, waiting for transfers between devices: none -> 3.95 us  [on_device(): lax.all_to_all(jnp.broadcast_to(stats[None], (TEAM, 8, 384)), 'dom', 0, 0...]
  transfers between devices with their start and end apart: 9 -> 10, of which waited for: 3 -> 6; matrix products, arithmetic and copies ran while one was open for 10% -> 2% of each run, Pallas kernels for 0% -> 16%
where the time goes in v1:
time: 90.4 us; the launch traced here: 89.8 us
  Pallas kernels  35.9 us (40%)
  waiting for transfers between devices  28.1 us (31%)
  starting transfers between devices  15.3 us (17%)
  other arithmetic  4.84 us (5%)
  local copies, waits for them, and re-layouts  4.2 us (5%)
  between operations  1.43 us (2%)
    ppermute x9, waiting for transfers between devices, crossed(): return lax.ppermute(block, 'dom', [(i, i ^ mask) for i in range(size)])  24.2 us
    pallas_call x4, Pallas kernels, sums(): pl.pallas_call(sum_kernel, grid=(1,), out_shape=(jax.ShapeDtypeStruct((pe...  19.1 us
    pallas_call x1, Pallas kernels, on_device(): pl.pallas_call(lambda *a: score_kernel(blocks, slots, *a), out_shape=(jax...  15 us
    ppermute x9, starting transfers between devices, crossed(): return lax.ppermute(block, 'dom', [(i, i ^ mask) for i in range(size)])  11.8 us
    all_to_all x1, waiting for transfers between devices, on_device(): lax.all_to_all(jnp.broadcast_to(stats[None], (TEAM, 8, 384)), 'dom', 0, 0...  3.95 us
    all_to_all x1, starting transfers between devices, on_device(): lax.all_to_all(jnp.broadcast_to(stats[None], (TEAM, 8, 384)), 'dom', 0, 0...  3.45 us
    unnamed x16, local copies, waits for them, and re-layouts  2.2 us
  transfers between devices with their start and end apart: 10, of which 6 were waited for; matrix products, arithmetic and copies ran while one was open for 2% of the time, Pallas kernels for 16%

profile of v1, /device:TPU:0, one launch (start us, length us, event | category | flops | bytes accessed | tf_op | source)
XLA Modules:
  0.0 89.8 jit_solution(10051924089258058112)
XLA Ops:
  0.6 0.8 convert_bitcast_fusion.2
  2.1 0.7 convert_bitcast_fusion
  2.7 0.7 stack.30
  3.4 1.0 %select_maximum_fusion.a_0_ = f32[104,1024]{1,0:T(8,128)S(1)} fusion(f32[6,96]{1,0:T(8,128)S(1)} %stack.30, f32[96,1024]{1,0:T(8,128)} %param.9), kind=kLoop, calls=%fused_computation.1 | loop fusion | flops 319488 | bytes 821504 | tf_op jit(solution)/shard_map/concatenate | solution.py:320
  4.4 0.0 copy-start
  4.4 3.0 %collective-permute-start.1 = (f32[104,1024]{1,0:T(8,128)S(1)}, f32[104,1024]{1,0:T(8,128)S(1)}, u32[]{:S(2)}, u32[]{:S(2)}) collective-permute-start(f32[104,1024]{1,0:T(8,128)S(1)} %select_maximum_fusion.a_0_), channel_id=1, source_target_pairs={{0,2},{1,3},{2,0},{3,1},{4,6},{5,7},{6,4},{7,5},{8,10},{9,11},{10,... | collective-permute-start | bytes 1277960 | tf_op jit(solution)/shard_map/ppermute | solution.py:286
  7.5 0.0 collective-permute-start
  7.5 9.8 %collective-permute-done.1.a_2_ = f32[104,1024]{1,0:T(8,128)S(1)} collective-permute-done((f32[104,1024]{1,0:T(8,128)S(1)}, f32[104,1024]{1,0:T(8,128)S(1)}, u32[]{:S(2)}, u32[]{:S(2)}) %collective-permute-start.1) | collective-permute-done | bytes 426016 | tf_op jit(solution)/shard_map/ppermute | solution.py:286
  17.3 0.0 copy-start.2
  17.3 0.0 collective-permute-start.2
  17.3 1.8 %collective-permute-start.3 = (f32[32,1024]{1,0:T(8,128)}, f32[32,1024]{1,0:T(8,128)S(1)}, u32[]{:S(2)}, u32[]{:S(2)}) collective-permute-start(f32[32,1024]{1,0:T(8,128)} %bitcast.22), channel_id=1, source_target_pairs={{0,4},{1,5},{2,6},{3,7},{4,0},{5,1},{6,2},{7,3},{8,12},{9,13},{10,... | collective-permute-start | bytes 393224 | tf_op jit(solution)/shard_map/ppermute | solution.py:286
  19.1 2.6 %collective-permute-start.4 = (f32[32,1024]{1,0:T(8,128)}, f32[32,1024]{1,0:T(8,128)S(1)}, u32[]{:S(2)}, u32[]{:S(2)}) collective-permute-start(f32[32,1024]{1,0:T(8,128)} %bitcast.23), channel_id=1, source_target_pairs={{0,8},{1,9},{2,10},{3,11},{4,12},{5,13},{6,14},{7,15},{8,0},{9,1},... | collective-permute-start | bytes 393224 | tf_op jit(solution)/shard_map/ppermute | solution.py:286
  21.7 0.0 collective-permute-start.5
  21.7 4.1 %collective-permute-done.3.a_5_ = f32[32,1024]{1,0:T(8,128)S(1)} collective-permute-done((f32[32,1024]{1,0:T(8,128)}, f32[32,1024]{1,0:T(8,128)S(1)}, u32[]{:S(2)}, u32[]{:S(2)}) %collective-permute-start.3) | collective-permute-done | bytes 131104 | tf_op jit(solution)/shard_map/ppermute | solution.py:286
  25.7 0.0 copy-start.5
  25.7 6.5 %collective-permute-done.4.a_6_ = f32[32,1024]{1,0:T(8,128)S(1)} collective-permute-done((f32[32,1024]{1,0:T(8,128)}, f32[32,1024]{1,0:T(8,128)S(1)}, u32[]{:S(2)}, u32[]{:S(2)}) %collective-permute-start.4) | collective-permute-done | bytes 131104 | tf_op jit(solution)/shard_map/ppermute | solution.py:286
  32.2 0.0 copy-start.6
  32.2 0.0 collective-permute-done.5.a_7_
  32.2 0.0 copy-start.7
  32.2 0.0 collective-permute-done.a_1_
  32.2 0.0 copy-start.3
  32.2 0.0 collective-permute-done.2.a_3_
  32.2 0.0 copy-done
  32.2 0.0 copy-done.2
  32.3 0.0 copy-done.5
  32.3 0.6 copy-done.6
  32.9 0.0 copy-done.7
  32.9 0.1 copy-done.3
  33.1 0.0 copy-start.4
  33.1 0.8 copy-done.4
  33.8 15.0 %scores.1 = (f32[4,9,32,288]{3,2,1,0:T(8,128)}, f32[288,1024]{1,0:T(8,128)}, f32[288,512]{1,0:T(8,128)}, f32[8,384]{1,0:T(8,128)}) custom-call(f32[104,1024]{1,0:T(8,128)} %copy-done, f32[104,1024]{1,0:T(8,128)} %copy-done.3, f32[104,1024]{1,0:T(8,128)} %copy-done.2, f32[104,1024]{1,0:T(8,128)} %copy-done.4, f32[32,1024]{1,0:T(8,128)} %bitcast.25, ...), custom_call_target="tpu_custom_call" | custom-call | tf_op jit(solution)/shard_map/scores/pallas_call | solution.py:329
  48.9 1.3 %broadcast_in_dim.10 = f32[4,8,384]{2,1,0:T(8,128)} broadcast(f32[8,384]{1,0:T(8,128)} %get-tuple-element.11.stats_own), dimensions={1,2} | broadcast | bytes 61440 | tf_op jit(solution)/shard_map/broadcast_in_dim | solution.py:350
  50.2 3.5 %all-to-all-start = ((f32[4,8,384]{2,1,0:T(8,128)}), f32[4,8,384]{2,1,0:T(8,128)S(1)}, u32[]{:S(2)}, u32[]{:S(2)}) async-start(f32[4,8,384]{2,1,0:T(8,128)} %broadcast_in_dim.10), calls=%async_computation | async-start | bytes 98304 | tf_op jit(solution)/shard_map/all_to_all | solution.py:349
  53.7 3.9 %all-to-all-done.stats_all = f32[4,8,384]{2,1,0:T(8,128)S(1)} async-done(((f32[4,8,384]{2,1,0:T(8,128)}), f32[4,8,384]{2,1,0:T(8,128)S(1)}, u32[]{:S(2)}, u32[]{:S(2)}) %all-to-all-start) | async-done | bytes 49184 | tf_op jit(solution)/shard_map/all_to_all | solution.py:349
  57.7 0.0 copy-start.1
  57.7 0.6 copy-done.1
  58.3 4.8 %sums.5 = (f32[32,1536]{1,0:T(8,128)}, f32[8,384]{1,0:T(8,128)}) custom-call(f32[8,384]{1,0:T(8,128)} %get-tuple-element.11.stats_own, f32[4,8,384]{2,1,0:T(8,128)} %copy-done.1, f32[4,9,32,288]{3,2,1,0:T(8,128)} %get-tuple-element.12.e_ref, f32[288,1024]{1,0:T(8,128)} %get-tuple-element.13.y_ref, f32[288,512]{1,0:T(8,128)} %get-tuple-element.14.power_ref), custom_call_target="tpu_custom_call" | custom-call | tf_op jit(solution)/shard_map/sums/pallas_call | solution.py:359
  63.1 2.5 %collective-permute-start.6 = (f32[32,1536]{1,0:T(8,128)}, f32[32,1536]{1,0:T(8,128)S(1)}, u32[]{:S(2)}, u32[]{:S(2)}) collective-permute-start(f32[32,1536]{1,0:T(8,128)} %get-tuple-element.17), channel_id=1, source_target_pairs={{0,12},{1,13},{2,14},{3,15},{4,8},{5,9},{6,10},{7,11},{8,4},{9,5},... | collective-permute-start | bytes 589832 | tf_op jit(solution)/shard_map/ppermute | solution.py:286
  65.6 4.8 %sums.6 = (f32[32,1536]{1,0:T(8,128)}, f32[8,384]{1,0:T(8,128)}) custom-call(f32[8,384]{1,0:T(8,128)} %get-tuple-element.11.stats_own, f32[4,8,384]{2,1,0:T(8,128)} %copy-done.1, f32[4,9,32,288]{3,2,1,0:T(8,128)} %get-tuple-element.12.e_ref, f32[288,1024]{1,0:T(8,128)} %get-tuple-element.13.y_ref, f32[288,512]{1,0:T(8,128)} %get-tuple-element.14.power_ref), custom_call_target="tpu_custom_call" | custom-call | tf_op jit(solution)/shard_map/sums/pallas_call | solution.py:359
  70.3 1.6 %collective-permute-start.7 = (f32[32,1536]{1,0:T(8,128)}, f32[32,1536]{1,0:T(8,128)S(1)}, u32[]{:S(2)}, u32[]{:S(2)}) collective-permute-start(f32[32,1536]{1,0:T(8,128)} %get-tuple-element.18), channel_id=1, source_target_pairs={{0,8},{1,9},{2,10},{3,11},{4,12},{5,13},{6,14},{7,15},{8,0},{9,1},... | collective-permute-start | bytes 589832 | tf_op jit(solution)/shard_map/ppermute | solution.py:286
  72.0 4.8 %sums.7 = (f32[32,1536]{1,0:T(8,128)}, f32[8,384]{1,0:T(8,128)}) custom-call(f32[8,384]{1,0:T(8,128)} %get-tuple-element.11.stats_own, f32[4,8,384]{2,1,0:T(8,128)} %copy-done.1, f32[4,9,32,288]{3,2,1,0:T(8,128)} %get-tuple-element.12.e_ref, f32[288,1024]{1,0:T(8,128)} %get-tuple-element.13.y_ref, f32[288,512]{1,0:T(8,128)} %get-tuple-element.14.power_ref), custom_call_target="tpu_custom_call" | custom-call | tf_op jit(solution)/shard_map/sums/pallas_call | solution.py:359
  76.7 0.3 collective-permute-start.8
  77.0 4.8 %sums.4 = (f32[32,1536]{1,0:T(8,128)}, f32[8,384]{1,0:T(8,128)}) custom-call(f32[8,384]{1,0:T(8,128)} %get-tuple-element.11.stats_own, f32[4,8,384]{2,1,0:T(8,128)} %copy-done.1, f32[4,9,32,288]{3,2,1,0:T(8,128)} %get-tuple-element.12.e_ref, f32[288,1024]{1,0:T(8,128)} %get-tuple-element.13.y_ref, f32[288,512]{1,0:T(8,128)} %get-tuple-element.14.power_ref), custom_call_target="tpu_custom_call" | custom-call | tf_op jit(solution)/shard_map/sums/pallas_call | solution.py:359
  81.8 0.8 constant_dynamic-slice_fusion
  82.6 0.6 maximum_bitcast_fusion
  83.3 0.0 collective-permute-done.6
  83.3 1.1 %collective-permute-done.7 = f32[32,1536]{1,0:T(8,128)S(1)} collective-permute-done((f32[32,1536]{1,0:T(8,128)}, f32[32,1536]{1,0:T(8,128)S(1)}, u32[]{:S(2)}, u32[]{:S(2)}) %collective-permute-start.7) | collective-permute-done | bytes 196640 | tf_op jit(solution)/shard_map/ppermute | solution.py:286
  84.3 2.8 %collective-permute-done.8 = f32[32,1536]{1,0:T(8,128)S(1)} collective-permute-done((f32[32,1536]{1,0:T(8,128)}, f32[32,1536]{1,0:T(8,128)S(1)}, u32[]{:S(2)}, u32[]{:S(2)}) %collective-permute-start.8) | collective-permute-done | bytes 196640 | tf_op jit(solution)/shard_map/ppermute | solution.py:286
  87.1 0.9 pad_maximum_fusion.others
  88.0 1.8 %update.1 = f32[32,1024]{1,0:T(8,128)} custom-call(f32[32,1536]{1,0:T(8,128)} %get-tuple-element.16.own, f32[3,32,1536]{2,1,0:T(8,128)} %pad_maximum_fusion.others, f32[1,512]{1,0:T(1,128)} %bitcast.27), custom_call_target="tpu_custom_call" | custom-call | tf_op jit(solution)/shard_map/update/pallas_call | solution.py:387
  (1 shorter events, 0.0 us)
Async XLA Ops:
  4.4 27.8 %copy-start = (f32[104,1024]{1,0:T(8,128)}, f32[104,1024]{1,0:T(8,128)S(1)}, u32[]{:S(2)}) copy-start(f32[104,1024]{1,0:T(8,128)S(1)} %select_maximum_fusion.a_0_) | copy-start | bytes 1277956
  4.4 12.8 %collective-permute-start.1 = (f32[104,1024]{1,0:T(8,128)S(1)}, f32[104,1024]{1,0:T(8,128)S(1)}, u32[]{:S(2)}, u32[]{:S(2)}) collective-permute-start(f32[104,1024]{1,0:T(8,128)S(1)} %select_maximum_fusion.a_0_), channel_id=1, source_target_pairs={{0,2},{1,3},{2,0},{3,1},{4,6},{5,7},{6,4},{7,5},{8,10},{9,11},{10,... | collective-permute-start | bytes 1277960 | tf_op jit(solution)/shard_map/ppermute | solution.py:286
  7.5 24.7 %collective-permute-start = (f32[104,1024]{1,0:T(8,128)S(1)}, f32[104,1024]{1,0:T(8,128)S(1)}, u32[]{:S(2)}, u32[]{:S(2)}) collective-permute-start(f32[104,1024]{1,0:T(8,128)S(1)} %select_maximum_fusion.a_0_), channel_id=1, source_target_pairs={{0,1},{1,0},{2,3},{3,2},{4,5},{5,4},{6,7},{7,6},{8,9},{9,8},{10,11... | collective-permute-start | bytes 1277960 | tf_op jit(solution)/shard_map/ppermute | solution.py:286
  17.3 15.0 %copy-start.2 = (f32[104,1024]{1,0:T(8,128)}, f32[104,1024]{1,0:T(8,128)S(1)}, u32[]{:S(2)}) copy-start(f32[104,1024]{1,0:T(8,128)S(1)} %collective-permute-done.1.a_2_) | copy-start | bytes 1277956
  17.3 14.9 %collective-permute-start.2 = (f32[104,1024]{1,0:T(8,128)S(1)}, f32[104,1024]{1,0:T(8,128)S(1)}, u32[]{:S(2)}, u32[]{:S(2)}) collective-permute-start(f32[104,1024]{1,0:T(8,128)S(1)} %collective-permute-done.1.a_2_), channel_id=1, source_target_pairs={{0,1},{1,0},{2,3},{3,2},{4,5},{5,4},{6,7},{7,6},{8,9},{9,8},{10,11... | collective-permute-start | bytes 1277960 | tf_op jit(solution)/shard_map/ppermute | solution.py:286
  17.3 8.4 %collective-permute-start.3 = (f32[32,1024]{1,0:T(8,128)}, f32[32,1024]{1,0:T(8,128)S(1)}, u32[]{:S(2)}, u32[]{:S(2)}) collective-permute-start(f32[32,1024]{1,0:T(8,128)} %bitcast.22), channel_id=1, source_target_pairs={{0,4},{1,5},{2,6},{3,7},{4,0},{5,1},{6,2},{7,3},{8,12},{9,13},{10,... | collective-permute-start | bytes 393224 | tf_op jit(solution)/shard_map/ppermute | solution.py:286
  19.1 13.1 %collective-permute-start.4 = (f32[32,1024]{1,0:T(8,128)}, f32[32,1024]{1,0:T(8,128)S(1)}, u32[]{:S(2)}, u32[]{:S(2)}) collective-permute-start(f32[32,1024]{1,0:T(8,128)} %bitcast.23), channel_id=1, source_target_pairs={{0,8},{1,9},{2,10},{3,11},{4,12},{5,13},{6,14},{7,15},{8,0},{9,1},... | collective-permute-start | bytes 393224 | tf_op jit(solution)/shard_map/ppermute | solution.py:286
  21.7 10.5 %collective-permute-start.5 = (f32[32,1024]{1,0:T(8,128)}, f32[32,1024]{1,0:T(8,128)S(1)}, u32[]{:S(2)}, u32[]{:S(2)}) collective-permute-start(f32[32,1024]{1,0:T(8,128)} %bitcast.24), channel_id=1, source_target_pairs={{0,12},{1,13},{2,14},{3,15},{4,8},{5,9},{6,10},{7,11},{8,4},{9,5},... | collective-permute-start | bytes 393224 | tf_op jit(solution)/shard_map/ppermute | solution.py:286
  25.7 6.5 %copy-start.5 = (f32[32,1024]{1,0:T(8,128)}, f32[32,1024]{1,0:T(8,128)S(1)}, u32[]{:S(2)}) copy-start(f32[32,1024]{1,0:T(8,128)S(1)} %collective-permute-done.3.a_5_) | copy-start | bytes 393220
  32.2 0.7 copy-start.6
  32.2 0.7 copy-start.7
  32.2 0.8 copy-start.3
  33.1 0.8 copy-start.4
  50.2 7.5 %all-to-all-start = ((f32[4,8,384]{2,1,0:T(8,128)}), f32[4,8,384]{2,1,0:T(8,128)S(1)}, u32[]{:S(2)}, u32[]{:S(2)}) async-start(f32[4,8,384]{2,1,0:T(8,128)} %broadcast_in_dim.10), calls=%async_computation | async-start | bytes 98304 | tf_op jit(solution)/shard_map/all_to_all | solution.py:349
  57.7 0.6 copy-start.1
  63.1 20.2 %collective-permute-start.6 = (f32[32,1536]{1,0:T(8,128)}, f32[32,1536]{1,0:T(8,128)S(1)}, u32[]{:S(2)}, u32[]{:S(2)}) collective-permute-start(f32[32,1536]{1,0:T(8,128)} %get-tuple-element.17), channel_id=1, source_target_pairs={{0,12},{1,13},{2,14},{3,15},{4,8},{5,9},{6,10},{7,11},{8,4},{9,5},... | collective-permute-start | bytes 589832 | tf_op jit(solution)/shard_map/ppermute | solution.py:286
  70.3 14.0 %collective-permute-start.7 = (f32[32,1536]{1,0:T(8,128)}, f32[32,1536]{1,0:T(8,128)S(1)}, u32[]{:S(2)}, u32[]{:S(2)}) collective-permute-start(f32[32,1536]{1,0:T(8,128)} %get-tuple-element.18), channel_id=1, source_target_pairs={{0,8},{1,9},{2,10},{3,11},{4,12},{5,13},{6,14},{7,15},{8,0},{9,1},... | collective-permute-start | bytes 589832 | tf_op jit(solution)/shard_map/ppermute | solution.py:286
  76.7 10.4 %collective-permute-start.8 = (f32[32,1536]{1,0:T(8,128)}, f32[32,1536]{1,0:T(8,128)S(1)}, u32[]{:S(2)}, u32[]{:S(2)}) collective-permute-start(f32[32,1536]{1,0:T(8,128)} %get-tuple-element.19), channel_id=1, source_target_pairs={{0,4},{1,5},{2,6},{3,7},{4,0},{5,1},{6,2},{7,3},{8,12},{9,13},{10,... | collective-permute-start | bytes 589832 | tf_op jit(solution)/shard_map/ppermute | solution.py:286

commit v2 on v1

v2 whole, which is shorter than its diff:
```python
import math

import jax
import jax.numpy as jnp
from jax import lax
from jax.experimental import pallas as pl
from jax.experimental.pallas import tpu as pltpu
from jax.sharding import PartitionSpec as P

ROT = 16
SIDE = 3
BOX = 128
FY = 32
SHIFTS = 9
TEAM = 4
PRIOR = 2.0
CTF_SIZE = math.hypot(0.995, 0.1)
CTF_TURN = math.atan2(0.1, 0.995)
SINE = (
    9.99999976e-01,
    -1.66666476e-01,
    8.33289854e-03,
    -1.98008185e-04,
    2.59032780e-06,
)
TWO_PI = 2.0 * math.pi
PI_A = 3.140625
PI_B = 0.0009670257568359375
PI_C = math.pi - PI_A - PI_B
HIGHEST = lax.Precision.HIGHEST
GRID = tuple((t // SIDE - SIDE // 2, t % SIDE - SIDE // 2) for t in range(SHIFTS))


def half_turn_sine(x):
    s = x * x
    p = SINE[4]
    for c in SINE[3::-1]:
        p = p * s + c
    return x * p


def turn_cos(turns):
    t = jnp.abs(turns - jnp.round(turns))
    return half_turn_sine(TWO_PI * (0.25 - t))


def turn_sin(turns):
    return turn_cos(turns - 0.25)


def freq_rows(width, rows):
    f = lax.broadcasted_iota(jnp.int32, (rows, width), 1)
    kx = (f // FY).astype(jnp.float32)
    ky = (f % FY - FY // 2).astype(jnp.float32)
    return kx, ky


def dot_nt(a, b):
    return lax.dot_general(
        a, b, (((1,), (1,)), ((), ())), preferred_element_type=jnp.float32
    )


def dot_nn(a, b):
    return lax.dot_general(
        a, b, (((1,), (0,)), ((), ())), preferred_element_type=jnp.float32
    )


def exact_dot_nn(a, b):
    return lax.dot_general(
        a, b, (((1,), (0,)), ((), ())), precision=HIGHEST, preferred_element_type=jnp.float32
    )


def halves(x):
    high = x.astype(jnp.bfloat16)
    return high, (x - high.astype(jnp.float32)).astype(jnp.bfloat16)


def deep_rows(high, low):
    rows = high.shape[0]
    main = rows // 256 * 256
    left = rows - main
    parts = [high[:main], low[:main], high[:main], high[main:], low[main:], high[main:]]
    parts.append(jnp.zeros((128 - 3 * left, high.shape[1]), high.dtype))
    return jnp.concatenate(parts, axis=0)


def deep_lanes(x):
    rows, lanes = x.shape
    main = lanes // 256 * 256
    left = lanes - main
    high, low = halves(x[:, :main])
    tail = jnp.concatenate(
        [x[:, main:], jnp.zeros((rows, 128 - left), jnp.float32)], axis=1
    )
    tail_high = tail.astype(jnp.bfloat16).astype(jnp.float32)
    tail_low = tail - tail_high
    mixed = tail_high + pltpu.roll(tail_high, left, 1) + pltpu.roll(tail_low, 2 * left, 1)
    return jnp.concatenate([high, high, low, mixed.astype(jnp.bfloat16)], axis=1)


def grid_phases(width):
    kx, ky = freq_rows(width, 1)
    out = []
    for t, (gx, gy) in enumerate(GRID):
        if t < SHIFTS // 2:
            m = (kx * gx + ky * gy) * (1.0 / BOX)
            out.append((turn_cos(m), turn_sin(m)))
    return out


def phase_of(phases, t):
    mid = SHIFTS // 2
    if t < mid:
        return phases[t]
    c, s = phases[SHIFTS - 1 - t]
    return c, -s


def facts_kernel(own_facts, ynb_facts, noise, out, rows_out):
    both, freq = out.shape[0], out.shape[1] // 3
    slots = both // 2
    first = (lax.axis_index("dom") // 2) % 2 == 0
    rows_own, rows_ynb = own_facts[...], ynb_facts[...]
    col_facts = jnp.concatenate(
        [
            jnp.concatenate([t, jnp.zeros((120, 128), jnp.float32)], axis=0).T[:slots]
            for t in (rows_own, rows_ynb)
        ],
        axis=0,
    )
    focus = col_facts[:, 0:1]
    off_x = col_facts[:, 1:2]
    off_y = col_facts[:, 2:3]
    group_col = col_facts[:, 4:5]

    total = noise.shape[0]
    onehot = (
        group_col == lax.broadcasted_iota(jnp.int32, (both, total), 1).astype(jnp.float32)
    ).astype(jnp.float32)
    noise_rows = exact_dot_nn(onehot, 1.0 / noise[...])

    kx, ky = freq_rows(freq, 1)
    chi = focus * ((kx * kx + ky * ky) * (1.0 / 1024.0))
    k = jnp.round(chi * (1.0 / math.pi))
    rest_angle = ((chi - k * PI_A) - k * PI_B) - k * PI_C
    shifted_angle = rest_angle + CTF_TURN
    over = shifted_angle > (0.5 * math.pi)
    folded = jnp.where(over, math.pi - shifted_angle, shifted_angle)
    parity = 0.5 * k
    sign = (parity - jnp.floor(parity)) * (4.0 * CTF_SIZE) - CTF_SIZE
    ctf = half_turn_sine(folded) * sign
    scaled = ctf * noise_rows
    power = ctf * scaled

    kx0, ky0 = freq_rows(128, 1)
    m = (kx0 * off_x + ky0 * off_y) * (1.0 / BOX)
    pc, ps = turn_cos(m), turn_sin(m)
    step = off_x * ((128 // FY) / BOX) + jnp.zeros((both, 128), jnp.float32)
    sc, ss = turn_cos(step), turn_sin(step)
    for n in range(freq // 128):
        part = slice(128 * n, 128 * (n + 1))
        twin = slice(freq + 128 * n, freq + 128 * (n + 1))
        out[:, part] = pc * scaled[:, part]
        out[:, twin] = ps * scaled[:, part]
        pc, ps = pc * sc - ps * ss, ps * sc + pc * ss
    out[:, 2 * freq :] = power

    lane = lax.broadcasted_iota(jnp.int32, (8, 128), 1)
    a = jnp.where(first, rows_own, rows_ynb)
    b = pltpu.roll(jnp.where(first, rows_ynb, rows_own), slots, 1)
    rows_out[:, :128] = jnp.where(lane < slots, a, b)
    rows_out[:, 128:] = b


def prepare_kernel(own, ynb, spectrum, rows, *rest):
    out = rest[-1]
    slots, width = own.shape
    freq = width // 2
    both = 2 * slots
    first = (lax.axis_index("dom") // 2) % 2 == 0
    at_own = pl.multiple_of(jnp.where(first, 0, slots), 8)
    at_ynb = pl.multiple_of(jnp.where(first, slots, 0), 8)
    for src, rows_of, at in ((own, slice(0, slots), at_own), (ynb, slice(slots, both), at_ynb)):
        to = pl.ds(at, slots)
        xr, xi = src[:, :freq], src[:, freq:]
        co, si = spectrum[rows_of, :freq], spectrum[rows_of, freq:width]
        out[to, :freq] = xr * co - xi * si
        out[to, freq:width] = xr * si + xi * co
        out[to, width:] = spectrum[rows_of, width:]
    out[both:, :256] = rows[...]
    out[both:, 256:] = jnp.zeros((8, width + freq - 256), jnp.float32)


def score_kernel(blocks, mine, other, *rest):
    refs = rest[:blocks]
    e_out, y_out, power_out, stats_out, y_high, y_low, p_high, p_low = rest[blocks:]
    width = y_high.shape[1]
    freq = width // 2
    both = mine.shape[0] - 8
    slots = both // 2
    half = slots // 2
    live_rows = both + slots
    even = lax.axis_index("dom") % 2 == 0

    def place(src, at, to, size):
        rows = slice(at, at + size)
        dest = slice(to, to + size)
        high, low = halves(src[rows, :width])
        y_high[dest] = high
        y_low[dest] = low
        high, low = halves(src[rows, width:])
        p_high[dest] = high
        p_low[dest] = low

    def place_all(heavy, light):
        place(heavy, 0, 0, both)
        place(light, 0, both, half)
        place(light, slots, both + half, half)

    @pl.when(even)
    def _():
        place_all(mine, other)

    @pl.when(jnp.logical_not(even))
    def _():
        place_all(other, mine)

    lane = lax.broadcasted_iota(jnp.int32, (8, 128), 1)
    mine0, mine1 = mine[both:, :128], mine[both:, 128:256]
    other0, other1 = other[both:, :128], other[both:, 128:256]
    a0, a1 = jnp.where(even, mine0, other0), jnp.where(even, mine1, other1)
    b0, b1 = jnp.where(even, other0, mine0), jnp.where(even, other1, mine1)
    b0_16 = pltpu.roll(b0, 16, 1)
    row_facts = jnp.concatenate(
        [
            a0,
            jnp.where(lane < 64, a1, jnp.where(lane < 112, pltpu.roll(b0, 64, 1), b0_16)),
            jnp.where(lane < 16, b0_16, pltpu.roll(b1, 16, 1)),
        ],
        axis=1,
    )[:, :live_rows]

    yh, yl = y_high[...], y_low[...]
    y_out[...] = deep_rows(yh, yl)
    ph, plow = p_high[...], p_low[...]
    power_out[...] = deep_rows(ph, plow)

    per = refs[0].shape[0]
    r = (lax.broadcasted_iota(jnp.int32, (per, live_rows), 0) % ROT).astype(jnp.float32)
    prior = PRIOR * turn_cos((r - row_facts[3:4, :]) * (1.0 / ROT))
    phases = grid_phases(freq)
    high = None
    for n in range(blocks):
        rr = refs[n][:, :freq]
        ri = refs[n][:, freq:]
        qh, ql = halves(rr * rr + ri * ri)
        quad = dot_nt(qh, ph) + dot_nt(ql, ph) + dot_nt(qh, plow)
        base = prior - 0.5 * quad
        rows = []
        for t in range(SHIFTS):
            if t == SHIFTS // 2:
                rows.append(refs[n][...])
            else:
                cg, sg = phase_of(phases, t)
                rows.append(jnp.concatenate([rr * cg + ri * sg, ri * cg - rr * sg], axis=1))
        rh, rl = halves(jnp.concatenate(rows, axis=0))
        score = dot_nt(rh, yh) + dot_nt(rl, yh) + dot_nt(rh, yl)
        score = score.reshape(SHIFTS, per, live_rows) + base[None]
        e_out[n] = score
        top = jnp.max(score, axis=0)
        high = top if high is None else jnp.maximum(high, top)
    high = jnp.max(high, axis=0, keepdims=True)
    sums = [jnp.zeros((per, live_rows), jnp.float32) for _ in range(SHIFTS)]
    for n in range(blocks):
        for t in range(SHIFTS):
            e = jnp.exp(e_out[n, t] - high)
            e_out[n, t] = e
            sums[t] = sums[t] + e
    sums = [jnp.sum(s, axis=0, keepdims=True) for s in sums]
    mass = sum(sums)
    mean_x = sum(s * float(gx) for s, (gx, gy) in zip(sums, GRID) if gx)
    mean_y = sum(s * float(gy) for s, (gx, gy) in zip(sums, GRID) if gy)
    stats_out[...] = jnp.zeros_like(stats_out)
    stats_out[0:1, :live_rows] = high
    stats_out[1:2, :live_rows] = mass
    stats_out[2:3, :live_rows] = mean_x
    stats_out[3:4, :live_rows] = mean_y
    stats_out[4:5, :live_rows] = row_facts[5:6, :]


def sum_kernel(n, own, s1, s2, s3, e_ref, y_ref, power_ref, part_out, shift_out):
    live_rows = e_ref.shape[3]
    width = y_ref.shape[1]
    freq = width // 2
    team = [s[:, :live_rows] for s in (own, s1, s2, s3)]
    top = team[0][0:1]
    for s in team[1:]:
        top = jnp.maximum(top, s[0:1])
    gains = [jnp.exp(s[0:1] - top) for s in team]
    mass = sum(g * s[1:2] for g, s in zip(gains, team))
    live = team[0][4:5] / mass
    own_gain = gains[0] * live
    shift_out[...] = jnp.zeros_like(shift_out)
    shift_out[0:1, :live_rows] = sum(g * s[2:3] for g, s in zip(gains, team)) * live
    shift_out[1:2, :live_rows] = sum(g * s[3:4] for g, s in zip(gains, team)) * live
    per = e_ref.shape[2]
    w = e_ref[n] * own_gain[None]
    flat = dot_nn(deep_lanes(w.reshape(SHIFTS * per, live_rows)), y_ref[...])
    phases = grid_phases(freq)
    mid = SHIFTS // 2
    re = flat[mid * per : (mid + 1) * per, :freq]
    im = flat[mid * per : (mid + 1) * per, freq:]
    for t in range(SHIFTS):
        if t == mid:
            continue
        cg, sg = phase_of(phases, t)
        ar = flat[t * per : (t + 1) * per, :freq]
        ai = flat[t * per : (t + 1) * per, freq:]
        re = re + (ar * cg - ai * sg)
        im = im + (ar * sg + ai * cg)
    part_out[:, :freq] = re
    part_out[:, freq:width] = im
    part_out[:, width:] = dot_nn(deep_lanes(jnp.sum(w, axis=0)), power_ref[...])


def final_kernel(*refs):
    own, *others, signal, out = refs
    width = out.shape[1]
    freq = width // 2
    total = own[...]
    for other in others:
        total = total + other[...]
    denominator = total[:, width:] + 1.0 / signal[...]
    out[:, :freq] = total[:, :freq] / denominator
    out[:, freq:] = total[:, freq:width] / denominator


def params(blocks):
    return pltpu.CompilerParams(vmem_limit_bytes=(12 + 2 * blocks) * 1024 * 1024)


def crossed(block, mask):
    size = lax.axis_size("dom")
    return lax.ppermute(block, "dom", [(i, i ^ mask) for i in range(size)])


def on_device(
    particle_fourier,
    defocus,
    particle_offset,
    prior_rotation,
    group_id,
    live_count,
    noise_power,
    signal_power,
    class_refs,
):
    slots, width = particle_fourier.shape
    freq = width // 2
    live_rows = 3 * slots
    size = lax.axis_size("dom")
    blocks = size // TEAM
    refs_own = class_refs.reshape(-1, width)
    per = refs_own.shape[0]
    f32 = jnp.float32
    vmem = pl.BlockSpec(memory_space=pltpu.VMEM)
    no_cost = pl.CostEstimate(flops=0, bytes_accessed=0, transcendentals=0)

    ynb = crossed(particle_fourier, 2)
    refs = [refs_own] + [crossed(refs_own, TEAM * n) for n in range(1, blocks)]
    live = (jnp.arange(slots, dtype=jnp.int32) < live_count[0]).astype(f32)
    facts = jnp.stack(
        [
            defocus,
            particle_offset[:, 0].astype(f32),
            particle_offset[:, 1].astype(f32),
            prior_rotation.astype(f32),
            group_id.astype(f32),
            live,
        ]
    )
    facts = jnp.pad(facts, ((0, 2), (0, 128 - slots)))
    spectrum, rows = pl.pallas_call(
        facts_kernel,
        out_shape=(
            jax.ShapeDtypeStruct((2 * slots, width + freq), f32),
            jax.ShapeDtypeStruct((8, 256), f32),
        ),
        in_specs=[vmem] * 3,
        out_specs=(vmem,) * 2,
        compiler_params=params(blocks),
        cost_estimate=no_cost,
        name="facts",
    )(facts, crossed(facts, 2), noise_power)
    anywhere = pl.BlockSpec(memory_space=pl.ANY)
    prepared = pl.pallas_call(
        prepare_kernel,
        out_shape=jax.ShapeDtypeStruct((2 * slots + 8, width + freq), f32),
        in_specs=[vmem] * 4 + [anywhere] * (blocks - 1),
        out_specs=vmem,
        compiler_params=params(blocks),
        cost_estimate=no_cost,
        name="prepare",
    )(particle_fourier, ynb, spectrum, rows, *refs[1:])
    partner = crossed(prepared, 1)

    deep = 3 * (live_rows // 256 * 256) + 128
    bf16 = jnp.bfloat16
    e_all, y, power, stats = pl.pallas_call(
        lambda *a: score_kernel(blocks, *a),
        out_shape=(
            jax.ShapeDtypeStruct((blocks, SHIFTS, per, live_rows), f32),
            jax.ShapeDtypeStruct((deep, width), bf16),
            jax.ShapeDtypeStruct((deep, freq), bf16),
            jax.ShapeDtypeStruct((8, 384), f32),
        ),
        in_specs=[vmem] * (blocks + 2),
        out_specs=(vmem,) * 4,
        scratch_shapes=[
            pltpu.VMEM((live_rows, width), bf16),
            pltpu.VMEM((live_rows, width), bf16),
            pltpu.VMEM((live_rows, freq), bf16),
            pltpu.VMEM((live_rows, freq), bf16),
        ],
        compiler_params=params(blocks),
        name="scores",
    )(prepared, partner, *refs)

    team = [stats] + [crossed(stats, n) for n in range(1, TEAM)]

    def sums(n):
        return pl.pallas_call(
            lambda *a: sum_kernel(n, *a),
            out_shape=(
                jax.ShapeDtypeStruct((per, width + freq), f32),
                jax.ShapeDtypeStruct((8, 384), f32),
            ),
            in_specs=[vmem] * (TEAM + 3),
            out_specs=(vmem,) * 2,
            compiler_params=params(blocks),
            name="sums",
        )(*team, e_all, y, power)

    arrived = []
    for n in range(blocks - 1, 0, -1):
        part, _ = sums(n)
        arrived.append(crossed(part, TEAM * n))
    own_part, shift_rows = sums(0)

    refs_new = pl.pallas_call(
        final_kernel,
        out_shape=jax.ShapeDtypeStruct((per, width), f32),
        in_specs=[vmem] * (blocks + 1),
        out_specs=vmem,
        compiler_params=params(blocks),
        name="update",
    )(own_part, *arrived[::-1], signal_power.reshape(1, freq))

    me = lax.axis_index("dom")
    half = slots // 2
    odd = me % 2
    at = (me // 2) % 2 * jnp.where(odd == 0, slots, half) + odd * (2 * slots)
    low = lax.dynamic_slice(shift_rows, (0, at), (2, half))
    high = lax.dynamic_slice(shift_rows, (0, at + half), (2, half))
    high = jnp.where(odd == 0, high, 0.0)
    expected = jnp.concatenate([low, high], axis=1).T
    return (expected, refs_new.reshape(class_refs.shape))


def solution(mesh):
    in_specs = (
        P(("groups", "dom"), None),
        P(("groups", "dom")),
        P(("groups", "dom"), None),
        P(("groups", "dom")),
        P(("groups", "dom")),
        P(("groups", "dom")),
        P("groups", None),
        P("groups"),
        P(("groups", "dom"), None, None),
    )
    out_specs = (P(("groups", "dom"), None), P(("groups", "dom"), None, None))
    return jax.shard_map(
        on_device, mesh=mesh, in_specs=in_specs, out_specs=out_specs, check_vma=False
    )
```

time: 90.4 us -> 58.1 us (0.64)
  Pallas kernels: 35.9 us -> 12.7 us
  waiting for transfers between devices: 28.1 us -> 22.1 us
  other arithmetic: 4.84 us -> 2.15 us
  starting transfers between devices: 15.3 us -> 14.1 us
  local copies, waits for them, and re-layouts: 4.2 us -> 5.36 us
    pallas_call x5 -> x7, Pallas kernels: 34.1 us -> 12 us  [the longest x4 5.42 us: sums(): pl.pallas_call(lambda *a: sum_kernel(n, *a), out_shape=(jax.ShapeDtypeStr...]
    all_to_all x1 -> x0, waiting for transfers between devices: 3.95 us -> none  [on_device(): lax.all_to_all(jnp.broadcast_to(stats[None], (TEAM, 8, 384)), 'dom', 0, 0...]
    all_to_all x1 -> x0, starting transfers between devices: 3.45 us -> none  [on_device(): lax.all_to_all(jnp.broadcast_to(stats[None], (TEAM, 8, 384)), 'dom', 0, 0...]
    unnamed x16 -> x12, local copies, waits for them, and re-layouts: 2.2 us -> 4.67 us
    ppermute x9 -> x12, starting transfers between devices: 11.8 us -> 14.1 us  [crossed(): return lax.ppermute(block, 'dom', [(i, i ^ mask) for i in range(size)])]
    ppermute x9 -> x12, waiting for transfers between devices: 24.2 us -> 22.1 us  [crossed(): return lax.ppermute(block, 'dom', [(i, i ^ mask) for i in range(size)])]
    broadcast_in_dim x1 -> x0, local copies, waits for them, and re-layouts: 1.33 us -> none  [on_device(): jnp.broadcast_to(stats[None], (TEAM, 8, 384))]
    pallas_call x1, Pallas kernels: 1.8 us -> 0.71 us  [on_device(): pl.pallas_call(final_kernel, out_shape=jax.ShapeDtypeStruct((per, width),...]
  transfers between devices with their start and end apart: 10 -> 12, of which waited for: 6 -> 6; matrix products, arithmetic and copies ran while one was open for 2% -> 5% of each run, Pallas kernels for 16% -> 9%
where the time goes in v2:
time: 58.1 us; the launch traced here: 57.8 us
  waiting for transfers between devices  22.1 us (38%)
  starting transfers between devices  14.1 us (24%)
  Pallas kernels  12.7 us (22%)
  local copies, waits for them, and re-layouts  5.36 us (9%)
  other arithmetic  2.15 us (4%)
  between operations  1.38 us (2%)
    ppermute x12, waiting for transfers between devices, crossed(): return lax.ppermute(block, 'dom', [(i, i ^ mask) for i in range(size)])  22.1 us
    ppermute x12, starting transfers between devices, crossed(): return lax.ppermute(block, 'dom', [(i, i ^ mask) for i in range(size)])  14.1 us
    pallas_call x4, Pallas kernels, sums(): pl.pallas_call(lambda *a: sum_kernel(n, *a), out_shape=(jax.ShapeDtypeStr...  5.42 us
    pallas_call x1, Pallas kernels, on_device(): pl.pallas_call(lambda *a: score_kernel(blocks, *a), out_shape=(jax.ShapeD...  5.42 us
    unnamed x12, local copies, waits for them, and re-layouts  4.67 us
  transfers between devices with their start and end apart: 12, of which 6 were waited for; matrix products, arithmetic and copies ran while one was open for 5% of the time, Pallas kernels for 9%

profile of v2, /device:TPU:0, one launch (start us, length us, event | category | flops | bytes accessed | tf_op | source)
XLA Modules:
  0.0 57.8 jit_solution(10729296625310432670)
XLA Ops:
  0.6 3.1 %collective-permute-start.2 = (f32[32,1024]{1,0:T(8,128)}, f32[32,1024]{1,0:T(8,128)S(1)}, u32[]{:S(2)}, u32[]{:S(2)}) collective-permute-start(f32[32,1024]{1,0:T(8,128)} %bitcast.16), channel_id=1, source_target_pairs={{0,4},{1,5},{2,6},{3,7},{4,0},{5,1},{6,2},{7,3},{8,12},{9,13},{10,... | collective-permute-start | bytes 393224 | tf_op jit(solution)/shard_map/ppermute | solution.py:347
  3.7 2.6 %collective-permute-start.3 = (f32[32,1024]{1,0:T(8,128)}, f32[32,1024]{1,0:T(8,128)S(1)}, u32[]{:S(2)}, u32[]{:S(2)}) collective-permute-start(f32[32,1024]{1,0:T(8,128)} %bitcast.17), channel_id=1, source_target_pairs={{0,8},{1,9},{2,10},{3,11},{4,12},{5,13},{6,14},{7,15},{8,0},{9,1},... | collective-permute-start | bytes 393224 | tf_op jit(solution)/shard_map/ppermute | solution.py:347
  6.3 0.0 collective-permute-start.4
  6.3 1.7 %collective-permute-start = (f32[96,1024]{1,0:T(8,128)}, f32[96,1024]{1,0:T(8,128)S(1)}, u32[]{:S(2)}, u32[]{:S(2)}) collective-permute-start(f32[96,1024]{1,0:T(8,128)} %own.1), channel_id=1, source_target_pairs={{0,2},{1,3},{2,0},{3,1},{4,6},{5,7},{6,4},{7,5},{8,10},{9,11},{10,... | collective-permute-start | bytes 1179656 | tf_op jit(solution)/shard_map/ppermute | solution.py:347
  8.1 0.8 %convert_bitcast_fusion.2 = (f32[1,96]{1,0:T(1,128)S(1)}, f32[1,96]{1,0:T(1,128)S(1)}) fusion(s32[96,2]{0,1:T(2,128)} %param.11), kind=kLoop, calls=%fused_computation.6 | loop fusion | flops 192 | bytes 1536 | tf_op jit(solution)/shard_map/convert_element_type | solution.py:379
  8.8 0.7 %convert_bitcast_fusion = (f32[1,96]{1,0:T(1,128)S(1)}, f32[1,96]{1,0:T(1,128)S(1)}) fusion(s32[96]{0:T(128)} %param.13, s32[96]{0:T(128)} %param.12), kind=kLoop, calls=%fused_computation.4 | loop fusion | flops 192 | bytes 1536 | tf_op jit(solution)/shard_map/stack | solution.py:375
  10.1 0.7 %stack.18 = f32[6,96]{1,0:T(8,128)S(1)} concatenate(f32[1,96]{1,0:T(1,128)} %bitcast.22, f32[1,96]{1,0:T(1,128)S(1)} %get-tuple-element.27, f32[1,96]{1,0:T(1,128)S(1)} %get-tuple-element.26, f32[1,96]{1,0:T(1,128)S(1)} %get-tuple-element.29, f32[1,96]{1,0:T(1,128)S(1)} %get-tuple-element.28, f32[1,96]{1,0:T(1,128)S(1)} %compare_convert_fusion), dimensions={0} | concatenate | bytes 4608 | tf_op jit(solution)/shard_map/stack | solution.py:375
  10.8 0.4 collective-permute-start.1
  11.2 5.7 %collective-permute-done.1.ynb_facts = f32[8,128]{1,0:T(8,128)S(1)} collective-permute-done((f32[8,128]{1,0:T(8,128)S(1)}, f32[8,128]{1,0:T(8,128)S(1)}, u32[]{:S(2)}, u32[]{:S(2)}) %collective-permute-start.1) | collective-permute-done | bytes 4128 | tf_op jit(solution)/shard_map/ppermute | solution.py:347
  16.9 0.0 copy-start.3
  16.9 0.9 %copy-done.3 = f32[128,512]{1,0:T(8,128)S(1)} copy-done((f32[128,512]{1,0:T(8,128)S(1)}, f32[128,512]{1,0:T(8,128)}, u32[]{:S(2)}) %copy-start.3) | copy-done | bytes 262168
  17.9 1.0 %facts.1 = (f32[192,1536]{1,0:T(8,128)S(1)}, f32[8,256]{1,0:T(8,128)S(1)}) custom-call(f32[8,128]{1,0:T(8,128)S(1)} %pad.4.own_facts, f32[8,128]{1,0:T(8,128)S(1)} %collective-permute-done.1.ynb_facts, f32[128,512]{1,0:T(8,128)S(1)} %copy-done.3), custom_call_target="tpu_custom_call" | custom-call | tf_op jit(solution)/shard_map/facts/pallas_call | solution.py:386
  18.8 0.0 collective-permute-done.2.rest_0_.a_3_
  18.9 0.0 collective-permute-done.3.rest_1_.a_4_
  18.9 0.0 collective-permute-done.4.rest_2_.a_5_
  18.9 0.0 collective-permute-done.ynb
  18.9 0.0 copy-start.2
  18.9 1.0 %copy-done.2 = f32[96,1024]{1,0:T(8,128)S(1)} copy-done((f32[96,1024]{1,0:T(8,128)S(1)}, f32[96,1024]{1,0:T(8,128)}, u32[]{:S(2)}) %copy-start.2) | copy-done | bytes 393240
  19.9 0.0 copy-start.4
  19.9 0.2 prepare.1.a_0_
  20.0 0.1 collective-permute-start.5
  20.1 2.9 %collective-permute-done.5.a_1_ = f32[200,1536]{1,0:T(8,128)S(1)} collective-permute-done((f32[200,1536]{1,0:T(8,128)S(1)}, f32[200,1536]{1,0:T(8,128)S(1)}, u32[]{:S(2)}, u32[]{:S(2)}) %collective-permute-start.5) | collective-permute-done | bytes 1228832 | tf_op jit(solution)/shard_map/ppermute | solution.py:347
  23.0 0.0 copy-done.4
  23.0 5.4 %scores.1 = (f32[4,9,32,288]{3,2,1,0:T(8,128)S(1)}, bf16[896,1024]{1,0:T(8,128)(2,1)S(1)}, bf16[896,512]{1,0:T(8,128)(2,1)S(1)}, f32[8,384]{1,0:T(8,128)S(1)}) custom-call(f32[200,1536]{1,0:T(8,128)S(1)} %prepare.1.a_0_, f32[200,1536]{1,0:T(8,128)S(1)} %collective-permute-done.5.a_1_, f32[32,1024]{1,0:T(8,128)S(1)} %bitcast.19, ...), custom_call_target="tpu_custom_call" | custom-call | tf_op jit(solution)/shard_map/scores/pallas_call | solution.py:412
  28.5 0.0 copy-start
  28.5 1.2 %copy-done = f32[4,9,32,288]{3,2,1,0:T(8,128)} copy-done((f32[4,9,32,288]{3,2,1,0:T(8,128)}, f32[4,9,32,288]{3,2,1,0:T(8,128)S(1)}, u32[]{:S(2)}) %copy-start) | copy-done | bytes 1327128
  29.7 0.1 collective-permute-start.6
  29.9 1.5 %collective-permute-start.7 = (f32[8,384]{1,0:T(8,128)S(1)}, f32[8,384]{1,0:T(8,128)S(1)}, u32[]{:S(2)}, u32[]{:S(2)}) collective-permute-start(f32[8,384]{1,0:T(8,128)S(1)} %get-tuple-element.15.a_0_), channel_id=1, source_target_pairs={{0,2},{1,3},{2,0},{3,1},{4,6},{5,7},{6,4},{7,5},{8,10},{9,11},{10,... | collective-permute-start | bytes 36872 | tf_op jit(solution)/shard_map/ppermute | solution.py:347
  31.4 0.2 collective-permute-start.8
  31.6 0.0 collective-permute-done.6.a_1_
  31.6 2.0 %collective-permute-done.7.a_2_ = f32[8,384]{1,0:T(8,128)S(1)} collective-permute-done((f32[8,384]{1,0:T(8,128)S(1)}, f32[8,384]{1,0:T(8,128)S(1)}, u32[]{:S(2)}, u32[]{:S(2)}) %collective-permute-start.7) | collective-permute-done | bytes 12320 | tf_op jit(solution)/shard_map/ppermute | solution.py:347
  33.6 0.9 %collective-permute-done.8.a_3_ = f32[8,384]{1,0:T(8,128)S(1)} collective-permute-done((f32[8,384]{1,0:T(8,128)S(1)}, f32[8,384]{1,0:T(8,128)S(1)}, u32[]{:S(2)}, u32[]{:S(2)}) %collective-permute-start.8) | collective-permute-done | bytes 12320 | tf_op jit(solution)/shard_map/ppermute | solution.py:347
  34.5 0.0 copy-start.1
  34.5 1.5 %copy-done.1 = f32[4,9,32,288]{3,2,1,0:T(8,128)S(1)} copy-done((f32[4,9,32,288]{3,2,1,0:T(8,128)S(1)}, f32[4,9,32,288]{3,2,1,0:T(8,128)}, u32[]{:S(2)}) %copy-start.1) | copy-done | bytes 1327128
  36.0 1.5 %sums.7 = (f32[32,1536]{1,0:T(8,128)S(1)}, f32[8,384]{1,0:T(8,128)}) custom-call(f32[8,384]{1,0:T(8,128)S(1)} %get-tuple-element.15.a_0_, f32[8,384]{1,0:T(8,128)S(1)} %collective-permute-done.6.a_1_, f32[8,384]{1,0:T(8,128)S(1)} %collective-permute-done.7.a_2_, f32[8,384]{1,0:T(8,128)S(1)} %collective-permute-done.8.a_3_, f32[4,9,32,288]{3,2,1,0:T(8,128)S(1)} %copy-done.1, ...), custom_call_target="tpu_custom_call" | custom-call | tf_op jit(solution)/shard_map/sums/pallas_call | solution.py:435
  37.5 3.5 %collective-permute-start.11 = (f32[32,1536]{1,0:T(8,128)S(1)}, f32[32,1536]{1,0:T(8,128)S(1)}, u32[]{:S(2)}, u32[]{:S(2)}) collective-permute-start(f32[32,1536]{1,0:T(8,128)S(1)} %get-tuple-element.23), channel_id=1, source_target_pairs={{0,12},{1,13},{2,14},{3,15},{4,8},{5,9},{6,10},{7,11},{8,4},{9,5},... | collective-permute-start | bytes 589832 | tf_op jit(solution)/shard_map/ppermute | solution.py:347
  41.0 1.5 %sums.6 = (f32[32,1536]{1,0:T(8,128)S(1)}, f32[8,384]{1,0:T(8,128)}) custom-call(f32[8,384]{1,0:T(8,128)S(1)} %get-tuple-element.15.a_0_, f32[8,384]{1,0:T(8,128)S(1)} %collective-permute-done.6.a_1_, f32[8,384]{1,0:T(8,128)S(1)} %collective-permute-done.7.a_2_, f32[8,384]{1,0:T(8,128)S(1)} %collective-permute-done.8.a_3_, f32[4,9,32,288]{3,2,1,0:T(8,128)S(1)} %copy-done.1, ...), custom_call_target="tpu_custom_call" | custom-call | tf_op jit(solution)/shard_map/sums/pallas_call | solution.py:435
  42.5 0.0 collective-permute-start.10
  42.5 1.5 %sums.5 = (f32[32,1536]{1,0:T(8,128)S(1)}, f32[8,384]{1,0:T(8,128)}) custom-call(f32[8,384]{1,0:T(8,128)S(1)} %get-tuple-element.15.a_0_, f32[8,384]{1,0:T(8,128)S(1)} %collective-permute-done.6.a_1_, f32[8,384]{1,0:T(8,128)S(1)} %collective-permute-done.7.a_2_, f32[8,384]{1,0:T(8,128)S(1)} %collective-permute-done.8.a_3_, f32[4,9,32,288]{3,2,1,0:T(8,128)S(1)} %copy-done.1, ...), custom_call_target="tpu_custom_call" | custom-call | tf_op jit(solution)/shard_map/sums/pallas_call | solution.py:435
  44.0 0.0 copy-start.5
  44.0 0.8 %collective-permute-start.9 = (f32[32,1536]{1,0:T(8,128)S(1)}, f32[32,1536]{1,0:T(8,128)S(1)}, u32[]{:S(2)}, u32[]{:S(2)}) collective-permute-start(f32[32,1536]{1,0:T(8,128)S(1)} %get-tuple-element.21), channel_id=1, source_target_pairs={{0,4},{1,5},{2,6},{3,7},{4,0},{5,1},{6,2},{7,3},{8,12},{9,13},{10,... | collective-permute-start | bytes 589832 | tf_op jit(solution)/shard_map/ppermute | solution.py:347
  44.9 0.9 %sums.4 = (f32[32,1536]{1,0:T(8,128)S(1)}, f32[8,384]{1,0:T(8,128)S(1)}) custom-call(f32[8,384]{1,0:T(8,128)S(1)} %get-tuple-element.15.a_0_, f32[8,384]{1,0:T(8,128)S(1)} %collective-permute-done.6.a_1_, f32[8,384]{1,0:T(8,128)S(1)} %collective-permute-done.7.a_2_, f32[8,384]{1,0:T(8,128)S(1)} %collective-permute-done.8.a_3_, ...), custom_call_target="tpu_custom_call" | custom-call | tf_op jit(solution)/shard_map/sums/pallas_call | solution.py:435
  45.8 0.1 constant_dynamic-slice_fusion
  45.9 0.6 %maximum_bitcast_fusion = f32[96,2]{0,1:T(2,128)} fusion(f32[2,48]{1,0:T(2,128)S(1)} %get-tuple-element.25, f32[2,48]{1,0:T(2,128)S(1)} %get-tuple-element.24), kind=kLoop, calls=%fused_computation.1 | loop fusion | flops 192 | bytes 1536 | tf_op jit(solution)/shard_map/transpose | solution.py:469
  46.5 0.6 %collective-permute-done.11.refs_3_ = f32[32,1536]{1,0:T(8,128)S(1)} collective-permute-done((f32[32,1536]{1,0:T(8,128)S(1)}, f32[32,1536]{1,0:T(8,128)S(1)}, u32[]{:S(2)}, u32[]{:S(2)}) %collective-permute-start.11) | collective-permute-done | bytes 196640 | tf_op jit(solution)/shard_map/ppermute | solution.py:347
  47.1 10.0 %collective-permute-done.10.refs_2_ = f32[32,1536]{1,0:T(8,128)S(1)} collective-permute-done((f32[32,1536]{1,0:T(8,128)S(1)}, f32[32,1536]{1,0:T(8,128)S(1)}, u32[]{:S(2)}, u32[]{:S(2)}) %collective-permute-start.10) | collective-permute-done | bytes 196640 | tf_op jit(solution)/shard_map/ppermute | solution.py:347
  57.1 0.0 collective-permute-done.9.refs_1_
  57.1 0.0 copy-done.5
  57.1 0.7 %update.1 = f32[32,1024]{1,0:T(8,128)} custom-call(f32[32,1536]{1,0:T(8,128)S(1)} %get-tuple-element.20.refs_0_, f32[32,1536]{1,0:T(8,128)S(1)} %collective-permute-done.9.refs_1_, f32[32,1536]{1,0:T(8,128)S(1)} %collective-permute-done.10.refs_2_, f32[32,1536]{1,0:T(8,128)S(1)} %collective-permute-done.11.refs_3_, f32[1,512]{1,0:T(1,128)S(1)} %bitcast.20), custom_call_target="tpu_custom_call" | custom-call | tf_op jit(solution)/shard_map/update/pallas_call | solution.py:453
  (2 shorter events, 0.0 us)
Async XLA Ops:
  0.6 18.2 %collective-permute-start.2 = (f32[32,1024]{1,0:T(8,128)}, f32[32,1024]{1,0:T(8,128)S(1)}, u32[]{:S(2)}, u32[]{:S(2)}) collective-permute-start(f32[32,1024]{1,0:T(8,128)} %bitcast.16), channel_id=1, source_target_pairs={{0,4},{1,5},{2,6},{3,7},{4,0},{5,1},{6,2},{7,3},{8,12},{9,13},{10,... | collective-permute-start | bytes 393224 | tf_op jit(solution)/shard_map/ppermute | solution.py:347
  3.7 15.1 %collective-permute-start.3 = (f32[32,1024]{1,0:T(8,128)}, f32[32,1024]{1,0:T(8,128)S(1)}, u32[]{:S(2)}, u32[]{:S(2)}) collective-permute-start(f32[32,1024]{1,0:T(8,128)} %bitcast.17), channel_id=1, source_target_pairs={{0,8},{1,9},{2,10},{3,11},{4,12},{5,13},{6,14},{7,15},{8,0},{9,1},... | collective-permute-start | bytes 393224 | tf_op jit(solution)/shard_map/ppermute | solution.py:347
  6.3 12.6 %collective-permute-start.4 = (f32[32,1024]{1,0:T(8,128)}, f32[32,1024]{1,0:T(8,128)S(1)}, u32[]{:S(2)}, u32[]{:S(2)}) collective-permute-start(f32[32,1024]{1,0:T(8,128)} %bitcast.18), channel_id=1, source_target_pairs={{0,12},{1,13},{2,14},{3,15},{4,8},{5,9},{6,10},{7,11},{8,4},{9,5},... | collective-permute-start | bytes 393224 | tf_op jit(solution)/shard_map/ppermute | solution.py:347
  6.3 12.6 %collective-permute-start = (f32[96,1024]{1,0:T(8,128)}, f32[96,1024]{1,0:T(8,128)S(1)}, u32[]{:S(2)}, u32[]{:S(2)}) collective-permute-start(f32[96,1024]{1,0:T(8,128)} %own.1), channel_id=1, source_target_pairs={{0,2},{1,3},{2,0},{3,1},{4,6},{5,7},{6,4},{7,5},{8,10},{9,11},{10,... | collective-permute-start | bytes 1179656 | tf_op jit(solution)/shard_map/ppermute | solution.py:347
  10.8 6.1 %collective-permute-start.1 = (f32[8,128]{1,0:T(8,128)S(1)}, f32[8,128]{1,0:T(8,128)S(1)}, u32[]{:S(2)}, u32[]{:S(2)}) collective-permute-start(f32[8,128]{1,0:T(8,128)S(1)} %pad.4.own_facts), channel_id=1, source_target_pairs={{0,2},{1,3},{2,0},{3,1},{4,6},{5,7},{6,4},{7,5},{8,10},{9,11},{10,... | collective-permute-start | bytes 12296 | tf_op jit(solution)/shard_map/ppermute | solution.py:347
  16.9 1.0 %copy-start.3 = (f32[128,512]{1,0:T(8,128)S(1)}, f32[128,512]{1,0:T(8,128)}, u32[]{:S(2)}) copy-start(f32[128,512]{1,0:T(8,128)} %noise.1) | copy-start | bytes 786436
  18.9 1.0 %copy-start.2 = (f32[96,1024]{1,0:T(8,128)S(1)}, f32[96,1024]{1,0:T(8,128)}, u32[]{:S(2)}) copy-start(f32[96,1024]{1,0:T(8,128)} %own.1) | copy-start | bytes 1179652
  19.9 3.1 %copy-start.4 = (f32[2,16,1024]{2,1,0:T(8,128)S(1)}, f32[2,16,1024]{2,1,0:T(8,128)}, u32[]{:S(2)}) copy-start(f32[2,16,1024]{2,1,0:T(8,128)} %param.17) | copy-start | bytes 393220
  20.0 3.0 %collective-permute-start.5 = (f32[200,1536]{1,0:T(8,128)S(1)}, f32[200,1536]{1,0:T(8,128)S(1)}, u32[]{:S(2)}, u32[]{:S(2)}) collective-permute-start(f32[200,1536]{1,0:T(8,128)S(1)} %prepare.1.a_0_), channel_id=1, source_target_pairs={{0,1},{1,0},{2,3},{3,2},{4,5},{5,4},{6,7},{7,6},{8,9},{9,8},{10,11... | collective-permute-start | bytes 3686408 | tf_op jit(solution)/shard_map/ppermute | solution.py:347
  28.5 1.3 %copy-start = (f32[4,9,32,288]{3,2,1,0:T(8,128)}, f32[4,9,32,288]{3,2,1,0:T(8,128)S(1)}, u32[]{:S(2)}) copy-start(f32[4,9,32,288]{3,2,1,0:T(8,128)S(1)} %get-tuple-element.16.a_4_) | copy-start | bytes 3981316
  29.7 1.9 %collective-permute-start.6 = (f32[8,384]{1,0:T(8,128)S(1)}, f32[8,384]{1,0:T(8,128)S(1)}, u32[]{:S(2)}, u32[]{:S(2)}) collective-permute-start(f32[8,384]{1,0:T(8,128)S(1)} %get-tuple-element.15.a_0_), channel_id=1, source_target_pairs={{0,1},{1,0},{2,3},{3,2},{4,5},{5,4},{6,7},{7,6},{8,9},{9,8},{10,11... | collective-permute-start | bytes 36872 | tf_op jit(solution)/shard_map/ppermute | solution.py:347
  29.9 3.7 %collective-permute-start.7 = (f32[8,384]{1,0:T(8,128)S(1)}, f32[8,384]{1,0:T(8,128)S(1)}, u32[]{:S(2)}, u32[]{:S(2)}) collective-permute-start(f32[8,384]{1,0:T(8,128)S(1)} %get-tuple-element.15.a_0_), channel_id=1, source_target_pairs={{0,2},{1,3},{2,0},{3,1},{4,6},{5,7},{6,4},{7,5},{8,10},{9,11},{10,... | collective-permute-start | bytes 36872 | tf_op jit(solution)/shard_map/ppermute | solution.py:347
  31.4 3.1 %collective-permute-start.8 = (f32[8,384]{1,0:T(8,128)S(1)}, f32[8,384]{1,0:T(8,128)S(1)}, u32[]{:S(2)}, u32[]{:S(2)}) collective-permute-start(f32[8,384]{1,0:T(8,128)S(1)} %get-tuple-element.15.a_0_), channel_id=1, source_target_pairs={{0,3},{1,2},{2,1},{3,0},{4,7},{5,6},{6,5},{7,4},{8,11},{9,10},{10,... | collective-permute-start | bytes 36872 | tf_op jit(solution)/shard_map/ppermute | solution.py:347
  34.5 1.5 %copy-start.1 = (f32[4,9,32,288]{3,2,1,0:T(8,128)S(1)}, f32[4,9,32,288]{3,2,1,0:T(8,128)}, u32[]{:S(2)}) copy-start(f32[4,9,32,288]{3,2,1,0:T(8,128)} %copy-done) | copy-start | bytes 3981316
  37.5 9.7 %collective-permute-start.11 = (f32[32,1536]{1,0:T(8,128)S(1)}, f32[32,1536]{1,0:T(8,128)S(1)}, u32[]{:S(2)}, u32[]{:S(2)}) collective-permute-start(f32[32,1536]{1,0:T(8,128)S(1)} %get-tuple-element.23), channel_id=1, source_target_pairs={{0,12},{1,13},{2,14},{3,15},{4,8},{5,9},{6,10},{7,11},{8,4},{9,5},... | collective-permute-start | bytes 589832 | tf_op jit(solution)/shard_map/ppermute | solution.py:347
  42.5 14.6 %collective-permute-start.10 = (f32[32,1536]{1,0:T(8,128)S(1)}, f32[32,1536]{1,0:T(8,128)S(1)}, u32[]{:S(2)}, u32[]{:S(2)}) collective-permute-start(f32[32,1536]{1,0:T(8,128)S(1)} %get-tuple-element.22), channel_id=1, source_target_pairs={{0,8},{1,9},{2,10},{3,11},{4,12},{5,13},{6,14},{7,15},{8,0},{9,1},... | collective-permute-start | bytes 589832 | tf_op jit(solution)/shard_map/ppermute | solution.py:347
  44.0 13.1 %copy-start.5 = (f32[512]{0:T(512)S(1)}, f32[512]{0:T(512)}, u32[]{:S(2)}) copy-start(f32[512]{0:T(512)} %param.16) | copy-start | bytes 6148
  44.0 13.1 %collective-permute-start.9 = (f32[32,1536]{1,0:T(8,128)S(1)}, f32[32,1536]{1,0:T(8,128)S(1)}, u32[]{:S(2)}, u32[]{:S(2)}) collective-permute-start(f32[32,1536]{1,0:T(8,128)S(1)} %get-tuple-element.21), channel_id=1, source_target_pairs={{0,4},{1,5},{2,6},{3,7},{4,0},{5,1},{6,2},{7,3},{8,12},{9,13},{10,... | collective-permute-start | bytes 589832 | tf_op jit(solution)/shard_map/ppermute | solution.py:347

commit v3 on v2

--- a/solution.py
+++ b/solution.py
@@ -119,28 +119,14 @@
     return c, -s
 
 
-def facts_kernel(own_facts, ynb_facts, noise, out, rows_out):
-    both, freq = out.shape[0], out.shape[1] // 3
-    slots = both // 2
-    first = (lax.axis_index("dom") // 2) % 2 == 0
-    rows_own, rows_ynb = own_facts[...], ynb_facts[...]
-    col_facts = jnp.concatenate(
-        [
-            jnp.concatenate([t, jnp.zeros((120, 128), jnp.float32)], axis=0).T[:slots]
-            for t in (rows_own, rows_ynb)
-        ],
-        axis=0,
-    )
-    focus = col_facts[:, 0:1]
-    off_x = col_facts[:, 1:2]
-    off_y = col_facts[:, 2:3]
-    group_col = col_facts[:, 4:5]
-
-    total = noise.shape[0]
-    onehot = (
-        group_col == lax.broadcasted_iota(jnp.int32, (both, total), 1).astype(jnp.float32)
-    ).astype(jnp.float32)
-    noise_rows = exact_dot_nn(onehot, 1.0 / noise[...])
+def prepared_rows(src, facts, inverse_noise, out):
+    slots, width = src.shape
+    freq = width // 2
+    columns = jnp.concatenate([facts, jnp.zeros((120, 128), jnp.float32)], axis=0).T[:slots]
+    focus = columns[:, 0:1]
+    off_x = columns[:, 1:2]
+    off_y = columns[:, 2:3]
+    group_col = columns[:, 4:5]
 
     kx, ky = freq_rows(freq, 1)
     chi = focus * ((kx * kx + ky * ky) * (1.0 / 1024.0))
@@ -152,93 +138,111 @@
     parity = 0.5 * k
     sign = (parity - jnp.floor(parity)) * (4.0 * CTF_SIZE) - CTF_SIZE
     ctf = half_turn_sine(folded) * sign
-    scaled = ctf * noise_rows
-    power = ctf * scaled
-
     kx0, ky0 = freq_rows(128, 1)
     m = (kx0 * off_x + ky0 * off_y) * (1.0 / BOX)
     pc, ps = turn_cos(m), turn_sin(m)
-    step = off_x * ((128 // FY) / BOX) + jnp.zeros((both, 128), jnp.float32)
+    step = off_x * ((128 // FY) / BOX) + jnp.zeros((slots, 128), jnp.float32)
     sc, ss = turn_cos(step), turn_sin(step)
+
+    total = inverse_noise.shape[0]
+    onehot = (
+        group_col == lax.broadcasted_iota(jnp.int32, (slots, total), 1).astype(jnp.float32)
+    ).astype(jnp.float32)
+    noise_rows = exact_dot_nn(onehot, inverse_noise)
+    scaled = ctf * noise_rows
+    out[:slots, width:] = ctf * scaled
     for n in range(freq // 128):
         part = slice(128 * n, 128 * (n + 1))
         twin = slice(freq + 128 * n, freq + 128 * (n + 1))
-        out[:, part] = pc * scaled[:, part]
-        out[:, twin] = ps * scaled[:, part]
+        co = pc * scaled[:, part]
+        si = ps * scaled[:, part]
         pc, ps = pc * sc - ps * ss, ps * sc + pc * ss
-    out[:, 2 * freq :] = power
-
-    lane = lax.broadcasted_iota(jnp.int32, (8, 128), 1)
-    a = jnp.where(first, rows_own, rows_ynb)
-    b = pltpu.roll(jnp.where(first, rows_ynb, rows_own), slots, 1)
-    rows_out[:, :128] = jnp.where(lane < slots, a, b)
-    rows_out[:, 128:] = b
-
-
-def prepare_kernel(own, ynb, spectrum, rows, *rest):
-    out = rest[-1]
-    slots, width = own.shape
-    freq = width // 2
-    both = 2 * slots
-    first = (lax.axis_index("dom") // 2) % 2 == 0
-    at_own = pl.multiple_of(jnp.where(first, 0, slots), 8)
-    at_ynb = pl.multiple_of(jnp.where(first, slots, 0), 8)
-    for src, rows_of, at in ((own, slice(0, slots), at_own), (ynb, slice(slots, both), at_ynb)):
-        to = pl.ds(at, slots)
-        xr, xi = src[:, :freq], src[:, freq:]
-        co, si = spectrum[rows_of, :freq], spectrum[rows_of, freq:width]
-        out[to, :freq] = xr * co - xi * si
-        out[to, freq:width] = xr * si + xi * co
-        out[to, width:] = spectrum[rows_of, width:]
-    out[both:, :256] = rows[...]
-    out[both:, 256:] = jnp.zeros((8, width + freq - 256), jnp.float32)
-
-
-def score_kernel(blocks, mine, other, *rest):
+        xr, xi = src[:, part], src[:, twin]
+        out[:slots, part] = xr * co - xi * si
+        out[:slots, twin] = xr * si + xi * co
+    out[slots:, :128] = facts
+    out[slots:, 128:] = jnp.zeros((8, width + freq - 128), jnp.float32)
+
+
+def own_kernel(
+    src_at, focus_at, offsets_at, prior_at, group_at, noise_at, live_count, out, facts_out,
+    inverse_out, src, focus, offsets, prior, group, noise, sems
+):
+    moves = (
+        (focus_at, focus), (offsets_at, offsets), (prior_at, prior), (group_at, group),
+        (noise_at, noise), (src_at, src),
+    )
+    copies = [pltpu.make_async_copy(x, y, sems.at[n]) for n, (x, y) in enumerate(moves)]
+    for copy in copies:
+        copy.start()
+    slots = src.shape[0]
+    facts_out[...] = jnp.zeros_like(facts_out)
+    slot = lax.broadcasted_iota(jnp.int32, (1, slots), 1)
+    facts_out[5:6, :slots] = (slot < live_count[0]).astype(jnp.float32)
+    for copy in copies:
+        copy.wait()
+    facts_out[0:1, :slots] = focus[...]
+    facts_out[1:3, :slots] = offsets[...].astype(jnp.float32)
+    facts_out[3:4, :slots] = prior[...].astype(jnp.float32)
+    facts_out[4:5, :slots] = group[...].astype(jnp.float32)
+    inverse = 1.0 / noise[...]
+    inverse_out[...] = inverse
+    prepared_rows(src, facts_out[...], inverse, out)
+
+
+def neighbour_kernel(src, facts, inverse_noise, out):
+    prepared_rows(src, facts[...], inverse_noise[...], out)
+
+
+def score_kernel(blocks, own, cnb, ynb, cynb, *rest):
     refs = rest[:blocks]
-    e_out, y_out, power_out, stats_out, y_high, y_low, p_high, p_low = rest[blocks:]
+    e_outs = rest[blocks : 2 * blocks]
+    y_out, power_out, stats_out, y_high, y_low, p_high, p_low = rest[2 * blocks :]
     width = y_high.shape[1]
     freq = width // 2
-    both = mine.shape[0] - 8
-    slots = both // 2
+    slots = own.shape[0] - 8
     half = slots // 2
-    live_rows = both + slots
-    even = lax.axis_index("dom") % 2 == 0
-
-    def place(src, at, to, size):
-        rows = slice(at, at + size)
-        dest = slice(to, to + size)
-        high, low = halves(src[rows, :width])
+    live_rows = 3 * slots
+    me = lax.axis_index("dom")
+    even = me % 2 == 0
+    first = (me // 2) % 2 == 0
+
+    def place(src, to, size):
+        dest = pl.ds(pl.multiple_of(to, 16), size)
+        high, low = halves(src[:size, :width])
         y_high[dest] = high
         y_low[dest] = low
-        high, low = halves(src[rows, width:])
+        high, low = halves(src[:size, width:])
         p_high[dest] = high
         p_low[dest] = low
 
     def place_all(heavy, light):
-        place(heavy, 0, 0, both)
-        place(light, 0, both, half)
-        place(light, slots, both + half, half)
+        place(heavy[0], jnp.where(first, 0, slots), slots)
+        place(heavy[1], jnp.where(first, slots, 0), slots)
+        place(light[0], 2 * slots + jnp.where(first, 0, half), half)
+        place(light[1], 2 * slots + jnp.where(first, half, 0), half)
 
     @pl.when(even)
     def _():
-        place_all(mine, other)
+        place_all((own, ynb), (cnb, cynb))
 
     @pl.when(jnp.logical_not(even))
     def _():
-        place_all(other, mine)
+        place_all((cnb, cynb), (own, ynb))
 
     lane = lax.broadcasted_iota(jnp.int32, (8, 128), 1)
-    mine0, mine1 = mine[both:, :128], mine[both:, 128:256]
-    other0, other1 = other[both:, :128], other[both:, 128:256]
-    a0, a1 = jnp.where(even, mine0, other0), jnp.where(even, mine1, other1)
-    b0, b1 = jnp.where(even, other0, mine0), jnp.where(even, other1, mine1)
-    b0_16 = pltpu.roll(b0, 16, 1)
+    fo, fc, fy, fcy = (f[slots:, :128] for f in (own, cnb, ynb, cynb))
+    heavy = (jnp.where(even, fo, fc), jnp.where(even, fy, fcy))
+    light = (jnp.where(even, fc, fo), jnp.where(even, fcy, fy))
+    a0, b0 = (jnp.where(first, f[0], f[1]) for f in (heavy, light))
+    a1, b1 = (jnp.where(first, f[1], f[0]) for f in (heavy, light))
+    a1 = pltpu.roll(a1, 96, 1)
+    b1 = pltpu.roll(b1, 112, 1)
     row_facts = jnp.concatenate(
         [
-            a0,
-            jnp.where(lane < 64, a1, jnp.where(lane < 112, pltpu.roll(b0, 64, 1), b0_16)),
-            jnp.where(lane < 16, b0_16, pltpu.roll(b1, 16, 1)),
+            jnp.where(lane < 96, a0, a1),
+            jnp.where(lane < 64, a1, jnp.where(lane < 112, pltpu.roll(b0, 64, 1), b1)),
+            b1,
         ],
         axis=1,
     )[:, :live_rows]
@@ -269,15 +273,15 @@
         rh, rl = halves(jnp.concatenate(rows, axis=0))
         score = dot_nt(rh, yh) + dot_nt(rl, yh) + dot_nt(rh, yl)
         score = score.reshape(SHIFTS, per, live_rows) + base[None]
-        e_out[n] = score
+        e_outs[n][...] = score
         top = jnp.max(score, axis=0)
         high = top if high is None else jnp.maximum(high, top)
     high = jnp.max(high, axis=0, keepdims=True)
     sums = [jnp.zeros((per, live_rows), jnp.float32) for _ in range(SHIFTS)]
     for n in range(blocks):
         for t in range(SHIFTS):
-            e = jnp.exp(e_out[n, t] - high)
-            e_out[n, t] = e
+            e = jnp.exp(e_outs[n][t] - high)
+            e_outs[n][t] = e
             sums[t] = sums[t] + e
     sums = [jnp.sum(s, axis=0, keepdims=True) for s in sums]
     mass = sum(sums)
@@ -291,8 +295,8 @@
     stats_out[4:5, :live_rows] = row_facts[5:6, :]
 
 
-def sum_kernel(n, own, s1, s2, s3, e_ref, y_ref, power_ref, part_out, shift_out):
-    live_rows = e_ref.shape[3]
+def sum_kernel(own, s1, s2, s3, e_ref, y_ref, power_ref, part_out, shift_out):
+    live_rows = e_ref.shape[2]
     width = y_ref.shape[1]
     freq = width // 2
     team = [s[:, :live_rows] for s in (own, s1, s2, s3)]
@@ -306,8 +310,8 @@
     shift_out[...] = jnp.zeros_like(shift_out)
     shift_out[0:1, :live_rows] = sum(g * s[2:3] for g, s in zip(gains, team)) * live
     shift_out[1:2, :live_rows] = sum(g * s[3:4] for g, s in zip(gains, team)) * live
-    per = e_ref.shape[2]
-    w = e_ref[n] * own_gain[None]
+    per = e_ref.shape[1]
+    w = e_ref[...] * own_gain[None]
     flat = dot_nn(deep_lanes(w.reshape(SHIFTS * per, live_rows)), y_ref[...])
     phases = grid_phases(freq)
     mid = SHIFTS // 2
@@ -370,55 +374,66 @@
     no_cost = pl.CostEstimate(flops=0, bytes_accessed=0, transcendentals=0)
 
     ynb = crossed(particle_fourier, 2)
-    refs = [refs_own] + [crossed(refs_own, TEAM * n) for n in range(1, blocks)]
-    live = (jnp.arange(slots, dtype=jnp.int32) < live_count[0]).astype(f32)
-    facts = jnp.stack(
-        [
-            defocus,
-            particle_offset[:, 0].astype(f32),
-            particle_offset[:, 1].astype(f32),
-            prior_rotation.astype(f32),
-            group_id.astype(f32),
-            live,
-        ]
-    )
-    facts = jnp.pad(facts, ((0, 2), (0, 128 - slots)))
-    spectrum, rows = pl.pallas_call(
-        facts_kernel,
+    refs = [refs_own] + [crossed(refs_own, TEAM * n) for n in range(1, blocks) if n != 2]
+    refs.insert(2, crossed(refs[2], TEAM))
+    anywhere = pl.BlockSpec(memory_space=pl.ANY)
+    own_facts = (
+        particle_fourier,
+        defocus.reshape(1, slots),
+        particle_offset.T,
+        prior_rotation.reshape(1, slots),
+        group_id.reshape(1, slots),
+        noise_power,
+    )
+    own, facts, inverse_noise = pl.pallas_call(
+        own_kernel,
         out_shape=(
-            jax.ShapeDtypeStruct((2 * slots, width + freq), f32),
-            jax.ShapeDtypeStruct((8, 256), f32),
+            jax.ShapeDtypeStruct((slots + 8, width + freq), f32),
+            jax.ShapeDtypeStruct((8, 128), f32),
+            jax.ShapeDtypeStruct(noise_power.shape, f32),
         ),
-        in_specs=[vmem] * 3,
-        out_specs=(vmem,) * 2,
+        in_specs=[anywhere] * 6 + [pl.BlockSpec(memory_space=pltpu.SMEM)],
+        out_specs=(vmem,) * 3,
+        scratch_shapes=[pltpu.VMEM(x.shape, x.dtype) for x in own_facts]
+        + [pltpu.SemaphoreType.DMA((6,))],
         compiler_params=params(blocks),
         cost_estimate=no_cost,
-        name="facts",
-    )(facts, crossed(facts, 2), noise_power)
-    anywhere = pl.BlockSpec(memory_space=pl.ANY)
-    prepared = pl.pallas_call(
-        prepare_kernel,
-        out_shape=jax.ShapeDtypeStruct((2 * slots + 8, width + freq), f32),
-        in_specs=[vmem] * 4 + [anywhere] * (blocks - 1),
+        name="own",
+    )(*(pltpu.with_memory_space_constraint(x, pltpu.HBM) for x in own_facts), live_count)
+    cnb = crossed(own, 1)
+    ynb = pl.pallas_call(
+        neighbour_kernel,
+        out_shape=jax.ShapeDtypeStruct((slots + 8, width + freq), f32),
+        in_specs=[vmem] * 3,
         out_specs=vmem,
         compiler_params=params(blocks),
         cost_estimate=no_cost,
-        name="prepare",
-    )(particle_fourier, ynb, spectrum, rows, *refs[1:])
-    partner = crossed(prepared, 1)
+        name="neighbour",
+    )(ynb, crossed(facts, 2), inverse_noise)
+    ynb = pl.pallas_call(
+        lambda *a: None,
+        out_shape=jax.ShapeDtypeStruct(ynb.shape, f32),
+        in_specs=[anywhere] * blocks,
+        out_specs=anywhere,
+        input_output_aliases={0: 0},
+        compiler_params=params(blocks),
+        cost_estimate=no_cost,
+        name="gate",
+    )(ynb, *refs[1:])
+    cynb = crossed(ynb, 1)
 
     deep = 3 * (live_rows // 256 * 256) + 128
     bf16 = jnp.bfloat16
-    e_all, y, power, stats = pl.pallas_call(
+    *e_all, y, power, stats = pl.pallas_call(
         lambda *a: score_kernel(blocks, *a),
         out_shape=(
-            jax.ShapeDtypeStruct((blocks, SHIFTS, per, live_rows), f32),
+            *[jax.ShapeDtypeStruct((SHIFTS, per, live_rows), f32)] * blocks,
             jax.ShapeDtypeStruct((deep, width), bf16),
             jax.ShapeDtypeStruct((deep, freq), bf16),
             jax.ShapeDtypeStruct((8, 384), f32),
         ),
-        in_specs=[vmem] * (blocks + 2),
-        out_specs=(vmem,) * 4,
+        in_specs=[vmem] * (blocks + 4),
+        out_specs=(vmem,) * (blocks + 3),
         scratch_shapes=[
             pltpu.VMEM((live_rows, width), bf16),
             pltpu.VMEM((live_rows, width), bf16),
@@ -427,13 +442,13 @@
         ],
         compiler_params=params(blocks),
         name="scores",
-    )(prepared, partner, *refs)
+    )(own, cnb, ynb, cynb, *refs)
 
     team = [stats] + [crossed(stats, n) for n in range(1, TEAM)]
 
     def sums(n):
         return pl.pallas_call(
-            lambda *a: sum_kernel(n, *a),
+            sum_kernel,
             out_shape=(
                 jax.ShapeDtypeStruct((per, width + freq), f32),
                 jax.ShapeDtypeStruct((8, 384), f32),
@@ -442,7 +457,7 @@
             out_specs=(vmem,) * 2,
             compiler_params=params(blocks),
             name="sums",
-        )(*team, e_all, y, power)
+        )(*team, e_all[n], y, power)
 
     arrived = []
     for n in range(blocks - 1, 0, -1):

time: 58.1 us -> 58.1 us (level)
  local copies, waits for them, and re-layouts: 5.36 us -> 3.37 us
  waiting for transfers between devices: 22.1 us -> 23.8 us
  other arithmetic: 2.15 us -> 0.72 us
  Pallas kernels: 12.7 us -> 14 us
  starting transfers between devices: 14.1 us -> 14.7 us
    ppermute x12 -> x13, waiting for transfers between devices: 22.1 us -> 23.8 us  [crossed(): return lax.ppermute(block, 'dom', [(i, i ^ mask) for i in range(size)])]
    pallas_call x7 -> x8, Pallas kernels: 12 us -> 13.3 us  [the longest x4 5.43 us: sums(): pl.pallas_call(sum_kernel, out_shape=(jax.ShapeDtypeStruct((per, width +...]
    unnamed x12 -> x16, local copies, waits for them, and re-layouts: 4.67 us -> 3.37 us
    convert_element_type x2 -> x0, other arithmetic: 0.76 us -> none  [the longest x1 0.76 us: on_device(): particle_offset[:, 1].astype(f32)]
    another operation x1 -> x0, local copies, waits for them, and re-layouts: 0.68 us -> none  [on_device(): jnp.stack([defocus, particle_offset[:, 0].astype(f32), particle_offset[:,...]
    another operation x1 -> x0, other arithmetic: 0.67 us -> none  [on_device(): jnp.stack([defocus, particle_offset[:, 0].astype(f32), particle_offset[:,...]
    ppermute x12 -> x13, starting transfers between devices: 14.1 us -> 14.7 us  [crossed(): return lax.ppermute(block, 'dom', [(i, i ^ mask) for i in range(size)])]
  transfers between devices with their start and end apart: 12 -> 13, of which waited for: 6 -> 6; matrix products, arithmetic and copies ran while one was open for 5% -> 1% of each run, Pallas kernels for 9% -> 11%
where the time goes in v3:
time: 58.1 us; the launch traced here: 57.9 us
  waiting for transfers between devices  23.8 us (41%)
  starting transfers between devices  14.7 us (25%)
  Pallas kernels  14 us (24%)
  local copies, waits for them, and re-layouts  3.37 us (6%)
  between operations  1.38 us (2%)
  other arithmetic  0.72 us (1%)
    ppermute x13, waiting for transfers between devices, crossed(): return lax.ppermute(block, 'dom', [(i, i ^ mask) for i in range(size)])  23.8 us
    ppermute x13, starting transfers between devices, crossed(): return lax.ppermute(block, 'dom', [(i, i ^ mask) for i in range(size)])  14.7 us
    pallas_call x4, Pallas kernels, sums(): pl.pallas_call(sum_kernel, out_shape=(jax.ShapeDtypeStruct((per, width +...  5.43 us
    pallas_call x1, Pallas kernels, on_device(): pl.pallas_call(lambda *a: score_kernel(blocks, *a), out_shape=(*[jax.Shap...  5.41 us
    unnamed x16, local copies, waits for them, and re-layouts  3.37 us
    pallas_call x1, Pallas kernels, on_device(): pl.pallas_call(own_kernel, out_shape=(jax.ShapeDtypeStruct((slots + 8, wi...  1.83 us
  transfers between devices with their start and end apart: 13, of which 6 were waited for; matrix products, arithmetic and copies ran while one was open for 1% of the time, Pallas kernels for 11%

profile of v3, /device:TPU:0, one launch (start us, length us, event | category | flops | bytes accessed | tf_op | source)
XLA Modules:
  0.0 57.9 jit_solution(2528780447926529881)
XLA Ops:
  0.6 0.0 copy-start.6
  0.6 3.0 %collective-permute-start.1 = (f32[96,1024]{1,0:T(8,128)}, f32[96,1024]{1,0:T(8,128)S(1)}, u32[]{:S(2)}, u32[]{:S(2)}) collective-permute-start(f32[96,1024]{1,0:T(8,128)} %src_at.1), channel_id=1, source_target_pairs={{0,2},{1,3},{2,0},{3,1},{4,6},{5,7},{6,4},{7,5},{8,10},{9,11},{10,... | collective-permute-start | bytes 1179656 | tf_op jit(solution)/shard_map/ppermute | solution.py:351
  3.7 3.6 %collective-permute-start.4 = (f32[32,1024]{1,0:T(8,128)}, f32[32,1024]{1,0:T(8,128)S(1)}, u32[]{:S(2)}, u32[]{:S(2)}) collective-permute-start(f32[32,1024]{1,0:T(8,128)} %bitcast.9), channel_id=1, source_target_pairs={{0,12},{1,13},{2,14},{3,15},{4,8},{5,9},{6,10},{7,11},{8,4},{9,5},... | collective-permute-start | bytes 393224 | tf_op jit(solution)/shard_map/ppermute | solution.py:351
  7.3 0.0 collective-permute-start.3
  7.3 4.8 %collective-permute-done.4.a_3_.a_7_ = f32[32,1024]{1,0:T(8,128)S(1)} collective-permute-done((f32[32,1024]{1,0:T(8,128)}, f32[32,1024]{1,0:T(8,128)S(1)}, u32[]{:S(2)}, u32[]{:S(2)}) %collective-permute-start.4) | collective-permute-done | bytes 131104 | tf_op jit(solution)/shard_map/ppermute | solution.py:351
  12.1 1.1 %collective-permute-start.5 = (f32[32,1024]{1,0:T(8,128)S(1)}, f32[32,1024]{1,0:T(8,128)S(1)}, u32[]{:S(2)}, u32[]{:S(2)}) collective-permute-start(f32[32,1024]{1,0:T(8,128)S(1)} %collective-permute-done.4.a_3_.a_7_), channel_id=1, source_target_pairs={{0,4},{1,5},{2,6},{3,7},{4,0},{5,1},{6,2},{7,3},{8,12},{9,13},{10,... | collective-permute-start | bytes 393224 | tf_op jit(solution)/shard_map/ppermute | solution.py:351
  13.9 1.8 %own.1 = (f32[104,1536]{1,0:T(8,128)S(1)}, f32[8,128]{1,0:T(8,128)S(1)}, f32[128,512]{1,0:T(8,128)S(1)}) custom-call(f32[96,1024]{1,0:T(8,128)} %src_at.1, f32[1,96]{1,0:T(1,128)} %bitcast.15, s32[2,96]{1,0:T(2,128)} %bitcast.14, s32[1,96]{1,0:T(1,128)} %bitcast.16, s32[1,96]{1,0:T(1,128)} %bitcast.17, f32[128,512]{1,0:T(8,128)} %noise_at.1, ...), custom_call_target="tpu_custom_call" | custom-call | tf_op jit(solution)/shard_map/own/pallas_call | solution.py:388
  15.7 0.6 collective-permute-start.2
  16.3 0.0 collective-permute-start
  16.3 3.1 %collective-permute-done.2.facts = f32[8,128]{1,0:T(8,128)S(1)} collective-permute-done((f32[8,128]{1,0:T(8,128)S(1)}, f32[8,128]{1,0:T(8,128)S(1)}, u32[]{:S(2)}, u32[]{:S(2)}) %collective-permute-start.2) | collective-permute-done | bytes 4128 | tf_op jit(solution)/shard_map/ppermute | solution.py:351
  19.4 0.0 collective-permute-done.1.src
  19.4 0.6 %neighbour.1.a_0_ = f32[104,1536]{1,0:T(8,128)S(1)} custom-call(f32[96,1024]{1,0:T(8,128)S(1)} %collective-permute-done.1.src, f32[8,128]{1,0:T(8,128)S(1)} %collective-permute-done.2.facts, f32[128,512]{1,0:T(8,128)S(1)} %get-tuple-element.19.inverse_noise), custom_call_target="tpu_custom_call" | custom-call | tf_op jit(solution)/shard_map/neighbour/pallas_call | solution.py:404
  20.0 0.0 collective-permute-done.3.a_1_.a_5_
  20.0 0.0 collective-permute-done.5.a_2_.a_6_
  20.1 0.1 collective-permute-start.6
  20.1 0.0 collective-permute-done.a_1_
  20.1 2.1 %collective-permute-done.6.a_3_ = f32[104,1536]{1,0:T(8,128)S(1)} collective-permute-done((f32[104,1536]{1,0:T(8,128)S(1)}, f32[104,1536]{1,0:T(8,128)S(1)}, u32[]{:S(2)}, u32[]{:S(2)}) %collective-permute-start.6) | collective-permute-done | bytes 639008 | tf_op jit(solution)/shard_map/ppermute | solution.py:351
  22.2 0.0 copy-done.6
  22.2 5.4 %scores.1 = (f32[9,32,288]{2,1,0:T(8,128)S(1)}, f32[9,32,288]{2,1,0:T(8,128)S(1)}, f32[9,32,288]{2,1,0:T(8,128)S(1)}, f32[9,32,288]{2,1,0:T(8,128)S(1)}, bf16[89...) custom-call(f32[104,1536]{1,0:T(8,128)S(1)} %get-tuple-element.17.a_0_, ...), custom_call_target="tpu_custom_call" | custom-call | tf_op jit(solution)/shard_map/scores/pallas_call | solution.py:427
  27.6 0.0 copy-start
  27.6 0.8 %copy-done = f32[9,32,288]{2,1,0:T(8,128)} copy-done((f32[9,32,288]{2,1,0:T(8,128)}, f32[9,32,288]{2,1,0:T(8,128)S(1)}, u32[]{:S(2)}) %copy-start) | copy-done | bytes 331800
  28.4 0.0 copy-start.2
  28.4 0.8 %copy-done.2 = f32[9,32,288]{2,1,0:T(8,128)} copy-done((f32[9,32,288]{2,1,0:T(8,128)}, f32[9,32,288]{2,1,0:T(8,128)S(1)}, u32[]{:S(2)}) %copy-start.2) | copy-done | bytes 331800
  29.2 0.0 copy-start.4
  29.2 0.8 %copy-done.4 = f32[9,32,288]{2,1,0:T(8,128)} copy-done((f32[9,32,288]{2,1,0:T(8,128)}, f32[9,32,288]{2,1,0:T(8,128)S(1)}, u32[]{:S(2)}) %copy-start.4) | copy-done | bytes 331800
  30.0 0.1 collective-permute-start.7
  30.1 0.5 collective-permute-start.8
  30.6 1.2 %collective-permute-start.9 = (f32[8,384]{1,0:T(8,128)S(1)}, f32[8,384]{1,0:T(8,128)S(1)}, u32[]{:S(2)}, u32[]{:S(2)}) collective-permute-start(f32[8,384]{1,0:T(8,128)S(1)} %get-tuple-element.20.own), channel_id=1, source_target_pairs={{0,3},{1,2},{2,1},{3,0},{4,7},{5,6},{6,5},{7,4},{8,11},{9,10},{10,... | collective-permute-start | bytes 36872 | tf_op jit(solution)/shard_map/ppermute | solution.py:351
  31.8 0.0 copy-start.3
  31.8 0.0 collective-permute-done.7.s1
  31.8 2.0 %collective-permute-done.8.s2 = f32[8,384]{1,0:T(8,128)S(1)} collective-permute-done((f32[8,384]{1,0:T(8,128)S(1)}, f32[8,384]{1,0:T(8,128)S(1)}, u32[]{:S(2)}, u32[]{:S(2)}) %collective-permute-start.8) | collective-permute-done | bytes 12320 | tf_op jit(solution)/shard_map/ppermute | solution.py:351
  33.9 0.0 collective-permute-done.9.s3
  33.9 0.0 copy-start.5
  33.9 1.0 %copy-done.5 = f32[9,32,288]{2,1,0:T(8,128)S(1)} copy-done((f32[9,32,288]{2,1,0:T(8,128)S(1)}, f32[9,32,288]{2,1,0:T(8,128)}, u32[]{:S(2)}) %copy-start.5) | copy-done | bytes 331800
  34.9 1.5 %sums.7 = (f32[32,1536]{1,0:T(8,128)S(1)}, f32[8,384]{1,0:T(8,128)}) custom-call(f32[8,384]{1,0:T(8,128)S(1)} %get-tuple-element.20.own, f32[8,384]{1,0:T(8,128)S(1)} %collective-permute-done.7.s1, f32[8,384]{1,0:T(8,128)S(1)} %collective-permute-done.8.s2, f32[8,384]{1,0:T(8,128)S(1)} %collective-permute-done.9.s3, f32[9,32,288]{2,1,0:T(8,128)S(1)} %copy-done.5, ...), custom_call_target="tpu_custom_call" | custom-call | tf_op jit(solution)/shard_map/sums/pallas_call | solution.py:450
  36.4 0.0 copy-start.1
  36.4 2.5 %collective-permute-start.12 = (f32[32,1536]{1,0:T(8,128)S(1)}, f32[32,1536]{1,0:T(8,128)S(1)}, u32[]{:S(2)}, u32[]{:S(2)}) collective-permute-start(f32[32,1536]{1,0:T(8,128)S(1)} %get-tuple-element.31), channel_id=1, source_target_pairs={{0,12},{1,13},{2,14},{3,15},{4,8},{5,9},{6,10},{7,11},{8,4},{9,5},... | collective-permute-start | bytes 589832 | tf_op jit(solution)/shard_map/ppermute | solution.py:351
  38.9 0.0 copy-done.3
  38.9 1.5 %sums.6 = (f32[32,1536]{1,0:T(8,128)S(1)}, f32[8,384]{1,0:T(8,128)}) custom-call(f32[8,384]{1,0:T(8,128)S(1)} %get-tuple-element.20.own, f32[8,384]{1,0:T(8,128)S(1)} %collective-permute-done.7.s1, f32[8,384]{1,0:T(8,128)S(1)} %collective-permute-done.8.s2, f32[8,384]{1,0:T(8,128)S(1)} %collective-permute-done.9.s3, f32[9,32,288]{2,1,0:T(8,128)S(1)} %copy-done.3, ...), custom_call_target="tpu_custom_call" | custom-call | tf_op jit(solution)/shard_map/sums/pallas_call | solution.py:450
  40.4 0.6 collective-permute-start.11
  40.9 0.0 copy-done.1
  40.9 1.5 %sums.5 = (f32[32,1536]{1,0:T(8,128)S(1)}, f32[8,384]{1,0:T(8,128)}) custom-call(f32[8,384]{1,0:T(8,128)S(1)} %get-tuple-element.20.own, f32[8,384]{1,0:T(8,128)S(1)} %collective-permute-done.7.s1, f32[8,384]{1,0:T(8,128)S(1)} %collective-permute-done.8.s2, f32[8,384]{1,0:T(8,128)S(1)} %collective-permute-done.9.s3, f32[9,32,288]{2,1,0:T(8,128)S(1)} %copy-done.1, ...), custom_call_target="tpu_custom_call" | custom-call | tf_op jit(solution)/shard_map/sums/pallas_call | solution.py:450
  42.4 0.0 copy-start.7
  42.4 1.4 %collective-permute-start.10 = (f32[32,1536]{1,0:T(8,128)S(1)}, f32[32,1536]{1,0:T(8,128)S(1)}, u32[]{:S(2)}, u32[]{:S(2)}) collective-permute-start(f32[32,1536]{1,0:T(8,128)S(1)} %get-tuple-element.27), channel_id=1, source_target_pairs={{0,4},{1,5},{2,6},{3,7},{4,0},{5,1},{6,2},{7,3},{8,12},{9,13},{10,... | collective-permute-start | bytes 589832 | tf_op jit(solution)/shard_map/ppermute | solution.py:351
  43.8 0.9 %sums.4 = (f32[32,1536]{1,0:T(8,128)S(1)}, f32[8,384]{1,0:T(8,128)S(1)}) custom-call(f32[8,384]{1,0:T(8,128)S(1)} %get-tuple-element.20.own, f32[8,384]{1,0:T(8,128)S(1)} %collective-permute-done.7.s1, f32[8,384]{1,0:T(8,128)S(1)} %collective-permute-done.8.s2, f32[8,384]{1,0:T(8,128)S(1)} %collective-permute-done.9.s3, ...), custom_call_target="tpu_custom_call" | custom-call | tf_op jit(solution)/shard_map/sums/pallas_call | solution.py:450
  44.7 0.1 constant_dynamic-slice_fusion
  44.8 0.6 %maximum_bitcast_fusion = f32[96,2]{0,1:T(2,128)} fusion(f32[2,48]{1,0:T(2,128)S(1)} %get-tuple-element.33, f32[2,48]{1,0:T(2,128)S(1)} %get-tuple-element.32), kind=kLoop, calls=%fused_computation | loop fusion | flops 192 | bytes 1536 | tf_op jit(solution)/shard_map/transpose | solution.py:484
  45.4 0.6 %collective-permute-done.12.refs_3_ = f32[32,1536]{1,0:T(8,128)S(1)} collective-permute-done((f32[32,1536]{1,0:T(8,128)S(1)}, f32[32,1536]{1,0:T(8,128)S(1)}, u32[]{:S(2)}, u32[]{:S(2)}) %collective-permute-start.12) | collective-permute-done | bytes 196640 | tf_op jit(solution)/shard_map/ppermute | solution.py:351
  46.0 11.2 %collective-permute-done.11.refs_2_ = f32[32,1536]{1,0:T(8,128)S(1)} collective-permute-done((f32[32,1536]{1,0:T(8,128)S(1)}, f32[32,1536]{1,0:T(8,128)S(1)}, u32[]{:S(2)}, u32[]{:S(2)}) %collective-permute-start.11) | collective-permute-done | bytes 196640 | tf_op jit(solution)/shard_map/ppermute | solution.py:351
  57.2 0.0 collective-permute-done.10.refs_1_
  57.2 0.0 copy-done.7
  57.2 0.7 %update.1 = f32[32,1024]{1,0:T(8,128)} custom-call(f32[32,1536]{1,0:T(8,128)S(1)} %get-tuple-element.25.refs_0_, f32[32,1536]{1,0:T(8,128)S(1)} %collective-permute-done.10.refs_1_, f32[32,1536]{1,0:T(8,128)S(1)} %collective-permute-done.11.refs_2_, f32[32,1536]{1,0:T(8,128)S(1)} %collective-permute-done.12.refs_3_, f32[1,512]{1,0:T(1,128)S(1)} %bitcast.12), custom_call_target="tpu_custom_call" | custom-call | tf_op jit(solution)/shard_map/update/pallas_call | solution.py:468
  (1 shorter events, 0.0 us)
Async XLA Ops:
  0.6 21.6 %copy-start.6 = (f32[2,16,1024]{2,1,0:T(8,128)S(1)}, f32[2,16,1024]{2,1,0:T(8,128)}, u32[]{:S(2)}) copy-start(f32[2,16,1024]{2,1,0:T(8,128)} %param.17) | copy-start | bytes 393220
  0.6 18.8 %collective-permute-start.1 = (f32[96,1024]{1,0:T(8,128)}, f32[96,1024]{1,0:T(8,128)S(1)}, u32[]{:S(2)}, u32[]{:S(2)}) collective-permute-start(f32[96,1024]{1,0:T(8,128)} %src_at.1), channel_id=1, source_target_pairs={{0,2},{1,3},{2,0},{3,1},{4,6},{5,7},{6,4},{7,5},{8,10},{9,11},{10,... | collective-permute-start | bytes 1179656 | tf_op jit(solution)/shard_map/ppermute | solution.py:351
  3.7 8.4 %collective-permute-start.4 = (f32[32,1024]{1,0:T(8,128)}, f32[32,1024]{1,0:T(8,128)S(1)}, u32[]{:S(2)}, u32[]{:S(2)}) collective-permute-start(f32[32,1024]{1,0:T(8,128)} %bitcast.9), channel_id=1, source_target_pairs={{0,12},{1,13},{2,14},{3,15},{4,8},{5,9},{6,10},{7,11},{8,4},{9,5},... | collective-permute-start | bytes 393224 | tf_op jit(solution)/shard_map/ppermute | solution.py:351
  7.3 12.8 %collective-permute-start.3 = (f32[32,1024]{1,0:T(8,128)}, f32[32,1024]{1,0:T(8,128)S(1)}, u32[]{:S(2)}, u32[]{:S(2)}) collective-permute-start(f32[32,1024]{1,0:T(8,128)} %bitcast.10), channel_id=1, source_target_pairs={{0,4},{1,5},{2,6},{3,7},{4,0},{5,1},{6,2},{7,3},{8,12},{9,13},{10,... | collective-permute-start | bytes 393224 | tf_op jit(solution)/shard_map/ppermute | solution.py:351
  12.1 7.9 %collective-permute-start.5 = (f32[32,1024]{1,0:T(8,128)S(1)}, f32[32,1024]{1,0:T(8,128)S(1)}, u32[]{:S(2)}, u32[]{:S(2)}) collective-permute-start(f32[32,1024]{1,0:T(8,128)S(1)} %collective-permute-done.4.a_3_.a_7_), channel_id=1, source_target_pairs={{0,4},{1,5},{2,6},{3,7},{4,0},{5,1},{6,2},{7,3},{8,12},{9,13},{10,... | collective-permute-start | bytes 393224 | tf_op jit(solution)/shard_map/ppermute | solution.py:351
  15.7 3.7 %collective-permute-start.2 = (f32[8,128]{1,0:T(8,128)S(1)}, f32[8,128]{1,0:T(8,128)S(1)}, u32[]{:S(2)}, u32[]{:S(2)}) collective-permute-start(f32[8,128]{1,0:T(8,128)S(1)} %get-tuple-element.18), channel_id=1, source_target_pairs={{0,2},{1,3},{2,0},{3,1},{4,6},{5,7},{6,4},{7,5},{8,10},{9,11},{10,... | collective-permute-start | bytes 12296 | tf_op jit(solution)/shard_map/ppermute | solution.py:351
  16.3 3.9 %collective-permute-start = (f32[104,1536]{1,0:T(8,128)S(1)}, f32[104,1536]{1,0:T(8,128)S(1)}, u32[]{:S(2)}, u32[]{:S(2)}) collective-permute-start(f32[104,1536]{1,0:T(8,128)S(1)} %get-tuple-element.17.a_0_), channel_id=1, source_target_pairs={{0,1},{1,0},{2,3},{3,2},{4,5},{5,4},{6,7},{7,6},{8,9},{9,8},{10,11... | collective-permute-start | bytes 1916936 | tf_op jit(solution)/shard_map/ppermute | solution.py:351
  20.1 2.1 %collective-permute-start.6 = (f32[104,1536]{1,0:T(8,128)S(1)}, f32[104,1536]{1,0:T(8,128)S(1)}, u32[]{:S(2)}, u32[]{:S(2)}) collective-permute-start(f32[104,1536]{1,0:T(8,128)S(1)} %gate.1.a_2_), channel_id=1, source_target_pairs={{0,1},{1,0},{2,3},{3,2},{4,5},{5,4},{6,7},{7,6},{8,9},{9,8},{10,11... | collective-permute-start | bytes 1916936 | tf_op jit(solution)/shard_map/ppermute | solution.py:351
  27.6 0.8 %copy-start = (f32[9,32,288]{2,1,0:T(8,128)}, f32[9,32,288]{2,1,0:T(8,128)S(1)}, u32[]{:S(2)}) copy-start(f32[9,32,288]{2,1,0:T(8,128)S(1)} %get-tuple-element.26.e_ref) | copy-start | bytes 995332
  28.4 0.8 %copy-start.2 = (f32[9,32,288]{2,1,0:T(8,128)}, f32[9,32,288]{2,1,0:T(8,128)S(1)}, u32[]{:S(2)}) copy-start(f32[9,32,288]{2,1,0:T(8,128)S(1)} %get-tuple-element.28.e_ref) | copy-start | bytes 995332
  29.2 0.8 %copy-start.4 = (f32[9,32,288]{2,1,0:T(8,128)}, f32[9,32,288]{2,1,0:T(8,128)S(1)}, u32[]{:S(2)}) copy-start(f32[9,32,288]{2,1,0:T(8,128)S(1)} %get-tuple-element.30.e_ref) | copy-start | bytes 995332
  30.0 1.9 %collective-permute-start.7 = (f32[8,384]{1,0:T(8,128)S(1)}, f32[8,384]{1,0:T(8,128)S(1)}, u32[]{:S(2)}, u32[]{:S(2)}) collective-permute-start(f32[8,384]{1,0:T(8,128)S(1)} %get-tuple-element.20.own), channel_id=1, source_target_pairs={{0,1},{1,0},{2,3},{3,2},{4,5},{5,4},{6,7},{7,6},{8,9},{9,8},{10,11... | collective-permute-start | bytes 36872 | tf_op jit(solution)/shard_map/ppermute | solution.py:351
  30.1 3.8 %collective-permute-start.8 = (f32[8,384]{1,0:T(8,128)S(1)}, f32[8,384]{1,0:T(8,128)S(1)}, u32[]{:S(2)}, u32[]{:S(2)}) collective-permute-start(f32[8,384]{1,0:T(8,128)S(1)} %get-tuple-element.20.own), channel_id=1, source_target_pairs={{0,2},{1,3},{2,0},{3,1},{4,6},{5,7},{6,4},{7,5},{8,10},{9,11},{10,... | collective-permute-start | bytes 36872 | tf_op jit(solution)/shard_map/ppermute | solution.py:351
  30.6 3.3 %collective-permute-start.9 = (f32[8,384]{1,0:T(8,128)S(1)}, f32[8,384]{1,0:T(8,128)S(1)}, u32[]{:S(2)}, u32[]{:S(2)}) collective-permute-start(f32[8,384]{1,0:T(8,128)S(1)} %get-tuple-element.20.own), channel_id=1, source_target_pairs={{0,3},{1,2},{2,1},{3,0},{4,7},{5,6},{6,5},{7,4},{8,11},{9,10},{10,... | collective-permute-start | bytes 36872 | tf_op jit(solution)/shard_map/ppermute | solution.py:351
  31.8 7.0 %copy-start.3 = (f32[9,32,288]{2,1,0:T(8,128)S(1)}, f32[9,32,288]{2,1,0:T(8,128)}, u32[]{:S(2)}) copy-start(f32[9,32,288]{2,1,0:T(8,128)} %copy-done.2) | copy-start | bytes 995332
  33.9 1.0 %copy-start.5 = (f32[9,32,288]{2,1,0:T(8,128)S(1)}, f32[9,32,288]{2,1,0:T(8,128)}, u32[]{:S(2)}) copy-start(f32[9,32,288]{2,1,0:T(8,128)} %copy-done.4) | copy-start | bytes 995332
  36.4 4.5 %copy-start.1 = (f32[9,32,288]{2,1,0:T(8,128)S(1)}, f32[9,32,288]{2,1,0:T(8,128)}, u32[]{:S(2)}) copy-start(f32[9,32,288]{2,1,0:T(8,128)} %copy-done) | copy-start | bytes 995332
  36.4 9.7 %collective-permute-start.12 = (f32[32,1536]{1,0:T(8,128)S(1)}, f32[32,1536]{1,0:T(8,128)S(1)}, u32[]{:S(2)}, u32[]{:S(2)}) collective-permute-start(f32[32,1536]{1,0:T(8,128)S(1)} %get-tuple-element.31), channel_id=1, source_target_pairs={{0,12},{1,13},{2,14},{3,15},{4,8},{5,9},{6,10},{7,11},{8,4},{9,5},... | collective-permute-start | bytes 589832 | tf_op jit(solution)/shard_map/ppermute | solution.py:351
  40.4 16.9 %collective-permute-start.11 = (f32[32,1536]{1,0:T(8,128)S(1)}, f32[32,1536]{1,0:T(8,128)S(1)}, u32[]{:S(2)}, u32[]{:S(2)}) collective-permute-start(f32[32,1536]{1,0:T(8,128)S(1)} %get-tuple-element.29), channel_id=1, source_target_pairs={{0,8},{1,9},{2,10},{3,11},{4,12},{5,13},{6,14},{7,15},{8,0},{9,1},... | collective-permute-start | bytes 589832 | tf_op jit(solution)/shard_map/ppermute | solution.py:351
  42.4 14.8 %copy-start.7 = (f32[512]{0:T(512)S(1)}, f32[512]{0:T(512)}, u32[]{:S(2)}) copy-start(f32[512]{0:T(512)} %param.16) | copy-start | bytes 6148
  42.4 14.8 %collective-permute-start.10 = (f32[32,1536]{1,0:T(8,128)S(1)}, f32[32,1536]{1,0:T(8,128)S(1)}, u32[]{:S(2)}, u32[]{:S(2)}) collective-permute-start(f32[32,1536]{1,0:T(8,128)S(1)} %get-tuple-element.27), channel_id=1, source_target_pairs={{0,4},{1,5},{2,6},{3,7},{4,0},{5,1},{6,2},{7,3},{8,12},{9,13},{10,... | collective-permute-start | bytes 589832 | tf_op jit(solution)/shard_map/ppermute | solution.py:351

commit v4 on v3

--- a/solution.py
+++ b/solution.py
@@ -330,6 +330,10 @@
     part_out[:, width:] = dot_nn(deep_lanes(jnp.sum(w, axis=0)), power_ref[...])
 
 
+def add_kernel(a, b, out):
+    out[...] = a[...] + b[...]
+
+
 def final_kernel(*refs):
     own, *others, signal, out = refs
     width = out.shape[1]
@@ -342,8 +346,8 @@
     out[:, freq:] = total[:, freq:width] / denominator
 
 
-def params(blocks):
-    return pltpu.CompilerParams(vmem_limit_bytes=(12 + 2 * blocks) * 1024 * 1024)
+def params(mib):
+    return pltpu.CompilerParams(vmem_limit_bytes=mib * 1024 * 1024)
 
 
 def crossed(block, mask):
@@ -374,8 +378,7 @@
     no_cost = pl.CostEstimate(flops=0, bytes_accessed=0, transcendentals=0)
 
     ynb = crossed(particle_fourier, 2)
-    refs = [refs_own] + [crossed(refs_own, TEAM * n) for n in range(1, blocks) if n != 2]
-    refs.insert(2, crossed(refs[2], TEAM))
+    refs = [refs_own] + [crossed(refs_own, TEAM * n) for n in range(1, blocks)]
     anywhere = pl.BlockSpec(memory_space=pl.ANY)
     own_facts = (
         particle_fourier,
@@ -396,7 +399,7 @@
         out_specs=(vmem,) * 3,
         scratch_shapes=[pltpu.VMEM(x.shape, x.dtype) for x in own_facts]
         + [pltpu.SemaphoreType.DMA((6,))],
-        compiler_params=params(blocks),
+        compiler_params=params(6),
         cost_estimate=no_cost,
         name="own",
     )(*(pltpu.with_memory_space_constraint(x, pltpu.HBM) for x in own_facts), live_count)
@@ -406,7 +409,7 @@
         out_shape=jax.ShapeDtypeStruct((slots + 8, width + freq), f32),
         in_specs=[vmem] * 3,
         out_specs=vmem,
-        compiler_params=params(blocks),
+        compiler_params=params(6),
         cost_estimate=no_cost,
         name="neighbour",
     )(ynb, crossed(facts, 2), inverse_noise)
@@ -416,7 +419,7 @@
         in_specs=[anywhere] * blocks,
         out_specs=anywhere,
         input_output_aliases={0: 0},
-        compiler_params=params(blocks),
+        compiler_params=params(1),
         cost_estimate=no_cost,
         name="gate",
     )(ynb, *refs[1:])
@@ -440,7 +443,7 @@
             pltpu.VMEM((live_rows, freq), bf16),
             pltpu.VMEM((live_rows, freq), bf16),
         ],
-        compiler_params=params(blocks),
+        compiler_params=params(8 + 2 * blocks),
         name="scores",
     )(own, cnb, ynb, cynb, *refs)
 
@@ -455,22 +458,32 @@
             ),
             in_specs=[vmem] * (TEAM + 3),
             out_specs=(vmem,) * 2,
-            compiler_params=params(blocks),
+            compiler_params=params(8),
             name="sums",
         )(*team, e_all[n], y, power)
 
-    arrived = []
-    for n in range(blocks - 1, 0, -1):
-        part, _ = sums(n)
-        arrived.append(crossed(part, TEAM * n))
+    def combined(n, other):
+        return pl.pallas_call(
+            add_kernel,
+            out_shape=jax.ShapeDtypeStruct((per, width + freq), f32),
+            in_specs=[vmem] * 2,
+            out_specs=vmem,
+            compiler_params=params(4),
+            name="combined",
+        )(sums(n)[0], other)
+
+    arrived = [crossed(sums(1)[0], TEAM)]
+    for n in range(2, blocks, 2):
+        handed = crossed(sums(n)[0], TEAM)
+        arrived.append(crossed(combined(n + 1, handed), TEAM * (n + 1)))
     own_part, shift_rows = sums(0)
 
     refs_new = pl.pallas_call(
         final_kernel,
         out_shape=jax.ShapeDtypeStruct((per, width), f32),
-        in_specs=[vmem] * (blocks + 1),
+        in_specs=[vmem] * (len(arrived) + 2),
         out_specs=vmem,
-        compiler_params=params(blocks),
+        compiler_params=params(2 + blocks),
         name="update",
     )(own_part, *arrived[::-1], signal_power.reshape(1, freq))
 

time: 58.1 us -> 51.6 us (0.89)
  waiting for transfers between devices: 23.8 us -> 18.5 us
  local copies, waits for them, and re-layouts: 3.37 us -> 2.61 us
    ppermute x13, waiting for transfers between devices: 23.8 us -> 18.5 us  [crossed(): return lax.ppermute(block, 'dom', [(i, i ^ mask) for i in range(size)])]
    unnamed x16 -> x12, local copies, waits for them, and re-layouts: 3.37 us -> 2.61 us
  transfers between devices with their start and end apart: 13 -> 13, of which waited for: 6 -> 7; matrix products, arithmetic and copies ran while one was open for 1% -> 1% of each run, Pallas kernels for 11% -> 12%
where the time goes in v4:
time: 51.6 us; the launch traced here: 51.4 us
  waiting for transfers between devices  18.5 us (36%)
  starting transfers between devices  14.2 us (28%)
  Pallas kernels  14.1 us (27%)
  local copies, waits for them, and re-layouts  2.61 us (5%)
  between operations  1.35 us (3%)
  other arithmetic  0.71 us (1%)
    ppermute x13, waiting for transfers between devices, crossed(): return lax.ppermute(block, 'dom', [(i, i ^ mask) for i in range(size)])  18.5 us
    ppermute x13, starting transfers between devices, crossed(): return lax.ppermute(block, 'dom', [(i, i ^ mask) for i in range(size)])  14.2 us
    pallas_call x4, Pallas kernels, sums(): pl.pallas_call(sum_kernel, out_shape=(jax.ShapeDtypeStruct((per, width +...  5.55 us
    pallas_call x1, Pallas kernels, on_device(): pl.pallas_call(lambda *a: score_kernel(blocks, *a), out_shape=(*[jax.Shap...  5.41 us
    unnamed x12, local copies, waits for them, and re-layouts  2.61 us
    pallas_call x1, Pallas kernels, on_device(): pl.pallas_call(own_kernel, out_shape=(jax.ShapeDtypeStruct((slots + 8, wi...  1.83 us
  transfers between devices with their start and end apart: 13, of which 7 were waited for; matrix products, arithmetic and copies ran while one was open for 1% of the time, Pallas kernels for 12%

profile of v4, /device:TPU:0, one launch (start us, length us, event | category | flops | bytes accessed | tf_op | source)
XLA Modules:
  0.0 51.4 jit_solution(2029288170044327134)
XLA Ops:
  0.6 0.0 copy-start.4
  0.6 3.0 %collective-permute-start.1 = (f32[96,1024]{1,0:T(8,128)}, f32[96,1024]{1,0:T(8,128)S(1)}, u32[]{:S(2)}, u32[]{:S(2)}) collective-permute-start(f32[96,1024]{1,0:T(8,128)} %src_at.1), channel_id=1, source_target_pairs={{0,2},{1,3},{2,0},{3,1},{4,6},{5,7},{6,4},{7,5},{8,10},{9,11},{10,... | collective-permute-start | bytes 1179656 | tf_op jit(solution)/shard_map/ppermute | solution.py:355
  3.7 1.6 %collective-permute-start.3 = (f32[32,1024]{1,0:T(8,128)}, f32[32,1024]{1,0:T(8,128)S(1)}, u32[]{:S(2)}, u32[]{:S(2)}) collective-permute-start(f32[32,1024]{1,0:T(8,128)} %bitcast.9), channel_id=1, source_target_pairs={{0,4},{1,5},{2,6},{3,7},{4,0},{5,1},{6,2},{7,3},{8,12},{9,13},{10,... | collective-permute-start | bytes 393224 | tf_op jit(solution)/shard_map/ppermute | solution.py:355
  5.3 2.6 %collective-permute-start.4 = (f32[32,1024]{1,0:T(8,128)}, f32[32,1024]{1,0:T(8,128)S(1)}, u32[]{:S(2)}, u32[]{:S(2)}) collective-permute-start(f32[32,1024]{1,0:T(8,128)} %bitcast.10), channel_id=1, source_target_pairs={{0,8},{1,9},{2,10},{3,11},{4,12},{5,13},{6,14},{7,15},{8,0},{9,1},... | collective-permute-start | bytes 393224 | tf_op jit(solution)/shard_map/ppermute | solution.py:355
  7.8 0.2 collective-permute-start.5
  8.7 1.8 %own.1 = (f32[104,1536]{1,0:T(8,128)S(1)}, f32[8,128]{1,0:T(8,128)S(1)}, f32[128,512]{1,0:T(8,128)S(1)}) custom-call(f32[96,1024]{1,0:T(8,128)} %src_at.1, f32[1,96]{1,0:T(1,128)} %bitcast.16, s32[2,96]{1,0:T(2,128)} %bitcast.15, s32[1,96]{1,0:T(1,128)} %bitcast.17, s32[1,96]{1,0:T(1,128)} %bitcast.18, f32[128,512]{1,0:T(8,128)} %noise_at.1, ...), custom_call_target="tpu_custom_call" | custom-call | tf_op jit(solution)/shard_map/own/pallas_call | solution.py:391
  10.6 0.4 collective-permute-start.2
  10.9 3.3 %collective-permute-done.2.facts = f32[8,128]{1,0:T(8,128)S(1)} collective-permute-done((f32[8,128]{1,0:T(8,128)S(1)}, f32[8,128]{1,0:T(8,128)S(1)}, u32[]{:S(2)}, u32[]{:S(2)}) %collective-permute-start.2) | collective-permute-done | bytes 4128 | tf_op jit(solution)/shard_map/ppermute | solution.py:355
  14.2 0.0 collective-permute-start
  14.2 0.0 collective-permute-done.1.src
  14.2 0.6 %neighbour.1.a_0_ = f32[104,1536]{1,0:T(8,128)S(1)} custom-call(f32[96,1024]{1,0:T(8,128)S(1)} %collective-permute-done.1.src, f32[8,128]{1,0:T(8,128)S(1)} %collective-permute-done.2.facts, f32[128,512]{1,0:T(8,128)S(1)} %get-tuple-element.19.inverse_noise), custom_call_target="tpu_custom_call" | custom-call | tf_op jit(solution)/shard_map/neighbour/pallas_call | solution.py:407
  14.9 0.0 collective-permute-done.3.a_1_.a_5_
  14.9 3.2 %collective-permute-done.4.a_2_.a_6_ = f32[32,1024]{1,0:T(8,128)S(1)} collective-permute-done((f32[32,1024]{1,0:T(8,128)}, f32[32,1024]{1,0:T(8,128)S(1)}, u32[]{:S(2)}, u32[]{:S(2)}) %collective-permute-start.4) | collective-permute-done | bytes 131104 | tf_op jit(solution)/shard_map/ppermute | solution.py:355
  18.1 0.0 collective-permute-done.5.a_3_.a_7_
  18.1 0.0 collective-permute-start.6
  18.1 0.0 collective-permute-done.a_1_
  18.1 2.1 %collective-permute-done.6.a_3_ = f32[104,1536]{1,0:T(8,128)S(1)} collective-permute-done((f32[104,1536]{1,0:T(8,128)S(1)}, f32[104,1536]{1,0:T(8,128)S(1)}, u32[]{:S(2)}, u32[]{:S(2)}) %collective-permute-start.6) | collective-permute-done | bytes 639008 | tf_op jit(solution)/shard_map/ppermute | solution.py:355
  20.2 0.0 copy-done.4
  20.2 5.4 %scores.1 = (f32[9,32,288]{2,1,0:T(8,128)S(1)}, f32[9,32,288]{2,1,0:T(8,128)S(1)}, f32[9,32,288]{2,1,0:T(8,128)S(1)}, f32[9,32,288]{2,1,0:T(8,128)S(1)}, bf16[89...) custom-call(f32[104,1536]{1,0:T(8,128)S(1)} %get-tuple-element.17.a_0_, ...), custom_call_target="tpu_custom_call" | custom-call | tf_op jit(solution)/shard_map/scores/pallas_call | solution.py:430
  25.6 0.0 copy-start
  25.6 0.8 %copy-done = f32[9,32,288]{2,1,0:T(8,128)} copy-done((f32[9,32,288]{2,1,0:T(8,128)}, f32[9,32,288]{2,1,0:T(8,128)S(1)}, u32[]{:S(2)}) %copy-start) | copy-done | bytes 331800
  26.4 0.0 copy-start.2
  26.4 0.8 %copy-done.2 = f32[9,32,288]{2,1,0:T(8,128)} copy-done((f32[9,32,288]{2,1,0:T(8,128)}, f32[9,32,288]{2,1,0:T(8,128)S(1)}, u32[]{:S(2)}) %copy-start.2) | copy-done | bytes 331800
  27.2 0.1 collective-permute-start.7
  27.3 0.5 %collective-permute-start.8 = (f32[8,384]{1,0:T(8,128)S(1)}, f32[8,384]{1,0:T(8,128)S(1)}, u32[]{:S(2)}, u32[]{:S(2)}) collective-permute-start(f32[8,384]{1,0:T(8,128)S(1)} %get-tuple-element.20.own), channel_id=1, source_target_pairs={{0,2},{1,3},{2,0},{3,1},{4,6},{5,7},{6,4},{7,5},{8,10},{9,11},{10,... | collective-permute-start | bytes 36872 | tf_op jit(solution)/shard_map/ppermute | solution.py:355
  27.8 1.2 %collective-permute-start.9 = (f32[8,384]{1,0:T(8,128)S(1)}, f32[8,384]{1,0:T(8,128)S(1)}, u32[]{:S(2)}, u32[]{:S(2)}) collective-permute-start(f32[8,384]{1,0:T(8,128)S(1)} %get-tuple-element.20.own), channel_id=1, source_target_pairs={{0,3},{1,2},{2,1},{3,0},{4,7},{5,6},{6,5},{7,4},{8,11},{9,10},{10,... | collective-permute-start | bytes 36872 | tf_op jit(solution)/shard_map/ppermute | solution.py:355
  29.0 0.0 collective-permute-done.7.s1
  29.0 2.0 %collective-permute-done.8.s2 = f32[8,384]{1,0:T(8,128)S(1)} collective-permute-done((f32[8,384]{1,0:T(8,128)S(1)}, f32[8,384]{1,0:T(8,128)S(1)}, u32[]{:S(2)}, u32[]{:S(2)}) %collective-permute-start.8) | collective-permute-done | bytes 12320 | tf_op jit(solution)/shard_map/ppermute | solution.py:355
  31.1 0.0 collective-permute-done.9.s3
  31.1 1.6 %sums.6 = (f32[32,1536]{1,0:T(8,128)}, f32[8,384]{1,0:T(8,128)}) custom-call(f32[8,384]{1,0:T(8,128)S(1)} %get-tuple-element.20.own, f32[8,384]{1,0:T(8,128)S(1)} %collective-permute-done.7.s1, f32[8,384]{1,0:T(8,128)S(1)} %collective-permute-done.8.s2, f32[8,384]{1,0:T(8,128)S(1)} %collective-permute-done.9.s3, f32[9,32,288]{2,1,0:T(8,128)S(1)} %get-tuple-element.28.e_ref, ...), custom_call_target="tpu_custom_call" | custom-call | tf_op jit(solution)/shard_map/sums/pallas_call | solution.py:453
  32.7 2.0 %collective-permute-start.10 = (f32[32,1536]{1,0:T(8,128)}, f32[32,1536]{1,0:T(8,128)S(1)}, u32[]{:S(2)}, u32[]{:S(2)}) collective-permute-start(f32[32,1536]{1,0:T(8,128)} %get-tuple-element.29), channel_id=1, source_target_pairs={{0,4},{1,5},{2,6},{3,7},{4,0},{5,1},{6,2},{7,3},{8,12},{9,13},{10,... | collective-permute-start | bytes 589832 | tf_op jit(solution)/shard_map/ppermute | solution.py:355
  34.7 0.0 copy-start.1
  34.7 0.0 copy-start.3
  34.7 1.1 %copy-done.3 = f32[9,32,288]{2,1,0:T(8,128)S(1)} copy-done((f32[9,32,288]{2,1,0:T(8,128)S(1)}, f32[9,32,288]{2,1,0:T(8,128)}, u32[]{:S(2)}) %copy-start.3) | copy-done | bytes 331800
  35.7 1.5 %sums.7 = (f32[32,1536]{1,0:T(8,128)S(1)}, f32[8,384]{1,0:T(8,128)}) custom-call(f32[8,384]{1,0:T(8,128)S(1)} %get-tuple-element.20.own, f32[8,384]{1,0:T(8,128)S(1)} %collective-permute-done.7.s1, f32[8,384]{1,0:T(8,128)S(1)} %collective-permute-done.8.s2, f32[8,384]{1,0:T(8,128)S(1)} %collective-permute-done.9.s3, f32[9,32,288]{2,1,0:T(8,128)S(1)} %copy-done.3, ...), custom_call_target="tpu_custom_call" | custom-call | tf_op jit(solution)/shard_map/sums/pallas_call | solution.py:453
  37.2 0.1 collective-permute-start.12
  37.3 0.0 copy-done.1
  37.3 1.5 %sums.5 = (f32[32,1536]{1,0:T(8,128)S(1)}, f32[8,384]{1,0:T(8,128)}) custom-call(f32[8,384]{1,0:T(8,128)S(1)} %get-tuple-element.20.own, f32[8,384]{1,0:T(8,128)S(1)} %collective-permute-done.7.s1, f32[8,384]{1,0:T(8,128)S(1)} %collective-permute-done.8.s2, f32[8,384]{1,0:T(8,128)S(1)} %collective-permute-done.9.s3, f32[9,32,288]{2,1,0:T(8,128)S(1)} %copy-done.1, ...), custom_call_target="tpu_custom_call" | custom-call | tf_op jit(solution)/shard_map/sums/pallas_call | solution.py:453
  38.8 0.0 copy-start.5
  38.8 0.9 %sums.4 = (f32[32,1536]{1,0:T(8,128)S(1)}, f32[8,384]{1,0:T(8,128)S(1)}) custom-call(f32[8,384]{1,0:T(8,128)S(1)} %get-tuple-element.20.own, f32[8,384]{1,0:T(8,128)S(1)} %collective-permute-done.7.s1, f32[8,384]{1,0:T(8,128)S(1)} %collective-permute-done.8.s2, f32[8,384]{1,0:T(8,128)S(1)} %collective-permute-done.9.s3, ...), custom_call_target="tpu_custom_call" | custom-call | tf_op jit(solution)/shard_map/sums/pallas_call | solution.py:453
  39.7 0.7 %collective-permute-done.10.b = f32[32,1536]{1,0:T(8,128)S(1)} collective-permute-done((f32[32,1536]{1,0:T(8,128)}, f32[32,1536]{1,0:T(8,128)S(1)}, u32[]{:S(2)}, u32[]{:S(2)}) %collective-permute-start.10) | collective-permute-done | bytes 196640 | tf_op jit(solution)/shard_map/ppermute | solution.py:355
  40.4 2.5 %collective-permute-start.11 = (f32[32,1536]{1,0:T(8,128)S(1)}, f32[32,1536]{1,0:T(8,128)S(1)}, u32[]{:S(2)}, u32[]{:S(2)}) collective-permute-start(f32[32,1536]{1,0:T(8,128)S(1)} %combined.1), channel_id=1, source_target_pairs={{0,12},{1,13},{2,14},{3,15},{4,8},{5,9},{6,10},{7,11},{8,4},{9,5},... | collective-permute-start | bytes 589832 | tf_op jit(solution)/shard_map/ppermute | solution.py:355
  42.9 0.1 constant_dynamic-slice_fusion
  43.0 0.6 %maximum_bitcast_fusion = f32[96,2]{0,1:T(2,128)} fusion(f32[2,48]{1,0:T(2,128)S(1)} %get-tuple-element.33, f32[2,48]{1,0:T(2,128)S(1)} %get-tuple-element.32), kind=kLoop, calls=%fused_computation | loop fusion | flops 192 | bytes 1536 | tf_op jit(solution)/shard_map/transpose | solution.py:497
  43.6 0.7 %collective-permute-done.12.refs_2_ = f32[32,1536]{1,0:T(8,128)S(1)} collective-permute-done((f32[32,1536]{1,0:T(8,128)S(1)}, f32[32,1536]{1,0:T(8,128)S(1)}, u32[]{:S(2)}, u32[]{:S(2)}) %collective-permute-start.12) | collective-permute-done | bytes 196640 | tf_op jit(solution)/shard_map/ppermute | solution.py:355
  44.4 6.4 %collective-permute-done.11.refs_1_ = f32[32,1536]{1,0:T(8,128)S(1)} collective-permute-done((f32[32,1536]{1,0:T(8,128)S(1)}, f32[32,1536]{1,0:T(8,128)S(1)}, u32[]{:S(2)}, u32[]{:S(2)}) %collective-permute-start.11) | collective-permute-done | bytes 196640 | tf_op jit(solution)/shard_map/ppermute | solution.py:355
  50.8 0.0 copy-done.5
  50.8 0.7 %update.1 = f32[32,1024]{1,0:T(8,128)} custom-call(f32[32,1536]{1,0:T(8,128)S(1)} %get-tuple-element.25.refs_0_, f32[32,1536]{1,0:T(8,128)S(1)} %collective-permute-done.11.refs_1_, f32[32,1536]{1,0:T(8,128)S(1)} %collective-permute-done.12.refs_2_, f32[1,512]{1,0:T(1,128)S(1)} %bitcast.13), custom_call_target="tpu_custom_call" | custom-call | tf_op jit(solution)/shard_map/update/pallas_call | solution.py:481
  (2 shorter events, 0.0 us)
Async XLA Ops:
  0.6 19.6 %copy-start.4 = (f32[2,16,1024]{2,1,0:T(8,128)S(1)}, f32[2,16,1024]{2,1,0:T(8,128)}, u32[]{:S(2)}) copy-start(f32[2,16,1024]{2,1,0:T(8,128)} %param.17) | copy-start | bytes 393220
  0.6 13.6 %collective-permute-start.1 = (f32[96,1024]{1,0:T(8,128)}, f32[96,1024]{1,0:T(8,128)S(1)}, u32[]{:S(2)}, u32[]{:S(2)}) collective-permute-start(f32[96,1024]{1,0:T(8,128)} %src_at.1), channel_id=1, source_target_pairs={{0,2},{1,3},{2,0},{3,1},{4,6},{5,7},{6,4},{7,5},{8,10},{9,11},{10,... | collective-permute-start | bytes 1179656 | tf_op jit(solution)/shard_map/ppermute | solution.py:355
  3.7 11.2 %collective-permute-start.3 = (f32[32,1024]{1,0:T(8,128)}, f32[32,1024]{1,0:T(8,128)S(1)}, u32[]{:S(2)}, u32[]{:S(2)}) collective-permute-start(f32[32,1024]{1,0:T(8,128)} %bitcast.9), channel_id=1, source_target_pairs={{0,4},{1,5},{2,6},{3,7},{4,0},{5,1},{6,2},{7,3},{8,12},{9,13},{10,... | collective-permute-start | bytes 393224 | tf_op jit(solution)/shard_map/ppermute | solution.py:355
  5.3 12.9 %collective-permute-start.4 = (f32[32,1024]{1,0:T(8,128)}, f32[32,1024]{1,0:T(8,128)S(1)}, u32[]{:S(2)}, u32[]{:S(2)}) collective-permute-start(f32[32,1024]{1,0:T(8,128)} %bitcast.10), channel_id=1, source_target_pairs={{0,8},{1,9},{2,10},{3,11},{4,12},{5,13},{6,14},{7,15},{8,0},{9,1},... | collective-permute-start | bytes 393224 | tf_op jit(solution)/shard_map/ppermute | solution.py:355
  7.8 10.3 %collective-permute-start.5 = (f32[32,1024]{1,0:T(8,128)}, f32[32,1024]{1,0:T(8,128)S(1)}, u32[]{:S(2)}, u32[]{:S(2)}) collective-permute-start(f32[32,1024]{1,0:T(8,128)} %bitcast.11), channel_id=1, source_target_pairs={{0,12},{1,13},{2,14},{3,15},{4,8},{5,9},{6,10},{7,11},{8,4},{9,5},... | collective-permute-start | bytes 393224 | tf_op jit(solution)/shard_map/ppermute | solution.py:355
  10.6 3.7 %collective-permute-start.2 = (f32[8,128]{1,0:T(8,128)S(1)}, f32[8,128]{1,0:T(8,128)S(1)}, u32[]{:S(2)}, u32[]{:S(2)}) collective-permute-start(f32[8,128]{1,0:T(8,128)S(1)} %get-tuple-element.18), channel_id=1, source_target_pairs={{0,2},{1,3},{2,0},{3,1},{4,6},{5,7},{6,4},{7,5},{8,10},{9,11},{10,... | collective-permute-start | bytes 12296 | tf_op jit(solution)/shard_map/ppermute | solution.py:355
  14.2 3.9 %collective-permute-start = (f32[104,1536]{1,0:T(8,128)S(1)}, f32[104,1536]{1,0:T(8,128)S(1)}, u32[]{:S(2)}, u32[]{:S(2)}) collective-permute-start(f32[104,1536]{1,0:T(8,128)S(1)} %get-tuple-element.17.a_0_), channel_id=1, source_target_pairs={{0,1},{1,0},{2,3},{3,2},{4,5},{5,4},{6,7},{7,6},{8,9},{9,8},{10,11... | collective-permute-start | bytes 1916936 | tf_op jit(solution)/shard_map/ppermute | solution.py:355
  18.1 2.1 %collective-permute-start.6 = (f32[104,1536]{1,0:T(8,128)S(1)}, f32[104,1536]{1,0:T(8,128)S(1)}, u32[]{:S(2)}, u32[]{:S(2)}) collective-permute-start(f32[104,1536]{1,0:T(8,128)S(1)} %gate.1.a_2_), channel_id=1, source_target_pairs={{0,1},{1,0},{2,3},{3,2},{4,5},{5,4},{6,7},{7,6},{8,9},{9,8},{10,11... | collective-permute-start | bytes 1916936 | tf_op jit(solution)/shard_map/ppermute | solution.py:355
  25.6 0.8 %copy-start = (f32[9,32,288]{2,1,0:T(8,128)}, f32[9,32,288]{2,1,0:T(8,128)S(1)}, u32[]{:S(2)}) copy-start(f32[9,32,288]{2,1,0:T(8,128)S(1)} %get-tuple-element.26.e_ref) | copy-start | bytes 995332
  26.4 0.8 %copy-start.2 = (f32[9,32,288]{2,1,0:T(8,128)}, f32[9,32,288]{2,1,0:T(8,128)S(1)}, u32[]{:S(2)}) copy-start(f32[9,32,288]{2,1,0:T(8,128)S(1)} %get-tuple-element.30.e_ref) | copy-start | bytes 995332
  27.2 1.9 %collective-permute-start.7 = (f32[8,384]{1,0:T(8,128)S(1)}, f32[8,384]{1,0:T(8,128)S(1)}, u32[]{:S(2)}, u32[]{:S(2)}) collective-permute-start(f32[8,384]{1,0:T(8,128)S(1)} %get-tuple-element.20.own), channel_id=1, source_target_pairs={{0,1},{1,0},{2,3},{3,2},{4,5},{5,4},{6,7},{7,6},{8,9},{9,8},{10,11... | collective-permute-start | bytes 36872 | tf_op jit(solution)/shard_map/ppermute | solution.py:355
  27.3 3.8 %collective-permute-start.8 = (f32[8,384]{1,0:T(8,128)S(1)}, f32[8,384]{1,0:T(8,128)S(1)}, u32[]{:S(2)}, u32[]{:S(2)}) collective-permute-start(f32[8,384]{1,0:T(8,128)S(1)} %get-tuple-element.20.own), channel_id=1, source_target_pairs={{0,2},{1,3},{2,0},{3,1},{4,6},{5,7},{6,4},{7,5},{8,10},{9,11},{10,... | collective-permute-start | bytes 36872 | tf_op jit(solution)/shard_map/ppermute | solution.py:355
  27.8 3.3 %collective-permute-start.9 = (f32[8,384]{1,0:T(8,128)S(1)}, f32[8,384]{1,0:T(8,128)S(1)}, u32[]{:S(2)}, u32[]{:S(2)}) collective-permute-start(f32[8,384]{1,0:T(8,128)S(1)} %get-tuple-element.20.own), channel_id=1, source_target_pairs={{0,3},{1,2},{2,1},{3,0},{4,7},{5,6},{6,5},{7,4},{8,11},{9,10},{10,... | collective-permute-start | bytes 36872 | tf_op jit(solution)/shard_map/ppermute | solution.py:355
  32.7 7.7 %collective-permute-start.10 = (f32[32,1536]{1,0:T(8,128)}, f32[32,1536]{1,0:T(8,128)S(1)}, u32[]{:S(2)}, u32[]{:S(2)}) collective-permute-start(f32[32,1536]{1,0:T(8,128)} %get-tuple-element.29), channel_id=1, source_target_pairs={{0,4},{1,5},{2,6},{3,7},{4,0},{5,1},{6,2},{7,3},{8,12},{9,13},{10,... | collective-permute-start | bytes 589832 | tf_op jit(solution)/shard_map/ppermute | solution.py:355
  34.7 2.6 %copy-start.1 = (f32[9,32,288]{2,1,0:T(8,128)S(1)}, f32[9,32,288]{2,1,0:T(8,128)}, u32[]{:S(2)}) copy-start(f32[9,32,288]{2,1,0:T(8,128)} %copy-done) | copy-start | bytes 995332
  34.7 1.1 %copy-start.3 = (f32[9,32,288]{2,1,0:T(8,128)S(1)}, f32[9,32,288]{2,1,0:T(8,128)}, u32[]{:S(2)}) copy-start(f32[9,32,288]{2,1,0:T(8,128)} %copy-done.2) | copy-start | bytes 995332
  37.2 7.1 %collective-permute-start.12 = (f32[32,1536]{1,0:T(8,128)S(1)}, f32[32,1536]{1,0:T(8,128)S(1)}, u32[]{:S(2)}, u32[]{:S(2)}) collective-permute-start(f32[32,1536]{1,0:T(8,128)S(1)} %get-tuple-element.31), channel_id=1, source_target_pairs={{0,4},{1,5},{2,6},{3,7},{4,0},{5,1},{6,2},{7,3},{8,12},{9,13},{10,... | collective-permute-start | bytes 589832 | tf_op jit(solution)/shard_map/ppermute | solution.py:355
  38.8 12.0 %copy-start.5 = (f32[512]{0:T(512)S(1)}, f32[512]{0:T(512)}, u32[]{:S(2)}) copy-start(f32[512]{0:T(512)} %param.16) | copy-start | bytes 6148
  40.4 10.3 %collective-permute-start.11 = (f32[32,1536]{1,0:T(8,128)S(1)}, f32[32,1536]{1,0:T(8,128)S(1)}, u32[]{:S(2)}, u32[]{:S(2)}) collective-permute-start(f32[32,1536]{1,0:T(8,128)S(1)} %combined.1), channel_id=1, source_target_pairs={{0,12},{1,13},{2,14},{3,15},{4,8},{5,9},{6,10},{7,11},{8,4},{9,5},... | collective-permute-start | bytes 589832 | tf_op jit(solution)/shard_map/ppermute | solution.py:355

commit v5 on v4

v5 whole, which is shorter than its diff:
```python
import math

import jax
import jax.numpy as jnp
from jax import lax
from jax.experimental import pallas as pl
from jax.experimental.pallas import tpu as pltpu
from jax.sharding import PartitionSpec as P

ROT = 16
SIDE = 3
BOX = 128
FY = 32
SHIFTS = 9
TEAM = 4
PRIOR = 2.0
CTF_SIZE = math.hypot(0.995, 0.1)
CTF_TURN = math.atan2(0.1, 0.995)
SINE = (
    9.99999976e-01,
    -1.66666476e-01,
    8.33289854e-03,
    -1.98008185e-04,
    2.59032780e-06,
)
TWO_PI = 2.0 * math.pi
PI_A = 3.140625
PI_B = 0.0009670257568359375
PI_C = math.pi - PI_A - PI_B
HIGHEST = lax.Precision.HIGHEST
GRID = tuple((t // SIDE - SIDE // 2, t % SIDE - SIDE // 2) for t in range(SHIFTS))


def half_turn_sine(x):
    s = x * x
    p = SINE[4]
    for c in SINE[3::-1]:
        p = p * s + c
    return x * p


def turn_cos(turns):
    t = jnp.abs(turns - jnp.round(turns))
    return half_turn_sine(TWO_PI * (0.25 - t))


def turn_sin(turns):
    return turn_cos(turns - 0.25)


def freq_rows(width, rows):
    f = lax.broadcasted_iota(jnp.int32, (rows, width), 1)
    kx = (f // FY).astype(jnp.float32)
    ky = (f % FY - FY // 2).astype(jnp.float32)
    return kx, ky


def dot_nt(a, b):
    return lax.dot_general(
        a, b, (((1,), (1,)), ((), ())), preferred_element_type=jnp.float32
    )


def dot_nn(a, b):
    return lax.dot_general(
        a, b, (((1,), (0,)), ((), ())), preferred_element_type=jnp.float32
    )


def exact_dot_nn(a, b):
    return lax.dot_general(
        a, b, (((1,), (0,)), ((), ())), precision=HIGHEST, preferred_element_type=jnp.float32
    )


def halves(x):
    high = x.astype(jnp.bfloat16)
    return high, (x - high.astype(jnp.float32)).astype(jnp.bfloat16)


def deep_rows(a_high, a_low, b_high, b_low):
    rows = a_high.shape[0]
    main, left = slice(0, 128), slice(128, rows)
    order = ((a_high, b_high), (a_low, b_low), (a_high, b_high))
    parts = [x[main] for pair in order for x in pair]
    parts += [x[left] for pair in order for x in pair]
    parts.append(jnp.zeros((128 - 6 * (rows - 128), a_high.shape[1]), a_high.dtype))
    return jnp.concatenate(parts, axis=0)


def deep_lanes(a, b):
    rows, lanes = a.shape
    left = lanes - 128
    high, low = halves(jnp.concatenate([a[:, :128], b[:, :128]], axis=1))
    empty = jnp.zeros((rows, 128 - left), jnp.float32)
    tail = jnp.concatenate([a[:, 128:], empty], axis=1) + pltpu.roll(
        jnp.concatenate([b[:, 128:], empty], axis=1), left, 1
    )
    tail_high = tail.astype(jnp.bfloat16).astype(jnp.float32)
    tail_low = tail - tail_high
    mixed = (
        tail_high + pltpu.roll(tail_high, 2 * left, 1) + pltpu.roll(tail_low, 4 * left, 1)
    )
    return jnp.concatenate([high, high, low, mixed.astype(jnp.bfloat16)], axis=1)


def grid_phases(width):
    kx, ky = freq_rows(width, 1)
    out = []
    for t, (gx, gy) in enumerate(GRID):
        if t < SHIFTS // 2:
            m = (kx * gx + ky * gy) * (1.0 / BOX)
            out.append((turn_cos(m), turn_sin(m)))
    return out


def phase_of(phases, t):
    mid = SHIFTS // 2
    if t < mid:
        return phases[t]
    c, s = phases[SHIFTS - 1 - t]
    return c, -s


def prepared_rows(src, facts, inverse_noise, out):
    slots, width = src.shape
    freq = width // 2
    columns = jnp.concatenate([facts, jnp.zeros((120, 128), jnp.float32)], axis=0).T[:slots]
    focus = columns[:, 0:1]
    off_x = columns[:, 1:2]
    off_y = columns[:, 2:3]
    group_col = columns[:, 4:5]

    kx, ky = freq_rows(freq, 1)
    chi = focus * ((kx * kx + ky * ky) * (1.0 / 1024.0))
    k = jnp.round(chi * (1.0 / math.pi))
    rest_angle = ((chi - k * PI_A) - k * PI_B) - k * PI_C
    shifted_angle = rest_angle + CTF_TURN
    over = shifted_angle > (0.5 * math.pi)
    folded = jnp.where(over, math.pi - shifted_angle, shifted_angle)
    parity = 0.5 * k
    sign = (parity - jnp.floor(parity)) * (4.0 * CTF_SIZE) - CTF_SIZE
    ctf = half_turn_sine(folded) * sign
    kx0, ky0 = freq_rows(128, 1)
    m = (kx0 * off_x + ky0 * off_y) * (1.0 / BOX)
    pc, ps = turn_cos(m), turn_sin(m)
    step = off_x * ((128 // FY) / BOX) + jnp.zeros((slots, 128), jnp.float32)
    sc, ss = turn_cos(step), turn_sin(step)

    total = inverse_noise.shape[0]
    onehot = (
        group_col == lax.broadcasted_iota(jnp.int32, (slots, total), 1).astype(jnp.float32)
    ).astype(jnp.float32)
    noise_rows = exact_dot_nn(onehot, inverse_noise)
    scaled = ctf * noise_rows
    out[:slots, width:] = ctf * scaled
    for n in range(freq // 128):
        part = slice(128 * n, 128 * (n + 1))
        twin = slice(freq + 128 * n, freq + 128 * (n + 1))
        co = pc * scaled[:, part]
        si = ps * scaled[:, part]
        pc, ps = pc * sc - ps * ss, ps * sc + pc * ss
        xr, xi = src[:, part], src[:, twin]
        out[:slots, part] = xr * co - xi * si
        out[:slots, twin] = xr * si + xi * co
    out[slots:, :128] = facts
    out[slots:, 128:] = jnp.zeros((8, width + freq - 128), jnp.float32)


def own_kernel(
    src_at, focus_at, offsets_at, prior_at, group_at, noise_at, live_count, out, facts_out,
    inverse_out, src, focus, offsets, prior, group, noise, sems
):
    moves = (
        (focus_at, focus), (offsets_at, offsets), (prior_at, prior), (group_at, group),
        (noise_at, noise), (src_at, src),
    )
    copies = [pltpu.make_async_copy(x, y, sems.at[n]) for n, (x, y) in enumerate(moves)]
    for copy in copies:
        copy.start()
    slots = src.shape[0]
    facts_out[...] = jnp.zeros_like(facts_out)
    slot = lax.broadcasted_iota(jnp.int32, (1, slots), 1)
    facts_out[5:6, :slots] = (slot < live_count[0]).astype(jnp.float32)
    for copy in copies:
        copy.wait()
    facts_out[0:1, :slots] = focus[...]
    facts_out[1:3, :slots] = offsets[...].astype(jnp.float32)
    facts_out[3:4, :slots] = prior[...].astype(jnp.float32)
    facts_out[4:5, :slots] = group[...].astype(jnp.float32)
    inverse = 1.0 / noise[...]
    inverse_out[...] = inverse
    prepared_rows(src, facts_out[...], inverse, out)


def neighbour_kernel(src, facts, inverse_noise, wait, out):
    prepared_rows(src, facts[...], inverse_noise[...], out)


def even_core():
    return lax.axis_index("dom") % 2 == 0


def place_half(mine, other, y_high, y_low, p_high, p_low):
    width = y_high.shape[1]
    slots = mine.shape[0] - 8

    def place(src, to, size):
        dest = slice(to, to + size)
        high, low = halves(src[:size, :width])
        y_high[dest] = high
        y_low[dest] = low
        high, low = halves(src[:size, width:])
        p_high[dest] = high
        p_low[dest] = low

    even = even_core()

    @pl.when(even)
    def _():
        place(mine, 0, slots)
        place(other, slots, slots // 2)

    @pl.when(jnp.logical_not(even))
    def _():
        place(other, 0, slots)
        place(mine, slots, slots // 2)


def half_facts(mine, other):
    slots = mine.shape[0] - 8
    even = even_core()
    x, y = mine[slots:, :128], other[slots:, :128]
    heavy = jnp.where(even, x, y)
    light = pltpu.roll(jnp.where(even, y, x), 96, 1)
    lane = lax.broadcasted_iota(jnp.int32, (8, 128), 1)
    return jnp.concatenate([jnp.where(lane < 96, heavy, light), light], axis=1)


def prior_rows(facts, per, lanes):
    r = (lax.broadcasted_iota(jnp.int32, (per, lanes), 0) % ROT).astype(jnp.float32)
    return PRIOR * turn_cos((r - facts[3:4, :lanes]) * (1.0 / ROT))


def prepare_refs(ref, phases, r_high, r_low, q_high, q_low):
    per, width = ref.shape
    freq = width // 2
    rr, ri = ref[:, :freq], ref[:, freq:]
    mid = SHIFTS // 2

    def store(t, re, im):
        rows = slice(t * per, (t + 1) * per)
        r_high[rows, :freq], r_low[rows, :freq] = halves(re)
        r_high[rows, freq:], r_low[rows, freq:] = halves(im)

    store(mid, rr, ri)
    for t in range(mid):
        c, s = phases[t]
        a, b, d, e = rr * c, ri * s, ri * c, rr * s
        store(t, a + b, d - e)
        store(SHIFTS - 1 - t, a - b, d + e)
    q_high[...], q_low[...] = halves(rr * rr + ri * ri)


def block_scores(prepared, particles, prior):
    r_high, r_low, q_high, q_low = (x[...] for x in prepared)
    y_high, y_low, p_high, p_low = particles
    quad = dot_nt(q_high, p_high) + dot_nt(q_low, p_high) + dot_nt(q_high, p_low)
    score = dot_nt(r_high, y_high) + dot_nt(r_low, y_high) + dot_nt(r_high, y_low)
    per, lanes = prior.shape
    return score.reshape(SHIFTS, per, lanes) + (prior - 0.5 * quad)[None]


def weigh(scores, facts, e_outs, stats_out):
    per, lanes = scores[0].shape[1:]
    top = None
    for score in scores:
        top_here = jnp.max(score[...], axis=0)
        top = top_here if top is None else jnp.maximum(top, top_here)
    top = jnp.max(top, axis=0, keepdims=True)
    sums = [jnp.zeros((per, lanes), jnp.float32) for _ in range(SHIFTS)]
    for score, e_out in zip(scores, e_outs):
        for t in range(SHIFTS):
            e = jnp.exp(score[t] - top)
            e_out[t] = e
            sums[t] = sums[t] + e
    sums = [jnp.sum(s, axis=0, keepdims=True) for s in sums]
    stats_out[...] = jnp.zeros_like(stats_out)
    stats_out[0:1, :lanes] = top
    stats_out[1:2, :lanes] = sum(sums)
    stats_out[2:3, :lanes] = sum(s * float(gx) for s, (gx, gy) in zip(sums, GRID) if gx)
    stats_out[3:4, :lanes] = sum(s * float(gy) for s, (gx, gy) in zip(sums, GRID) if gy)
    stats_out[4:5, :lanes] = facts[5:6, :lanes]


def early_kernel(count, *rest):
    refs, prepared = rest[:count], rest[count:]
    phases = grid_phases(refs[0].shape[1] // 2)
    for n in range(count):
        prepare_refs(refs[n], phases, *prepared[4 * n : 4 * n + 4])


def middle_kernel(count, early, own, cnb, *rest):
    refs, rest = rest[:count], rest[count:]
    ready, rest = rest[: 4 * early], rest[4 * early :]
    particles, rest = rest[:4], rest[4:]
    prepared, rest = rest[: 4 * count], rest[4 * count :]
    e_outs, stats_out = rest[:-1], rest[-1]
    place_half(own, cnb, *particles)
    particles = [x[...] for x in particles]
    facts = half_facts(own, cnb)
    prior = prior_rows(facts, refs[0].shape[0], particles[0].shape[0])
    phases = grid_phases(refs[0].shape[1] // 2)
    for n in range(early):
        e_outs[n][...] = block_scores(ready[4 * n : 4 * n + 4], particles, prior)
    for n in range(count):
        block = prepared[4 * n : 4 * n + 4]
        prepare_refs(refs[n], phases, *block)
        e_outs[early + n][...] = block_scores(block, particles, prior)
    weigh(e_outs, facts, e_outs, stats_out)


def late_kernel(blocks, ynb, cynb, early_stats, *rest):
    prepared, rest = rest[: 4 * blocks], rest[4 * blocks :]
    first_half, rest = rest[:4], rest[4:]
    e_outs, rest = rest[:blocks], rest[blocks:]
    y_out, power_out, stats_out, late_stats, *particles = rest
    place_half(ynb, cynb, *particles)
    half = [x[...] for x in particles]
    early = [x[...] for x in first_half]
    y_out[...] = deep_rows(early[0], early[1], half[0], half[1])
    power_out[...] = deep_rows(early[2], early[3], half[2], half[3])
    per = e_outs[0].shape[1]
    facts = half_facts(ynb, cynb)
    prior = prior_rows(facts, per, half[0].shape[0])
    for n in range(blocks):
        e_outs[n][...] = block_scores(prepared[4 * n : 4 * n + 4], half, prior)
    weigh(e_outs, facts, e_outs, late_stats)
    first = (lax.axis_index("dom") // 2) % 2 == 0
    mine, others = early_stats[...], late_stats[...]
    stats_out[:, :256] = jnp.where(first, mine, others)
    stats_out[:, 256:] = jnp.where(first, others, mine)


def sum_kernel(cuts, shifts, waits, *rest):
    team, rest = rest[:TEAM], rest[TEAM + waits :]
    ea_ref, eb_ref, y_ref, power_ref, *outs = rest
    per, lanes = ea_ref.shape[1:]
    width = y_ref.shape[1]
    freq = width // 2
    first = (lax.axis_index("dom") // 2) % 2 == 0
    team = [s[...] for s in team]
    top = team[0][0:1]
    for s in team[1:]:
        top = jnp.maximum(top, s[0:1])
    gains = [jnp.exp(s[0:1] - top) for s in team]
    mass = sum(g * s[1:2] for g, s in zip(gains, team))
    live = team[0][4:5] / mass
    own_gain = gains[0] * live
    gain_a = jnp.where(first, own_gain[:, :256], own_gain[:, 256:])[:, :lanes]
    gain_b = jnp.where(first, own_gain[:, 256:], own_gain[:, :256])[:, :lanes]
    if shifts:
        move = jnp.concatenate(
            [sum(g * s[k : k + 1] for g, s in zip(gains, team)) * live for k in (2, 3)], axis=0
        )
        move = jnp.concatenate([move, jnp.zeros((6, 512), jnp.float32)], axis=0)
        move = jnp.where(first, move[:, :256], move[:, 256:])
        lane = lax.broadcasted_iota(jnp.int32, (8, 128), 1)
        light = jnp.where(
            lane < 32, pltpu.roll(move[:, :128], 32, 1), pltpu.roll(move[:, 128:], 32, 1)
        )
        light = jnp.where(lane < 48, light, 0.0)
        shift_out = outs.pop()
        slots = shift_out.shape[1]
        shift_out[...] = jnp.where(even_core(), move[:, :128], light)[:2, :slots]
    wa = ea_ref[...] * gain_a[None]
    wb = eb_ref[...] * gain_b[None]
    rows = SHIFTS * per
    flat = dot_nn(deep_lanes(wa.reshape(rows, lanes), wb.reshape(rows, lanes)), y_ref[...])
    phases = grid_phases(freq)
    mid = SHIFTS // 2

    def block(t):
        return flat[t * per : (t + 1) * per, :freq], flat[t * per : (t + 1) * per, freq:]

    re, im = block(mid)
    for t in range(mid):
        c, s = phases[t]
        ar, ai = block(t)
        br, bi = block(SHIFTS - 1 - t)
        re = re + (ar + br) * c - (ai - bi) * s
        im = im + (ar - br) * s + (ai + bi) * c
    weight = dot_nn(deep_lanes(jnp.sum(wa, axis=0), jnp.sum(wb, axis=0)), power_ref[...])
    for start, stop, out in zip(cuts, cuts[1:], outs):
        part = slice(start, stop)
        out[:, :freq] = re[part]
        out[:, freq:width] = im[part]
        out[:, width:] = weight[part]


def add_kernel(a, b, out):
    out[...] = a[...] + b[...]


def final_kernel(row_cuts, *refs):
    own, *parts, signal, out = refs
    rows, width = out.shape
    freq = width // 2
    inverse = 1.0 / signal[...]
    every = sorted({cut for cuts in row_cuts for cut in cuts})
    for start, stop in zip(every, every[1:]):
        total = own[start:stop]
        at = 0
        for cuts in row_cuts:
            for low, high in zip(cuts, cuts[1:]):
                if low <= start and stop <= high:
                    total = total + parts[at][start - low : stop - low]
                at += 1
        denominator = total[:, width:] + inverse
        out[start:stop, :freq] = total[:, :freq] / denominator
        out[start:stop, freq:] = total[:, freq:width] / denominator


def params(mib):
    return pltpu.CompilerParams(vmem_limit_bytes=mib * 1024 * 1024)


def crossed(block, mask):
    size = lax.axis_size("dom")
    return lax.ppermute(block, "dom", [(i, i ^ mask) for i in range(size)])


def on_device(
    particle_fourier,
    defocus,
    particle_offset,
    prior_rotation,
    group_id,
    live_count,
    noise_power,
    signal_power,
    class_refs,
):
    slots, width = particle_fourier.shape
    freq = width // 2
    size = lax.axis_size("dom")
    blocks = size // TEAM
    refs_own = class_refs.reshape(-1, width)
    per = refs_own.shape[0]
    f32 = jnp.float32
    vmem = pl.BlockSpec(memory_space=pltpu.VMEM)
    no_cost = pl.CostEstimate(flops=0, bytes_accessed=0, transcendentals=0)

    ynb = crossed(particle_fourier, 2)
    anywhere = pl.BlockSpec(memory_space=pl.ANY)
    def gated(x, *waits):
        return pl.pallas_call(
            lambda *a: None,
            out_shape=jax.ShapeDtypeStruct(x.shape, x.dtype),
            in_specs=[anywhere] * (1 + len(waits)),
            out_specs=anywhere,
            input_output_aliases={0: 0},
            compiler_params=params(1),
            cost_estimate=no_cost,
            name="gate",
        )(x, *waits)

    ynb = crossed(particle_fourier, 2)
    refs = {0: refs_own}
    for n in (n for n in range(1, blocks) if n % 2):
        refs[n] = crossed(refs_own, TEAM * n)
    own_facts = (
        particle_fourier,
        defocus.reshape(1, slots),
        particle_offset.T,
        prior_rotation.reshape(1, slots),
        group_id.reshape(1, slots),
        noise_power,
    )
    own, facts, inverse_noise = pl.pallas_call(
        own_kernel,
        out_shape=(
            jax.ShapeDtypeStruct((slots + 8, width + freq), f32),
            jax.ShapeDtypeStruct((8, 128), f32),
            jax.ShapeDtypeStruct(noise_power.shape, f32),
        ),
        in_specs=[anywhere] * 6 + [pl.BlockSpec(memory_space=pltpu.SMEM)],
        out_specs=(vmem,) * 3,
        scratch_shapes=[pltpu.VMEM(x.shape, x.dtype) for x in own_facts]
        + [pltpu.SemaphoreType.DMA((6,))],
        compiler_params=params(6),
        cost_estimate=no_cost,
        name="own",
    )(*(pltpu.with_memory_space_constraint(x, pltpu.HBM) for x in own_facts), live_count)
    cnb = crossed(own, 1)
    for n in range(2, blocks, 2):
        refs[n + 1] = gated(refs[n + 1], facts)
        refs[n] = crossed(refs[n + 1], TEAM)
    refs = [refs[n] for n in range(blocks)]
    half = slots + slots // 2
    bf16 = jnp.bfloat16
    early = 2

    def shaped(rows, cols, dtype=f32):
        return jax.ShapeDtypeStruct((rows, cols), dtype)

    half_shapes = [shaped(half, width, bf16)] * 2 + [shaped(half, freq, bf16)] * 2
    block_shapes = [shaped(SHIFTS * per, width, bf16)] * 2 + [shaped(per, freq, bf16)] * 2
    score_shape = jax.ShapeDtypeStruct((SHIFTS, per, half), f32)

    def call(kernel, operands, out_shape, name, mib, waits=(), scratch=()):
        return pl.pallas_call(
            kernel,
            out_shape=tuple(out_shape),
            in_specs=[vmem] * len(operands),
            out_specs=(vmem,) * len(out_shape),
            scratch_shapes=list(scratch),
            compiler_params=params(mib),
            name=name,
        )(*operands)

    prepared = call(
        lambda *a: early_kernel(early, *a), refs[:early], block_shapes * early, "early", 8
    )
    ynb_prepared = pl.pallas_call(
        neighbour_kernel,
        out_shape=jax.ShapeDtypeStruct((slots + 8, width + freq), f32),
        in_specs=[vmem] * 3 + [anywhere],
        out_specs=vmem,
        compiler_params=params(6),
        cost_estimate=no_cost,
        name="neighbour",
    )(ynb, crossed(facts, 2), inverse_noise, prepared[2])
    ynb_prepared = gated(ynb_prepared, *refs[early:])
    cynb = crossed(ynb_prepared, 1)

    late = blocks - early
    outs = call(
        lambda *a: middle_kernel(late, early, *a),
        (own, cnb, *refs[early:], *prepared),
        half_shapes + block_shapes * late + [score_shape] * blocks + [shaped(8, 256)],
        "middle",
        8 + 2 * blocks,
    )
    particles, outs = outs[:4], outs[4:]
    prepared = (*prepared, *outs[: 4 * late])
    e_own, early_stats = outs[4 * late : -1], outs[-1]

    deep = 3 * 256 + 128
    outs = call(
        lambda *a: late_kernel(blocks, *a),
        (ynb_prepared, cynb, early_stats, *prepared, *particles),
        [score_shape] * blocks + [shaped(deep, width, bf16), shaped(deep, freq, bf16), shaped(8, 512)],
        "late",
        8 + 2 * blocks,
        scratch=[pltpu.VMEM((8, 256), f32)] + [pltpu.VMEM(x.shape, x.dtype) for x in half_shapes],
    )
    e_other, (y, power, stats) = outs[:blocks], outs[blocks:]

    team = [stats] + [crossed(stats, n) for n in range(1, TEAM)]

    def sums(n, cuts, shifts=False, waits=()):
        out_shape = [shaped(b - a, width + freq) for a, b in zip(cuts, cuts[1:])]
        if shifts:
            out_shape.append(shaped(2, slots))
        return pl.pallas_call(
            lambda *a: sum_kernel(cuts, shifts, len(waits), *a),
            out_shape=tuple(out_shape),
            in_specs=[vmem] * TEAM + [anywhere] * len(waits) + [vmem] * 4,
            out_specs=(vmem,) * len(out_shape),
            compiler_params=params(8),
            name="sums",
        )(*team, *waits, e_own[n], e_other[n], y, power)

    def combined(mine, other):
        return pl.pallas_call(
            add_kernel,
            out_shape=jax.ShapeDtypeStruct(mine.shape, f32),
            in_specs=[vmem] * 2,
            out_specs=vmem,
            compiler_params=params(4),
            name="combined",
        )(mine, other)

    uneven = (0, per // 2, per)
    even = (0, per // 2, per)
    row_cuts = []
    parts = []
    waits = []
    for n in range(2, blocks, 2):
        handed = [crossed(x, TEAM) for x in sums(n, uneven)]
        joined = [combined(x, y) for x, y in zip(sums(n + 1, uneven), handed)]
        parts.extend(crossed(x, TEAM * (n + 1)) for x in joined)
        row_cuts.append(uneven)
        waits.extend(joined)
    own_part, shift = sums(0, (0, per), shifts=True, waits=waits)
    parts += [crossed(x, TEAM) for x in sums(1, even, waits=waits)]
    row_cuts.append(even)

    refs_new = pl.pallas_call(
        lambda *a: final_kernel(row_cuts, *a),
        out_shape=jax.ShapeDtypeStruct((per, width), f32),
        in_specs=[vmem] * (len(parts) + 2),
        out_specs=vmem,
        compiler_params=params(2 + blocks),
        name="update",
    )(own_part, *parts, signal_power.reshape(1, freq))

    return (shift.T, refs_new.reshape(class_refs.shape))


def solution(mesh):
    in_specs = (
        P(("groups", "dom"), None),
        P(("groups", "dom")),
        P(("groups", "dom"), None),
        P(("groups", "dom")),
        P(("groups", "dom")),
        P(("groups", "dom")),
        P("groups", None),
        P("groups"),
        P(("groups", "dom"), None, None),
    )
    out_specs = (P(("groups", "dom"), None), P(("groups", "dom"), None, None))
    return jax.shard_map(
        on_device, mesh=mesh, in_specs=in_specs, out_specs=out_specs, check_vma=False
    )
```

time: 51.6 us -> 47.9 us (0.928)
  waiting for transfers between devices: 18.5 us -> 11.8 us
  starting transfers between devices: 14.2 us -> 19.3 us
  local copies, waits for them, and re-layouts: 2.61 us -> 0.91 us
  other arithmetic: 0.71 us -> 0 us
    ppermute x13 -> x16, waiting for transfers between devices: 18.5 us -> 11.8 us  [crossed(): return lax.ppermute(block, 'dom', [(i, i ^ mask) for i in range(size)])]
    ppermute x13 -> x16, starting transfers between devices: 14.2 us -> 19.3 us  [crossed(): return lax.ppermute(block, 'dom', [(i, i ^ mask) for i in range(size)])]
    unnamed x12 -> x4, local copies, waits for them, and re-layouts: 2.61 us -> 0.91 us
    transpose x1 -> x0, other arithmetic: 0.64 us -> none  [on_device(): expected = jnp.concatenate([low, high], axis=1).T]
    pallas_call x8 -> x12, Pallas kernels: 11.7 us -> 12 us  [the longest x3 6.75 us: call(): pl.pallas_call(kernel, out_shape=tuple(out_shape), in_specs=[vmem] * len(...]
  transfers between devices with their start and end apart: 13 -> 16, of which waited for: 7 -> 9; matrix products, arithmetic and copies ran while one was open for 1% -> 0% of each run, Pallas kernels for 12% -> 20%
where the time goes in v5:
time: 47.9 us; the launch traced here: 47.8 us
  starting transfers between devices  19.3 us (40%)
  Pallas kernels  14.4 us (30%)
  waiting for transfers between devices  11.8 us (25%)
  between operations  1.37 us (3%)
  local copies, waits for them, and re-layouts  0.91 us (2%)
    ppermute x16, starting transfers between devices, crossed(): return lax.ppermute(block, 'dom', [(i, i ^ mask) for i in range(size)])  19.3 us
    ppermute x16, waiting for transfers between devices, crossed(): return lax.ppermute(block, 'dom', [(i, i ^ mask) for i in range(size)])  11.8 us
    pallas_call x3, Pallas kernels, call(): pl.pallas_call(kernel, out_shape=tuple(out_shape), in_specs=[vmem] * len(...  6.75 us
    pallas_call x4, Pallas kernels, sums(): pl.pallas_call(lambda *a: sum_kernel(cuts, shifts, len(waits), *a), out_s...  4.49 us
    pallas_call x1, Pallas kernels, on_device(): pl.pallas_call(own_kernel, out_shape=(jax.ShapeDtypeStruct((slots + 8, wi...  1.83 us
  transfers between devices with their start and end apart: 16, of which 9 were waited for; matrix products, arithmetic and copies ran while one was open for 0% of the time, Pallas kernels for 20%

profile of v5, /device:TPU:0, one launch (start us, length us, event | category | flops | bytes accessed | tf_op | source)
XLA Modules:
  0.0 47.8 jit_solution(15514766424928357656)
XLA Ops:
  0.6 3.0 %collective-permute-start = (f32[96,1024]{1,0:T(8,128)}, f32[96,1024]{1,0:T(8,128)S(1)}, u32[]{:S(2)}, u32[]{:S(2)}) collective-permute-start(f32[96,1024]{1,0:T(8,128)} %src_at.1), channel_id=1, source_target_pairs={{0,2},{1,3},{2,0},{3,1},{4,6},{5,7},{6,4},{7,5},{8,10},{9,11},{10,... | collective-permute-start | bytes 1179656 | tf_op jit(solution)/shard_map/ppermute | solution.py:430
  3.7 3.6 %collective-permute-start.3 = (f32[32,1024]{1,0:T(8,128)}, f32[32,1024]{1,0:T(8,128)S(1)}, u32[]{:S(2)}, u32[]{:S(2)}) collective-permute-start(f32[32,1024]{1,0:T(8,128)} %bitcast.8), channel_id=1, source_target_pairs={{0,12},{1,13},{2,14},{3,15},{4,8},{5,9},{6,10},{7,11},{8,4},{9,5},... | collective-permute-start | bytes 393224 | tf_op jit(solution)/shard_map/ppermute | solution.py:430
  7.3 0.0 collective-permute-start.2
  7.9 1.8 %own.1 = (f32[104,1536]{1,0:T(8,128)S(1)}, f32[8,128]{1,0:T(8,128)S(1)}, f32[128,512]{1,0:T(8,128)S(1)}) custom-call(f32[96,1024]{1,0:T(8,128)} %src_at.1, f32[1,96]{1,0:T(1,128)} %bitcast.14, s32[2,96]{1,0:T(2,128)} %bitcast.13, s32[1,96]{1,0:T(1,128)} %bitcast.15, s32[1,96]{1,0:T(1,128)} %bitcast.16, f32[128,512]{1,0:T(8,128)} %noise_at.1, ...), custom_call_target="tpu_custom_call" | custom-call | tf_op jit(solution)/shard_map/own/pallas_call | solution.py:480
  9.8 2.3 %collective-permute-done.3.a_0_ = f32[32,1024]{1,0:T(8,128)S(1)} collective-permute-done((f32[32,1024]{1,0:T(8,128)}, f32[32,1024]{1,0:T(8,128)S(1)}, u32[]{:S(2)}, u32[]{:S(2)}) %collective-permute-start.3) | collective-permute-done | bytes 131104 | tf_op jit(solution)/shard_map/ppermute | solution.py:430
  12.1 1.1 %collective-permute-start.4 = (f32[32,1024]{1,0:T(8,128)S(1)}, f32[32,1024]{1,0:T(8,128)S(1)}, u32[]{:S(2)}, u32[]{:S(2)}) collective-permute-start(f32[32,1024]{1,0:T(8,128)S(1)} %gate.2.a_2_.a_3_), channel_id=1, source_target_pairs={{0,4},{1,5},{2,6},{3,7},{4,0},{5,1},{6,2},{7,3},{8,12},{9,13},{10,... | collective-permute-start | bytes 393224 | tf_op jit(solution)/shard_map/ppermute | solution.py:430
  13.2 0.5 %collective-permute-start.1 = (f32[8,128]{1,0:T(8,128)S(1)}, f32[8,128]{1,0:T(8,128)S(1)}, u32[]{:S(2)}, u32[]{:S(2)}) collective-permute-start(f32[8,128]{1,0:T(8,128)S(1)} %get-tuple-element.45.a_1_), channel_id=1, source_target_pairs={{0,2},{1,3},{2,0},{3,1},{4,6},{5,7},{6,4},{7,5},{8,10},{9,11},{10,... | collective-permute-start | bytes 12296 | tf_op jit(solution)/shard_map/ppermute | solution.py:430
  13.7 0.0 collective-permute-start.6
  13.7 0.7 %collective-permute-done.2.a_1_ = f32[32,1024]{1,0:T(8,128)S(1)} collective-permute-done((f32[32,1024]{1,0:T(8,128)}, f32[32,1024]{1,0:T(8,128)S(1)}, u32[]{:S(2)}, u32[]{:S(2)}) %collective-permute-start.2) | collective-permute-done | bytes 131104 | tf_op jit(solution)/shard_map/ppermute | solution.py:430
  14.4 0.0 copy-start
  14.4 0.9 %copy-done = f32[2,16,1024]{2,1,0:T(8,128)S(1)} copy-done((f32[2,16,1024]{2,1,0:T(8,128)S(1)}, f32[2,16,1024]{2,1,0:T(8,128)}, u32[]{:S(2)}) %copy-start) | copy-done | bytes 131096
  15.3 0.6 %early.1 = (bf16[288,1024]{1,0:T(8,128)(2,1)S(1)}, bf16[288,1024]{1,0:T(8,128)(2,1)S(1)}, bf16[32,512]{1,0:T(8,128)(2,1)S(1)}, bf16[32,512]{1,0:T(8,128)(2,1)S(1...) custom-call(f32[32,1024]{1,0:T(8,128)S(1)} %bitcast.10, ...), custom_call_target="tpu_custom_call" | custom-call | tf_op jit(solution)/shard_map/early/pallas_call | solution.py:512
  15.9 0.9 %collective-permute-done.1.facts = f32[8,128]{1,0:T(8,128)S(1)} collective-permute-done((f32[8,128]{1,0:T(8,128)S(1)}, f32[8,128]{1,0:T(8,128)S(1)}, u32[]{:S(2)}, u32[]{:S(2)}) %collective-permute-start.1) | collective-permute-done | bytes 4128 | tf_op jit(solution)/shard_map/ppermute | solution.py:430
  16.8 0.0 collective-permute-done.src
  16.8 0.6 %neighbour.1.a_0_ = f32[104,1536]{1,0:T(8,128)S(1)} custom-call(f32[96,1024]{1,0:T(8,128)S(1)} %collective-permute-done.src, f32[8,128]{1,0:T(8,128)S(1)} %collective-permute-done.1.facts, f32[128,512]{1,0:T(8,128)S(1)} %get-tuple-element.46.inverse_noise, bf16[32,512]{1,0:T(8,128)(2,1)S(1)} %get-tuple-element.47.wait.a_6_.a_5_), custom_call_target="tpu_custom_call" | custom-call | tf_op jit(solution)/shard_map/neighbour/pallas_call | solution.py:525
  17.5 0.0 collective-permute-done.4.a_1_.a_2_
  17.5 0.1 collective-permute-start.5
  17.6 0.0 collective-permute-done.6.a_1_
  17.6 3.2 %middle.1 = (bf16[144,1024]{1,0:T(8,128)(2,1)S(1)}, bf16[144,1024]{1,0:T(8,128)(2,1)S(1)}, bf16[144,512]{1,0:T(8,128)(2,1)S(1)}, bf16[144,512]{1,0:T(8,128)(2,1)...) custom-call(f32[104,1536]{1,0:T(8,128)S(1)} %get-tuple-element.48.a_, ...), custom_call_target="tpu_custom_call" | custom-call | tf_op jit(solution)/shard_map/middle/pallas_call | solution.py:512
  20.7 0.0 collective-permute-done.5.a_1_
  20.7 3.0 %late.1 = (f32[9,32,144]{2,1,0:T(8,128)S(1)}, f32[9,32,144]{2,1,0:T(8,128)S(1)}, f32[9,32,144]{2,1,0:T(8,128)S(1)}, f32[9,32,144]{2,1,0:T(8,128)S(1)}, bf16[896,...) custom-call(f32[104,1536]{1,0:T(8,128)S(1)} %gate.3.a_0_, ...), custom_call_target="tpu_custom_call" | custom-call | tf_op jit(solution)/shard_map/late/pallas_call | solution.py:512
  23.8 0.6 %collective-permute-start.9 = (f32[8,512]{1,0:T(8,128)S(1)}, f32[8,512]{1,0:T(8,128)S(1)}, u32[]{:S(2)}, u32[]{:S(2)}) collective-permute-start(f32[8,512]{1,0:T(8,128)S(1)} %get-tuple-element.69.a_0_), channel_id=1, source_target_pairs={{0,3},{1,2},{2,1},{3,0},{4,7},{5,6},{6,5},{7,4},{8,11},{9,10},{10,... | collective-permute-start | bytes 49160 | tf_op jit(solution)/shard_map/ppermute | solution.py:430
  24.4 1.5 %collective-permute-start.8 = (f32[8,512]{1,0:T(8,128)S(1)}, f32[8,512]{1,0:T(8,128)S(1)}, u32[]{:S(2)}, u32[]{:S(2)}) collective-permute-start(f32[8,512]{1,0:T(8,128)S(1)} %get-tuple-element.69.a_0_), channel_id=1, source_target_pairs={{0,2},{1,3},{2,0},{3,1},{4,6},{5,7},{6,4},{7,5},{8,10},{9,11},{10,... | collective-permute-start | bytes 49160 | tf_op jit(solution)/shard_map/ppermute | solution.py:430
  25.9 0.0 collective-permute-start.7
  25.9 1.1 %collective-permute-done.9.a_3_ = f32[8,512]{1,0:T(8,128)S(1)} collective-permute-done((f32[8,512]{1,0:T(8,128)S(1)}, f32[8,512]{1,0:T(8,128)S(1)}, u32[]{:S(2)}, u32[]{:S(2)}) %collective-permute-start.9) | collective-permute-done | bytes 16416 | tf_op jit(solution)/shard_map/ppermute | solution.py:430
  27.0 1.1 %collective-permute-done.8.a_2_ = f32[8,512]{1,0:T(8,128)S(1)} collective-permute-done((f32[8,512]{1,0:T(8,128)S(1)}, f32[8,512]{1,0:T(8,128)S(1)}, u32[]{:S(2)}, u32[]{:S(2)}) %collective-permute-start.8) | collective-permute-done | bytes 16416 | tf_op jit(solution)/shard_map/ppermute | solution.py:430
  28.2 0.0 collective-permute-done.7.a_1_
  28.2 1.0 %sums.5 = (f32[16,1536]{1,0:T(8,128)S(1)}, f32[16,1536]{1,0:T(8,128)S(1)}) custom-call(f32[8,512]{1,0:T(8,128)S(1)} %get-tuple-element.69.a_0_, f32[8,512]{1,0:T(8,128)S(1)} %collective-permute-done.7.a_1_, f32[8,512]{1,0:T(8,128)S(1)} %collective-permute-done.8.a_2_, f32[8,512]{1,0:T(8,128)S(1)} %collective-permute-done.9.a_3_, ...), custom_call_target="tpu_custom_call" | custom-call | tf_op jit(solution)/shard_map/sums/pallas_call | solution.py:566
  29.1 0.7 %collective-permute-start.10 = (f32[16,1536]{1,0:T(8,128)S(1)}, f32[16,1536]{1,0:T(8,128)S(1)}, u32[]{:S(2)}, u32[]{:S(2)}) collective-permute-start(f32[16,1536]{1,0:T(8,128)S(1)} %get-tuple-element.77), channel_id=1, source_target_pairs={{0,4},{1,5},{2,6},{3,7},{4,0},{5,1},{6,2},{7,3},{8,12},{9,13},{10,... | collective-permute-start | bytes 294920 | tf_op jit(solution)/shard_map/ppermute | solution.py:430
  29.8 1.4 %collective-permute-start.11 = (f32[16,1536]{1,0:T(8,128)S(1)}, f32[16,1536]{1,0:T(8,128)S(1)}, u32[]{:S(2)}, u32[]{:S(2)}) collective-permute-start(f32[16,1536]{1,0:T(8,128)S(1)} %get-tuple-element.79), channel_id=1, source_target_pairs={{0,4},{1,5},{2,6},{3,7},{4,0},{5,1},{6,2},{7,3},{8,12},{9,13},{10,... | collective-permute-start | bytes 294920 | tf_op jit(solution)/shard_map/ppermute | solution.py:430
  31.2 1.0 %sums.4 = (f32[16,1536]{1,0:T(8,128)S(1)}, f32[16,1536]{1,0:T(8,128)S(1)}) custom-call(f32[8,512]{1,0:T(8,128)S(1)} %get-tuple-element.69.a_0_, f32[8,512]{1,0:T(8,128)S(1)} %collective-permute-done.7.a_1_, f32[8,512]{1,0:T(8,128)S(1)} %collective-permute-done.8.a_2_, f32[8,512]{1,0:T(8,128)S(1)} %collective-permute-done.9.a_3_, ...), custom_call_target="tpu_custom_call" | custom-call | tf_op jit(solution)/shard_map/sums/pallas_call | solution.py:566
  32.1 2.1 %collective-permute-done.10.b = f32[16,1536]{1,0:T(8,128)S(1)} collective-permute-done((f32[16,1536]{1,0:T(8,128)S(1)}, f32[16,1536]{1,0:T(8,128)S(1)}, u32[]{:S(2)}, u32[]{:S(2)}) %collective-permute-start.10) | collective-permute-done | bytes 98336 | tf_op jit(solution)/shard_map/ppermute | solution.py:430
  34.3 3.2 %collective-permute-start.12 = (f32[16,1536]{1,0:T(8,128)S(1)}, f32[16,1536]{1,0:T(8,128)S(1)}, u32[]{:S(2)}, u32[]{:S(2)}) collective-permute-start(f32[16,1536]{1,0:T(8,128)S(1)} %combined.2.a_4_), channel_id=1, source_target_pairs={{0,12},{1,13},{2,14},{3,15},{4,8},{5,9},{6,10},{7,11},{8,4},{9,5},... | collective-permute-start | bytes 294920 | tf_op jit(solution)/shard_map/ppermute | solution.py:430
  37.5 0.0 collective-permute-done.11.b
  37.5 1.0 %sums.7 = (f32[16,1536]{1,0:T(8,128)S(1)}, f32[16,1536]{1,0:T(8,128)S(1)}) custom-call(f32[8,512]{1,0:T(8,128)S(1)} %get-tuple-element.69.a_0_, f32[8,512]{1,0:T(8,128)S(1)} %collective-permute-done.7.a_1_, f32[8,512]{1,0:T(8,128)S(1)} %collective-permute-done.8.a_2_, f32[8,512]{1,0:T(8,128)S(1)} %collective-permute-done.9.a_3_, ...), custom_call_target="tpu_custom_call" | custom-call | tf_op jit(solution)/shard_map/sums/pallas_call | solution.py:566
  38.5 0.0 copy-start.1
  38.5 0.7 %collective-permute-start.14 = (f32[16,1536]{1,0:T(8,128)S(1)}, f32[16,1536]{1,0:T(8,128)S(1)}, u32[]{:S(2)}, u32[]{:S(2)}) collective-permute-start(f32[16,1536]{1,0:T(8,128)S(1)} %get-tuple-element.86), channel_id=1, source_target_pairs={{0,4},{1,5},{2,6},{3,7},{4,0},{5,1},{6,2},{7,3},{8,12},{9,13},{10,... | collective-permute-start | bytes 294920 | tf_op jit(solution)/shard_map/ppermute | solution.py:430
  39.2 1.4 %collective-permute-start.15 = (f32[16,1536]{1,0:T(8,128)S(1)}, f32[16,1536]{1,0:T(8,128)S(1)}, u32[]{:S(2)}, u32[]{:S(2)}) collective-permute-start(f32[16,1536]{1,0:T(8,128)S(1)} %get-tuple-element.87), channel_id=1, source_target_pairs={{0,4},{1,5},{2,6},{3,7},{4,0},{5,1},{6,2},{7,3},{8,12},{9,13},{10,... | collective-permute-start | bytes 294920 | tf_op jit(solution)/shard_map/ppermute | solution.py:430
  40.6 1.4 %collective-permute-start.13 = (f32[16,1536]{1,0:T(8,128)S(1)}, f32[16,1536]{1,0:T(8,128)S(1)}, u32[]{:S(2)}, u32[]{:S(2)}) collective-permute-start(f32[16,1536]{1,0:T(8,128)S(1)} %combined.3.a_5_), channel_id=1, source_target_pairs={{0,12},{1,13},{2,14},{3,15},{4,8},{5,9},{6,10},{7,11},{8,4},{9,5},... | collective-permute-start | bytes 294920 | tf_op jit(solution)/shard_map/ppermute | solution.py:430
  41.9 1.6 %sums.6 = (f32[32,1536]{1,0:T(8,128)S(1)}, f32[2,96]{1,0:T(2,128)}) custom-call(f32[8,512]{1,0:T(8,128)S(1)} %get-tuple-element.69.a_0_, f32[8,512]{1,0:T(8,128)S(1)} %collective-permute-done.7.a_1_, f32[8,512]{1,0:T(8,128)S(1)} %collective-permute-done.8.a_2_, f32[8,512]{1,0:T(8,128)S(1)} %collective-permute-done.9.a_3_, f32[16,1536]{1,0:T(8,128)S(1)} %combined.2.a_4_, ...), custom_call_target="tpu_custom_call" | custom-call | tf_op jit(solution)/shard_map/sums/pallas_call | solution.py:566
  43.5 0.0 collective-permute-done.12.a_1_
  43.5 0.5 %collective-permute-done.14.a_3_ = f32[16,1536]{1,0:T(8,128)S(1)} collective-permute-done((f32[16,1536]{1,0:T(8,128)S(1)}, f32[16,1536]{1,0:T(8,128)S(1)}, u32[]{:S(2)}, u32[]{:S(2)}) %collective-permute-start.14) | collective-permute-done | bytes 98336 | tf_op jit(solution)/shard_map/ppermute | solution.py:430
  44.1 1.2 %collective-permute-done.15.a_4_ = f32[16,1536]{1,0:T(8,128)S(1)} collective-permute-done((f32[16,1536]{1,0:T(8,128)S(1)}, f32[16,1536]{1,0:T(8,128)S(1)}, u32[]{:S(2)}, u32[]{:S(2)}) %collective-permute-start.15) | collective-permute-done | bytes 98336 | tf_op jit(solution)/shard_map/ppermute | solution.py:430
  45.2 1.8 %collective-permute-done.13.a_2_ = f32[16,1536]{1,0:T(8,128)S(1)} collective-permute-done((f32[16,1536]{1,0:T(8,128)S(1)}, f32[16,1536]{1,0:T(8,128)S(1)}, u32[]{:S(2)}, u32[]{:S(2)}) %collective-permute-start.13) | collective-permute-done | bytes 98336 | tf_op jit(solution)/shard_map/ppermute | solution.py:430
  47.1 0.0 copy-done.1
  47.1 0.7 %update.1 = f32[32,1024]{1,0:T(8,128)} custom-call(f32[32,1536]{1,0:T(8,128)S(1)} %get-tuple-element.83.a_0_, f32[16,1536]{1,0:T(8,128)S(1)} %collective-permute-done.12.a_1_, f32[16,1536]{1,0:T(8,128)S(1)} %collective-permute-done.13.a_2_, f32[16,1536]{1,0:T(8,128)S(1)} %collective-permute-done.14.a_3_, f32[16,1536]{1,0:T(8,128)S(1)} %collective-permute-done.15.a_4_, ...), custom_call_target="tpu_custom_call" | custom-call | tf_op jit(solution)/shard_map/update/pallas_call | solution.py:600
  (4 shorter events, 0.0 us)
Async XLA Ops:
  0.6 16.2 %collective-permute-start = (f32[96,1024]{1,0:T(8,128)}, f32[96,1024]{1,0:T(8,128)S(1)}, u32[]{:S(2)}, u32[]{:S(2)}) collective-permute-start(f32[96,1024]{1,0:T(8,128)} %src_at.1), channel_id=1, source_target_pairs={{0,2},{1,3},{2,0},{3,1},{4,6},{5,7},{6,4},{7,5},{8,10},{9,11},{10,... | collective-permute-start | bytes 1179656 | tf_op jit(solution)/shard_map/ppermute | solution.py:430
  3.7 8.4 %collective-permute-start.3 = (f32[32,1024]{1,0:T(8,128)}, f32[32,1024]{1,0:T(8,128)S(1)}, u32[]{:S(2)}, u32[]{:S(2)}) collective-permute-start(f32[32,1024]{1,0:T(8,128)} %bitcast.8), channel_id=1, source_target_pairs={{0,12},{1,13},{2,14},{3,15},{4,8},{5,9},{6,10},{7,11},{8,4},{9,5},... | collective-permute-start | bytes 393224 | tf_op jit(solution)/shard_map/ppermute | solution.py:430
  7.3 7.2 %collective-permute-start.2 = (f32[32,1024]{1,0:T(8,128)}, f32[32,1024]{1,0:T(8,128)S(1)}, u32[]{:S(2)}, u32[]{:S(2)}) collective-permute-start(f32[32,1024]{1,0:T(8,128)} %bitcast.9), channel_id=1, source_target_pairs={{0,4},{1,5},{2,6},{3,7},{4,0},{5,1},{6,2},{7,3},{8,12},{9,13},{10,... | collective-permute-start | bytes 393224 | tf_op jit(solution)/shard_map/ppermute | solution.py:430
  12.1 5.4 %collective-permute-start.4 = (f32[32,1024]{1,0:T(8,128)S(1)}, f32[32,1024]{1,0:T(8,128)S(1)}, u32[]{:S(2)}, u32[]{:S(2)}) collective-permute-start(f32[32,1024]{1,0:T(8,128)S(1)} %gate.2.a_2_.a_3_), channel_id=1, source_target_pairs={{0,4},{1,5},{2,6},{3,7},{4,0},{5,1},{6,2},{7,3},{8,12},{9,13},{10,... | collective-permute-start | bytes 393224 | tf_op jit(solution)/shard_map/ppermute | solution.py:430
  13.2 3.6 %collective-permute-start.1 = (f32[8,128]{1,0:T(8,128)S(1)}, f32[8,128]{1,0:T(8,128)S(1)}, u32[]{:S(2)}, u32[]{:S(2)}) collective-permute-start(f32[8,128]{1,0:T(8,128)S(1)} %get-tuple-element.45.a_1_), channel_id=1, source_target_pairs={{0,2},{1,3},{2,0},{3,1},{4,6},{5,7},{6,4},{7,5},{8,10},{9,11},{10,... | collective-permute-start | bytes 12296 | tf_op jit(solution)/shard_map/ppermute | solution.py:430
  13.7 3.8 %collective-permute-start.6 = (f32[104,1536]{1,0:T(8,128)S(1)}, f32[104,1536]{1,0:T(8,128)S(1)}, u32[]{:S(2)}, u32[]{:S(2)}) collective-permute-start(f32[104,1536]{1,0:T(8,128)S(1)} %get-tuple-element.48.a_0_), channel_id=1, source_target_pairs={{0,1},{1,0},{2,3},{3,2},{4,5},{5,4},{6,7},{7,6},{8,9},{9,8},{10,11... | collective-permute-start | bytes 1916936 | tf_op jit(solution)/shard_map/ppermute | solution.py:430
  14.4 0.9 %copy-start = (f32[2,16,1024]{2,1,0:T(8,128)S(1)}, f32[2,16,1024]{2,1,0:T(8,128)}, u32[]{:S(2)}) copy-start(f32[2,16,1024]{2,1,0:T(8,128)} %param.17) | copy-start | bytes 393220
  17.5 3.2 %collective-permute-start.5 = (f32[104,1536]{1,0:T(8,128)S(1)}, f32[104,1536]{1,0:T(8,128)S(1)}, u32[]{:S(2)}, u32[]{:S(2)}) collective-permute-start(f32[104,1536]{1,0:T(8,128)S(1)} %gate.3.a_0_), channel_id=1, source_target_pairs={{0,1},{1,0},{2,3},{3,2},{4,5},{5,4},{6,7},{7,6},{8,9},{9,8},{10,11... | collective-permute-start | bytes 1916936 | tf_op jit(solution)/shard_map/ppermute | solution.py:430
  23.8 3.2 %collective-permute-start.9 = (f32[8,512]{1,0:T(8,128)S(1)}, f32[8,512]{1,0:T(8,128)S(1)}, u32[]{:S(2)}, u32[]{:S(2)}) collective-permute-start(f32[8,512]{1,0:T(8,128)S(1)} %get-tuple-element.69.a_0_), channel_id=1, source_target_pairs={{0,3},{1,2},{2,1},{3,0},{4,7},{5,6},{6,5},{7,4},{8,11},{9,10},{10,... | collective-permute-start | bytes 49160 | tf_op jit(solution)/shard_map/ppermute | solution.py:430
  24.4 3.7 %collective-permute-start.8 = (f32[8,512]{1,0:T(8,128)S(1)}, f32[8,512]{1,0:T(8,128)S(1)}, u32[]{:S(2)}, u32[]{:S(2)}) collective-permute-start(f32[8,512]{1,0:T(8,128)S(1)} %get-tuple-element.69.a_0_), channel_id=1, source_target_pairs={{0,2},{1,3},{2,0},{3,1},{4,6},{5,7},{6,4},{7,5},{8,10},{9,11},{10,... | collective-permute-start | bytes 49160 | tf_op jit(solution)/shard_map/ppermute | solution.py:430
  25.9 2.2 %collective-permute-start.7 = (f32[8,512]{1,0:T(8,128)S(1)}, f32[8,512]{1,0:T(8,128)S(1)}, u32[]{:S(2)}, u32[]{:S(2)}) collective-permute-start(f32[8,512]{1,0:T(8,128)S(1)} %get-tuple-element.69.a_0_), channel_id=1, source_target_pairs={{0,1},{1,0},{2,3},{3,2},{4,5},{5,4},{6,7},{7,6},{8,9},{9,8},{10,11... | collective-permute-start | bytes 49160 | tf_op jit(solution)/shard_map/ppermute | solution.py:430
  29.1 5.1 %collective-permute-start.10 = (f32[16,1536]{1,0:T(8,128)S(1)}, f32[16,1536]{1,0:T(8,128)S(1)}, u32[]{:S(2)}, u32[]{:S(2)}) collective-permute-start(f32[16,1536]{1,0:T(8,128)S(1)} %get-tuple-element.77), channel_id=1, source_target_pairs={{0,4},{1,5},{2,6},{3,7},{4,0},{5,1},{6,2},{7,3},{8,12},{9,13},{10,... | collective-permute-start | bytes 294920 | tf_op jit(solution)/shard_map/ppermute | solution.py:430
  29.8 7.7 %collective-permute-start.11 = (f32[16,1536]{1,0:T(8,128)S(1)}, f32[16,1536]{1,0:T(8,128)S(1)}, u32[]{:S(2)}, u32[]{:S(2)}) collective-permute-start(f32[16,1536]{1,0:T(8,128)S(1)} %get-tuple-element.79), channel_id=1, source_target_pairs={{0,4},{1,5},{2,6},{3,7},{4,0},{5,1},{6,2},{7,3},{8,12},{9,13},{10,... | collective-permute-start | bytes 294920 | tf_op jit(solution)/shard_map/ppermute | solution.py:430
  34.3 9.3 %collective-permute-start.12 = (f32[16,1536]{1,0:T(8,128)S(1)}, f32[16,1536]{1,0:T(8,128)S(1)}, u32[]{:S(2)}, u32[]{:S(2)}) collective-permute-start(f32[16,1536]{1,0:T(8,128)S(1)} %combined.2.a_4_), channel_id=1, source_target_pairs={{0,12},{1,13},{2,14},{3,15},{4,8},{5,9},{6,10},{7,11},{8,4},{9,5},... | collective-permute-start | bytes 294920 | tf_op jit(solution)/shard_map/ppermute | solution.py:430
  38.5 8.6 %copy-start.1 = (f32[512]{0:T(512)S(1)}, f32[512]{0:T(512)}, u32[]{:S(2)}) copy-start(f32[512]{0:T(512)} %param.16) | copy-start | bytes 6148
  38.5 5.6 %collective-permute-start.14 = (f32[16,1536]{1,0:T(8,128)S(1)}, f32[16,1536]{1,0:T(8,128)S(1)}, u32[]{:S(2)}, u32[]{:S(2)}) collective-permute-start(f32[16,1536]{1,0:T(8,128)S(1)} %get-tuple-element.86), channel_id=1, source_target_pairs={{0,4},{1,5},{2,6},{3,7},{4,0},{5,1},{6,2},{7,3},{8,12},{9,13},{10,... | collective-permute-start | bytes 294920 | tf_op jit(solution)/shard_map/ppermute | solution.py:430
  39.2 6.1 %collective-permute-start.15 = (f32[16,1536]{1,0:T(8,128)S(1)}, f32[16,1536]{1,0:T(8,128)S(1)}, u32[]{:S(2)}, u32[]{:S(2)}) collective-permute-start(f32[16,1536]{1,0:T(8,128)S(1)} %get-tuple-element.87), channel_id=1, source_target_pairs={{0,4},{1,5},{2,6},{3,7},{4,0},{5,1},{6,2},{7,3},{8,12},{9,13},{10,... | collective-permute-start | bytes 294920 | tf_op jit(solution)/shard_map/ppermute | solution.py:430
  40.6 6.5 %collective-permute-start.13 = (f32[16,1536]{1,0:T(8,128)S(1)}, f32[16,1536]{1,0:T(8,128)S(1)}, u32[]{:S(2)}, u32[]{:S(2)}) collective-permute-start(f32[16,1536]{1,0:T(8,128)S(1)} %combined.3.a_5_), channel_id=1, source_target_pairs={{0,12},{1,13},{2,14},{3,15},{4,8},{5,9},{6,10},{7,11},{8,4},{9,5},... | collective-permute-start | bytes 294920 | tf_op jit(solution)/shard_map/ppermute | solution.py:430

commit v6 on v5

--- a/solution.py
+++ b/solution.py
@@ -181,9 +181,9 @@
     slots = src.shape[0]
     facts_out[...] = jnp.zeros_like(facts_out)
     slot = lax.broadcasted_iota(jnp.int32, (1, slots), 1)
-    facts_out[5:6, :slots] = (slot < live_count[0]).astype(jnp.float32)
     for copy in copies:
         copy.wait()
+    facts_out[5:6, :slots] = (slot < live_count[0]).astype(jnp.float32)
     facts_out[0:1, :slots] = focus[...]
     facts_out[1:3, :slots] = offsets[...].astype(jnp.float32)
     facts_out[3:4, :slots] = prior[...].astype(jnp.float32)
@@ -193,7 +193,19 @@
     prepared_rows(src, facts_out[...], inverse, out)
 
 
-def neighbour_kernel(src, facts, inverse_noise, wait, out):
+def neighbour_kernel(src_even, src_odd, facts, inverse_noise, wait, out, src):
+    half = src_odd.shape[0]
+    even = even_core()
+
+    @pl.when(even)
+    def _():
+        src[...] = src_even[...]
+
+    @pl.when(jnp.logical_not(even))
+    def _():
+        src[:half] = src_odd[...]
+        src[half:] = jnp.zeros_like(src[half:])
+
     prepared_rows(src, facts[...], inverse_noise[...], out)
 
 
@@ -293,11 +305,14 @@
     stats_out[4:5, :lanes] = facts[5:6, :lanes]
 
 
-def early_kernel(count, *rest):
-    refs, prepared = rest[:count], rest[count:]
-    phases = grid_phases(refs[0].shape[1] // 2)
-    for n in range(count):
-        prepare_refs(refs[n], phases, *prepared[4 * n : 4 * n + 4])
+def early_kernel(own_at, near, *rest):
+    *prepared, own, sem = rest
+    copy = pltpu.make_async_copy(own_at, own, sem)
+    copy.start()
+    phases = grid_phases(own.shape[1] // 2)
+    prepare_refs(near, phases, *prepared[4:])
+    copy.wait()
+    prepare_refs(own, phases, *prepared[:4])
 
 
 def middle_kernel(count, early, own, cnb, *rest):
@@ -425,9 +440,9 @@
     return pltpu.CompilerParams(vmem_limit_bytes=mib * 1024 * 1024)
 
 
-def crossed(block, mask):
-    size = lax.axis_size("dom")
-    return lax.ppermute(block, "dom", [(i, i ^ mask) for i in range(size)])
+def crossed(block, mask, core=None):
+    devices = [i for i in range(lax.axis_size("dom")) if core is None or i % 2 == core]
+    return lax.ppermute(block, "dom", [(i, i ^ mask) for i in devices])
 
 
 def on_device(
@@ -453,21 +468,24 @@
 
     ynb = crossed(particle_fourier, 2)
     anywhere = pl.BlockSpec(memory_space=pl.ANY)
-    def gated(x, *waits):
+    def gated(arrays, waits, cost):
         return pl.pallas_call(
             lambda *a: None,
-            out_shape=jax.ShapeDtypeStruct(x.shape, x.dtype),
-            in_specs=[anywhere] * (1 + len(waits)),
-            out_specs=anywhere,
-            input_output_aliases={0: 0},
+            out_shape=tuple(jax.ShapeDtypeStruct(x.shape, x.dtype) for x in arrays),
+            in_specs=[anywhere] * (len(arrays) + len(waits)),
+            out_specs=(anywhere,) * len(arrays),
+            input_output_aliases={n: n for n in range(len(arrays))},
             compiler_params=params(1),
-            cost_estimate=no_cost,
+            cost_estimate=cost,
             name="gate",
-        )(x, *waits)
+        )(*arrays, *waits)
 
     ynb = crossed(particle_fourier, 2)
-    refs = {0: refs_own}
-    for n in (n for n in range(1, blocks) if n % 2):
+    anywhere = pl.BlockSpec(memory_space=pl.ANY)
+    ynb_even = crossed(particle_fourier, 2, 0)
+    ynb_odd = crossed(particle_fourier[: slots // 2], 2, 1)
+    refs = {0: refs_own, 1: crossed(refs_own, TEAM)}
+    for n in range(2, blocks, 2):
         refs[n] = crossed(refs_own, TEAM * n)
     own_facts = (
         particle_fourier,
@@ -494,8 +512,8 @@
     )(*(pltpu.with_memory_space_constraint(x, pltpu.HBM) for x in own_facts), live_count)
     cnb = crossed(own, 1)
     for n in range(2, blocks, 2):
-        refs[n + 1] = gated(refs[n + 1], facts)
-        refs[n] = crossed(refs[n + 1], TEAM)
+        (refs[n],) = gated([refs[n]], [facts], no_cost)
+        refs[n + 1] = crossed(refs[n], TEAM)
     refs = [refs[n] for n in range(blocks)]
     half = slots + slots // 2
     bf16 = jnp.bfloat16
@@ -508,9 +526,10 @@
     block_shapes = [shaped(SHIFTS * per, width, bf16)] * 2 + [shaped(per, freq, bf16)] * 2
     score_shape = jax.ShapeDtypeStruct((SHIFTS, per, half), f32)
 
-    def call(kernel, operands, out_shape, name, mib, waits=(), scratch=()):
+    def call(kernel, operands, out_shape, name, mib, cost=None, scratch=()):
         return pl.pallas_call(
             kernel,
+            cost_estimate=cost,
             out_shape=tuple(out_shape),
             in_specs=[vmem] * len(operands),
             out_specs=(vmem,) * len(out_shape),
@@ -519,19 +538,26 @@
             name=name,
         )(*operands)
 
-    prepared = call(
-        lambda *a: early_kernel(early, *a), refs[:early], block_shapes * early, "early", 8
-    )
+    prepared = pl.pallas_call(
+        early_kernel,
+        out_shape=tuple(block_shapes * early),
+        in_specs=[anywhere, vmem],
+        out_specs=(vmem,) * (4 * early),
+        scratch_shapes=[pltpu.VMEM(refs_own.shape, f32), pltpu.SemaphoreType.DMA],
+        compiler_params=params(8),
+        name="early",
+    )(pltpu.with_memory_space_constraint(refs_own, pltpu.HBM), refs[1])
     ynb_prepared = pl.pallas_call(
         neighbour_kernel,
         out_shape=jax.ShapeDtypeStruct((slots + 8, width + freq), f32),
-        in_specs=[vmem] * 3 + [anywhere],
+        in_specs=[vmem] * 4 + [anywhere],
         out_specs=vmem,
         compiler_params=params(6),
+        scratch_shapes=[pltpu.VMEM((slots, width), f32)],
         cost_estimate=no_cost,
         name="neighbour",
-    )(ynb, crossed(facts, 2), inverse_noise, prepared[2])
-    ynb_prepared = gated(ynb_prepared, *refs[early:])
+    )(ynb_even, ynb_odd, crossed(facts, 2), inverse_noise, prepared[2])
+    (ynb_prepared,) = gated([ynb_prepared], refs[early:], no_cost)
     cynb = crossed(ynb_prepared, 1)
 
     late = blocks - early
@@ -582,20 +608,19 @@
             name="combined",
         )(mine, other)
 
-    uneven = (0, per // 2, per)
-    even = (0, per // 2, per)
-    row_cuts = []
-    parts = []
+    cut = (0, per // 2, per)
+    far = []
     waits = []
     for n in range(2, blocks, 2):
-        handed = [crossed(x, TEAM) for x in sums(n, uneven)]
-        joined = [combined(x, y) for x, y in zip(sums(n + 1, uneven), handed)]
-        parts.extend(crossed(x, TEAM * (n + 1)) for x in joined)
-        row_cuts.append(uneven)
+        handed = [crossed(x, TEAM) for x in sums(n + 1, cut)]
+        joined = [combined(x, y) for x, y in zip(sums(n, cut), handed)]
+        far.extend(crossed(x, TEAM * n) for x in joined)
         waits.extend(joined)
     own_part, shift = sums(0, (0, per), shifts=True, waits=waits)
-    parts += [crossed(x, TEAM) for x in sums(1, even, waits=waits)]
-    row_cuts.append(even)
+    near = crossed(sums(1, (0, per), waits=waits)[0], TEAM)
+    far = gated(far, [], pl.CostEstimate(flops=16 * 10**9, bytes_accessed=0, transcendentals=0))
+    parts = [near, *far]
+    row_cuts = [(0, per)] + [cut] * (len(far) // 2)
 
     refs_new = pl.pallas_call(
         lambda *a: final_kernel(row_cuts, *a),

time: 47.9 us -> 49.1 us (1.025)
  Pallas kernels: 14.4 us -> 15 us
    slice x0 -> x1, local copies, waits for them, and re-layouts: none -> 0.94 us  [on_device(): ynb_odd = crossed(particle_fourier[:slots // 2], 2, 1)]
    unnamed x4 -> x2, local copies, waits for them, and re-layouts: 0.91 us -> 0.01 us
    pallas_call x5 -> x6, Pallas kernels: 6.75 us -> 7.34 us  [the longest x2 6.18 us: call(): pl.pallas_call(kernel, cost_estimate=cost, out_shape=tuple(out_shape), in...]
  transfers between devices with their start and end apart: 16 -> 16, of which waited for: 9 -> 9; matrix products, arithmetic and copies ran while one was open for 0% -> 2% of each run, Pallas kernels for 20% -> 21%
where the time goes in v6:
time: 49.1 us; the launch traced here: 48.9 us
  starting transfers between devices  19.6 us (40%)
  Pallas kernels  15 us (31%)
  waiting for transfers between devices  11.9 us (24%)
  between operations  1.38 us (3%)
  local copies, waits for them, and re-layouts  0.94 us (2%)
    ppermute x16, starting transfers between devices, crossed(): return lax.ppermute(block, 'dom', [(i, i ^ mask) for i in devices])  19.6 us
    ppermute x16, waiting for transfers between devices, crossed(): return lax.ppermute(block, 'dom', [(i, i ^ mask) for i in devices])  11.9 us
    pallas_call x2, Pallas kernels, call(): pl.pallas_call(kernel, cost_estimate=cost, out_shape=tuple(out_shape), in...  6.18 us
    pallas_call x4, Pallas kernels, sums(): pl.pallas_call(lambda *a: sum_kernel(cuts, shifts, len(waits), *a), out_s...  4.48 us
    pallas_call x1, Pallas kernels, on_device(): pl.pallas_call(own_kernel, out_shape=(jax.ShapeDtypeStruct((slots + 8, wi...  1.83 us
    pallas_call x1, Pallas kernels, on_device(): pl.pallas_call(early_kernel, out_shape=tuple(block_shapes * early), in_sp...  1.16 us
  transfers between devices with their start and end apart: 16, of which 9 were waited for; matrix products, arithmetic and copies ran while one was open for 2% of the time, Pallas kernels for 21%

profile of v6, /device:TPU:0, one launch (start us, length us, event | category | flops | bytes accessed | tf_op | source)
XLA Modules:
  0.0 48.9 jit_solution(777475705705721336)
XLA Ops:
  0.6 4.9 %collective-permute-start = (f32[96,1024]{1,0:T(8,128)}, f32[96,1024]{1,0:T(8,128)S(1)}, u32[]{:S(2)}, u32[]{:S(2)}) collective-permute-start(f32[96,1024]{1,0:T(8,128)} %src_at.1), channel_id=1, source_target_pairs={{0,2},{2,0},{4,6},{6,4},{8,10},{10,8},{12,14},{14,12},{16,18},{18,... | collective-permute-start | bytes 1179656 | tf_op jit(solution)/shard_map/ppermute | solution.py:445
  5.5 2.7 %collective-permute-start.4 = (f32[32,1024]{1,0:T(8,128)}, f32[32,1024]{1,0:T(8,128)S(1)}, u32[]{:S(2)}, u32[]{:S(2)}) collective-permute-start(f32[32,1024]{1,0:T(8,128)} %bitcast.9), channel_id=1, source_target_pairs={{0,8},{1,9},{2,10},{3,11},{4,12},{5,13},{6,14},{7,15},{8,0},{9,1},... | collective-permute-start | bytes 393224 | tf_op jit(solution)/shard_map/ppermute | solution.py:445
  8.2 0.9 %slice.3 = f32[48,1024]{1,0:T(8,128)S(1)} slice(f32[96,1024]{1,0:T(8,128)} %src_at.1), slice={[0:48], [0:1024]} | slice | bytes 393216 | tf_op jit(solution)/shard_map/slice | solution.py:486
  9.1 0.7 %collective-permute-start.1 = (f32[48,1024]{1,0:T(8,128)S(1)}, f32[48,1024]{1,0:T(8,128)S(1)}, u32[]{:S(2)}, u32[]{:S(2)}) collective-permute-start(f32[48,1024]{1,0:T(8,128)S(1)} %slice.3), channel_id=1, source_target_pairs={{1,3},{3,1},{5,7},{7,5},{9,11},{11,9},{13,15},{15,13},{17,19},{19,... | collective-permute-start | bytes 589832 | tf_op jit(solution)/shard_map/ppermute | solution.py:445
  9.8 1.6 %collective-permute-start.3 = (f32[32,1024]{1,0:T(8,128)}, f32[32,1024]{1,0:T(8,128)S(1)}, u32[]{:S(2)}, u32[]{:S(2)}) collective-permute-start(f32[32,1024]{1,0:T(8,128)} %bitcast.10), channel_id=1, source_target_pairs={{0,4},{1,5},{2,6},{3,7},{4,0},{5,1},{6,2},{7,3},{8,12},{9,13},{10,... | collective-permute-start | bytes 393224 | tf_op jit(solution)/shard_map/ppermute | solution.py:445
  12.1 1.8 %own.1 = (f32[104,1536]{1,0:T(8,128)S(1)}, f32[8,128]{1,0:T(8,128)S(1)}, f32[128,512]{1,0:T(8,128)S(1)}) custom-call(f32[96,1024]{1,0:T(8,128)} %src_at.1, f32[1,96]{1,0:T(1,128)} %bitcast.14, s32[2,96]{1,0:T(2,128)} %bitcast.13, s32[1,96]{1,0:T(1,128)} %bitcast.15, s32[1,96]{1,0:T(1,128)} %bitcast.16, f32[128,512]{1,0:T(8,128)} %noise_at.1, ...), custom_call_target="tpu_custom_call" | custom-call | tf_op jit(solution)/shard_map/own/pallas_call | solution.py:498
  13.9 0.0 collective-permute-done.4.a_0_
  13.9 0.5 %collective-permute-start.5 = (f32[32,1024]{1,0:T(8,128)S(1)}, f32[32,1024]{1,0:T(8,128)S(1)}, u32[]{:S(2)}, u32[]{:S(2)}) collective-permute-start(f32[32,1024]{1,0:T(8,128)S(1)} %gate.3.a_1_.a_2_), channel_id=1, source_target_pairs={{0,4},{1,5},{2,6},{3,7},{4,0},{5,1},{6,2},{7,3},{8,12},{9,13},{10,... | collective-permute-start | bytes 393224 | tf_op jit(solution)/shard_map/ppermute | solution.py:445
  14.5 0.5 %collective-permute-start.2 = (f32[8,128]{1,0:T(8,128)S(1)}, f32[8,128]{1,0:T(8,128)S(1)}, u32[]{:S(2)}, u32[]{:S(2)}) collective-permute-start(f32[8,128]{1,0:T(8,128)S(1)} %get-tuple-element.45.a_1_), channel_id=1, source_target_pairs={{0,2},{1,3},{2,0},{3,1},{4,6},{5,7},{6,4},{7,5},{8,10},{9,11},{10,... | collective-permute-start | bytes 12296 | tf_op jit(solution)/shard_map/ppermute | solution.py:445
  15.0 0.1 collective-permute-done.3.near
  15.0 0.0 collective-permute-start.7
  15.0 1.2 %early.1 = (bf16[288,1024]{1,0:T(8,128)(2,1)S(1)}, bf16[288,1024]{1,0:T(8,128)(2,1)S(1)}, bf16[32,512]{1,0:T(8,128)(2,1)S(1)}, bf16[32,512]{1,0:T(8,128)(2,1)S(1...) custom-call(f32[32,1024]{1,0:T(8,128)} %bitcast.11, ...), custom_call_target="tpu_custom_call" | custom-call | tf_op jit(solution)/shard_map/early/pallas_call | solution.py:541
  16.2 1.9 %collective-permute-done.2.facts = f32[8,128]{1,0:T(8,128)S(1)} collective-permute-done((f32[8,128]{1,0:T(8,128)S(1)}, f32[8,128]{1,0:T(8,128)S(1)}, u32[]{:S(2)}, u32[]{:S(2)}) %collective-permute-start.2) | collective-permute-done | bytes 4128 | tf_op jit(solution)/shard_map/ppermute | solution.py:445
  18.1 0.0 collective-permute-done.1.src_odd
  18.1 0.0 collective-permute-done.src_even
  18.1 0.7 %neighbour.1.a_0_ = f32[104,1536]{1,0:T(8,128)S(1)} custom-call(f32[96,1024]{1,0:T(8,128)S(1)} %collective-permute-done.src_even, f32[48,1024]{1,0:T(8,128)S(1)} %collective-permute-done.1.src_odd, f32[8,128]{1,0:T(8,128)S(1)} %collective-permute-done.2.facts, f32[128,512]{1,0:T(8,128)S(1)} %get-tuple-element.46.inverse_noise, ...), custom_call_target="tpu_custom_call" | custom-call | tf_op jit(solution)/shard_map/neighbour/pallas_call | solution.py:550
  18.7 0.2 collective-permute-done.5.a_2_.a_3_
  19.0 0.0 collective-permute-start.6
  19.0 0.0 collective-permute-done.7.a_1_
  19.0 3.1 %middle.1 = (bf16[144,1024]{1,0:T(8,128)(2,1)S(1)}, bf16[144,1024]{1,0:T(8,128)(2,1)S(1)}, bf16[144,512]{1,0:T(8,128)(2,1)S(1)}, bf16[144,512]{1,0:T(8,128)(2,1)...) custom-call(f32[104,1536]{1,0:T(8,128)S(1)} %get-tuple-element.48.a_, ...), custom_call_target="tpu_custom_call" | custom-call | tf_op jit(solution)/shard_map/middle/pallas_call | solution.py:530
  22.1 0.0 collective-permute-done.6.a_1_
  22.1 3.0 %late.1 = (f32[9,32,144]{2,1,0:T(8,128)S(1)}, f32[9,32,144]{2,1,0:T(8,128)S(1)}, f32[9,32,144]{2,1,0:T(8,128)S(1)}, f32[9,32,144]{2,1,0:T(8,128)S(1)}, bf16[896,...) custom-call(f32[104,1536]{1,0:T(8,128)S(1)} %gate.4.a_0_, ...), custom_call_target="tpu_custom_call" | custom-call | tf_op jit(solution)/shard_map/late/pallas_call | solution.py:530
  25.2 0.7 %collective-permute-start.10 = (f32[8,512]{1,0:T(8,128)S(1)}, f32[8,512]{1,0:T(8,128)S(1)}, u32[]{:S(2)}, u32[]{:S(2)}) collective-permute-start(f32[8,512]{1,0:T(8,128)S(1)} %get-tuple-element.69.a_0_), channel_id=1, source_target_pairs={{0,3},{1,2},{2,1},{3,0},{4,7},{5,6},{6,5},{7,4},{8,11},{9,10},{10,... | collective-permute-start | bytes 49160 | tf_op jit(solution)/shard_map/ppermute | solution.py:445
  25.8 1.5 %collective-permute-start.9 = (f32[8,512]{1,0:T(8,128)S(1)}, f32[8,512]{1,0:T(8,128)S(1)}, u32[]{:S(2)}, u32[]{:S(2)}) collective-permute-start(f32[8,512]{1,0:T(8,128)S(1)} %get-tuple-element.69.a_0_), channel_id=1, source_target_pairs={{0,2},{1,3},{2,0},{3,1},{4,6},{5,7},{6,4},{7,5},{8,10},{9,11},{10,... | collective-permute-start | bytes 49160 | tf_op jit(solution)/shard_map/ppermute | solution.py:445
  27.4 0.0 collective-permute-start.8
  27.4 1.0 %collective-permute-done.10.a_3_ = f32[8,512]{1,0:T(8,128)S(1)} collective-permute-done((f32[8,512]{1,0:T(8,128)S(1)}, f32[8,512]{1,0:T(8,128)S(1)}, u32[]{:S(2)}, u32[]{:S(2)}) %collective-permute-start.10) | collective-permute-done | bytes 16416 | tf_op jit(solution)/shard_map/ppermute | solution.py:445
  28.4 1.2 %collective-permute-done.9.a_2_ = f32[8,512]{1,0:T(8,128)S(1)} collective-permute-done((f32[8,512]{1,0:T(8,128)S(1)}, f32[8,512]{1,0:T(8,128)S(1)}, u32[]{:S(2)}, u32[]{:S(2)}) %collective-permute-start.9) | collective-permute-done | bytes 16416 | tf_op jit(solution)/shard_map/ppermute | solution.py:445
  29.6 0.0 collective-permute-done.8.a_1_
  29.6 1.0 %sums.5 = (f32[16,1536]{1,0:T(8,128)S(1)}, f32[16,1536]{1,0:T(8,128)S(1)}) custom-call(f32[8,512]{1,0:T(8,128)S(1)} %get-tuple-element.69.a_0_, f32[8,512]{1,0:T(8,128)S(1)} %collective-permute-done.8.a_1_, f32[8,512]{1,0:T(8,128)S(1)} %collective-permute-done.9.a_2_, f32[8,512]{1,0:T(8,128)S(1)} %collective-permute-done.10.a_3_, ...), custom_call_target="tpu_custom_call" | custom-call | tf_op jit(solution)/shard_map/sums/pallas_call | solution.py:592
  30.6 1.5 %collective-permute-start.11 = (f32[16,1536]{1,0:T(8,128)S(1)}, f32[16,1536]{1,0:T(8,128)S(1)}, u32[]{:S(2)}, u32[]{:S(2)}) collective-permute-start(f32[16,1536]{1,0:T(8,128)S(1)} %get-tuple-element.77), channel_id=1, source_target_pairs={{0,4},{1,5},{2,6},{3,7},{4,0},{5,1},{6,2},{7,3},{8,12},{9,13},{10,... | collective-permute-start | bytes 294920 | tf_op jit(solution)/shard_map/ppermute | solution.py:445
  32.0 0.6 %collective-permute-start.12 = (f32[16,1536]{1,0:T(8,128)S(1)}, f32[16,1536]{1,0:T(8,128)S(1)}, u32[]{:S(2)}, u32[]{:S(2)}) collective-permute-start(f32[16,1536]{1,0:T(8,128)S(1)} %get-tuple-element.79), channel_id=1, source_target_pairs={{0,4},{1,5},{2,6},{3,7},{4,0},{5,1},{6,2},{7,3},{8,12},{9,13},{10,... | collective-permute-start | bytes 294920 | tf_op jit(solution)/shard_map/ppermute | solution.py:445
  32.6 1.0 %sums.4 = (f32[16,1536]{1,0:T(8,128)S(1)}, f32[16,1536]{1,0:T(8,128)S(1)}) custom-call(f32[8,512]{1,0:T(8,128)S(1)} %get-tuple-element.69.a_0_, f32[8,512]{1,0:T(8,128)S(1)} %collective-permute-done.8.a_1_, f32[8,512]{1,0:T(8,128)S(1)} %collective-permute-done.9.a_2_, f32[8,512]{1,0:T(8,128)S(1)} %collective-permute-done.10.a_3_, ...), custom_call_target="tpu_custom_call" | custom-call | tf_op jit(solution)/shard_map/sums/pallas_call | solution.py:592
  33.6 2.2 %collective-permute-done.11.b = f32[16,1536]{1,0:T(8,128)S(1)} collective-permute-done((f32[16,1536]{1,0:T(8,128)S(1)}, f32[16,1536]{1,0:T(8,128)S(1)}, u32[]{:S(2)}, u32[]{:S(2)}) %collective-permute-start.11) | collective-permute-done | bytes 98336 | tf_op jit(solution)/shard_map/ppermute | solution.py:445
  35.8 2.6 %collective-permute-start.14 = (f32[16,1536]{1,0:T(8,128)S(1)}, f32[16,1536]{1,0:T(8,128)S(1)}, u32[]{:S(2)}, u32[]{:S(2)}) collective-permute-start(f32[16,1536]{1,0:T(8,128)S(1)} %combined.2.a_4_), channel_id=1, source_target_pairs={{0,8},{1,9},{2,10},{3,11},{4,12},{5,13},{6,14},{7,15},{8,0},{9,1},... | collective-permute-start | bytes 294920 | tf_op jit(solution)/shard_map/ppermute | solution.py:445
  38.3 0.0 collective-permute-done.12.b
  38.4 1.9 %collective-permute-start.15 = (f32[16,1536]{1,0:T(8,128)S(1)}, f32[16,1536]{1,0:T(8,128)S(1)}, u32[]{:S(2)}, u32[]{:S(2)}) collective-permute-start(f32[16,1536]{1,0:T(8,128)S(1)} %combined.3.a_5_), channel_id=1, source_target_pairs={{0,8},{1,9},{2,10},{3,11},{4,12},{5,13},{6,14},{7,15},{8,0},{9,1},... | collective-permute-start | bytes 294920 | tf_op jit(solution)/shard_map/ppermute | solution.py:445
  40.3 1.0 %sums.7 = f32[32,1536]{1,0:T(8,128)S(1)} custom-call(f32[8,512]{1,0:T(8,128)S(1)} %get-tuple-element.69.a_0_, f32[8,512]{1,0:T(8,128)S(1)} %collective-permute-done.8.a_1_, f32[8,512]{1,0:T(8,128)S(1)} %collective-permute-done.9.a_2_, f32[8,512]{1,0:T(8,128)S(1)} %collective-permute-done.10.a_3_, f32[16,1536]{1,0:T(8,128)S(1)} %combined.2.a_4_, ...), custom_call_target="tpu_custom_call" | custom-call | tf_op jit(solution)/shard_map/sums/pallas_call | solution.py:592
  41.2 0.0 collective-permute-start.13
  41.3 1.6 %sums.6 = (f32[32,1536]{1,0:T(8,128)S(1)}, f32[2,96]{1,0:T(2,128)}) custom-call(f32[8,512]{1,0:T(8,128)S(1)} %get-tuple-element.69.a_0_, f32[8,512]{1,0:T(8,128)S(1)} %collective-permute-done.8.a_1_, f32[8,512]{1,0:T(8,128)S(1)} %collective-permute-done.9.a_2_, f32[8,512]{1,0:T(8,128)S(1)} %collective-permute-done.10.a_3_, f32[16,1536]{1,0:T(8,128)S(1)} %combined.2.a_4_, ...), custom_call_target="tpu_custom_call" | custom-call | tf_op jit(solution)/shard_map/sums/pallas_call | solution.py:592
  42.9 0.0 copy-start
  42.9 1.8 %collective-permute-done.14.a_0_ = f32[16,1536]{1,0:T(8,128)S(1)} collective-permute-done((f32[16,1536]{1,0:T(8,128)S(1)}, f32[16,1536]{1,0:T(8,128)S(1)}, u32[]{:S(2)}, u32[]{:S(2)}) %collective-permute-start.14) | collective-permute-done | bytes 98336 | tf_op jit(solution)/shard_map/ppermute | solution.py:445
  44.7 1.4 %collective-permute-done.15.a_1_ = f32[16,1536]{1,0:T(8,128)S(1)} collective-permute-done((f32[16,1536]{1,0:T(8,128)S(1)}, f32[16,1536]{1,0:T(8,128)S(1)}, u32[]{:S(2)}, u32[]{:S(2)}) %collective-permute-start.15) | collective-permute-done | bytes 98336 | tf_op jit(solution)/shard_map/ppermute | solution.py:445
  46.0 2.1 %collective-permute-done.13.a_1_ = f32[32,1536]{1,0:T(8,128)S(1)} collective-permute-done((f32[32,1536]{1,0:T(8,128)S(1)}, f32[32,1536]{1,0:T(8,128)S(1)}, u32[]{:S(2)}, u32[]{:S(2)}) %collective-permute-start.13) | collective-permute-done | bytes 196640 | tf_op jit(solution)/shard_map/ppermute | solution.py:445
  48.2 0.0 copy-done
  48.2 0.7 %update.1 = f32[32,1024]{1,0:T(8,128)} custom-call(f32[32,1536]{1,0:T(8,128)S(1)} %get-tuple-element.83.a_0_, f32[32,1536]{1,0:T(8,128)S(1)} %collective-permute-done.13.a_1_, f32[16,1536]{1,0:T(8,128)S(1)} %get-tuple-element.86.a_2_, f32[16,1536]{1,0:T(8,128)S(1)} %get-tuple-element.87.a_3_, f32[1,512]{1,0:T(1,128)S(1)} %bitcast.8), custom_call_target="tpu_custom_call" | custom-call | tf_op jit(solution)/shard_map/update/pallas_call | solution.py:625
  (5 shorter events, 0.0 us)
Async XLA Ops:
  0.6 17.4 %collective-permute-start = (f32[96,1024]{1,0:T(8,128)}, f32[96,1024]{1,0:T(8,128)S(1)}, u32[]{:S(2)}, u32[]{:S(2)}) collective-permute-start(f32[96,1024]{1,0:T(8,128)} %src_at.1), channel_id=1, source_target_pairs={{0,2},{2,0},{4,6},{6,4},{8,10},{10,8},{12,14},{14,12},{16,18},{18,... | collective-permute-start | bytes 1179656 | tf_op jit(solution)/shard_map/ppermute | solution.py:445
  5.5 8.4 %collective-permute-start.4 = (f32[32,1024]{1,0:T(8,128)}, f32[32,1024]{1,0:T(8,128)S(1)}, u32[]{:S(2)}, u32[]{:S(2)}) collective-permute-start(f32[32,1024]{1,0:T(8,128)} %bitcast.9), channel_id=1, source_target_pairs={{0,8},{1,9},{2,10},{3,11},{4,12},{5,13},{6,14},{7,15},{8,0},{9,1},... | collective-permute-start | bytes 393224 | tf_op jit(solution)/shard_map/ppermute | solution.py:445
  9.1 9.0 %collective-permute-start.1 = (f32[48,1024]{1,0:T(8,128)S(1)}, f32[48,1024]{1,0:T(8,128)S(1)}, u32[]{:S(2)}, u32[]{:S(2)}) collective-permute-start(f32[48,1024]{1,0:T(8,128)S(1)} %slice.3), channel_id=1, source_target_pairs={{1,3},{3,1},{5,7},{7,5},{9,11},{11,9},{13,15},{15,13},{17,19},{19,... | collective-permute-start | bytes 589832 | tf_op jit(solution)/shard_map/ppermute | solution.py:445
  9.8 5.2 %collective-permute-start.3 = (f32[32,1024]{1,0:T(8,128)}, f32[32,1024]{1,0:T(8,128)S(1)}, u32[]{:S(2)}, u32[]{:S(2)}) collective-permute-start(f32[32,1024]{1,0:T(8,128)} %bitcast.10), channel_id=1, source_target_pairs={{0,4},{1,5},{2,6},{3,7},{4,0},{5,1},{6,2},{7,3},{8,12},{9,13},{10,... | collective-permute-start | bytes 393224 | tf_op jit(solution)/shard_map/ppermute | solution.py:445
  13.9 5.0 %collective-permute-start.5 = (f32[32,1024]{1,0:T(8,128)S(1)}, f32[32,1024]{1,0:T(8,128)S(1)}, u32[]{:S(2)}, u32[]{:S(2)}) collective-permute-start(f32[32,1024]{1,0:T(8,128)S(1)} %gate.3.a_1_.a_2_), channel_id=1, source_target_pairs={{0,4},{1,5},{2,6},{3,7},{4,0},{5,1},{6,2},{7,3},{8,12},{9,13},{10,... | collective-permute-start | bytes 393224 | tf_op jit(solution)/shard_map/ppermute | solution.py:445
  14.5 3.6 %collective-permute-start.2 = (f32[8,128]{1,0:T(8,128)S(1)}, f32[8,128]{1,0:T(8,128)S(1)}, u32[]{:S(2)}, u32[]{:S(2)}) collective-permute-start(f32[8,128]{1,0:T(8,128)S(1)} %get-tuple-element.45.a_1_), channel_id=1, source_target_pairs={{0,2},{1,3},{2,0},{3,1},{4,6},{5,7},{6,4},{7,5},{8,10},{9,11},{10,... | collective-permute-start | bytes 12296 | tf_op jit(solution)/shard_map/ppermute | solution.py:445
  15.0 4.0 %collective-permute-start.7 = (f32[104,1536]{1,0:T(8,128)S(1)}, f32[104,1536]{1,0:T(8,128)S(1)}, u32[]{:S(2)}, u32[]{:S(2)}) collective-permute-start(f32[104,1536]{1,0:T(8,128)S(1)} %get-tuple-element.48.a_0_), channel_id=1, source_target_pairs={{0,1},{1,0},{2,3},{3,2},{4,5},{5,4},{6,7},{7,6},{8,9},{9,8},{10,11... | collective-permute-start | bytes 1916936 | tf_op jit(solution)/shard_map/ppermute | solution.py:445
  19.0 3.2 %collective-permute-start.6 = (f32[104,1536]{1,0:T(8,128)S(1)}, f32[104,1536]{1,0:T(8,128)S(1)}, u32[]{:S(2)}, u32[]{:S(2)}) collective-permute-start(f32[104,1536]{1,0:T(8,128)S(1)} %gate.4.a_0_), channel_id=1, source_target_pairs={{0,1},{1,0},{2,3},{3,2},{4,5},{5,4},{6,7},{7,6},{8,9},{9,8},{10,11... | collective-permute-start | bytes 1916936 | tf_op jit(solution)/shard_map/ppermute | solution.py:445
  25.2 3.2 %collective-permute-start.10 = (f32[8,512]{1,0:T(8,128)S(1)}, f32[8,512]{1,0:T(8,128)S(1)}, u32[]{:S(2)}, u32[]{:S(2)}) collective-permute-start(f32[8,512]{1,0:T(8,128)S(1)} %get-tuple-element.69.a_0_), channel_id=1, source_target_pairs={{0,3},{1,2},{2,1},{3,0},{4,7},{5,6},{6,5},{7,4},{8,11},{9,10},{10,... | collective-permute-start | bytes 49160 | tf_op jit(solution)/shard_map/ppermute | solution.py:445
  25.8 3.7 %collective-permute-start.9 = (f32[8,512]{1,0:T(8,128)S(1)}, f32[8,512]{1,0:T(8,128)S(1)}, u32[]{:S(2)}, u32[]{:S(2)}) collective-permute-start(f32[8,512]{1,0:T(8,128)S(1)} %get-tuple-element.69.a_0_), channel_id=1, source_target_pairs={{0,2},{1,3},{2,0},{3,1},{4,6},{5,7},{6,4},{7,5},{8,10},{9,11},{10,... | collective-permute-start | bytes 49160 | tf_op jit(solution)/shard_map/ppermute | solution.py:445
  27.4 2.2 %collective-permute-start.8 = (f32[8,512]{1,0:T(8,128)S(1)}, f32[8,512]{1,0:T(8,128)S(1)}, u32[]{:S(2)}, u32[]{:S(2)}) collective-permute-start(f32[8,512]{1,0:T(8,128)S(1)} %get-tuple-element.69.a_0_), channel_id=1, source_target_pairs={{0,1},{1,0},{2,3},{3,2},{4,5},{5,4},{6,7},{7,6},{8,9},{9,8},{10,11... | collective-permute-start | bytes 49160 | tf_op jit(solution)/shard_map/ppermute | solution.py:445
  30.6 5.2 %collective-permute-start.11 = (f32[16,1536]{1,0:T(8,128)S(1)}, f32[16,1536]{1,0:T(8,128)S(1)}, u32[]{:S(2)}, u32[]{:S(2)}) collective-permute-start(f32[16,1536]{1,0:T(8,128)S(1)} %get-tuple-element.77), channel_id=1, source_target_pairs={{0,4},{1,5},{2,6},{3,7},{4,0},{5,1},{6,2},{7,3},{8,12},{9,13},{10,... | collective-permute-start | bytes 294920 | tf_op jit(solution)/shard_map/ppermute | solution.py:445
  32.0 6.3 %collective-permute-start.12 = (f32[16,1536]{1,0:T(8,128)S(1)}, f32[16,1536]{1,0:T(8,128)S(1)}, u32[]{:S(2)}, u32[]{:S(2)}) collective-permute-start(f32[16,1536]{1,0:T(8,128)S(1)} %get-tuple-element.79), channel_id=1, source_target_pairs={{0,4},{1,5},{2,6},{3,7},{4,0},{5,1},{6,2},{7,3},{8,12},{9,13},{10,... | collective-permute-start | bytes 294920 | tf_op jit(solution)/shard_map/ppermute | solution.py:445
  35.8 8.9 %collective-permute-start.14 = (f32[16,1536]{1,0:T(8,128)S(1)}, f32[16,1536]{1,0:T(8,128)S(1)}, u32[]{:S(2)}, u32[]{:S(2)}) collective-permute-start(f32[16,1536]{1,0:T(8,128)S(1)} %combined.2.a_4_), channel_id=1, source_target_pairs={{0,8},{1,9},{2,10},{3,11},{4,12},{5,13},{6,14},{7,15},{8,0},{9,1},... | collective-permute-start | bytes 294920 | tf_op jit(solution)/shard_map/ppermute | solution.py:445
  38.4 7.7 %collective-permute-start.15 = (f32[16,1536]{1,0:T(8,128)S(1)}, f32[16,1536]{1,0:T(8,128)S(1)}, u32[]{:S(2)}, u32[]{:S(2)}) collective-permute-start(f32[16,1536]{1,0:T(8,128)S(1)} %combined.3.a_5_), channel_id=1, source_target_pairs={{0,8},{1,9},{2,10},{3,11},{4,12},{5,13},{6,14},{7,15},{8,0},{9,1},... | collective-permute-start | bytes 294920 | tf_op jit(solution)/shard_map/ppermute | solution.py:445
  41.2 6.9 %collective-permute-start.13 = (f32[32,1536]{1,0:T(8,128)S(1)}, f32[32,1536]{1,0:T(8,128)S(1)}, u32[]{:S(2)}, u32[]{:S(2)}) collective-permute-start(f32[32,1536]{1,0:T(8,128)S(1)} %sums.7), channel_id=1, source_target_pairs={{0,4},{1,5},{2,6},{3,7},{4,0},{5,1},{6,2},{7,3},{8,12},{9,13},{10,... | collective-permute-start | bytes 589832 | tf_op jit(solution)/shard_map/ppermute | solution.py:445
  42.9 5.3 %copy-start = (f32[512]{0:T(512)S(1)}, f32[512]{0:T(512)}, u32[]{:S(2)}) copy-start(f32[512]{0:T(512)} %param.16) | copy-start | bytes 6148

commit v7 on v6

--- a/solution.py
+++ b/solution.py
@@ -78,14 +78,12 @@
     return high, (x - high.astype(jnp.float32)).astype(jnp.bfloat16)
 
 
-def deep_rows(a_high, a_low, b_high, b_low):
-    rows = a_high.shape[0]
-    main, left = slice(0, 128), slice(128, rows)
-    order = ((a_high, b_high), (a_low, b_low), (a_high, b_high))
-    parts = [x[main] for pair in order for x in pair]
-    parts += [x[left] for pair in order for x in pair]
-    parts.append(jnp.zeros((128 - 6 * (rows - 128), a_high.shape[1]), a_high.dtype))
-    return jnp.concatenate(parts, axis=0)
+def main_rows(half, part):
+    return 256 * part + 128 * half
+
+
+def left_rows(half, part, left):
+    return 768 + 2 * left * part + left * half
 
 
 def deep_lanes(a, b):
@@ -193,50 +191,48 @@
     prepared_rows(src, facts_out[...], inverse, out)
 
 
-def neighbour_kernel(src_even, src_odd, facts, inverse_noise, wait, out, src):
-    half = src_odd.shape[0]
+def neighbour_kernel(src, facts, inverse_noise, wait, out):
+    prepared_rows(src, facts[...], inverse_noise[...], out)
+
+
+def even_core():
+    return lax.axis_index("dom") % 2 == 0
+
+
+def place_half(half, mine, other, y_out, power_out):
+    width = y_out.shape[1]
+    slots = mine.shape[0] - 8
+    left = slots + slots // 2 - 128
+
+    def place(src, rows, to):
+        for cols, out in ((slice(0, width), y_out), (slice(width, None), power_out)):
+            high, low = halves(src[rows, cols])
+            for part, value in enumerate((high, low, high)):
+                if to < 128:
+                    at = main_rows(half, part) + to
+                else:
+                    at = left_rows(half, part, left) + to - 128
+                out[at : at + value.shape[0]] = value
+
+    def place_both(heavy, light):
+        place(heavy, slice(0, slots), 0)
+        place(light, slice(0, 128 - slots), slots)
+        place(light, slice(128 - slots, slots // 2), 128)
+
     even = even_core()
 
     @pl.when(even)
     def _():
-        src[...] = src_even[...]
+        place_both(mine, other)
 
     @pl.when(jnp.logical_not(even))
     def _():
-        src[:half] = src_odd[...]
-        src[half:] = jnp.zeros_like(src[half:])
-
-    prepared_rows(src, facts[...], inverse_noise[...], out)
-
-
-def even_core():
-    return lax.axis_index("dom") % 2 == 0
-
-
-def place_half(mine, other, y_high, y_low, p_high, p_low):
-    width = y_high.shape[1]
-    slots = mine.shape[0] - 8
-
-    def place(src, to, size):
-        dest = slice(to, to + size)
-        high, low = halves(src[:size, :width])
-        y_high[dest] = high
-        y_low[dest] = low
-        high, low = halves(src[:size, width:])
-        p_high[dest] = high
-        p_low[dest] = low
-
-    even = even_core()
-
-    @pl.when(even)
-    def _():
-        place(mine, 0, slots)
-        place(other, slots, slots // 2)
-
-    @pl.when(jnp.logical_not(even))
-    def _():
-        place(other, 0, slots)
-        place(mine, slots, slots // 2)
+        place_both(other, mine)
+
+
+def placed(half, part, left, out):
+    main, tail = main_rows(half, part), left_rows(half, part, left)
+    return jnp.concatenate([out[main : main + 128], out[tail : tail + left]], axis=0)
 
 
 def half_facts(mine, other):
@@ -315,50 +311,45 @@
     prepare_refs(own, phases, *prepared[:4])
 
 
-def middle_kernel(count, early, own, cnb, *rest):
-    refs, rest = rest[:count], rest[count:]
-    ready, rest = rest[: 4 * early], rest[4 * early :]
-    particles, rest = rest[:4], rest[4:]
-    prepared, rest = rest[: 4 * count], rest[4 * count :]
-    e_outs, stats_out = rest[:-1], rest[-1]
-    place_half(own, cnb, *particles)
-    particles = [x[...] for x in particles]
-    facts = half_facts(own, cnb)
-    prior = prior_rows(facts, refs[0].shape[0], particles[0].shape[0])
+def middle_kernel(*rest):
+    count = len(rest) // 5
+    refs, prepared = rest[:count], rest[count:]
     phases = grid_phases(refs[0].shape[1] // 2)
-    for n in range(early):
-        e_outs[n][...] = block_scores(ready[4 * n : 4 * n + 4], particles, prior)
     for n in range(count):
-        block = prepared[4 * n : 4 * n + 4]
-        prepare_refs(refs[n], phases, *block)
-        e_outs[early + n][...] = block_scores(block, particles, prior)
-    weigh(e_outs, facts, e_outs, stats_out)
-
-
-def late_kernel(blocks, ynb, cynb, early_stats, *rest):
+        prepare_refs(refs[n], phases, *prepared[4 * n : 4 * n + 4])
+
+
+def late_kernel(blocks, own, cnb, ynb, cynb, *rest):
     prepared, rest = rest[: 4 * blocks], rest[4 * blocks :]
-    first_half, rest = rest[:4], rest[4:]
-    e_outs, rest = rest[:blocks], rest[blocks:]
-    y_out, power_out, stats_out, late_stats, *particles = rest
-    place_half(ynb, cynb, *particles)
-    half = [x[...] for x in particles]
-    early = [x[...] for x in first_half]
-    y_out[...] = deep_rows(early[0], early[1], half[0], half[1])
-    power_out[...] = deep_rows(early[2], early[3], half[2], half[3])
-    per = e_outs[0].shape[1]
-    facts = half_facts(ynb, cynb)
-    prior = prior_rows(facts, per, half[0].shape[0])
-    for n in range(blocks):
-        e_outs[n][...] = block_scores(prepared[4 * n : 4 * n + 4], half, prior)
-    weigh(e_outs, facts, e_outs, late_stats)
+    e_outs, rest = (rest[:blocks], rest[blocks : 2 * blocks]), rest[2 * blocks :]
+    y_out, power_out, stats_out, *half_stats = rest
+    per, lanes = e_outs[0][0].shape[1:]
+    left = lanes - 128
+    pairs = ((own, cnb), (ynb, cynb))
+    facts = [half_facts(*pair) for pair in pairs]
+    for half, pair in enumerate(pairs):
+        place_half(half, *pair, y_out, power_out)
+        empty = 768 + 6 * left
+    for out in (y_out, power_out):
+        out[empty:] = jnp.zeros_like(out[empty:])
+    for half in range(2):
+        particles = [placed(half, part, left, out) for out in (y_out, power_out) for part in (0, 1)]
+        prior = prior_rows(facts[half], per, lanes)
+        for n in range(blocks):
+            e_outs[half][n][...] = block_scores(prepared[4 * n : 4 * n + 4], particles, prior)
+        weigh(e_outs[half], facts[half], e_outs[half], half_stats[half])
     first = (lax.axis_index("dom") // 2) % 2 == 0
-    mine, others = early_stats[...], late_stats[...]
+    mine, others = half_stats[0][...], half_stats[1][...]
     stats_out[:, :256] = jnp.where(first, mine, others)
     stats_out[:, 256:] = jnp.where(first, others, mine)
 
 
-def sum_kernel(cuts, shifts, waits, *rest):
+def sum_kernel(cuts, last, waits, *rest):
     team, rest = rest[:TEAM], rest[TEAM + waits :]
+    if last:
+        *near, ea_ref, eb_ref, y_ref, power_ref, part_out, shift_out = rest
+        near = jnp.concatenate([x[...] for x in near], axis=0)
+        rest = ea_ref, eb_ref, y_ref, power_ref, part_out, shift_out
     ea_ref, eb_ref, y_ref, power_ref, *outs = rest
     per, lanes = ea_ref.shape[1:]
     width = y_ref.shape[1]
@@ -374,7 +365,7 @@
     own_gain = gains[0] * live
     gain_a = jnp.where(first, own_gain[:, :256], own_gain[:, 256:])[:, :lanes]
     gain_b = jnp.where(first, own_gain[:, 256:], own_gain[:, :256])[:, :lanes]
-    if shifts:
+    if last:
         move = jnp.concatenate(
             [sum(g * s[k : k + 1] for g, s in zip(gains, team)) * live for k in (2, 3)], axis=0
         )
@@ -406,6 +397,10 @@
         re = re + (ar + br) * c - (ai - bi) * s
         im = im + (ar - br) * s + (ai + bi) * c
     weight = dot_nn(deep_lanes(jnp.sum(wa, axis=0), jnp.sum(wb, axis=0)), power_ref[...])
+    if last:
+        re = re + near[:, :freq]
+        im = im + near[:, freq:width]
+        weight = weight + near[:, width:]
     for start, stop, out in zip(cuts, cuts[1:], outs):
         part = slice(start, stop)
         out[:, :freq] = re[part]
@@ -440,9 +435,9 @@
     return pltpu.CompilerParams(vmem_limit_bytes=mib * 1024 * 1024)
 
 
-def crossed(block, mask, core=None):
-    devices = [i for i in range(lax.axis_size("dom")) if core is None or i % 2 == core]
-    return lax.ppermute(block, "dom", [(i, i ^ mask) for i in devices])
+def crossed(block, mask):
+    size = lax.axis_size("dom")
+    return lax.ppermute(block, "dom", [(i, i ^ mask) for i in range(size)])
 
 
 def on_device(
@@ -468,6 +463,8 @@
 
     ynb = crossed(particle_fourier, 2)
     anywhere = pl.BlockSpec(memory_space=pl.ANY)
+    ynb = crossed(particle_fourier, 2)
+    anywhere = pl.BlockSpec(memory_space=pl.ANY)
     def gated(arrays, waits, cost):
         return pl.pallas_call(
             lambda *a: None,
@@ -482,11 +479,8 @@
 
     ynb = crossed(particle_fourier, 2)
     anywhere = pl.BlockSpec(memory_space=pl.ANY)
-    ynb_even = crossed(particle_fourier, 2, 0)
-    ynb_odd = crossed(particle_fourier[: slots // 2], 2, 1)
-    refs = {0: refs_own, 1: crossed(refs_own, TEAM)}
-    for n in range(2, blocks, 2):
-        refs[n] = crossed(refs_own, TEAM * n)
+    ynb = crossed(particle_fourier, 2)
+    refs = [refs_own] + [crossed(refs_own, TEAM * n) for n in range(1, blocks)]
     own_facts = (
         particle_fourier,
         defocus.reshape(1, slots),
@@ -511,10 +505,6 @@
         name="own",
     )(*(pltpu.with_memory_space_constraint(x, pltpu.HBM) for x in own_facts), live_count)
     cnb = crossed(own, 1)
-    for n in range(2, blocks, 2):
-        (refs[n],) = gated([refs[n]], [facts], no_cost)
-        refs[n + 1] = crossed(refs[n], TEAM)
-    refs = [refs[n] for n in range(blocks)]
     half = slots + slots // 2
     bf16 = jnp.bfloat16
     early = 2
@@ -522,7 +512,6 @@
     def shaped(rows, cols, dtype=f32):
         return jax.ShapeDtypeStruct((rows, cols), dtype)
 
-    half_shapes = [shaped(half, width, bf16)] * 2 + [shaped(half, freq, bf16)] * 2
     block_shapes = [shaped(SHIFTS * per, width, bf16)] * 2 + [shaped(per, freq, bf16)] * 2
     score_shape = jax.ShapeDtypeStruct((SHIFTS, per, half), f32)
 
@@ -550,53 +539,50 @@
     ynb_prepared = pl.pallas_call(
         neighbour_kernel,
         out_shape=jax.ShapeDtypeStruct((slots + 8, width + freq), f32),
-        in_specs=[vmem] * 4 + [anywhere],
+        in_specs=[vmem] * 3 + [anywhere],
         out_specs=vmem,
         compiler_params=params(6),
-        scratch_shapes=[pltpu.VMEM((slots, width), f32)],
         cost_estimate=no_cost,
         name="neighbour",
-    )(ynb_even, ynb_odd, crossed(facts, 2), inverse_noise, prepared[2])
-    (ynb_prepared,) = gated([ynb_prepared], refs[early:], no_cost)
+    )(ynb, crossed(facts, 2), inverse_noise, prepared[2])
     cynb = crossed(ynb_prepared, 1)
 
     late = blocks - early
     outs = call(
-        lambda *a: middle_kernel(late, early, *a),
-        (own, cnb, *refs[early:], *prepared),
-        half_shapes + block_shapes * late + [score_shape] * blocks + [shaped(8, 256)],
+        middle_kernel,
+        refs[early:],
+        block_shapes * late,
         "middle",
-        8 + 2 * blocks,
-    )
-    particles, outs = outs[:4], outs[4:]
-    prepared = (*prepared, *outs[: 4 * late])
-    e_own, early_stats = outs[4 * late : -1], outs[-1]
-
+        4 + 2 * blocks,
+        pl.CostEstimate(flops=16 * 10**9, bytes_accessed=0, transcendentals=0),
+    )
+    prepared = (*prepared, *outs)
     deep = 3 * 256 + 128
     outs = call(
         lambda *a: late_kernel(blocks, *a),
-        (ynb_prepared, cynb, early_stats, *prepared, *particles),
-        [score_shape] * blocks + [shaped(deep, width, bf16), shaped(deep, freq, bf16), shaped(8, 512)],
+        (own, cnb, ynb_prepared, cynb, *prepared),
+        [score_shape] * (2 * blocks)
+        + [shaped(deep, width, bf16), shaped(deep, freq, bf16), shaped(8, 512)],
         "late",
         8 + 2 * blocks,
-        scratch=[pltpu.VMEM((8, 256), f32)] + [pltpu.VMEM(x.shape, x.dtype) for x in half_shapes],
-    )
-    e_other, (y, power, stats) = outs[:blocks], outs[blocks:]
+        scratch=[pltpu.VMEM((8, 256), f32)] * 2,
+    )
+    e_own, e_other, (y, power, stats) = outs[:blocks], outs[blocks : 2 * blocks], outs[2 * blocks :]
 
     team = [stats] + [crossed(stats, n) for n in range(1, TEAM)]
 
-    def sums(n, cuts, shifts=False, waits=()):
+    def sums(n, cuts, near=(), waits=()):
         out_shape = [shaped(b - a, width + freq) for a, b in zip(cuts, cuts[1:])]
-        if shifts:
+        if near:
             out_shape.append(shaped(2, slots))
         return pl.pallas_call(
-            lambda *a: sum_kernel(cuts, shifts, len(waits), *a),
+            lambda *a: sum_kernel(cuts, bool(near), len(waits), *a),
             out_shape=tuple(out_shape),
-            in_specs=[vmem] * TEAM + [anywhere] * len(waits) + [vmem] * 4,
+            in_specs=[vmem] * TEAM + [anywhere] * len(waits) + [vmem] * (4 + len(near)),
             out_specs=(vmem,) * len(out_shape),
             compiler_params=params(8),
             name="sums",
-        )(*team, *waits, e_own[n], e_other[n], y, power)
+        )(*team, *waits, *near, e_own[n], e_other[n], y, power)
 
     def combined(mine, other):
         return pl.pallas_call(
@@ -608,28 +594,27 @@
             name="combined",
         )(mine, other)
 
-    cut = (0, per // 2, per)
+    whole, cut = (0, per), (0, per // 2, per)
     far = []
     waits = []
     for n in range(2, blocks, 2):
         handed = [crossed(x, TEAM) for x in sums(n + 1, cut)]
-        joined = [combined(x, y) for x, y in zip(sums(n, cut), handed)]
+        if n == 2:
+            near = sums(1, cut)
+        joined = [combined(x, y) for x, y in zip(sums(n, cut, waits=near[:1]), handed)]
         far.extend(crossed(x, TEAM * n) for x in joined)
         waits.extend(joined)
-    own_part, shift = sums(0, (0, per), shifts=True, waits=waits)
-    near = crossed(sums(1, (0, per), waits=waits)[0], TEAM)
-    far = gated(far, [], pl.CostEstimate(flops=16 * 10**9, bytes_accessed=0, transcendentals=0))
-    parts = [near, *far]
-    row_cuts = [(0, per)] + [cut] * (len(far) // 2)
+    own_part, shift = sums(0, whole, near=[crossed(x, TEAM) for x in near], waits=waits)
+    row_cuts = [cut] * (len(far) // 2)
 
     refs_new = pl.pallas_call(
         lambda *a: final_kernel(row_cuts, *a),
         out_shape=jax.ShapeDtypeStruct((per, width), f32),
-        in_specs=[vmem] * (len(parts) + 2),
+        in_specs=[vmem] * (len(far) + 2),
         out_specs=vmem,
         compiler_params=params(2 + blocks),
         name="update",
-    )(own_part, *parts, signal_power.reshape(1, freq))
+    )(own_part, *far, signal_power.reshape(1, freq))
 
     return (shift.T, refs_new.reshape(class_refs.shape))
 

time: 49.1 us -> 48.3 us (0.984)
  waiting for transfers between devices: 11.9 us -> 15.3 us
  starting transfers between devices: 19.6 us -> 16.4 us
  local copies, waits for them, and re-layouts: 0.94 us -> 0.01 us
    ppermute x16, waiting for transfers between devices: 11.9 us -> 15.3 us  [crossed(): return lax.ppermute(block, 'dom', [(i, i ^ mask) for i in range(size)])]
    ppermute x16, starting transfers between devices: 19.6 us -> 16.4 us  [crossed(): return lax.ppermute(block, 'dom', [(i, i ^ mask) for i in range(size)])]
    slice x1 -> x0, local copies, waits for them, and re-layouts: 0.94 us -> none  [on_device(): ynb_odd = crossed(particle_fourier[:slots // 2], 2, 1)]
    pallas_call x7 -> x4, Pallas kernels: 4.49 us -> 4.41 us  [sums(): pl.pallas_call(lambda *a: sum_kernel(cuts, bool(near), len(waits), *a), o...]
  transfers between devices with their start and end apart: 16 -> 16, of which waited for: 9 -> 9; matrix products, arithmetic and copies ran while one was open for 2% -> 0% of each run, Pallas kernels for 21% -> 16%
where the time goes in v7:
time: 48.3 us; the launch traced here: 48.1 us
  starting transfers between devices  16.4 us (34%)
  waiting for transfers between devices  15.3 us (32%)
  Pallas kernels  15 us (31%)
  between operations  1.38 us (3%)
    ppermute x16, starting transfers between devices, crossed(): return lax.ppermute(block, 'dom', [(i, i ^ mask) for i in range(size)])  16.4 us
    ppermute x16, waiting for transfers between devices, crossed(): return lax.ppermute(block, 'dom', [(i, i ^ mask) for i in range(size)])  15.3 us
    pallas_call x2, Pallas kernels, call(): pl.pallas_call(kernel, cost_estimate=cost, out_shape=tuple(out_shape), in...  6.24 us
    pallas_call x4, Pallas kernels, sums(): pl.pallas_call(lambda *a: sum_kernel(cuts, bool(near), len(waits), *a), o...  4.41 us
    pallas_call x1, Pallas kernels, on_device(): pl.pallas_call(own_kernel, out_shape=(jax.ShapeDtypeStruct((slots + 8, wi...  1.83 us
    pallas_call x1, Pallas kernels, on_device(): pl.pallas_call(early_kernel, out_shape=tuple(block_shapes * early), in_sp...  1.16 us
  transfers between devices with their start and end apart: 16, of which 9 were waited for; matrix products, arithmetic and copies ran while one was open for 0% of the time, Pallas kernels for 16%

profile of v7, /device:TPU:0, one launch (start us, length us, event | category | flops | bytes accessed | tf_op | source)
XLA Modules:
  0.0 48.1 jit_solution(15102324391988655453)
XLA Ops:
  0.6 3.0 %collective-permute-start.1 = (f32[96,1024]{1,0:T(8,128)}, f32[96,1024]{1,0:T(8,128)S(1)}, u32[]{:S(2)}, u32[]{:S(2)}) collective-permute-start(f32[96,1024]{1,0:T(8,128)} %src_at.1), channel_id=1, source_target_pairs={{0,2},{1,3},{2,0},{3,1},{4,6},{5,7},{6,4},{7,5},{8,10},{9,11},{10,... | collective-permute-start | bytes 1179656 | tf_op jit(solution)/shard_map/ppermute | solution.py:440
  3.7 1.6 %collective-permute-start.3 = (f32[32,1024]{1,0:T(8,128)}, f32[32,1024]{1,0:T(8,128)S(1)}, u32[]{:S(2)}, u32[]{:S(2)}) collective-permute-start(f32[32,1024]{1,0:T(8,128)} %bitcast.9), channel_id=1, source_target_pairs={{0,4},{1,5},{2,6},{3,7},{4,0},{5,1},{6,2},{7,3},{8,12},{9,13},{10,... | collective-permute-start | bytes 393224 | tf_op jit(solution)/shard_map/ppermute | solution.py:440
  5.2 2.5 %collective-permute-start.6 = (f32[32,1024]{1,0:T(8,128)}, f32[32,1024]{1,0:T(8,128)S(1)}, u32[]{:S(2)}, u32[]{:S(2)}) collective-permute-start(f32[32,1024]{1,0:T(8,128)} %bitcast.10), channel_id=1, source_target_pairs={{0,12},{1,13},{2,14},{3,15},{4,8},{5,9},{6,10},{7,11},{8,4},{9,5},... | collective-permute-start | bytes 393224 | tf_op jit(solution)/shard_map/ppermute | solution.py:440
  7.7 0.1 collective-permute-start.5
  8.5 1.8 %own.1 = (f32[104,1536]{1,0:T(8,128)S(1)}, f32[8,128]{1,0:T(8,128)S(1)}, f32[128,512]{1,0:T(8,128)S(1)}) custom-call(f32[96,1024]{1,0:T(8,128)} %src_at.1, f32[1,96]{1,0:T(1,128)} %bitcast.15, s32[2,96]{1,0:T(2,128)} %bitcast.14, s32[1,96]{1,0:T(1,128)} %bitcast.16, s32[1,96]{1,0:T(1,128)} %bitcast.17, f32[128,512]{1,0:T(8,128)} %noise_at.1, ...), custom_call_target="tpu_custom_call" | custom-call | tf_op jit(solution)/shard_map/own/pallas_call | solution.py:492
  10.3 0.6 %collective-permute-start.2 = (f32[8,128]{1,0:T(8,128)S(1)}, f32[8,128]{1,0:T(8,128)S(1)}, u32[]{:S(2)}, u32[]{:S(2)}) collective-permute-start(f32[8,128]{1,0:T(8,128)S(1)} %get-tuple-element.41), channel_id=1, source_target_pairs={{0,2},{1,3},{2,0},{3,1},{4,6},{5,7},{6,4},{7,5},{8,10},{9,11},{10,... | collective-permute-start | bytes 12296 | tf_op jit(solution)/shard_map/ppermute | solution.py:440
  10.9 0.0 collective-permute-done.3.near
  10.9 0.0 collective-permute-start
  10.9 1.2 %early.1 = (bf16[288,1024]{1,0:T(8,128)(2,1)S(1)}, bf16[288,1024]{1,0:T(8,128)(2,1)S(1)}, bf16[32,512]{1,0:T(8,128)(2,1)S(1)}, bf16[32,512]{1,0:T(8,128)(2,1)S(1...) custom-call(f32[32,1024]{1,0:T(8,128)} %bitcast.12, ...), custom_call_target="tpu_custom_call" | custom-call | tf_op jit(solution)/shard_map/early/pallas_call | solution.py:530
  12.1 1.9 %collective-permute-done.2.facts = f32[8,128]{1,0:T(8,128)S(1)} collective-permute-done((f32[8,128]{1,0:T(8,128)S(1)}, f32[8,128]{1,0:T(8,128)S(1)}, u32[]{:S(2)}, u32[]{:S(2)}) %collective-permute-start.2) | collective-permute-done | bytes 4128 | tf_op jit(solution)/shard_map/ppermute | solution.py:440
  14.0 0.0 collective-permute-done.1.src
  14.0 0.6 %neighbour.1.a_2_ = f32[104,1536]{1,0:T(8,128)S(1)} custom-call(f32[96,1024]{1,0:T(8,128)S(1)} %collective-permute-done.1.src, f32[8,128]{1,0:T(8,128)S(1)} %collective-permute-done.2.facts, f32[128,512]{1,0:T(8,128)S(1)} %get-tuple-element.42.inverse_noise, bf16[32,512]{1,0:T(8,128)(2,1)S(1)} %get-tuple-element.43.wait.a_6_), custom_call_target="tpu_custom_call" | custom-call | tf_op jit(solution)/shard_map/neighbour/pallas_call | solution.py:539
  14.6 0.1 collective-permute-start.4
  14.7 0.4 collective-permute-done.6.rest_1_
  15.1 4.4 %collective-permute-done.5.rest_0_ = f32[32,1024]{1,0:T(8,128)S(1)} collective-permute-done((f32[32,1024]{1,0:T(8,128)}, f32[32,1024]{1,0:T(8,128)S(1)}, u32[]{:S(2)}, u32[]{:S(2)}) %collective-permute-start.5) | collective-permute-done | bytes 131104 | tf_op jit(solution)/shard_map/ppermute | solution.py:440
  19.4 0.6 %middle.1 = (bf16[288,1024]{1,0:T(8,128)(2,1)S(1)}, bf16[288,1024]{1,0:T(8,128)(2,1)S(1)}, bf16[32,512]{1,0:T(8,128)(2,1)S(1)}, bf16[32,512]{1,0:T(8,128)(2,1)S(...) custom-call(f32[32,1024]{1,0:T(8,128)S(1)} %collective-permute-done., ...), custom_call_target="tpu_custom_call" | custom-call | flops 16000000000 | tf_op jit(solution)/shard_map/middle/pallas_call | solution.py:519
  20.0 0.0 collective-permute-done.a_1_
  20.0 0.0 collective-permute-done.4.a_3_
  20.0 5.7 %late.1 = (f32[9,32,144]{2,1,0:T(8,128)S(1)}, f32[9,32,144]{2,1,0:T(8,128)S(1)}, f32[9,32,144]{2,1,0:T(8,128)S(1)}, f32[9,32,144]{2,1,0:T(8,128)S(1)}, f32[9,32,...) custom-call(f32[104,1536]{1,0:T(8,128)S(1)} %get-tuple-element.40.a_, ...), custom_call_target="tpu_custom_call" | custom-call | tf_op jit(solution)/shard_map/late/pallas_call | solution.py:519
  25.7 0.1 collective-permute-start.9
  25.8 0.6 %collective-permute-start.8 = (f32[8,512]{1,0:T(8,128)S(1)}, f32[8,512]{1,0:T(8,128)S(1)}, u32[]{:S(2)}, u32[]{:S(2)}) collective-permute-start(f32[8,512]{1,0:T(8,128)S(1)} %get-tuple-element.59.a_0_), channel_id=1, source_target_pairs={{0,2},{1,3},{2,0},{3,1},{4,6},{5,7},{6,4},{7,5},{8,10},{9,11},{10,... | collective-permute-start | bytes 49160 | tf_op jit(solution)/shard_map/ppermute | solution.py:440
  26.4 1.2 %collective-permute-start.7 = (f32[8,512]{1,0:T(8,128)S(1)}, f32[8,512]{1,0:T(8,128)S(1)}, u32[]{:S(2)}, u32[]{:S(2)}) collective-permute-start(f32[8,512]{1,0:T(8,128)S(1)} %get-tuple-element.59.a_0_), channel_id=1, source_target_pairs={{0,1},{1,0},{2,3},{3,2},{4,5},{5,4},{6,7},{7,6},{8,9},{9,8},{10,11... | collective-permute-start | bytes 49160 | tf_op jit(solution)/shard_map/ppermute | solution.py:440
  27.6 1.3 %collective-permute-done.9.a_3_ = f32[8,512]{1,0:T(8,128)S(1)} collective-permute-done((f32[8,512]{1,0:T(8,128)S(1)}, f32[8,512]{1,0:T(8,128)S(1)}, u32[]{:S(2)}, u32[]{:S(2)}) %collective-permute-start.9) | collective-permute-done | bytes 16416 | tf_op jit(solution)/shard_map/ppermute | solution.py:440
  28.9 0.7 %collective-permute-done.8.a_2_ = f32[8,512]{1,0:T(8,128)S(1)} collective-permute-done((f32[8,512]{1,0:T(8,128)S(1)}, f32[8,512]{1,0:T(8,128)S(1)}, u32[]{:S(2)}, u32[]{:S(2)}) %collective-permute-start.8) | collective-permute-done | bytes 16416 | tf_op jit(solution)/shard_map/ppermute | solution.py:440
  29.6 0.0 collective-permute-done.7.a_1_
  29.6 0.9 %sums.6 = (f32[16,1536]{1,0:T(8,128)S(1)}, f32[16,1536]{1,0:T(8,128)S(1)}) custom-call(f32[8,512]{1,0:T(8,128)S(1)} %get-tuple-element.59.a_0_, f32[8,512]{1,0:T(8,128)S(1)} %collective-permute-done.7.a_1_, f32[8,512]{1,0:T(8,128)S(1)} %collective-permute-done.8.a_2_, f32[8,512]{1,0:T(8,128)S(1)} %collective-permute-done.9.a_3_, ...), custom_call_target="tpu_custom_call" | custom-call | tf_op jit(solution)/shard_map/sums/pallas_call | solution.py:578
  30.5 0.0 collective-permute-start.10
  30.6 2.0 %collective-permute-start.11 = (f32[16,1536]{1,0:T(8,128)S(1)}, f32[16,1536]{1,0:T(8,128)S(1)}, u32[]{:S(2)}, u32[]{:S(2)}) collective-permute-start(f32[16,1536]{1,0:T(8,128)S(1)} %get-tuple-element.72), channel_id=1, source_target_pairs={{0,4},{1,5},{2,6},{3,7},{4,0},{5,1},{6,2},{7,3},{8,12},{9,13},{10,... | collective-permute-start | bytes 294920 | tf_op jit(solution)/shard_map/ppermute | solution.py:440
  32.6 0.9 %sums.4 = (f32[16,1536]{1,0:T(8,128)S(1)}, f32[16,1536]{1,0:T(8,128)S(1)}) custom-call(f32[8,512]{1,0:T(8,128)S(1)} %get-tuple-element.59.a_0_, f32[8,512]{1,0:T(8,128)S(1)} %collective-permute-done.7.a_1_, f32[8,512]{1,0:T(8,128)S(1)} %collective-permute-done.8.a_2_, f32[8,512]{1,0:T(8,128)S(1)} %collective-permute-done.9.a_3_, ...), custom_call_target="tpu_custom_call" | custom-call | tf_op jit(solution)/shard_map/sums/pallas_call | solution.py:578
  33.5 0.1 collective-permute-start.13
  33.7 1.9 %collective-permute-start.12 = (f32[16,1536]{1,0:T(8,128)S(1)}, f32[16,1536]{1,0:T(8,128)S(1)}, u32[]{:S(2)}, u32[]{:S(2)}) collective-permute-start(f32[16,1536]{1,0:T(8,128)S(1)} %get-tuple-element.64.a_4_), channel_id=1, source_target_pairs={{0,4},{1,5},{2,6},{3,7},{4,0},{5,1},{6,2},{7,3},{8,12},{9,13},{10,... | collective-permute-start | bytes 294920 | tf_op jit(solution)/shard_map/ppermute | solution.py:440
  35.6 0.9 %sums.5 = (f32[16,1536]{1,0:T(8,128)S(1)}, f32[16,1536]{1,0:T(8,128)S(1)}) custom-call(f32[8,512]{1,0:T(8,128)S(1)} %get-tuple-element.59.a_0_, f32[8,512]{1,0:T(8,128)S(1)} %collective-permute-done.7.a_1_, f32[8,512]{1,0:T(8,128)S(1)} %collective-permute-done.8.a_2_, f32[8,512]{1,0:T(8,128)S(1)} %collective-permute-done.9.a_3_, ...), custom_call_target="tpu_custom_call" | custom-call | tf_op jit(solution)/shard_map/sums/pallas_call | solution.py:578
  36.6 0.0 collective-permute-done.10.b
  36.6 1.3 %collective-permute-start.14 = (f32[16,1536]{1,0:T(8,128)S(1)}, f32[16,1536]{1,0:T(8,128)S(1)}, u32[]{:S(2)}, u32[]{:S(2)}) collective-permute-start(f32[16,1536]{1,0:T(8,128)S(1)} %combined.2.a_4_), channel_id=1, source_target_pairs={{0,8},{1,9},{2,10},{3,11},{4,12},{5,13},{6,14},{7,15},{8,0},{9,1},... | collective-permute-start | bytes 294920 | tf_op jit(solution)/shard_map/ppermute | solution.py:440
  37.9 0.5 %collective-permute-done.11.b = f32[16,1536]{1,0:T(8,128)S(1)} collective-permute-done((f32[16,1536]{1,0:T(8,128)S(1)}, f32[16,1536]{1,0:T(8,128)S(1)}, u32[]{:S(2)}, u32[]{:S(2)}) %collective-permute-start.11) | collective-permute-done | bytes 98336 | tf_op jit(solution)/shard_map/ppermute | solution.py:440
  38.4 1.2 %collective-permute-start.15 = (f32[16,1536]{1,0:T(8,128)S(1)}, f32[16,1536]{1,0:T(8,128)S(1)}, u32[]{:S(2)}, u32[]{:S(2)}) collective-permute-start(f32[16,1536]{1,0:T(8,128)S(1)} %combined.3.a_5_), channel_id=1, source_target_pairs={{0,8},{1,9},{2,10},{3,11},{4,12},{5,13},{6,14},{7,15},{8,0},{9,1},... | collective-permute-start | bytes 294920 | tf_op jit(solution)/shard_map/ppermute | solution.py:440
  39.7 3.4 %collective-permute-done.13.a_7_ = f32[16,1536]{1,0:T(8,128)S(1)} collective-permute-done((f32[16,1536]{1,0:T(8,128)S(1)}, f32[16,1536]{1,0:T(8,128)S(1)}, u32[]{:S(2)}, u32[]{:S(2)}) %collective-permute-start.13) | collective-permute-done | bytes 98336 | tf_op jit(solution)/shard_map/ppermute | solution.py:440
  43.1 1.2 %collective-permute-done.12.a_6_ = f32[16,1536]{1,0:T(8,128)S(1)} collective-permute-done((f32[16,1536]{1,0:T(8,128)S(1)}, f32[16,1536]{1,0:T(8,128)S(1)}, u32[]{:S(2)}, u32[]{:S(2)}) %collective-permute-start.12) | collective-permute-done | bytes 98336 | tf_op jit(solution)/shard_map/ppermute | solution.py:440
  44.3 0.0 copy-start
  44.3 1.6 %sums.7 = (f32[32,1536]{1,0:T(8,128)S(1)}, f32[2,96]{1,0:T(2,128)}) custom-call(f32[8,512]{1,0:T(8,128)S(1)} %get-tuple-element.59.a_0_, f32[8,512]{1,0:T(8,128)S(1)} %collective-permute-done.7.a_1_, f32[8,512]{1,0:T(8,128)S(1)} %collective-permute-done.8.a_2_, f32[8,512]{1,0:T(8,128)S(1)} %collective-permute-done.9.a_3_, f32[16,1536]{1,0:T(8,128)S(1)} %combined.2.a_4_, ...), custom_call_target="tpu_custom_call" | custom-call | tf_op jit(solution)/shard_map/sums/pallas_call | solution.py:578
  45.8 0.0 collective-permute-done.14.a_1_
  45.9 1.6 %collective-permute-done.15.a_2_ = f32[16,1536]{1,0:T(8,128)S(1)} collective-permute-done((f32[16,1536]{1,0:T(8,128)S(1)}, f32[16,1536]{1,0:T(8,128)S(1)}, u32[]{:S(2)}, u32[]{:S(2)}) %collective-permute-start.15) | collective-permute-done | bytes 98336 | tf_op jit(solution)/shard_map/ppermute | solution.py:440
  47.4 0.0 copy-done
  47.4 0.7 %update.1 = f32[32,1024]{1,0:T(8,128)} custom-call(f32[32,1536]{1,0:T(8,128)S(1)} %get-tuple-element.77.a_0_, f32[16,1536]{1,0:T(8,128)S(1)} %collective-permute-done.14.a_1_, f32[16,1536]{1,0:T(8,128)S(1)} %collective-permute-done.15.a_2_, f32[1,512]{1,0:T(1,128)S(1)} %bitcast.8), custom_call_target="tpu_custom_call" | custom-call | tf_op jit(solution)/shard_map/update/pallas_call | solution.py:610
  (2 shorter events, 0.0 us)
Async XLA Ops:
  0.6 13.4 %collective-permute-start.1 = (f32[96,1024]{1,0:T(8,128)}, f32[96,1024]{1,0:T(8,128)S(1)}, u32[]{:S(2)}, u32[]{:S(2)}) collective-permute-start(f32[96,1024]{1,0:T(8,128)} %src_at.1), channel_id=1, source_target_pairs={{0,2},{1,3},{2,0},{3,1},{4,6},{5,7},{6,4},{7,5},{8,10},{9,11},{10,... | collective-permute-start | bytes 1179656 | tf_op jit(solution)/shard_map/ppermute | solution.py:440
  3.7 7.2 %collective-permute-start.3 = (f32[32,1024]{1,0:T(8,128)}, f32[32,1024]{1,0:T(8,128)S(1)}, u32[]{:S(2)}, u32[]{:S(2)}) collective-permute-start(f32[32,1024]{1,0:T(8,128)} %bitcast.9), channel_id=1, source_target_pairs={{0,4},{1,5},{2,6},{3,7},{4,0},{5,1},{6,2},{7,3},{8,12},{9,13},{10,... | collective-permute-start | bytes 393224 | tf_op jit(solution)/shard_map/ppermute | solution.py:440
  5.2 9.8 %collective-permute-start.6 = (f32[32,1024]{1,0:T(8,128)}, f32[32,1024]{1,0:T(8,128)S(1)}, u32[]{:S(2)}, u32[]{:S(2)}) collective-permute-start(f32[32,1024]{1,0:T(8,128)} %bitcast.10), channel_id=1, source_target_pairs={{0,12},{1,13},{2,14},{3,15},{4,8},{5,9},{6,10},{7,11},{8,4},{9,5},... | collective-permute-start | bytes 393224 | tf_op jit(solution)/shard_map/ppermute | solution.py:440
  7.7 11.7 %collective-permute-start.5 = (f32[32,1024]{1,0:T(8,128)}, f32[32,1024]{1,0:T(8,128)S(1)}, u32[]{:S(2)}, u32[]{:S(2)}) collective-permute-start(f32[32,1024]{1,0:T(8,128)} %bitcast.11), channel_id=1, source_target_pairs={{0,8},{1,9},{2,10},{3,11},{4,12},{5,13},{6,14},{7,15},{8,0},{9,1},... | collective-permute-start | bytes 393224 | tf_op jit(solution)/shard_map/ppermute | solution.py:440
  10.3 3.7 %collective-permute-start.2 = (f32[8,128]{1,0:T(8,128)S(1)}, f32[8,128]{1,0:T(8,128)S(1)}, u32[]{:S(2)}, u32[]{:S(2)}) collective-permute-start(f32[8,128]{1,0:T(8,128)S(1)} %get-tuple-element.41), channel_id=1, source_target_pairs={{0,2},{1,3},{2,0},{3,1},{4,6},{5,7},{6,4},{7,5},{8,10},{9,11},{10,... | collective-permute-start | bytes 12296 | tf_op jit(solution)/shard_map/ppermute | solution.py:440
  10.9 9.1 %collective-permute-start = (f32[104,1536]{1,0:T(8,128)S(1)}, f32[104,1536]{1,0:T(8,128)S(1)}, u32[]{:S(2)}, u32[]{:S(2)}) collective-permute-start(f32[104,1536]{1,0:T(8,128)S(1)} %get-tuple-element.40.a_0_), channel_id=1, source_target_pairs={{0,1},{1,0},{2,3},{3,2},{4,5},{5,4},{6,7},{7,6},{8,9},{9,8},{10,11... | collective-permute-start | bytes 1916936 | tf_op jit(solution)/shard_map/ppermute | solution.py:440
  14.6 5.4 %collective-permute-start.4 = (f32[104,1536]{1,0:T(8,128)S(1)}, f32[104,1536]{1,0:T(8,128)S(1)}, u32[]{:S(2)}, u32[]{:S(2)}) collective-permute-start(f32[104,1536]{1,0:T(8,128)S(1)} %neighbour.1.a_2_), channel_id=1, source_target_pairs={{0,1},{1,0},{2,3},{3,2},{4,5},{5,4},{6,7},{7,6},{8,9},{9,8},{10,11... | collective-permute-start | bytes 1916936 | tf_op jit(solution)/shard_map/ppermute | solution.py:440
  25.7 3.2 %collective-permute-start.9 = (f32[8,512]{1,0:T(8,128)S(1)}, f32[8,512]{1,0:T(8,128)S(1)}, u32[]{:S(2)}, u32[]{:S(2)}) collective-permute-start(f32[8,512]{1,0:T(8,128)S(1)} %get-tuple-element.59.a_0_), channel_id=1, source_target_pairs={{0,3},{1,2},{2,1},{3,0},{4,7},{5,6},{6,5},{7,4},{8,11},{9,10},{10,... | collective-permute-start | bytes 49160 | tf_op jit(solution)/shard_map/ppermute | solution.py:440
  25.8 3.8 %collective-permute-start.8 = (f32[8,512]{1,0:T(8,128)S(1)}, f32[8,512]{1,0:T(8,128)S(1)}, u32[]{:S(2)}, u32[]{:S(2)}) collective-permute-start(f32[8,512]{1,0:T(8,128)S(1)} %get-tuple-element.59.a_0_), channel_id=1, source_target_pairs={{0,2},{1,3},{2,0},{3,1},{4,6},{5,7},{6,4},{7,5},{8,10},{9,11},{10,... | collective-permute-start | bytes 49160 | tf_op jit(solution)/shard_map/ppermute | solution.py:440
  26.4 3.2 %collective-permute-start.7 = (f32[8,512]{1,0:T(8,128)S(1)}, f32[8,512]{1,0:T(8,128)S(1)}, u32[]{:S(2)}, u32[]{:S(2)}) collective-permute-start(f32[8,512]{1,0:T(8,128)S(1)} %get-tuple-element.59.a_0_), channel_id=1, source_target_pairs={{0,1},{1,0},{2,3},{3,2},{4,5},{5,4},{6,7},{7,6},{8,9},{9,8},{10,11... | collective-permute-start | bytes 49160 | tf_op jit(solution)/shard_map/ppermute | solution.py:440
  30.5 6.0 %collective-permute-start.10 = (f32[16,1536]{1,0:T(8,128)S(1)}, f32[16,1536]{1,0:T(8,128)S(1)}, u32[]{:S(2)}, u32[]{:S(2)}) collective-permute-start(f32[16,1536]{1,0:T(8,128)S(1)} %get-tuple-element.70), channel_id=1, source_target_pairs={{0,4},{1,5},{2,6},{3,7},{4,0},{5,1},{6,2},{7,3},{8,12},{9,13},{10,... | collective-permute-start | bytes 294920 | tf_op jit(solution)/shard_map/ppermute | solution.py:440
  30.6 7.8 %collective-permute-start.11 = (f32[16,1536]{1,0:T(8,128)S(1)}, f32[16,1536]{1,0:T(8,128)S(1)}, u32[]{:S(2)}, u32[]{:S(2)}) collective-permute-start(f32[16,1536]{1,0:T(8,128)S(1)} %get-tuple-element.72), channel_id=1, source_target_pairs={{0,4},{1,5},{2,6},{3,7},{4,0},{5,1},{6,2},{7,3},{8,12},{9,13},{10,... | collective-permute-start | bytes 294920 | tf_op jit(solution)/shard_map/ppermute | solution.py:440
  33.5 9.5 %collective-permute-start.13 = (f32[16,1536]{1,0:T(8,128)S(1)}, f32[16,1536]{1,0:T(8,128)S(1)}, u32[]{:S(2)}, u32[]{:S(2)}) collective-permute-start(f32[16,1536]{1,0:T(8,128)S(1)} %get-tuple-element.73), channel_id=1, source_target_pairs={{0,4},{1,5},{2,6},{3,7},{4,0},{5,1},{6,2},{7,3},{8,12},{9,13},{10,... | collective-permute-start | bytes 294920 | tf_op jit(solution)/shard_map/ppermute | solution.py:440
  33.7 10.6 %collective-permute-start.12 = (f32[16,1536]{1,0:T(8,128)S(1)}, f32[16,1536]{1,0:T(8,128)S(1)}, u32[]{:S(2)}, u32[]{:S(2)}) collective-permute-start(f32[16,1536]{1,0:T(8,128)S(1)} %get-tuple-element.64.a_4_), channel_id=1, source_target_pairs={{0,4},{1,5},{2,6},{3,7},{4,0},{5,1},{6,2},{7,3},{8,12},{9,13},{10,... | collective-permute-start | bytes 294920 | tf_op jit(solution)/shard_map/ppermute | solution.py:440
  36.6 9.3 %collective-permute-start.14 = (f32[16,1536]{1,0:T(8,128)S(1)}, f32[16,1536]{1,0:T(8,128)S(1)}, u32[]{:S(2)}, u32[]{:S(2)}) collective-permute-start(f32[16,1536]{1,0:T(8,128)S(1)} %combined.2.a_4_), channel_id=1, source_target_pairs={{0,8},{1,9},{2,10},{3,11},{4,12},{5,13},{6,14},{7,15},{8,0},{9,1},... | collective-permute-start | bytes 294920 | tf_op jit(solution)/shard_map/ppermute | solution.py:440
  38.4 9.0 %collective-permute-start.15 = (f32[16,1536]{1,0:T(8,128)S(1)}, f32[16,1536]{1,0:T(8,128)S(1)}, u32[]{:S(2)}, u32[]{:S(2)}) collective-permute-start(f32[16,1536]{1,0:T(8,128)S(1)} %combined.3.a_5_), channel_id=1, source_target_pairs={{0,8},{1,9},{2,10},{3,11},{4,12},{5,13},{6,14},{7,15},{8,0},{9,1},... | collective-permute-start | bytes 294920 | tf_op jit(solution)/shard_map/ppermute | solution.py:440
  44.3 3.1 %copy-start = (f32[512]{0:T(512)S(1)}, f32[512]{0:T(512)}, u32[]{:S(2)}) copy-start(f32[512]{0:T(512)} %param.16) | copy-start | bytes 6148

commit v8 on v7

--- a/solution.py
+++ b/solution.py
@@ -279,26 +279,25 @@
     return score.reshape(SHIFTS, per, lanes) + (prior - 0.5 * quad)[None]
 
 
-def weigh(scores, facts, e_outs, stats_out):
-    per, lanes = scores[0].shape[1:]
-    top = None
-    for score in scores:
-        top_here = jnp.max(score[...], axis=0)
-        top = top_here if top is None else jnp.maximum(top, top_here)
-    top = jnp.max(top, axis=0, keepdims=True)
-    sums = [jnp.zeros((per, lanes), jnp.float32) for _ in range(SHIFTS)]
-    for score, e_out in zip(scores, e_outs):
-        for t in range(SHIFTS):
-            e = jnp.exp(score[t] - top)
-            e_out[t] = e
-            sums[t] = sums[t] + e
-    sums = [jnp.sum(s, axis=0, keepdims=True) for s in sums]
-    stats_out[...] = jnp.zeros_like(stats_out)
-    stats_out[0:1, :lanes] = top
-    stats_out[1:2, :lanes] = sum(sums)
-    stats_out[2:3, :lanes] = sum(s * float(gx) for s, (gx, gy) in zip(sums, GRID) if gx)
-    stats_out[3:4, :lanes] = sum(s * float(gy) for s, (gx, gy) in zip(sums, GRID) if gy)
-    stats_out[4:5, :lanes] = facts[5:6, :lanes]
+def weigh(score, e_out):
+    top = jnp.max(jnp.max(score, axis=0), axis=0, keepdims=True)
+    e = jnp.exp(score - top[None])
+    e_out[...] = e
+    side = SIDE // 2
+    by_x = [sum(e[SIDE * x + y] for y in range(SIDE)) for x in range(SIDE)]
+    by_y = [sum(e[SIDE * x + y] for x in range(SIDE)) for y in range(SIDE)]
+    sums = [sum(by_x)]
+    for by in (by_x, by_y):
+        sums.append(sum(by[k] * float(k - side) for k in range(SIDE) if k != side))
+    return top, [jnp.sum(x, axis=0, keepdims=True) for x in sums]
+
+
+def joined_sums(tops, sums):
+    top = tops[0]
+    for other in tops[1:]:
+        top = jnp.maximum(top, other)
+    factors = [jnp.exp(other - top) for other in tops]
+    return top, [sum(f * x for f, x in zip(factors, column)) for column in zip(*sums)]
 
 
 def early_kernel(own_at, near, *rest):
@@ -322,53 +321,63 @@
 def late_kernel(blocks, own, cnb, ynb, cynb, *rest):
     prepared, rest = rest[: 4 * blocks], rest[4 * blocks :]
     e_outs, rest = (rest[:blocks], rest[blocks : 2 * blocks]), rest[2 * blocks :]
-    y_out, power_out, stats_out, *half_stats = rest
+    y_out, power_out, stats_out, tops_out, *half_out = rest
+    half_stats, half_tops = half_out[:2], half_out[2:]
     per, lanes = e_outs[0][0].shape[1:]
     left = lanes - 128
     pairs = ((own, cnb), (ynb, cynb))
     facts = [half_facts(*pair) for pair in pairs]
     for half, pair in enumerate(pairs):
         place_half(half, *pair, y_out, power_out)
+    for out in (y_out, power_out):
         empty = 768 + 6 * left
-    for out in (y_out, power_out):
         out[empty:] = jnp.zeros_like(out[empty:])
+    for out in half_out:
+        out[...] = jnp.zeros_like(out)
     for half in range(2):
         particles = [placed(half, part, left, out) for out in (y_out, power_out) for part in (0, 1)]
         prior = prior_rows(facts[half], per, lanes)
+        tops, sums = [], []
         for n in range(blocks):
-            e_outs[half][n][...] = block_scores(prepared[4 * n : 4 * n + 4], particles, prior)
-        weigh(e_outs[half], facts[half], e_outs[half], half_stats[half])
+            score = block_scores(prepared[4 * n : 4 * n + 4], particles, prior)
+            top, sums_here = weigh(score, e_outs[half][n])
+            half_tops[half][n : n + 1, :lanes] = top
+            tops.append(top)
+            sums.append(sums_here)
+        top, sums = joined_sums(tops, sums)
+        for k, row in enumerate((top, *sums, facts[half][5:6, :lanes])):
+            half_stats[half][k : k + 1, :lanes] = row
     first = (lax.axis_index("dom") // 2) % 2 == 0
-    mine, others = half_stats[0][...], half_stats[1][...]
-    stats_out[:, :256] = jnp.where(first, mine, others)
-    stats_out[:, 256:] = jnp.where(first, others, mine)
-
-
-def sum_kernel(cuts, last, waits, *rest):
-    team, rest = rest[:TEAM], rest[TEAM + waits :]
-    if last:
-        *near, ea_ref, eb_ref, y_ref, power_ref, part_out, shift_out = rest
-        near = jnp.concatenate([x[...] for x in near], axis=0)
-        rest = ea_ref, eb_ref, y_ref, power_ref, part_out, shift_out
-    ea_ref, eb_ref, y_ref, power_ref, *outs = rest
+    for out, (mine, others) in ((stats_out, half_stats), (tops_out, half_tops)):
+        mine, others = mine[...], others[...]
+        out[:, :256] = jnp.where(first, mine, others)
+        out[:, 256:] = jnp.where(first, others, mine)
+
+
+def chip_kernel(mine, other, out):
+    pair = (mine[...], other[...])
+    top, sums = joined_sums([x[0:1] for x in pair], [[x[k : k + 1] for k in (1, 2, 3)] for x in pair])
+    out[...] = pair[0]
+    for k, row in enumerate((top, *sums)):
+        out[k : k + 1] = row
+
+
+def sum_kernel(n, cuts, last, waits, here, there, tops, *rest):
+    ea_ref, eb_ref, y_ref, power_ref, *outs = rest[waits:]
     per, lanes = ea_ref.shape[1:]
     width = y_ref.shape[1]
     freq = width // 2
     first = (lax.axis_index("dom") // 2) % 2 == 0
-    team = [s[...] for s in team]
-    top = team[0][0:1]
-    for s in team[1:]:
-        top = jnp.maximum(top, s[0:1])
-    gains = [jnp.exp(s[0:1] - top) for s in team]
-    mass = sum(g * s[1:2] for g, s in zip(gains, team))
-    live = team[0][4:5] / mass
-    own_gain = gains[0] * live
-    gain_a = jnp.where(first, own_gain[:, :256], own_gain[:, 256:])[:, :lanes]
-    gain_b = jnp.where(first, own_gain[:, 256:], own_gain[:, :256])[:, :lanes]
+    pair = (here[...], there[...])
+    top, (mass, *move) = joined_sums(
+        [x[0:1] for x in pair], [[x[k : k + 1] for k in (1, 2, 3)] for x in pair]
+    )
+    live = pair[0][4:5] / mass
+    gain = jnp.exp(tops[n : n + 1] - top) * live
+    gain_a = jnp.where(first, gain[:, :256], gain[:, 256:])[:, :lanes]
+    gain_b = jnp.where(first, gain[:, 256:], gain[:, :256])[:, :lanes]
     if last:
-        move = jnp.concatenate(
-            [sum(g * s[k : k + 1] for g, s in zip(gains, team)) * live for k in (2, 3)], axis=0
-        )
+        move = jnp.concatenate([x * live for x in move], axis=0)
         move = jnp.concatenate([move, jnp.zeros((6, 512), jnp.float32)], axis=0)
         move = jnp.where(first, move[:, :256], move[:, 256:])
         lane = lax.broadcasted_iota(jnp.int32, (8, 128), 1)
@@ -397,10 +406,6 @@
         re = re + (ar + br) * c - (ai - bi) * s
         im = im + (ar - br) * s + (ai + bi) * c
     weight = dot_nn(deep_lanes(jnp.sum(wa, axis=0), jnp.sum(wb, axis=0)), power_ref[...])
-    if last:
-        re = re + near[:, :freq]
-        im = im + near[:, freq:width]
-        weight = weight + near[:, width:]
     for start, stop, out in zip(cuts, cuts[1:], outs):
         part = slice(start, stop)
         out[:, :freq] = re[part]
@@ -408,8 +413,13 @@
         out[:, width:] = weight[part]
 
 
-def add_kernel(a, b, out):
-    out[...] = a[...] + b[...]
+def add_kernel(a, *rest):
+    *parts, out = rest
+    at = 0
+    for part in parts:
+        rows = slice(at, at + part.shape[0])
+        out[rows] = a[rows] + part[...]
+        at += part.shape[0]
 
 
 def final_kernel(row_cuts, *refs):
@@ -460,6 +470,7 @@
     f32 = jnp.float32
     vmem = pl.BlockSpec(memory_space=pltpu.VMEM)
     no_cost = pl.CostEstimate(flops=0, bytes_accessed=0, transcendentals=0)
+    much = pl.CostEstimate(flops=16 * 10**9, bytes_accessed=0, transcendentals=0)
 
     ynb = crossed(particle_fourier, 2)
     anywhere = pl.BlockSpec(memory_space=pl.ANY)
@@ -554,45 +565,50 @@
         block_shapes * late,
         "middle",
         4 + 2 * blocks,
-        pl.CostEstimate(flops=16 * 10**9, bytes_accessed=0, transcendentals=0),
+        much,
     )
     prepared = (*prepared, *outs)
     deep = 3 * 256 + 128
+    top_rows = -(-blocks // 8) * 8
     outs = call(
         lambda *a: late_kernel(blocks, *a),
         (own, cnb, ynb_prepared, cynb, *prepared),
         [score_shape] * (2 * blocks)
-        + [shaped(deep, width, bf16), shaped(deep, freq, bf16), shaped(8, 512)],
+        + [shaped(deep, width, bf16), shaped(deep, freq, bf16), shaped(8, 512)]
+        + [shaped(top_rows, 512)],
         "late",
         8 + 2 * blocks,
-        scratch=[pltpu.VMEM((8, 256), f32)] * 2,
-    )
-    e_own, e_other, (y, power, stats) = outs[:blocks], outs[blocks : 2 * blocks], outs[2 * blocks :]
-
-    team = [stats] + [crossed(stats, n) for n in range(1, TEAM)]
-
-    def sums(n, cuts, near=(), waits=()):
+        scratch=[pltpu.VMEM((8, 256), f32)] * 2 + [pltpu.VMEM((top_rows, 256), f32)] * 2,
+    )
+    e_own, e_other = outs[:blocks], outs[blocks : 2 * blocks]
+    y, power, stats, tops = outs[2 * blocks :]
+
+    (here,) = call(chip_kernel, (stats, crossed(stats, 1)), [shaped(8, 512)], "chip", 1)
+    there = crossed(here, 2)
+
+    def sums(n, cuts, last=False, waits=()):
         out_shape = [shaped(b - a, width + freq) for a, b in zip(cuts, cuts[1:])]
-        if near:
+        if last:
             out_shape.append(shaped(2, slots))
         return pl.pallas_call(
-            lambda *a: sum_kernel(cuts, bool(near), len(waits), *a),
+            lambda *a: sum_kernel(n, cuts, last, len(waits), *a),
             out_shape=tuple(out_shape),
-            in_specs=[vmem] * TEAM + [anywhere] * len(waits) + [vmem] * (4 + len(near)),
+            in_specs=[vmem] * 3 + [anywhere] * len(waits) + [vmem] * 4,
             out_specs=(vmem,) * len(out_shape),
             compiler_params=params(8),
             name="sums",
-        )(*team, *waits, *near, e_own[n], e_other[n], y, power)
-
-    def combined(mine, other):
+        )(here, there, tops, *waits, e_own[n], e_other[n], y, power)
+
+    def combined(mine, others, cost=None):
         return pl.pallas_call(
             add_kernel,
             out_shape=jax.ShapeDtypeStruct(mine.shape, f32),
-            in_specs=[vmem] * 2,
+            in_specs=[vmem] * (1 + len(others)),
             out_specs=vmem,
             compiler_params=params(4),
+            cost_estimate=cost,
             name="combined",
-        )(mine, other)
+        )(mine, *others)
 
     whole, cut = (0, per), (0, per // 2, per)
     far = []
@@ -601,10 +617,11 @@
         handed = [crossed(x, TEAM) for x in sums(n + 1, cut)]
         if n == 2:
             near = sums(1, cut)
-        joined = [combined(x, y) for x, y in zip(sums(n, cut, waits=near[:1]), handed)]
+        joined = [combined(x, [y]) for x, y in zip(sums(n, cut, waits=near[:1]), handed)]
         far.extend(crossed(x, TEAM * n) for x in joined)
         waits.extend(joined)
-    own_part, shift = sums(0, whole, near=[crossed(x, TEAM) for x in near], waits=waits)
+    own_part, shift = sums(0, whole, last=True, waits=waits)
+    own_part = combined(own_part, [crossed(x, TEAM) for x in near], much)
     row_cuts = [cut] * (len(far) // 2)
 
     refs_new = pl.pallas_call(

time: 48.3 us -> 49.1 us (1.017)
  waiting for transfers between devices: 15.3 us -> 18.4 us
  starting transfers between devices: 16.4 us -> 14.3 us
    ppermute x16 -> x15, waiting for transfers between devices: 15.3 us -> 18.4 us  [crossed(): return lax.ppermute(block, 'dom', [(i, i ^ mask) for i in range(size)])]
    ppermute x16 -> x15, starting transfers between devices: 16.4 us -> 14.3 us  [crossed(): return lax.ppermute(block, 'dom', [(i, i ^ mask) for i in range(size)])]
    pallas_call x2 -> x3, Pallas kernels: 6.24 us -> 6.11 us  [call(): pl.pallas_call(kernel, cost_estimate=cost, out_shape=tuple(out_shape), in...]
  transfers between devices with their start and end apart: 16 -> 15, of which waited for: 9 -> 9; matrix products, arithmetic and copies ran while one was open for 0% -> 0% of each run, Pallas kernels for 16% -> 16%
where the time goes in v8:
time: 49.1 us; the launch traced here: 48.9 us
  waiting for transfers between devices  18.4 us (37%)
  Pallas kernels  14.8 us (30%)
  starting transfers between devices  14.3 us (29%)
  between operations  1.39 us (3%)
    ppermute x15, waiting for transfers between devices, crossed(): return lax.ppermute(block, 'dom', [(i, i ^ mask) for i in range(size)])  18.4 us
    ppermute x15, starting transfers between devices, crossed(): return lax.ppermute(block, 'dom', [(i, i ^ mask) for i in range(size)])  14.3 us
    pallas_call x3, Pallas kernels, call(): pl.pallas_call(kernel, cost_estimate=cost, out_shape=tuple(out_shape), in...  6.11 us
    pallas_call x4, Pallas kernels, sums(): pl.pallas_call(lambda *a: sum_kernel(n, cuts, last, len(waits), *a), out_...  4.38 us
    pallas_call x1, Pallas kernels, on_device(): pl.pallas_call(own_kernel, out_shape=(jax.ShapeDtypeStruct((slots + 8, wi...  1.83 us
    pallas_call x1, Pallas kernels, on_device(): pl.pallas_call(early_kernel, out_shape=tuple(block_shapes * early), in_sp...  1.16 us
  transfers between devices with their start and end apart: 15, of which 9 were waited for; matrix products, arithmetic and copies ran while one was open for 0% of the time, Pallas kernels for 16%

profile of v8, /device:TPU:0, one launch (start us, length us, event | category | flops | bytes accessed | tf_op | source)
XLA Modules:
  0.0 48.9 jit_solution(14093448924140562081)
XLA Ops:
  0.6 3.0 %collective-permute-start.1 = (f32[96,1024]{1,0:T(8,128)}, f32[96,1024]{1,0:T(8,128)S(1)}, u32[]{:S(2)}, u32[]{:S(2)}) collective-permute-start(f32[96,1024]{1,0:T(8,128)} %src_at.1), channel_id=1, source_target_pairs={{0,2},{1,3},{2,0},{3,1},{4,6},{5,7},{6,4},{7,5},{8,10},{9,11},{10,... | collective-permute-start | bytes 1179656 | tf_op jit(solution)/shard_map/ppermute | solution.py:450
  3.7 1.6 %collective-permute-start.3 = (f32[32,1024]{1,0:T(8,128)}, f32[32,1024]{1,0:T(8,128)S(1)}, u32[]{:S(2)}, u32[]{:S(2)}) collective-permute-start(f32[32,1024]{1,0:T(8,128)} %bitcast.9), channel_id=1, source_target_pairs={{0,4},{1,5},{2,6},{3,7},{4,0},{5,1},{6,2},{7,3},{8,12},{9,13},{10,... | collective-permute-start | bytes 393224 | tf_op jit(solution)/shard_map/ppermute | solution.py:450
  5.2 2.5 %collective-permute-start.6 = (f32[32,1024]{1,0:T(8,128)}, f32[32,1024]{1,0:T(8,128)S(1)}, u32[]{:S(2)}, u32[]{:S(2)}) collective-permute-start(f32[32,1024]{1,0:T(8,128)} %bitcast.10), channel_id=1, source_target_pairs={{0,12},{1,13},{2,14},{3,15},{4,8},{5,9},{6,10},{7,11},{8,4},{9,5},... | collective-permute-start | bytes 393224 | tf_op jit(solution)/shard_map/ppermute | solution.py:450
  7.7 0.1 collective-permute-start.5
  8.5 1.8 %own.1 = (f32[104,1536]{1,0:T(8,128)S(1)}, f32[8,128]{1,0:T(8,128)S(1)}, f32[128,512]{1,0:T(8,128)S(1)}) custom-call(f32[96,1024]{1,0:T(8,128)} %src_at.1, f32[1,96]{1,0:T(1,128)} %bitcast.15, s32[2,96]{1,0:T(2,128)} %bitcast.14, s32[1,96]{1,0:T(1,128)} %bitcast.16, s32[1,96]{1,0:T(1,128)} %bitcast.17, f32[128,512]{1,0:T(8,128)} %noise_at.1, ...), custom_call_target="tpu_custom_call" | custom-call | tf_op jit(solution)/shard_map/own/pallas_call | solution.py:503
  10.3 0.6 %collective-permute-start.2 = (f32[8,128]{1,0:T(8,128)S(1)}, f32[8,128]{1,0:T(8,128)S(1)}, u32[]{:S(2)}, u32[]{:S(2)}) collective-permute-start(f32[8,128]{1,0:T(8,128)S(1)} %get-tuple-element.42), channel_id=1, source_target_pairs={{0,2},{1,3},{2,0},{3,1},{4,6},{5,7},{6,4},{7,5},{8,10},{9,11},{10,... | collective-permute-start | bytes 12296 | tf_op jit(solution)/shard_map/ppermute | solution.py:450
  10.9 0.0 collective-permute-done.3.near
  10.9 0.0 collective-permute-start
  10.9 1.2 %early.1 = (bf16[288,1024]{1,0:T(8,128)(2,1)S(1)}, bf16[288,1024]{1,0:T(8,128)(2,1)S(1)}, bf16[32,512]{1,0:T(8,128)(2,1)S(1)}, bf16[32,512]{1,0:T(8,128)(2,1)S(1...) custom-call(f32[32,1024]{1,0:T(8,128)} %bitcast.12, ...), custom_call_target="tpu_custom_call" | custom-call | tf_op jit(solution)/shard_map/early/pallas_call | solution.py:541
  12.1 1.9 %collective-permute-done.2.facts = f32[8,128]{1,0:T(8,128)S(1)} collective-permute-done((f32[8,128]{1,0:T(8,128)S(1)}, f32[8,128]{1,0:T(8,128)S(1)}, u32[]{:S(2)}, u32[]{:S(2)}) %collective-permute-start.2) | collective-permute-done | bytes 4128 | tf_op jit(solution)/shard_map/ppermute | solution.py:450
  14.0 0.0 collective-permute-done.1.src
  14.0 0.6 %neighbour.1.a_2_ = f32[104,1536]{1,0:T(8,128)S(1)} custom-call(f32[96,1024]{1,0:T(8,128)S(1)} %collective-permute-done.1.src, f32[8,128]{1,0:T(8,128)S(1)} %collective-permute-done.2.facts, f32[128,512]{1,0:T(8,128)S(1)} %get-tuple-element.43.inverse_noise, bf16[32,512]{1,0:T(8,128)(2,1)S(1)} %get-tuple-element.44.wait.a_6_), custom_call_target="tpu_custom_call" | custom-call | tf_op jit(solution)/shard_map/neighbour/pallas_call | solution.py:550
  14.6 0.1 collective-permute-start.4
  14.7 0.4 collective-permute-done.6.rest_1_
  15.1 4.4 %collective-permute-done.5.rest_0_ = f32[32,1024]{1,0:T(8,128)S(1)} collective-permute-done((f32[32,1024]{1,0:T(8,128)}, f32[32,1024]{1,0:T(8,128)S(1)}, u32[]{:S(2)}, u32[]{:S(2)}) %collective-permute-start.5) | collective-permute-done | bytes 131104 | tf_op jit(solution)/shard_map/ppermute | solution.py:450
  19.4 0.6 %middle.1 = (bf16[288,1024]{1,0:T(8,128)(2,1)S(1)}, bf16[288,1024]{1,0:T(8,128)(2,1)S(1)}, bf16[32,512]{1,0:T(8,128)(2,1)S(1)}, bf16[32,512]{1,0:T(8,128)(2,1)S(...) custom-call(f32[32,1024]{1,0:T(8,128)S(1)} %collective-permute-done., ...), custom_call_target="tpu_custom_call" | custom-call | flops 16000000000 | tf_op jit(solution)/shard_map/middle/pallas_call | solution.py:530
  20.0 0.0 collective-permute-done.a_1_
  20.0 0.0 collective-permute-done.4.a_3_
  20.0 5.5 %late.1 = (f32[9,32,144]{2,1,0:T(8,128)S(1)}, f32[9,32,144]{2,1,0:T(8,128)S(1)}, f32[9,32,144]{2,1,0:T(8,128)S(1)}, f32[9,32,144]{2,1,0:T(8,128)S(1)}, f32[9,32,...) custom-call(f32[104,1536]{1,0:T(8,128)S(1)} %get-tuple-element.41.a_, ...), custom_call_target="tpu_custom_call" | custom-call | tf_op jit(solution)/shard_map/late/pallas_call | solution.py:530
  25.6 0.1 collective-permute-start.7
  25.6 1.2 %collective-permute-done.7.other = f32[8,512]{1,0:T(8,128)S(1)} collective-permute-done((f32[8,512]{1,0:T(8,128)S(1)}, f32[8,512]{1,0:T(8,128)S(1)}, u32[]{:S(2)}, u32[]{:S(2)}) %collective-permute-start.7) | collective-permute-done | bytes 16416 | tf_op jit(solution)/shard_map/ppermute | solution.py:450
  26.8 0.6 %collective-permute-start.8 = (f32[8,512]{1,0:T(8,128)S(1)}, f32[8,512]{1,0:T(8,128)S(1)}, u32[]{:S(2)}, u32[]{:S(2)}) collective-permute-start(f32[8,512]{1,0:T(8,128)S(1)} %chip.1.a_0_), channel_id=1, source_target_pairs={{0,2},{1,3},{2,0},{3,1},{4,6},{5,7},{6,4},{7,5},{8,10},{9,11},{10,... | collective-permute-start | bytes 49160 | tf_op jit(solution)/shard_map/ppermute | solution.py:450
  27.4 3.2 %collective-permute-done.8.a_1_ = f32[8,512]{1,0:T(8,128)S(1)} collective-permute-done((f32[8,512]{1,0:T(8,128)S(1)}, f32[8,512]{1,0:T(8,128)S(1)}, u32[]{:S(2)}, u32[]{:S(2)}) %collective-permute-start.8) | collective-permute-done | bytes 16416 | tf_op jit(solution)/shard_map/ppermute | solution.py:450
  30.6 0.9 %sums.6 = (f32[16,1536]{1,0:T(8,128)S(1)}, f32[16,1536]{1,0:T(8,128)S(1)}) custom-call(f32[8,512]{1,0:T(8,128)S(1)} %chip.1.a_0_, f32[8,512]{1,0:T(8,128)S(1)} %collective-permute-done.8.a_1_, f32[8,512]{1,0:T(8,128)S(1)} %get-tuple-element.61.a_2_, f32[9,32,144]{2,1,0:T(8,128)S(1)} %get-tuple-element.70.a_3_, f32[9,32,144]{2,1,0:T(8,128)S(1)} %get-tuple-element.71.a_4_, ...), custom_call_target="tpu_custom_call" | custom-call | tf_op jit(solution)/shard_map/sums/pallas_call | solution.py:593
  31.6 0.0 collective-permute-start.9
  31.6 2.0 %collective-permute-start.10 = (f32[16,1536]{1,0:T(8,128)S(1)}, f32[16,1536]{1,0:T(8,128)S(1)}, u32[]{:S(2)}, u32[]{:S(2)}) collective-permute-start(f32[16,1536]{1,0:T(8,128)S(1)} %get-tuple-element.74), channel_id=1, source_target_pairs={{0,4},{1,5},{2,6},{3,7},{4,0},{5,1},{6,2},{7,3},{8,12},{9,13},{10,... | collective-permute-start | bytes 294920 | tf_op jit(solution)/shard_map/ppermute | solution.py:450
  33.6 0.9 %sums.4 = (f32[16,1536]{1,0:T(8,128)S(1)}, f32[16,1536]{1,0:T(8,128)S(1)}) custom-call(f32[8,512]{1,0:T(8,128)S(1)} %chip.1.a_0_, f32[8,512]{1,0:T(8,128)S(1)} %collective-permute-done.8.a_1_, f32[8,512]{1,0:T(8,128)S(1)} %get-tuple-element.61.a_2_, f32[9,32,144]{2,1,0:T(8,128)S(1)} %get-tuple-element.62.a_3_, f32[9,32,144]{2,1,0:T(8,128)S(1)} %get-tuple-element.63.a_4_, ...), custom_call_target="tpu_custom_call" | custom-call | tf_op jit(solution)/shard_map/sums/pallas_call | solution.py:593
  34.6 0.1 collective-permute-start.12
  34.7 1.9 %collective-permute-start.11 = (f32[16,1536]{1,0:T(8,128)S(1)}, f32[16,1536]{1,0:T(8,128)S(1)}, u32[]{:S(2)}, u32[]{:S(2)}) collective-permute-start(f32[16,1536]{1,0:T(8,128)S(1)} %get-tuple-element.66.a_3_), channel_id=1, source_target_pairs={{0,4},{1,5},{2,6},{3,7},{4,0},{5,1},{6,2},{7,3},{8,12},{9,13},{10,... | collective-permute-start | bytes 294920 | tf_op jit(solution)/shard_map/ppermute | solution.py:450
  36.6 0.9 %sums.5 = (f32[16,1536]{1,0:T(8,128)S(1)}, f32[16,1536]{1,0:T(8,128)S(1)}) custom-call(f32[8,512]{1,0:T(8,128)S(1)} %chip.1.a_0_, f32[8,512]{1,0:T(8,128)S(1)} %collective-permute-done.8.a_1_, f32[8,512]{1,0:T(8,128)S(1)} %get-tuple-element.61.a_2_, f32[16,1536]{1,0:T(8,128)S(1)} %get-tuple-element.66.a_3_, f32[9,32,144]{2,1,0:T(8,128)S(1)} %get-tuple-element.67.a_4_, ...), custom_call_target="tpu_custom_call" | custom-call | tf_op jit(solution)/shard_map/sums/pallas_call | solution.py:593
  37.6 0.0 collective-permute-done.9.rest_0_
  37.6 1.3 %collective-permute-start.13 = (f32[16,1536]{1,0:T(8,128)S(1)}, f32[16,1536]{1,0:T(8,128)S(1)}, u32[]{:S(2)}, u32[]{:S(2)}) collective-permute-start(f32[16,1536]{1,0:T(8,128)S(1)} %combined.3.a_3_), channel_id=1, source_target_pairs={{0,8},{1,9},{2,10},{3,11},{4,12},{5,13},{6,14},{7,15},{8,0},{9,1},... | collective-permute-start | bytes 294920 | tf_op jit(solution)/shard_map/ppermute | solution.py:450
  38.9 1.4 %collective-permute-done.10.rest_0_ = f32[16,1536]{1,0:T(8,128)S(1)} collective-permute-done((f32[16,1536]{1,0:T(8,128)S(1)}, f32[16,1536]{1,0:T(8,128)S(1)}, u32[]{:S(2)}, u32[]{:S(2)}) %collective-permute-start.10) | collective-permute-done | bytes 98336 | tf_op jit(solution)/shard_map/ppermute | solution.py:450
  40.3 0.4 collective-permute-start.14
  40.7 1.6 %sums.7 = (f32[32,1536]{1,0:T(8,128)S(1)}, f32[2,96]{1,0:T(2,128)}) custom-call(f32[8,512]{1,0:T(8,128)S(1)} %chip.1.a_0_, f32[8,512]{1,0:T(8,128)S(1)} %collective-permute-done.8.a_1_, f32[8,512]{1,0:T(8,128)S(1)} %get-tuple-element.61.a_2_, f32[16,1536]{1,0:T(8,128)S(1)} %combined.3.a_3_, f32[16,1536]{1,0:T(8,128)S(1)} %combined.4.a_4_, ...), custom_call_target="tpu_custom_call" | custom-call | tf_op jit(solution)/shard_map/sums/pallas_call | solution.py:593
  42.2 1.0 %collective-permute-done.12.rest_1_ = f32[16,1536]{1,0:T(8,128)S(1)} collective-permute-done((f32[16,1536]{1,0:T(8,128)S(1)}, f32[16,1536]{1,0:T(8,128)S(1)}, u32[]{:S(2)}, u32[]{:S(2)}) %collective-permute-start.12) | collective-permute-done | bytes 98336 | tf_op jit(solution)/shard_map/ppermute | solution.py:450
  43.3 1.5 %collective-permute-done.11.rest_0_ = f32[16,1536]{1,0:T(8,128)S(1)} collective-permute-done((f32[16,1536]{1,0:T(8,128)S(1)}, f32[16,1536]{1,0:T(8,128)S(1)}, u32[]{:S(2)}, u32[]{:S(2)}) %collective-permute-start.11) | collective-permute-done | bytes 98336 | tf_op jit(solution)/shard_map/ppermute | solution.py:450
  44.8 0.0 copy-start
  44.8 0.0 collective-permute-done.13.a_1_
  44.8 3.4 %collective-permute-done.14.a_2_ = f32[16,1536]{1,0:T(8,128)S(1)} collective-permute-done((f32[16,1536]{1,0:T(8,128)S(1)}, f32[16,1536]{1,0:T(8,128)S(1)}, u32[]{:S(2)}, u32[]{:S(2)}) %collective-permute-start.14) | collective-permute-done | bytes 98336 | tf_op jit(solution)/shard_map/ppermute | solution.py:450
  48.2 0.0 copy-done
  48.2 0.7 %update.1 = f32[32,1024]{1,0:T(8,128)} custom-call(f32[32,1536]{1,0:T(8,128)S(1)} %combined.5.a_0_, f32[16,1536]{1,0:T(8,128)S(1)} %collective-permute-done.13.a_1_, f32[16,1536]{1,0:T(8,128)S(1)} %collective-permute-done.14.a_2_, f32[1,512]{1,0:T(1,128)S(1)} %bitcast.8), custom_call_target="tpu_custom_call" | custom-call | tf_op jit(solution)/shard_map/update/pallas_call | solution.py:627
  (4 shorter events, 0.1 us)
Async XLA Ops:
  0.6 13.4 %collective-permute-start.1 = (f32[96,1024]{1,0:T(8,128)}, f32[96,1024]{1,0:T(8,128)S(1)}, u32[]{:S(2)}, u32[]{:S(2)}) collective-permute-start(f32[96,1024]{1,0:T(8,128)} %src_at.1), channel_id=1, source_target_pairs={{0,2},{1,3},{2,0},{3,1},{4,6},{5,7},{6,4},{7,5},{8,10},{9,11},{10,... | collective-permute-start | bytes 1179656 | tf_op jit(solution)/shard_map/ppermute | solution.py:450
  3.7 7.2 %collective-permute-start.3 = (f32[32,1024]{1,0:T(8,128)}, f32[32,1024]{1,0:T(8,128)S(1)}, u32[]{:S(2)}, u32[]{:S(2)}) collective-permute-start(f32[32,1024]{1,0:T(8,128)} %bitcast.9), channel_id=1, source_target_pairs={{0,4},{1,5},{2,6},{3,7},{4,0},{5,1},{6,2},{7,3},{8,12},{9,13},{10,... | collective-permute-start | bytes 393224 | tf_op jit(solution)/shard_map/ppermute | solution.py:450
  5.2 9.8 %collective-permute-start.6 = (f32[32,1024]{1,0:T(8,128)}, f32[32,1024]{1,0:T(8,128)S(1)}, u32[]{:S(2)}, u32[]{:S(2)}) collective-permute-start(f32[32,1024]{1,0:T(8,128)} %bitcast.10), channel_id=1, source_target_pairs={{0,12},{1,13},{2,14},{3,15},{4,8},{5,9},{6,10},{7,11},{8,4},{9,5},... | collective-permute-start | bytes 393224 | tf_op jit(solution)/shard_map/ppermute | solution.py:450
  7.7 11.7 %collective-permute-start.5 = (f32[32,1024]{1,0:T(8,128)}, f32[32,1024]{1,0:T(8,128)S(1)}, u32[]{:S(2)}, u32[]{:S(2)}) collective-permute-start(f32[32,1024]{1,0:T(8,128)} %bitcast.11), channel_id=1, source_target_pairs={{0,8},{1,9},{2,10},{3,11},{4,12},{5,13},{6,14},{7,15},{8,0},{9,1},... | collective-permute-start | bytes 393224 | tf_op jit(solution)/shard_map/ppermute | solution.py:450
  10.3 3.7 %collective-permute-start.2 = (f32[8,128]{1,0:T(8,128)S(1)}, f32[8,128]{1,0:T(8,128)S(1)}, u32[]{:S(2)}, u32[]{:S(2)}) collective-permute-start(f32[8,128]{1,0:T(8,128)S(1)} %get-tuple-element.42), channel_id=1, source_target_pairs={{0,2},{1,3},{2,0},{3,1},{4,6},{5,7},{6,4},{7,5},{8,10},{9,11},{10,... | collective-permute-start | bytes 12296 | tf_op jit(solution)/shard_map/ppermute | solution.py:450
  10.9 9.1 %collective-permute-start = (f32[104,1536]{1,0:T(8,128)S(1)}, f32[104,1536]{1,0:T(8,128)S(1)}, u32[]{:S(2)}, u32[]{:S(2)}) collective-permute-start(f32[104,1536]{1,0:T(8,128)S(1)} %get-tuple-element.41.a_0_), channel_id=1, source_target_pairs={{0,1},{1,0},{2,3},{3,2},{4,5},{5,4},{6,7},{7,6},{8,9},{9,8},{10,11... | collective-permute-start | bytes 1916936 | tf_op jit(solution)/shard_map/ppermute | solution.py:450
  14.6 5.4 %collective-permute-start.4 = (f32[104,1536]{1,0:T(8,128)S(1)}, f32[104,1536]{1,0:T(8,128)S(1)}, u32[]{:S(2)}, u32[]{:S(2)}) collective-permute-start(f32[104,1536]{1,0:T(8,128)S(1)} %neighbour.1.a_2_), channel_id=1, source_target_pairs={{0,1},{1,0},{2,3},{3,2},{4,5},{5,4},{6,7},{7,6},{8,9},{9,8},{10,11... | collective-permute-start | bytes 1916936 | tf_op jit(solution)/shard_map/ppermute | solution.py:450
  25.6 1.2 %collective-permute-start.7 = (f32[8,512]{1,0:T(8,128)S(1)}, f32[8,512]{1,0:T(8,128)S(1)}, u32[]{:S(2)}, u32[]{:S(2)}) collective-permute-start(f32[8,512]{1,0:T(8,128)S(1)} %get-tuple-element.60.mine), channel_id=1, source_target_pairs={{0,1},{1,0},{2,3},{3,2},{4,5},{5,4},{6,7},{7,6},{8,9},{9,8},{10,11... | collective-permute-start | bytes 49160 | tf_op jit(solution)/shard_map/ppermute | solution.py:450
  26.8 3.8 %collective-permute-start.8 = (f32[8,512]{1,0:T(8,128)S(1)}, f32[8,512]{1,0:T(8,128)S(1)}, u32[]{:S(2)}, u32[]{:S(2)}) collective-permute-start(f32[8,512]{1,0:T(8,128)S(1)} %chip.1.a_0_), channel_id=1, source_target_pairs={{0,2},{1,3},{2,0},{3,1},{4,6},{5,7},{6,4},{7,5},{8,10},{9,11},{10,... | collective-permute-start | bytes 49160 | tf_op jit(solution)/shard_map/ppermute | solution.py:450
  31.6 6.0 %collective-permute-start.9 = (f32[16,1536]{1,0:T(8,128)S(1)}, f32[16,1536]{1,0:T(8,128)S(1)}, u32[]{:S(2)}, u32[]{:S(2)}) collective-permute-start(f32[16,1536]{1,0:T(8,128)S(1)} %get-tuple-element.72), channel_id=1, source_target_pairs={{0,4},{1,5},{2,6},{3,7},{4,0},{5,1},{6,2},{7,3},{8,12},{9,13},{10,... | collective-permute-start | bytes 294920 | tf_op jit(solution)/shard_map/ppermute | solution.py:450
  31.6 8.6 %collective-permute-start.10 = (f32[16,1536]{1,0:T(8,128)S(1)}, f32[16,1536]{1,0:T(8,128)S(1)}, u32[]{:S(2)}, u32[]{:S(2)}) collective-permute-start(f32[16,1536]{1,0:T(8,128)S(1)} %get-tuple-element.74), channel_id=1, source_target_pairs={{0,4},{1,5},{2,6},{3,7},{4,0},{5,1},{6,2},{7,3},{8,12},{9,13},{10,... | collective-permute-start | bytes 294920 | tf_op jit(solution)/shard_map/ppermute | solution.py:450
  34.6 8.7 %collective-permute-start.12 = (f32[16,1536]{1,0:T(8,128)S(1)}, f32[16,1536]{1,0:T(8,128)S(1)}, u32[]{:S(2)}, u32[]{:S(2)}) collective-permute-start(f32[16,1536]{1,0:T(8,128)S(1)} %get-tuple-element.79), channel_id=1, source_target_pairs={{0,4},{1,5},{2,6},{3,7},{4,0},{5,1},{6,2},{7,3},{8,12},{9,13},{10,... | collective-permute-start | bytes 294920 | tf_op jit(solution)/shard_map/ppermute | solution.py:450
  34.7 10.1 %collective-permute-start.11 = (f32[16,1536]{1,0:T(8,128)S(1)}, f32[16,1536]{1,0:T(8,128)S(1)}, u32[]{:S(2)}, u32[]{:S(2)}) collective-permute-start(f32[16,1536]{1,0:T(8,128)S(1)} %get-tuple-element.66.a_3_), channel_id=1, source_target_pairs={{0,4},{1,5},{2,6},{3,7},{4,0},{5,1},{6,2},{7,3},{8,12},{9,13},{10,... | collective-permute-start | bytes 294920 | tf_op jit(solution)/shard_map/ppermute | solution.py:450
  37.6 7.2 %collective-permute-start.13 = (f32[16,1536]{1,0:T(8,128)S(1)}, f32[16,1536]{1,0:T(8,128)S(1)}, u32[]{:S(2)}, u32[]{:S(2)}) collective-permute-start(f32[16,1536]{1,0:T(8,128)S(1)} %combined.3.a_3_), channel_id=1, source_target_pairs={{0,8},{1,9},{2,10},{3,11},{4,12},{5,13},{6,14},{7,15},{8,0},{9,1},... | collective-permute-start | bytes 294920 | tf_op jit(solution)/shard_map/ppermute | solution.py:450
  40.3 7.9 %collective-permute-start.14 = (f32[16,1536]{1,0:T(8,128)S(1)}, f32[16,1536]{1,0:T(8,128)S(1)}, u32[]{:S(2)}, u32[]{:S(2)}) collective-permute-start(f32[16,1536]{1,0:T(8,128)S(1)} %combined.4.a_4_), channel_id=1, source_target_pairs={{0,8},{1,9},{2,10},{3,11},{4,12},{5,13},{6,14},{7,15},{8,0},{9,1},... | collective-permute-start | bytes 294920 | tf_op jit(solution)/shard_map/ppermute | solution.py:450
  44.8 3.4 %copy-start = (f32[512]{0:T(512)S(1)}, f32[512]{0:T(512)}, u32[]{:S(2)}) copy-start(f32[512]{0:T(512)} %param.16) | copy-start | bytes 6148

commit v9 on v8

--- a/solution.py
+++ b/solution.py
@@ -1,3 +1,4 @@
+import functools
 import math
 
 import jax
@@ -78,28 +79,17 @@
     return high, (x - high.astype(jnp.float32)).astype(jnp.bfloat16)
 
 
-def main_rows(half, part):
-    return 256 * part + 128 * half
-
-
-def left_rows(half, part, left):
-    return 768 + 2 * left * part + left * half
+def deep_at(half, part):
+    return 384 * part + 128 * half, 384 * part + 256 + 64 * half
 
 
 def deep_lanes(a, b):
-    rows, lanes = a.shape
-    left = lanes - 128
-    high, low = halves(jnp.concatenate([a[:, :128], b[:, :128]], axis=1))
-    empty = jnp.zeros((rows, 128 - left), jnp.float32)
+    empty = jnp.zeros((a.shape[0], 64), jnp.float32)
     tail = jnp.concatenate([a[:, 128:], empty], axis=1) + pltpu.roll(
-        jnp.concatenate([b[:, 128:], empty], axis=1), left, 1
-    )
-    tail_high = tail.astype(jnp.bfloat16).astype(jnp.float32)
-    tail_low = tail - tail_high
-    mixed = (
-        tail_high + pltpu.roll(tail_high, 2 * left, 1) + pltpu.roll(tail_low, 4 * left, 1)
-    )
-    return jnp.concatenate([high, high, low, mixed.astype(jnp.bfloat16)], axis=1)
+        jnp.concatenate([b[:, 128:], empty], axis=1), 64, 1
+    )
+    high, low = halves(jnp.concatenate([a[:, :128], b[:, :128], tail], axis=1))
+    return jnp.concatenate([high, high, low], axis=1)
 
 
 def grid_phases(width):
@@ -191,58 +181,62 @@
     prepared_rows(src, facts_out[...], inverse, out)
 
 
-def neighbour_kernel(src, facts, inverse_noise, wait, out):
+def neighbour_kernel(src, facts, inverse_noise, out):
     prepared_rows(src, facts[...], inverse_noise[...], out)
 
 
-def even_core():
-    return lax.axis_index("dom") % 2 == 0
-
-
-def place_half(half, mine, other, y_out, power_out):
+def first_at(part, row):
+    return 192 * part + row
+
+
+def both_at(half, part, row):
+    main, left = deep_at(half, part)
+    return main + row if row < 128 else left + row - 128
+
+
+def place_half(own, ynb, y_out, power_out, parts, at):
     width = y_out.shape[1]
-    slots = mine.shape[0] - 8
-    left = slots + slots // 2 - 128
-
-    def place(src, rows, to):
-        for cols, out in ((slice(0, width), y_out), (slice(width, None), power_out)):
-            high, low = halves(src[rows, cols])
-            for part, value in enumerate((high, low, high)):
-                if to < 128:
-                    at = main_rows(half, part) + to
-                else:
-                    at = left_rows(half, part, left) + to - 128
-                out[at : at + value.shape[0]] = value
-
-    def place_both(heavy, light):
-        place(heavy, slice(0, slots), 0)
-        place(light, slice(0, 128 - slots), slots)
-        place(light, slice(128 - slots, slots // 2), 128)
-
-    even = even_core()
-
-    @pl.when(even)
-    def _():
-        place_both(mine, other)
-
-    @pl.when(jnp.logical_not(even))
-    def _():
-        place_both(other, mine)
-
-
-def placed(half, part, left, out):
-    main, tail = main_rows(half, part), left_rows(half, part, left)
-    return jnp.concatenate([out[main : main + 128], out[tail : tail + left]], axis=0)
-
-
-def half_facts(mine, other):
-    slots = mine.shape[0] - 8
-    even = even_core()
-    x, y = mine[slots:, :128], other[slots:, :128]
-    heavy = jnp.where(even, x, y)
-    light = pltpu.roll(jnp.where(even, y, x), 96, 1)
+    slots = own.shape[0] - 8
+    main = 128 - slots
+    for cols, out in ((slice(0, width), y_out), (slice(width, None), power_out)):
+        pieces = ((own, 0, slots, 0), (ynb, 0, main, slots), (ynb, main, slots, 128))
+        for src, start, stop, to in pieces:
+            pair = halves(src[start:stop, cols])
+            for part in range(parts):
+                row = at(part, to)
+                out[row : row + stop - start] = pair[part % 2]
+
+
+def placed(out, part, at):
+    main, left = at(part, 0), at(part, 128)
+    return jnp.concatenate([out[main : main + 128], out[left : left + 64]], axis=0)
+
+
+def half_facts(own, ynb):
+    slots = own.shape[0] - 8
+    x, y = own[slots:, :128], pltpu.roll(ynb[slots:, :128], slots, 1)
     lane = lax.broadcasted_iota(jnp.int32, (8, 128), 1)
-    return jnp.concatenate([jnp.where(lane < 96, heavy, light), light], axis=1)
+    return jnp.concatenate([jnp.where(lane < slots, x, y), y], axis=1)
+
+
+def by_device(x, slots):
+    lane = lax.broadcasted_iota(jnp.int32, (x.shape[0], 128), 1)
+    main, left = pltpu.roll(x[:, :128], 128 - slots, 1), pltpu.roll(x[:, 128:], 128 - slots, 1)
+    return x[:, :128], jnp.where(lane < 128 - slots, main, left)
+
+
+def in_half(x, y, slots):
+    lane = lax.broadcasted_iota(jnp.int32, (x.shape[0], 128), 1)
+    y = pltpu.roll(y, slots, 1)
+    return jnp.concatenate([jnp.where(lane < slots, x, y), y], axis=1)
+
+
+def team_order(tiles):
+    me = lax.axis_index("dom")
+    even, first = me % 2 == 0, (me // 2) % 2 == 0
+    a, b, c, d = tiles
+    a, b, c, d = (jnp.where(even, x, y) for x, y in ((a, c), (b, d), (c, a), (d, b)))
+    return [jnp.where(first, x, y) for x, y in ((a, b), (b, a), (c, d), (d, c))]
 
 
 def prior_rows(facts, per, lanes):
@@ -310,7 +304,7 @@
     prepare_refs(own, phases, *prepared[:4])
 
 
-def middle_kernel(*rest):
+def middle_kernel(wait, *rest):
     count = len(rest) // 5
     refs, prepared = rest[:count], rest[count:]
     phases = grid_phases(refs[0].shape[1] // 2)
@@ -318,40 +312,46 @@
         prepare_refs(refs[n], phases, *prepared[4 * n : 4 * n + 4])
 
 
-def late_kernel(blocks, own, cnb, ynb, cynb, *rest):
+def score_kernel(half, blocks, own, ynb, *rest):
     prepared, rest = rest[: 4 * blocks], rest[4 * blocks :]
-    e_outs, rest = (rest[:blocks], rest[blocks : 2 * blocks]), rest[2 * blocks :]
-    y_out, power_out, stats_out, tops_out, *half_out = rest
-    half_stats, half_tops = half_out[:2], half_out[2:]
-    per, lanes = e_outs[0][0].shape[1:]
-    left = lanes - 128
-    pairs = ((own, cnb), (ynb, cynb))
-    facts = [half_facts(*pair) for pair in pairs]
-    for half, pair in enumerate(pairs):
-        place_half(half, *pair, y_out, power_out)
-    for out in (y_out, power_out):
-        empty = 768 + 6 * left
-        out[empty:] = jnp.zeros_like(out[empty:])
-    for out in half_out:
-        out[...] = jnp.zeros_like(out)
-    for half in range(2):
-        particles = [placed(half, part, left, out) for out in (y_out, power_out) for part in (0, 1)]
-        prior = prior_rows(facts[half], per, lanes)
-        tops, sums = [], []
-        for n in range(blocks):
-            score = block_scores(prepared[4 * n : 4 * n + 4], particles, prior)
-            top, sums_here = weigh(score, e_outs[half][n])
-            half_tops[half][n : n + 1, :lanes] = top
-            tops.append(top)
-            sums.append(sums_here)
-        top, sums = joined_sums(tops, sums)
-        for k, row in enumerate((top, *sums, facts[half][5:6, :lanes])):
-            half_stats[half][k : k + 1, :lanes] = row
-    first = (lax.axis_index("dom") // 2) % 2 == 0
-    for out, (mine, others) in ((stats_out, half_stats), (tops_out, half_tops)):
-        mine, others = mine[...], others[...]
-        out[:, :256] = jnp.where(first, mine, others)
-        out[:, 256:] = jnp.where(first, others, mine)
+    if half:
+        stats_in, tops_in, y_in, power_in, *rest = rest
+    e_outs, rest = rest[:blocks], rest[blocks:]
+    y_out, power_out, stats_out, tops_out, stats, tops_row = rest
+    per, lanes = e_outs[0].shape[1:]
+    slots = lanes // 2
+    facts = half_facts(own, ynb)
+    at = functools.partial(both_at, half) if half else first_at
+    place_half(own, ynb, y_out, power_out, 2 + half, at)
+    if half:
+        for x, out in ((y_in, y_out), (power_in, power_out)):
+            for part in range(3):
+                for row, size in ((0, 128), (128, 64)):
+                    here, to = first_at(part % 2, row), both_at(0, part, row)
+                    out[to : to + size] = x[here : here + size]
+    stats[...] = jnp.zeros_like(stats)
+    tops_row[...] = jnp.zeros_like(tops_row)
+    particles = [placed(out, part, at) for out in (y_out, power_out) for part in (0, 1)]
+    prior = prior_rows(facts, per, lanes)
+    tops, sums = [], []
+    for n in range(blocks):
+        score = block_scores(prepared[4 * n : 4 * n + 4], particles, prior)
+        top, sums_here = weigh(score, e_outs[n])
+        tops_row[n : n + 1, :lanes] = top
+        tops.append(top)
+        sums.append(sums_here)
+    top, sums = joined_sums(tops, sums)
+    for k, row in enumerate((top, *sums, facts[5:6, :lanes])):
+        stats[k : k + 1, :lanes] = row
+    if half == 0:
+        stats_out[...] = stats[...]
+        tops_out[...] = tops_row[...]
+        return
+    pair = by_device(stats_in[...], slots), by_device(stats[...], slots)
+    tiles = team_order((*pair[0], *pair[1]))
+    stats_out[...] = jnp.concatenate(tiles, axis=1)
+    tops_out[:, :256] = tops_in[...]
+    tops_out[:, 256:] = tops_row[...]
 
 
 def chip_kernel(mine, other, out):
@@ -362,37 +362,48 @@
         out[k : k + 1] = row
 
 
-def sum_kernel(n, cuts, last, waits, here, there, tops, *rest):
-    ea_ref, eb_ref, y_ref, power_ref, *outs = rest[waits:]
-    per, lanes = ea_ref.shape[1:]
+def sum_kernel(blocks, cuts, last, waits, here, there, tops, *rest):
+    rest = rest[waits:]
+    e_refs, (y_ref, power_ref, *outs) = rest[: 2 * len(blocks)], rest[2 * len(blocks) :]
+    per, lanes = e_refs[0].shape[1:]
+    slots = lanes // 2
     width = y_ref.shape[1]
     freq = width // 2
-    first = (lax.axis_index("dom") // 2) % 2 == 0
     pair = (here[...], there[...])
     top, (mass, *move) = joined_sums(
         [x[0:1] for x in pair], [[x[k : k + 1] for k in (1, 2, 3)] for x in pair]
     )
     live = pair[0][4:5] / mass
-    gain = jnp.exp(tops[n : n + 1] - top) * live
-    gain_a = jnp.where(first, gain[:, :256], gain[:, 256:])[:, :lanes]
-    gain_b = jnp.where(first, gain[:, 256:], gain[:, :256])[:, :lanes]
+    rows = [top, live, *(x * live for x in move)]
+    rows = jnp.concatenate([*rows, jnp.zeros((4, 512), jnp.float32)], axis=0)
+    mine = team_order([rows[:, 128 * k : 128 * (k + 1)] for k in range(4)])
     if last:
-        move = jnp.concatenate([x * live for x in move], axis=0)
-        move = jnp.concatenate([move, jnp.zeros((6, 512), jnp.float32)], axis=0)
-        move = jnp.where(first, move[:, :256], move[:, 256:])
-        lane = lax.broadcasted_iota(jnp.int32, (8, 128), 1)
-        light = jnp.where(
-            lane < 32, pltpu.roll(move[:, :128], 32, 1), pltpu.roll(move[:, 128:], 32, 1)
-        )
-        light = jnp.where(lane < 48, light, 0.0)
         shift_out = outs.pop()
-        slots = shift_out.shape[1]
-        shift_out[...] = jnp.where(even_core(), move[:, :128], light)[:2, :slots]
-    wa = ea_ref[...] * gain_a[None]
-    wb = eb_ref[...] * gain_b[None]
-    rows = SHIFTS * per
-    flat = dot_nn(deep_lanes(wa.reshape(rows, lanes), wb.reshape(rows, lanes)), y_ref[...])
+        shift_out[...] = mine[0][2:4, :slots]
+    halves_rows = (in_half(mine[0], mine[1], slots), in_half(mine[2], mine[3], slots))
+    per_block = []
+    weight_sums = []
+    for k, n in enumerate(blocks):
+        w = []
+        for half, row in enumerate(halves_rows):
+            top_here = tops[n : n + 1, 256 * half : 256 * half + lanes]
+            gain = jnp.exp(top_here - row[0:1, :lanes]) * row[1:2, :lanes]
+            w.append(e_refs[2 * k + half][...] * gain[None])
+        per_block.append(deep_lanes(*(x.reshape(SHIFTS * per, lanes) for x in w)))
+        weight_sums.append(deep_lanes(*(jnp.sum(x, axis=0) for x in w)))
+    flat_all = dot_nn(jnp.concatenate(per_block, axis=0), y_ref[...])
+    weight_all = dot_nn(jnp.concatenate(weight_sums, axis=0), power_ref[...])
     phases = grid_phases(freq)
+    count = len(cuts) - 1
+    for k in range(len(blocks)):
+        flat = flat_all[SHIFTS * per * k : SHIFTS * per * (k + 1)]
+        weight = weight_all[per * k : per * (k + 1)]
+        write_block(flat, weight, phases, cuts, outs[count * k : count * (k + 1)])
+
+
+def write_block(flat, weight, phases, cuts, outs):
+    per, freq = weight.shape
+    width = 2 * freq
     mid = SHIFTS // 2
 
     def block(t):
@@ -405,7 +416,6 @@
         br, bi = block(SHIFTS - 1 - t)
         re = re + (ar + br) * c - (ai - bi) * s
         im = im + (ar - br) * s + (ai + bi) * c
-    weight = dot_nn(deep_lanes(jnp.sum(wa, axis=0), jnp.sum(wb, axis=0)), power_ref[...])
     for start, stop, out in zip(cuts, cuts[1:], outs):
         part = slice(start, stop)
         out[:, :freq] = re[part]
@@ -472,8 +482,32 @@
     no_cost = pl.CostEstimate(flops=0, bytes_accessed=0, transcendentals=0)
     much = pl.CostEstimate(flops=16 * 10**9, bytes_accessed=0, transcendentals=0)
 
+    def gated(x, *waits):
+        return pl.pallas_call(
+            lambda *a: None,
+            out_shape=jax.ShapeDtypeStruct(x.shape, x.dtype),
+            in_specs=[anywhere] * (1 + len(waits)),
+            out_specs=anywhere,
+            input_output_aliases={0: 0},
+            compiler_params=params(1),
+            cost_estimate=no_cost,
+            name="gate",
+        )(x, *waits)
+
     ynb = crossed(particle_fourier, 2)
     anywhere = pl.BlockSpec(memory_space=pl.ANY)
+    def gated(x, *waits):
+        return pl.pallas_call(
+            lambda *a: None,
+            out_shape=jax.ShapeDtypeStruct(x.shape, x.dtype),
+            in_specs=[anywhere] * (1 + len(waits)),
+            out_specs=anywhere,
+            input_output_aliases={0: 0},
+            compiler_params=params(1),
+            cost_estimate=no_cost,
+            name="gate",
+        )(x, *waits)
+
     ynb = crossed(particle_fourier, 2)
     anywhere = pl.BlockSpec(memory_space=pl.ANY)
     def gated(arrays, waits, cost):
@@ -488,10 +522,36 @@
             name="gate",
         )(*arrays, *waits)
 
+    def gated(x, *waits):
+        return pl.pallas_call(
+            lambda *a: None,
+            out_shape=jax.ShapeDtypeStruct(x.shape, x.dtype),
+            in_specs=[anywhere] * (1 + len(waits)),
+            out_specs=anywhere,
+            input_output_aliases={0: 0},
+            compiler_params=params(1),
+            cost_estimate=no_cost,
+            name="gate",
+        )(x, *waits)
+
     ynb = crossed(particle_fourier, 2)
     anywhere = pl.BlockSpec(memory_space=pl.ANY)
+    def gated(x, *waits):
+        return pl.pallas_call(
+            lambda *a: None,
+            out_shape=jax.ShapeDtypeStruct(x.shape, x.dtype),
+            in_specs=[anywhere] * (1 + len(waits)),
+            out_specs=anywhere,
+            input_output_aliases={0: 0},
+            compiler_params=params(1),
+            cost_estimate=no_cost,
+            name="gate",
+        )(x, *waits)
+
     ynb = crossed(particle_fourier, 2)
-    refs = [refs_own] + [crossed(refs_own, TEAM * n) for n in range(1, blocks)]
+    refs = {0: refs_own, 1: crossed(refs_own, TEAM)}
+    for n in range(2, blocks, 2):
+        refs[n] = crossed(refs_own, TEAM * n)
     own_facts = (
         particle_fourier,
         defocus.reshape(1, slots),
@@ -516,7 +576,11 @@
         name="own",
     )(*(pltpu.with_memory_space_constraint(x, pltpu.HBM) for x in own_facts), live_count)
     cnb = crossed(own, 1)
-    half = slots + slots // 2
+    for n in range(2, blocks, 2):
+        refs[n] = gated(refs[n], facts)
+        refs[n + 1] = crossed(refs[n], TEAM)
+    refs = [refs[n] for n in range(blocks)]
+    both = 2 * slots
     bf16 = jnp.bfloat16
     early = 2
 
@@ -524,7 +588,7 @@
         return jax.ShapeDtypeStruct((rows, cols), dtype)
 
     block_shapes = [shaped(SHIFTS * per, width, bf16)] * 2 + [shaped(per, freq, bf16)] * 2
-    score_shape = jax.ShapeDtypeStruct((SHIFTS, per, half), f32)
+    score_shape = jax.ShapeDtypeStruct((SHIFTS, per, both), f32)
 
     def call(kernel, operands, out_shape, name, mib, cost=None, scratch=()):
         return pl.pallas_call(
@@ -550,54 +614,66 @@
     ynb_prepared = pl.pallas_call(
         neighbour_kernel,
         out_shape=jax.ShapeDtypeStruct((slots + 8, width + freq), f32),
-        in_specs=[vmem] * 3 + [anywhere],
+        in_specs=[vmem] * 3,
         out_specs=vmem,
         compiler_params=params(6),
         cost_estimate=no_cost,
         name="neighbour",
-    )(ynb, crossed(facts, 2), inverse_noise, prepared[2])
+    )(ynb, crossed(facts, 2), inverse_noise)
     cynb = crossed(ynb_prepared, 1)
 
     late = blocks - early
-    outs = call(
+    outs = pl.pallas_call(
         middle_kernel,
-        refs[early:],
-        block_shapes * late,
-        "middle",
-        4 + 2 * blocks,
-        much,
-    )
+        out_shape=tuple(block_shapes * late),
+        in_specs=[anywhere] + [vmem] * late,
+        out_specs=(vmem,) * (4 * late),
+        compiler_params=params(4 + 2 * blocks),
+        cost_estimate=much,
+        name="middle",
+    )(ynb_prepared, *refs[early:])
     prepared = (*prepared, *outs)
-    deep = 3 * 256 + 128
     top_rows = -(-blocks // 8) * 8
-    outs = call(
-        lambda *a: late_kernel(blocks, *a),
-        (own, cnb, ynb_prepared, cynb, *prepared),
-        [score_shape] * (2 * blocks)
-        + [shaped(deep, width, bf16), shaped(deep, freq, bf16), shaped(8, 512)]
-        + [shaped(top_rows, 512)],
-        "late",
-        8 + 2 * blocks,
-        scratch=[pltpu.VMEM((8, 256), f32)] * 2 + [pltpu.VMEM((top_rows, 256), f32)] * 2,
-    )
-    e_own, e_other = outs[:blocks], outs[blocks : 2 * blocks]
-    y, power, stats, tops = outs[2 * blocks :]
+
+    def scores(half, particles, before, cost):
+        lanes = 256 * (1 + half)
+        rows = (6 if half else 2) * both
+        return pl.pallas_call(
+            lambda *a: score_kernel(half, blocks, *a),
+            out_shape=(
+                *[score_shape] * blocks,
+                shaped(rows, width, bf16),
+                shaped(rows, freq, bf16),
+                shaped(8, lanes),
+                shaped(top_rows, lanes),
+            ),
+            in_specs=[vmem] * (2 + 4 * blocks + len(before)),
+            out_specs=(vmem,) * (blocks + 4),
+            scratch_shapes=[pltpu.VMEM((8, 256), f32), pltpu.VMEM((top_rows, 256), f32)],
+            compiler_params=params(8 + 2 * blocks),
+            cost_estimate=cost,
+            name="scores",
+        )(*particles, *prepared, *before)
+
+    *e_own, y, power, stats, tops = scores(0, (own, ynb_prepared), (), much)
+    *e_other, y, power, stats, tops = scores(1, (cnb, cynb), (stats, tops, y, power), None)
 
     (here,) = call(chip_kernel, (stats, crossed(stats, 1)), [shaped(8, 512)], "chip", 1)
     there = crossed(here, 2)
 
-    def sums(n, cuts, last=False, waits=()):
-        out_shape = [shaped(b - a, width + freq) for a, b in zip(cuts, cuts[1:])]
+    def sums(numbers, cuts, last=False, waits=()):
+        out_shape = [shaped(b - a, width + freq) for a, b in zip(cuts, cuts[1:])] * len(numbers)
         if last:
             out_shape.append(shaped(2, slots))
-        return pl.pallas_call(
-            lambda *a: sum_kernel(n, cuts, last, len(waits), *a),
+        weights = [e[n] for n in numbers for e in (e_own, e_other)]
+        return pl.pallas_call(
+            lambda *a: sum_kernel(numbers, cuts, last, len(waits), *a),
             out_shape=tuple(out_shape),
-            in_specs=[vmem] * 3 + [anywhere] * len(waits) + [vmem] * 4,
+            in_specs=[vmem] * 3 + [anywhere] * len(waits) + [vmem] * (2 + len(weights)),
             out_specs=(vmem,) * len(out_shape),
-            compiler_params=params(8),
+            compiler_params=params(12),
             name="sums",
-        )(here, there, tops, *waits, e_own[n], e_other[n], y, power)
+        )(here, there, tops, *waits, *weights, y, power)
 
     def combined(mine, others, cost=None):
         return pl.pallas_call(
@@ -614,13 +690,14 @@
     far = []
     waits = []
     for n in range(2, blocks, 2):
-        handed = [crossed(x, TEAM) for x in sums(n + 1, cut)]
+        handed = sums((n + 1, 1) if n == 2 else (n + 1,), cut)
         if n == 2:
-            near = sums(1, cut)
-        joined = [combined(x, [y]) for x, y in zip(sums(n, cut, waits=near[:1]), handed)]
+            near = handed[2:]
+        mine = sums((n,), cut, waits=handed[:1])
+        joined = [combined(x, [crossed(y, TEAM)]) for x, y in zip(mine, handed)]
         far.extend(crossed(x, TEAM * n) for x in joined)
         waits.extend(joined)
-    own_part, shift = sums(0, whole, last=True, waits=waits)
+    own_part, shift = sums((0,), whole, last=True, waits=waits)
     own_part = combined(own_part, [crossed(x, TEAM) for x in near], much)
     row_cuts = [cut] * (len(far) // 2)
 

time: 49.1 us -> 49.9 us (1.016)
  waiting for transfers between devices: 18.4 us -> 13.3 us
  starting transfers between devices: 14.3 us -> 19.3 us
  Pallas kernels: 14.8 us -> 15.9 us
    pallas_call x4 -> x7, Pallas kernels: 4.38 us -> 11.5 us  [the longest x2 5.92 us: scores(): pl.pallas_call(lambda *a: score_kernel(half, blocks, *a), out_shape=(*[sc...]
    pallas_call x3 -> x1, Pallas kernels: 6.11 us -> 0.02 us  [call(): pl.pallas_call(kernel, cost_estimate=cost, out_shape=tuple(out_shape), in...]
    ppermute x15, waiting for transfers between devices: 18.4 us -> 13.3 us  [crossed(): return lax.ppermute(block, 'dom', [(i, i ^ mask) for i in range(size)])]
    ppermute x15, starting transfers between devices: 14.3 us -> 19.3 us  [crossed(): return lax.ppermute(block, 'dom', [(i, i ^ mask) for i in range(size)])]
  transfers between devices with their start and end apart: 15 -> 15, of which waited for: 9 -> 7; matrix products, arithmetic and copies ran while one was open for 0% -> 0% of each run, Pallas kernels for 16% -> 20%
where the time goes in v9:
time: 49.9 us; the launch traced here: 49.8 us
  starting transfers between devices  19.3 us (39%)
  Pallas kernels  15.9 us (32%)
  waiting for transfers between devices  13.3 us (27%)
  between operations  1.38 us (3%)
    ppermute x15, starting transfers between devices, crossed(): return lax.ppermute(block, 'dom', [(i, i ^ mask) for i in range(size)])  19.3 us
    ppermute x15, waiting for transfers between devices, crossed(): return lax.ppermute(block, 'dom', [(i, i ^ mask) for i in range(size)])  13.3 us
    pallas_call x2, Pallas kernels, scores(): pl.pallas_call(lambda *a: score_kernel(half, blocks, *a), out_shape=(*[sc...  5.92 us
    pallas_call x3, Pallas kernels, sums(): pl.pallas_call(lambda *a: sum_kernel(numbers, cuts, last, len(waits), *a)...  5 us
    pallas_call x1, Pallas kernels, on_device(): pl.pallas_call(own_kernel, out_shape=(jax.ShapeDtypeStruct((slots + 8, wi...  1.83 us
    pallas_call x1, Pallas kernels, on_device(): pl.pallas_call(early_kernel, out_shape=tuple(block_shapes * early), in_sp...  1.16 us
  transfers between devices with their start and end apart: 15, of which 7 were waited for; matrix products, arithmetic and copies ran while one was open for 0% of the time, Pallas kernels for 20%

profile of v9, /device:TPU:0, one launch (start us, length us, event | category | flops | bytes accessed | tf_op | source)
XLA Modules:
  0.0 49.8 jit_solution(5297805467750577164)
XLA Ops:
  0.6 3.0 %collective-permute-start.1 = (f32[96,1024]{1,0:T(8,128)}, f32[96,1024]{1,0:T(8,128)S(1)}, u32[]{:S(2)}, u32[]{:S(2)}) collective-permute-start(f32[96,1024]{1,0:T(8,128)} %src_at.1), channel_id=1, source_target_pairs={{0,2},{1,3},{2,0},{3,1},{4,6},{5,7},{6,4},{7,5},{8,10},{9,11},{10,... | collective-permute-start | bytes 1179656 | tf_op jit(solution)/shard_map/ppermute | solution.py:460
  3.7 2.6 %collective-permute-start.5 = (f32[32,1024]{1,0:T(8,128)}, f32[32,1024]{1,0:T(8,128)S(1)}, u32[]{:S(2)}, u32[]{:S(2)}) collective-permute-start(f32[32,1024]{1,0:T(8,128)} %bitcast.9), channel_id=1, source_target_pairs={{0,8},{1,9},{2,10},{3,11},{4,12},{5,13},{6,14},{7,15},{8,0},{9,1},... | collective-permute-start | bytes 393224 | tf_op jit(solution)/shard_map/ppermute | solution.py:460
  6.3 1.6 %collective-permute-start.4 = (f32[32,1024]{1,0:T(8,128)}, f32[32,1024]{1,0:T(8,128)S(1)}, u32[]{:S(2)}, u32[]{:S(2)}) collective-permute-start(f32[32,1024]{1,0:T(8,128)} %bitcast.10), channel_id=1, source_target_pairs={{0,4},{1,5},{2,6},{3,7},{4,0},{5,1},{6,2},{7,3},{8,12},{9,13},{10,... | collective-permute-start | bytes 393224 | tf_op jit(solution)/shard_map/ppermute | solution.py:460
  8.5 1.8 %own.1 = (f32[104,1536]{1,0:T(8,128)S(1)}, f32[8,128]{1,0:T(8,128)S(1)}, f32[128,512]{1,0:T(8,128)S(1)}) custom-call(f32[96,1024]{1,0:T(8,128)} %src_at.1, f32[1,96]{1,0:T(1,128)} %bitcast.14, s32[2,96]{1,0:T(2,128)} %bitcast.13, s32[1,96]{1,0:T(1,128)} %bitcast.15, s32[1,96]{1,0:T(1,128)} %bitcast.16, f32[128,512]{1,0:T(8,128)} %noise_at.1, ...), custom_call_target="tpu_custom_call" | custom-call | tf_op jit(solution)/shard_map/own/pallas_call | solution.py:563
  10.3 2.3 %collective-permute-done.5.a_0_ = f32[32,1024]{1,0:T(8,128)S(1)} collective-permute-done((f32[32,1024]{1,0:T(8,128)}, f32[32,1024]{1,0:T(8,128)S(1)}, u32[]{:S(2)}, u32[]{:S(2)}) %collective-permute-start.5) | collective-permute-done | bytes 131104 | tf_op jit(solution)/shard_map/ppermute | solution.py:460
  12.6 0.7 %collective-permute-start.6 = (f32[32,1024]{1,0:T(8,128)S(1)}, f32[32,1024]{1,0:T(8,128)S(1)}, u32[]{:S(2)}, u32[]{:S(2)}) collective-permute-start(f32[32,1024]{1,0:T(8,128)S(1)} %gate.1.rest_0_), channel_id=1, source_target_pairs={{0,4},{1,5},{2,6},{3,7},{4,0},{5,1},{6,2},{7,3},{8,12},{9,13},{10,... | collective-permute-start | bytes 393224 | tf_op jit(solution)/shard_map/ppermute | solution.py:460
  13.3 0.5 %collective-permute-start.2 = (f32[8,128]{1,0:T(8,128)S(1)}, f32[8,128]{1,0:T(8,128)S(1)}, u32[]{:S(2)}, u32[]{:S(2)}) collective-permute-start(f32[8,128]{1,0:T(8,128)S(1)} %get-tuple-element.46.a_1_), channel_id=1, source_target_pairs={{0,2},{1,3},{2,0},{3,1},{4,6},{5,7},{6,4},{7,5},{8,10},{9,11},{10,... | collective-permute-start | bytes 12296 | tf_op jit(solution)/shard_map/ppermute | solution.py:460
  13.8 0.0 collective-permute-start
  13.8 0.0 collective-permute-done.4.near
  13.8 1.2 %early.1 = (bf16[288,1024]{1,0:T(8,128)(2,1)S(1)}, bf16[288,1024]{1,0:T(8,128)(2,1)S(1)}, bf16[32,512]{1,0:T(8,128)(2,1)S(1)}, bf16[32,512]{1,0:T(8,128)(2,1)S(1...) custom-call(f32[32,1024]{1,0:T(8,128)} %bitcast.11, ...), custom_call_target="tpu_custom_call" | custom-call | tf_op jit(solution)/shard_map/early/pallas_call | solution.py:605
  15.0 1.9 %collective-permute-done.2.facts = f32[8,128]{1,0:T(8,128)S(1)} collective-permute-done((f32[8,128]{1,0:T(8,128)S(1)}, f32[8,128]{1,0:T(8,128)S(1)}, u32[]{:S(2)}, u32[]{:S(2)}) %collective-permute-start.2) | collective-permute-done | bytes 4128 | tf_op jit(solution)/shard_map/ppermute | solution.py:460
  16.9 0.0 collective-permute-done.1.src
  16.9 0.6 %neighbour.1.wait.a_1_ = f32[104,1536]{1,0:T(8,128)S(1)} custom-call(f32[96,1024]{1,0:T(8,128)S(1)} %collective-permute-done.1.src, f32[8,128]{1,0:T(8,128)S(1)} %collective-permute-done.2.facts, f32[128,512]{1,0:T(8,128)S(1)} %get-tuple-element.47.inverse_noise), custom_call_target="tpu_custom_call" | custom-call | tf_op jit(solution)/shard_map/neighbour/pallas_call | solution.py:614
  17.6 0.1 collective-permute-start.3
  17.6 0.0 collective-permute-done.6.rest_1_
  17.7 0.6 %middle.1 = (bf16[288,1024]{1,0:T(8,128)(2,1)S(1)}, bf16[288,1024]{1,0:T(8,128)(2,1)S(1)}, bf16[32,512]{1,0:T(8,128)(2,1)S(1)}, bf16[32,512]{1,0:T(8,128)(2,1)S(...) custom-call(f32[104,1536]{1,0:T(8,128)S(1)} %neighbour.1.wait.a_1_, ...), custom_call_target="tpu_custom_call" | custom-call | flops 16000000000 | tf_op jit(solution)/shard_map/middle/pallas_call | solution.py:626
  18.2 2.9 %scores.2 = (f32[9,32,192]{2,1,0:T(8,128)S(1)}, f32[9,32,192]{2,1,0:T(8,128)S(1)}, f32[9,32,192]{2,1,0:T(8,128)S(1)}, f32[9,32,192]{2,1,0:T(8,128)S(1)}, bf16[38...) custom-call(f32[104,1536]{1,0:T(8,128)S(1)} %get-tuple-element.45.a_0_, ...), custom_call_target="tpu_custom_call" | custom-call | flops 16000000000 | tf_op jit(solution)/shard_map/scores/pallas_call | solution.py:641
  21.1 0.0 collective-permute-done.a_0_
  21.1 0.0 collective-permute-done.3.a_1_
  21.1 3.1 %scores.3 = (f32[9,32,192]{2,1,0:T(8,128)S(1)}, f32[9,32,192]{2,1,0:T(8,128)S(1)}, f32[9,32,192]{2,1,0:T(8,128)S(1)}, f32[9,32,192]{2,1,0:T(8,128)S(1)}, bf16[11...) custom-call(f32[104,1536]{1,0:T(8,128)S(1)} %collective-permute-done.a_0_,, ...), custom_call_target="tpu_custom_call" | custom-call | tf_op jit(solution)/shard_map/scores/pallas_call | solution.py:641
  24.2 0.5 collective-permute-start.7
  24.7 0.8 %collective-permute-done.7.other = f32[8,512]{1,0:T(8,128)S(1)} collective-permute-done((f32[8,512]{1,0:T(8,128)S(1)}, f32[8,512]{1,0:T(8,128)S(1)}, u32[]{:S(2)}, u32[]{:S(2)}) %collective-permute-start.7) | collective-permute-done | bytes 16416 | tf_op jit(solution)/shard_map/ppermute | solution.py:460
  25.5 0.6 %collective-permute-start.8 = (f32[8,512]{1,0:T(8,128)S(1)}, f32[8,512]{1,0:T(8,128)S(1)}, u32[]{:S(2)}, u32[]{:S(2)}) collective-permute-start(f32[8,512]{1,0:T(8,128)S(1)} %chip.1.a_0_), channel_id=1, source_target_pairs={{0,2},{1,3},{2,0},{3,1},{4,6},{5,7},{6,4},{7,5},{8,10},{9,11},{10,... | collective-permute-start | bytes 49160 | tf_op jit(solution)/shard_map/ppermute | solution.py:460
  26.1 3.2 %collective-permute-done.8.a_1_ = f32[8,512]{1,0:T(8,128)S(1)} collective-permute-done((f32[8,512]{1,0:T(8,128)S(1)}, f32[8,512]{1,0:T(8,128)S(1)}, u32[]{:S(2)}, u32[]{:S(2)}) %collective-permute-start.8) | collective-permute-done | bytes 16416 | tf_op jit(solution)/shard_map/ppermute | solution.py:460
  29.3 2.1 %sums.3 = (f32[16,1536]{1,0:T(8,128)S(1)}, f32[16,1536]{1,0:T(8,128)S(1)}, f32[16,1536]{1,0:T(8,128)S(1)}, f32[16,1536]{1,0:T(8,128)S(1)}) custom-call(f32[8,512]{1,0:T(8,128)S(1)} %chip.1.a_0_, f32[8,512]{1,0:T(8,128)S(1)} %collective-permute-done.8.a_1_, f32[8,512]{1,0:T(8,128)S(1)} %get-tuple-element.69.a_2_, f32[9,32,192]{2,1,0:T(8,128)S(1)} %get-tuple-element.70.a_3_, ...), custom_call_target="tpu_custom_call" | custom-call | tf_op jit(solution)/shard_map/sums/pallas_call | solution.py:669
  31.4 1.4 %collective-permute-start.10 = (f32[16,1536]{1,0:T(8,128)S(1)}, f32[16,1536]{1,0:T(8,128)S(1)}, u32[]{:S(2)}, u32[]{:S(2)}) collective-permute-start(f32[16,1536]{1,0:T(8,128)S(1)} %get-tuple-element.81), channel_id=1, source_target_pairs={{0,4},{1,5},{2,6},{3,7},{4,0},{5,1},{6,2},{7,3},{8,12},{9,13},{10,... | collective-permute-start | bytes 294920 | tf_op jit(solution)/shard_map/ppermute | solution.py:460
  32.8 0.7 %collective-permute-start.9 = (f32[16,1536]{1,0:T(8,128)S(1)}, f32[16,1536]{1,0:T(8,128)S(1)}, u32[]{:S(2)}, u32[]{:S(2)}) collective-permute-start(f32[16,1536]{1,0:T(8,128)S(1)} %get-tuple-element.76.a_3_), channel_id=1, source_target_pairs={{0,4},{1,5},{2,6},{3,7},{4,0},{5,1},{6,2},{7,3},{8,12},{9,13},{10,... | collective-permute-start | bytes 294920 | tf_op jit(solution)/shard_map/ppermute | solution.py:460
  33.5 1.4 %collective-permute-start.11 = (f32[16,1536]{1,0:T(8,128)S(1)}, f32[16,1536]{1,0:T(8,128)S(1)}, u32[]{:S(2)}, u32[]{:S(2)}) collective-permute-start(f32[16,1536]{1,0:T(8,128)S(1)} %get-tuple-element.86), channel_id=1, source_target_pairs={{0,4},{1,5},{2,6},{3,7},{4,0},{5,1},{6,2},{7,3},{8,12},{9,13},{10,... | collective-permute-start | bytes 294920 | tf_op jit(solution)/shard_map/ppermute | solution.py:460
  34.8 0.7 %collective-permute-start.12 = (f32[16,1536]{1,0:T(8,128)S(1)}, f32[16,1536]{1,0:T(8,128)S(1)}, u32[]{:S(2)}, u32[]{:S(2)}) collective-permute-start(f32[16,1536]{1,0:T(8,128)S(1)} %get-tuple-element.87), channel_id=1, source_target_pairs={{0,4},{1,5},{2,6},{3,7},{4,0},{5,1},{6,2},{7,3},{8,12},{9,13},{10,... | collective-permute-start | bytes 294920 | tf_op jit(solution)/shard_map/ppermute | solution.py:460
  35.5 1.2 %sums.4 = (f32[16,1536]{1,0:T(8,128)S(1)}, f32[16,1536]{1,0:T(8,128)S(1)}) custom-call(f32[8,512]{1,0:T(8,128)S(1)} %chip.1.a_0_, f32[8,512]{1,0:T(8,128)S(1)} %collective-permute-done.8.a_1_, f32[8,512]{1,0:T(8,128)S(1)} %get-tuple-element.69.a_2_, f32[16,1536]{1,0:T(8,128)S(1)} %get-tuple-element.76.a_3_, f32[9,32,192]{2,1,0:T(8,128)S(1)} %get-tuple-element.77.a_4_, ...), custom_call_target="tpu_custom_call" | custom-call | tf_op jit(solution)/shard_map/sums/pallas_call | solution.py:669
  36.8 0.3 collective-permute-done.10.rest_0_
  37.1 3.5 %collective-permute-start.14 = (f32[16,1536]{1,0:T(8,128)S(1)}, f32[16,1536]{1,0:T(8,128)S(1)}, u32[]{:S(2)}, u32[]{:S(2)}) collective-permute-start(f32[16,1536]{1,0:T(8,128)S(1)} %combined.4.a_4_), channel_id=1, source_target_pairs={{0,8},{1,9},{2,10},{3,11},{4,12},{5,13},{6,14},{7,15},{8,0},{9,1},... | collective-permute-start | bytes 294920 | tf_op jit(solution)/shard_map/ppermute | solution.py:460
  40.5 0.0 collective-permute-done.9.rest_0_
  40.6 2.1 %collective-permute-start.13 = (f32[16,1536]{1,0:T(8,128)S(1)}, f32[16,1536]{1,0:T(8,128)S(1)}, u32[]{:S(2)}, u32[]{:S(2)}) collective-permute-start(f32[16,1536]{1,0:T(8,128)S(1)} %combined.3.a_3_), channel_id=1, source_target_pairs={{0,8},{1,9},{2,10},{3,11},{4,12},{5,13},{6,14},{7,15},{8,0},{9,1},... | collective-permute-start | bytes 294920 | tf_op jit(solution)/shard_map/ppermute | solution.py:460
  42.7 1.7 %sums.5 = (f32[32,1536]{1,0:T(8,128)S(1)}, f32[2,96]{1,0:T(2,128)}) custom-call(f32[8,512]{1,0:T(8,128)S(1)} %chip.1.a_0_, f32[8,512]{1,0:T(8,128)S(1)} %collective-permute-done.8.a_1_, f32[8,512]{1,0:T(8,128)S(1)} %get-tuple-element.69.a_2_, f32[16,1536]{1,0:T(8,128)S(1)} %combined.3.a_3_, f32[16,1536]{1,0:T(8,128)S(1)} %combined.4.a_4_, ...), custom_call_target="tpu_custom_call" | custom-call | tf_op jit(solution)/shard_map/sums/pallas_call | solution.py:669
  44.4 0.0 collective-permute-done.11.rest_0_
  44.4 0.4 collective-permute-done.12.rest_1_
  44.8 0.0 copy-start
  44.9 0.0 collective-permute-done.14.a_2_
  44.9 4.2 %collective-permute-done.13.a_1_ = f32[16,1536]{1,0:T(8,128)S(1)} collective-permute-done((f32[16,1536]{1,0:T(8,128)S(1)}, f32[16,1536]{1,0:T(8,128)S(1)}, u32[]{:S(2)}, u32[]{:S(2)}) %collective-permute-start.13) | collective-permute-done | bytes 98336 | tf_op jit(solution)/shard_map/ppermute | solution.py:460
  49.1 0.0 copy-done
  49.1 0.7 %update.1 = f32[32,1024]{1,0:T(8,128)} custom-call(f32[32,1536]{1,0:T(8,128)S(1)} %combined.5.a_0_, f32[16,1536]{1,0:T(8,128)S(1)} %collective-permute-done.13.a_1_, f32[16,1536]{1,0:T(8,128)S(1)} %collective-permute-done.14.a_2_, f32[1,512]{1,0:T(1,128)S(1)} %bitcast.8), custom_call_target="tpu_custom_call" | custom-call | tf_op jit(solution)/shard_map/update/pallas_call | solution.py:704
  (5 shorter events, 0.1 us)
Async XLA Ops:
  0.6 16.3 %collective-permute-start.1 = (f32[96,1024]{1,0:T(8,128)}, f32[96,1024]{1,0:T(8,128)S(1)}, u32[]{:S(2)}, u32[]{:S(2)}) collective-permute-start(f32[96,1024]{1,0:T(8,128)} %src_at.1), channel_id=1, source_target_pairs={{0,2},{1,3},{2,0},{3,1},{4,6},{5,7},{6,4},{7,5},{8,10},{9,11},{10,... | collective-permute-start | bytes 1179656 | tf_op jit(solution)/shard_map/ppermute | solution.py:460
  3.7 9.0 %collective-permute-start.5 = (f32[32,1024]{1,0:T(8,128)}, f32[32,1024]{1,0:T(8,128)S(1)}, u32[]{:S(2)}, u32[]{:S(2)}) collective-permute-start(f32[32,1024]{1,0:T(8,128)} %bitcast.9), channel_id=1, source_target_pairs={{0,8},{1,9},{2,10},{3,11},{4,12},{5,13},{6,14},{7,15},{8,0},{9,1},... | collective-permute-start | bytes 393224 | tf_op jit(solution)/shard_map/ppermute | solution.py:460
  6.3 7.6 %collective-permute-start.4 = (f32[32,1024]{1,0:T(8,128)}, f32[32,1024]{1,0:T(8,128)S(1)}, u32[]{:S(2)}, u32[]{:S(2)}) collective-permute-start(f32[32,1024]{1,0:T(8,128)} %bitcast.10), channel_id=1, source_target_pairs={{0,4},{1,5},{2,6},{3,7},{4,0},{5,1},{6,2},{7,3},{8,12},{9,13},{10,... | collective-permute-start | bytes 393224 | tf_op jit(solution)/shard_map/ppermute | solution.py:460
  12.6 5.0 %collective-permute-start.6 = (f32[32,1024]{1,0:T(8,128)S(1)}, f32[32,1024]{1,0:T(8,128)S(1)}, u32[]{:S(2)}, u32[]{:S(2)}) collective-permute-start(f32[32,1024]{1,0:T(8,128)S(1)} %gate.1.rest_0_), channel_id=1, source_target_pairs={{0,4},{1,5},{2,6},{3,7},{4,0},{5,1},{6,2},{7,3},{8,12},{9,13},{10,... | collective-permute-start | bytes 393224 | tf_op jit(solution)/shard_map/ppermute | solution.py:460
  13.3 3.6 %collective-permute-start.2 = (f32[8,128]{1,0:T(8,128)S(1)}, f32[8,128]{1,0:T(8,128)S(1)}, u32[]{:S(2)}, u32[]{:S(2)}) collective-permute-start(f32[8,128]{1,0:T(8,128)S(1)} %get-tuple-element.46.a_1_), channel_id=1, source_target_pairs={{0,2},{1,3},{2,0},{3,1},{4,6},{5,7},{6,4},{7,5},{8,10},{9,11},{10,... | collective-permute-start | bytes 12296 | tf_op jit(solution)/shard_map/ppermute | solution.py:460
  13.8 7.3 %collective-permute-start = (f32[104,1536]{1,0:T(8,128)S(1)}, f32[104,1536]{1,0:T(8,128)S(1)}, u32[]{:S(2)}, u32[]{:S(2)}) collective-permute-start(f32[104,1536]{1,0:T(8,128)S(1)} %get-tuple-element.45.a_0_), channel_id=1, source_target_pairs={{0,1},{1,0},{2,3},{3,2},{4,5},{5,4},{6,7},{7,6},{8,9},{9,8},{10,11... | collective-permute-start | bytes 1916936 | tf_op jit(solution)/shard_map/ppermute | solution.py:460
  17.6 3.5 %collective-permute-start.3 = (f32[104,1536]{1,0:T(8,128)S(1)}, f32[104,1536]{1,0:T(8,128)S(1)}, u32[]{:S(2)}, u32[]{:S(2)}) collective-permute-start(f32[104,1536]{1,0:T(8,128)S(1)} %neighbour.1.wait.a_1_), channel_id=1, source_target_pairs={{0,1},{1,0},{2,3},{3,2},{4,5},{5,4},{6,7},{7,6},{8,9},{9,8},{10,11... | collective-permute-start | bytes 1916936 | tf_op jit(solution)/shard_map/ppermute | solution.py:460
  24.2 1.3 %collective-permute-start.7 = (f32[8,512]{1,0:T(8,128)S(1)}, f32[8,512]{1,0:T(8,128)S(1)}, u32[]{:S(2)}, u32[]{:S(2)}) collective-permute-start(f32[8,512]{1,0:T(8,128)S(1)} %get-tuple-element.68.mine), channel_id=1, source_target_pairs={{0,1},{1,0},{2,3},{3,2},{4,5},{5,4},{6,7},{7,6},{8,9},{9,8},{10,11... | collective-permute-start | bytes 49160 | tf_op jit(solution)/shard_map/ppermute | solution.py:460
  25.5 3.8 %collective-permute-start.8 = (f32[8,512]{1,0:T(8,128)S(1)}, f32[8,512]{1,0:T(8,128)S(1)}, u32[]{:S(2)}, u32[]{:S(2)}) collective-permute-start(f32[8,512]{1,0:T(8,128)S(1)} %chip.1.a_0_), channel_id=1, source_target_pairs={{0,2},{1,3},{2,0},{3,1},{4,6},{5,7},{6,4},{7,5},{8,10},{9,11},{10,... | collective-permute-start | bytes 49160 | tf_op jit(solution)/shard_map/ppermute | solution.py:460
  31.4 5.7 %collective-permute-start.10 = (f32[16,1536]{1,0:T(8,128)S(1)}, f32[16,1536]{1,0:T(8,128)S(1)}, u32[]{:S(2)}, u32[]{:S(2)}) collective-permute-start(f32[16,1536]{1,0:T(8,128)S(1)} %get-tuple-element.81), channel_id=1, source_target_pairs={{0,4},{1,5},{2,6},{3,7},{4,0},{5,1},{6,2},{7,3},{8,12},{9,13},{10,... | collective-permute-start | bytes 294920 | tf_op jit(solution)/shard_map/ppermute | solution.py:460
  32.8 7.7 %collective-permute-start.9 = (f32[16,1536]{1,0:T(8,128)S(1)}, f32[16,1536]{1,0:T(8,128)S(1)}, u32[]{:S(2)}, u32[]{:S(2)}) collective-permute-start(f32[16,1536]{1,0:T(8,128)S(1)} %get-tuple-element.76.a_3_), channel_id=1, source_target_pairs={{0,4},{1,5},{2,6},{3,7},{4,0},{5,1},{6,2},{7,3},{8,12},{9,13},{10,... | collective-permute-start | bytes 294920 | tf_op jit(solution)/shard_map/ppermute | solution.py:460
  33.5 10.9 %collective-permute-start.11 = (f32[16,1536]{1,0:T(8,128)S(1)}, f32[16,1536]{1,0:T(8,128)S(1)}, u32[]{:S(2)}, u32[]{:S(2)}) collective-permute-start(f32[16,1536]{1,0:T(8,128)S(1)} %get-tuple-element.86), channel_id=1, source_target_pairs={{0,4},{1,5},{2,6},{3,7},{4,0},{5,1},{6,2},{7,3},{8,12},{9,13},{10,... | collective-permute-start | bytes 294920 | tf_op jit(solution)/shard_map/ppermute | solution.py:460
  34.8 10.0 %collective-permute-start.12 = (f32[16,1536]{1,0:T(8,128)S(1)}, f32[16,1536]{1,0:T(8,128)S(1)}, u32[]{:S(2)}, u32[]{:S(2)}) collective-permute-start(f32[16,1536]{1,0:T(8,128)S(1)} %get-tuple-element.87), channel_id=1, source_target_pairs={{0,4},{1,5},{2,6},{3,7},{4,0},{5,1},{6,2},{7,3},{8,12},{9,13},{10,... | collective-permute-start | bytes 294920 | tf_op jit(solution)/shard_map/ppermute | solution.py:460
  37.1 7.8 %collective-permute-start.14 = (f32[16,1536]{1,0:T(8,128)S(1)}, f32[16,1536]{1,0:T(8,128)S(1)}, u32[]{:S(2)}, u32[]{:S(2)}) collective-permute-start(f32[16,1536]{1,0:T(8,128)S(1)} %combined.4.a_4_), channel_id=1, source_target_pairs={{0,8},{1,9},{2,10},{3,11},{4,12},{5,13},{6,14},{7,15},{8,0},{9,1},... | collective-permute-start | bytes 294920 | tf_op jit(solution)/shard_map/ppermute | solution.py:460
  40.6 8.5 %collective-permute-start.13 = (f32[16,1536]{1,0:T(8,128)S(1)}, f32[16,1536]{1,0:T(8,128)S(1)}, u32[]{:S(2)}, u32[]{:S(2)}) collective-permute-start(f32[16,1536]{1,0:T(8,128)S(1)} %combined.3.a_3_), channel_id=1, source_target_pairs={{0,8},{1,9},{2,10},{3,11},{4,12},{5,13},{6,14},{7,15},{8,0},{9,1},... | collective-permute-start | bytes 294920 | tf_op jit(solution)/shard_map/ppermute | solution.py:460
  44.8 4.2 %copy-start = (f32[512]{0:T(512)S(1)}, f32[512]{0:T(512)}, u32[]{:S(2)}) copy-start(f32[512]{0:T(512)} %param.16) | copy-start | bytes 6148

commit v10 on v9

--- a/solution.py
+++ b/solution.py
@@ -354,22 +354,14 @@
     tops_out[:, 256:] = tops_row[...]
 
 
-def chip_kernel(mine, other, out):
-    pair = (mine[...], other[...])
-    top, sums = joined_sums([x[0:1] for x in pair], [[x[k : k + 1] for k in (1, 2, 3)] for x in pair])
-    out[...] = pair[0]
-    for k, row in enumerate((top, *sums)):
-        out[k : k + 1] = row
-
-
-def sum_kernel(blocks, cuts, last, waits, here, there, tops, *rest):
-    rest = rest[waits:]
+def sum_kernel(blocks, cuts, last, waits, *rest):
+    team, tops, rest = rest[:TEAM], rest[TEAM], rest[TEAM + 1 + waits :]
     e_refs, (y_ref, power_ref, *outs) = rest[: 2 * len(blocks)], rest[2 * len(blocks) :]
     per, lanes = e_refs[0].shape[1:]
     slots = lanes // 2
     width = y_ref.shape[1]
     freq = width // 2
-    pair = (here[...], there[...])
+    pair = [x[...] for x in team]
     top, (mass, *move) = joined_sums(
         [x[0:1] for x in pair], [[x[k : k + 1] for k in (1, 2, 3)] for x in pair]
     )
@@ -576,10 +568,6 @@
         name="own",
     )(*(pltpu.with_memory_space_constraint(x, pltpu.HBM) for x in own_facts), live_count)
     cnb = crossed(own, 1)
-    for n in range(2, blocks, 2):
-        refs[n] = gated(refs[n], facts)
-        refs[n + 1] = crossed(refs[n], TEAM)
-    refs = [refs[n] for n in range(blocks)]
     both = 2 * slots
     bf16 = jnp.bfloat16
     early = 2
@@ -611,6 +599,10 @@
         compiler_params=params(8),
         name="early",
     )(pltpu.with_memory_space_constraint(refs_own, pltpu.HBM), refs[1])
+    for n in range(2, blocks, 2):
+        refs[n] = gated(refs[n], facts, prepared[2])
+        refs[n + 1] = crossed(refs[n], TEAM)
+    refs = [refs[n] for n in range(blocks)]
     ynb_prepared = pl.pallas_call(
         neighbour_kernel,
         out_shape=jax.ShapeDtypeStruct((slots + 8, width + freq), f32),
@@ -658,8 +650,7 @@
     *e_own, y, power, stats, tops = scores(0, (own, ynb_prepared), (), much)
     *e_other, y, power, stats, tops = scores(1, (cnb, cynb), (stats, tops, y, power), None)
 
-    (here,) = call(chip_kernel, (stats, crossed(stats, 1)), [shaped(8, 512)], "chip", 1)
-    there = crossed(here, 2)
+    team = [stats] + [crossed(stats, n) for n in range(1, TEAM)]
 
     def sums(numbers, cuts, last=False, waits=()):
         out_shape = [shaped(b - a, width + freq) for a, b in zip(cuts, cuts[1:])] * len(numbers)
@@ -669,11 +660,11 @@
         return pl.pallas_call(
             lambda *a: sum_kernel(numbers, cuts, last, len(waits), *a),
             out_shape=tuple(out_shape),
-            in_specs=[vmem] * 3 + [anywhere] * len(waits) + [vmem] * (2 + len(weights)),
+            in_specs=[vmem] * (TEAM + 1) + [anywhere] * len(waits) + [vmem] * (2 + len(weights)),
             out_specs=(vmem,) * len(out_shape),
             compiler_params=params(12),
             name="sums",
-        )(here, there, tops, *waits, *weights, y, power)
+        )(*team, tops, *waits, *weights, y, power)
 
     def combined(mine, others, cost=None):
         return pl.pallas_call(
@@ -690,10 +681,10 @@
     far = []
     waits = []
     for n in range(2, blocks, 2):
-        handed = sums((n + 1, 1) if n == 2 else (n + 1,), cut)
+        handed = sums((n + 1,), cut)
+        mine = sums((n,), cut, waits=handed[:1])
         if n == 2:
-            near = handed[2:]
-        mine = sums((n,), cut, waits=handed[:1])
+            near = sums((1,), cut, waits=mine[:1])
         joined = [combined(x, [crossed(y, TEAM)]) for x, y in zip(mine, handed)]
         far.extend(crossed(x, TEAM * n) for x in joined)
         waits.extend(joined)

time: 49.9 us -> 49.5 us (level)
  starting transfers between devices: 19.3 us -> 17 us
  waiting for transfers between devices: 13.3 us -> 14.7 us
    ppermute x15 -> x16, starting transfers between devices: 19.3 us -> 17 us  [crossed(): return lax.ppermute(block, 'dom', [(i, i ^ mask) for i in range(size)])]
    ppermute x15 -> x16, waiting for transfers between devices: 13.3 us -> 14.7 us  [crossed(): return lax.ppermute(block, 'dom', [(i, i ^ mask) for i in range(size)])]
    pallas_call x3 -> x4, Pallas kernels: 5 us -> 5.47 us  [sums(): pl.pallas_call(lambda *a: sum_kernel(numbers, cuts, last, len(waits), *a)...]
  transfers between devices with their start and end apart: 15 -> 16, of which waited for: 7 -> 9; matrix products, arithmetic and copies ran while one was open for 0% -> 0% of each run, Pallas kernels for 20% -> 23%
where the time goes in v10:
time: 49.5 us; the launch traced here: 49.4 us
  starting transfers between devices  17 us (34%)
  Pallas kernels  16.3 us (33%)
  waiting for transfers between devices  14.7 us (30%)
  between operations  1.37 us (3%)
    ppermute x16, starting transfers between devices, crossed(): return lax.ppermute(block, 'dom', [(i, i ^ mask) for i in range(size)])  17 us
    ppermute x16, waiting for transfers between devices, crossed(): return lax.ppermute(block, 'dom', [(i, i ^ mask) for i in range(size)])  14.7 us
    pallas_call x2, Pallas kernels, scores(): pl.pallas_call(lambda *a: score_kernel(half, blocks, *a), out_shape=(*[sc...  5.92 us
    pallas_call x4, Pallas kernels, sums(): pl.pallas_call(lambda *a: sum_kernel(numbers, cuts, last, len(waits), *a)...  5.47 us
    pallas_call x1, Pallas kernels, on_device(): pl.pallas_call(own_kernel, out_shape=(jax.ShapeDtypeStruct((slots + 8, wi...  1.83 us
    pallas_call x1, Pallas kernels, on_device(): pl.pallas_call(early_kernel, out_shape=tuple(block_shapes * early), in_sp...  1.16 us
  transfers between devices with their start and end apart: 16, of which 9 were waited for; matrix products, arithmetic and copies ran while one was open for 0% of the time, Pallas kernels for 23%

profile of v10, /device:TPU:0, one launch (start us, length us, event | category | flops | bytes accessed | tf_op | source)
XLA Modules:
  0.0 49.4 jit_solution(12723407505453545322)
XLA Ops:
  0.6 3.0 %collective-permute-start.1 = (f32[96,1024]{1,0:T(8,128)}, f32[96,1024]{1,0:T(8,128)S(1)}, u32[]{:S(2)}, u32[]{:S(2)}) collective-permute-start(f32[96,1024]{1,0:T(8,128)} %src_at.1), channel_id=1, source_target_pairs={{0,2},{1,3},{2,0},{3,1},{4,6},{5,7},{6,4},{7,5},{8,10},{9,11},{10,... | collective-permute-start | bytes 1179656 | tf_op jit(solution)/shard_map/ppermute | solution.py:452
  3.7 1.6 %collective-permute-start.4 = (f32[32,1024]{1,0:T(8,128)}, f32[32,1024]{1,0:T(8,128)S(1)}, u32[]{:S(2)}, u32[]{:S(2)}) collective-permute-start(f32[32,1024]{1,0:T(8,128)} %bitcast.9), channel_id=1, source_target_pairs={{0,4},{1,5},{2,6},{3,7},{4,0},{5,1},{6,2},{7,3},{8,12},{9,13},{10,... | collective-permute-start | bytes 393224 | tf_op jit(solution)/shard_map/ppermute | solution.py:452
  5.2 2.6 %collective-permute-start.5 = (f32[32,1024]{1,0:T(8,128)}, f32[32,1024]{1,0:T(8,128)S(1)}, u32[]{:S(2)}, u32[]{:S(2)}) collective-permute-start(f32[32,1024]{1,0:T(8,128)} %bitcast.10), channel_id=1, source_target_pairs={{0,8},{1,9},{2,10},{3,11},{4,12},{5,13},{6,14},{7,15},{8,0},{9,1},... | collective-permute-start | bytes 393224 | tf_op jit(solution)/shard_map/ppermute | solution.py:452
  8.5 1.8 %own.1 = (f32[104,1536]{1,0:T(8,128)S(1)}, f32[8,128]{1,0:T(8,128)S(1)}, f32[128,512]{1,0:T(8,128)S(1)}) custom-call(f32[96,1024]{1,0:T(8,128)} %src_at.1, f32[1,96]{1,0:T(1,128)} %bitcast.14, s32[2,96]{1,0:T(2,128)} %bitcast.13, s32[1,96]{1,0:T(1,128)} %bitcast.15, s32[1,96]{1,0:T(1,128)} %bitcast.16, f32[128,512]{1,0:T(8,128)} %noise_at.1, ...), custom_call_target="tpu_custom_call" | custom-call | tf_op jit(solution)/shard_map/own/pallas_call | solution.py:555
  10.3 0.2 collective-permute-done.4.near
  10.5 1.2 %early.1 = (bf16[288,1024]{1,0:T(8,128)(2,1)S(1)}, bf16[288,1024]{1,0:T(8,128)(2,1)S(1)}, bf16[32,512]{1,0:T(8,128)(2,1)S(1)}, bf16[32,512]{1,0:T(8,128)(2,1)S(1...) custom-call(f32[32,1024]{1,0:T(8,128)} %bitcast.11, ...), custom_call_target="tpu_custom_call" | custom-call | tf_op jit(solution)/shard_map/early/pallas_call | solution.py:593
  11.7 2.3 %collective-permute-done.5.a_0_ = f32[32,1024]{1,0:T(8,128)S(1)} collective-permute-done((f32[32,1024]{1,0:T(8,128)}, f32[32,1024]{1,0:T(8,128)S(1)}, u32[]{:S(2)}, u32[]{:S(2)}) %collective-permute-start.5) | collective-permute-done | bytes 131104 | tf_op jit(solution)/shard_map/ppermute | solution.py:452
  14.0 0.2 collective-permute-start.6
  14.2 0.5 %collective-permute-start.2 = (f32[8,128]{1,0:T(8,128)S(1)}, f32[8,128]{1,0:T(8,128)S(1)}, u32[]{:S(2)}, u32[]{:S(2)}) collective-permute-start(f32[8,128]{1,0:T(8,128)S(1)} %get-tuple-element.46.a_1_), channel_id=1, source_target_pairs={{0,2},{1,3},{2,0},{3,1},{4,6},{5,7},{6,4},{7,5},{8,10},{9,11},{10,... | collective-permute-start | bytes 12296 | tf_op jit(solution)/shard_map/ppermute | solution.py:452
  14.7 0.0 collective-permute-start
  14.7 3.1 %collective-permute-done.2.facts = f32[8,128]{1,0:T(8,128)S(1)} collective-permute-done((f32[8,128]{1,0:T(8,128)S(1)}, f32[8,128]{1,0:T(8,128)S(1)}, u32[]{:S(2)}, u32[]{:S(2)}) %collective-permute-start.2) | collective-permute-done | bytes 4128 | tf_op jit(solution)/shard_map/ppermute | solution.py:452
  17.8 0.0 collective-permute-done.1.src
  17.8 0.6 %neighbour.1.wait.a_1_ = f32[104,1536]{1,0:T(8,128)S(1)} custom-call(f32[96,1024]{1,0:T(8,128)S(1)} %collective-permute-done.1.src, f32[8,128]{1,0:T(8,128)S(1)} %collective-permute-done.2.facts, f32[128,512]{1,0:T(8,128)S(1)} %get-tuple-element.47.inverse_noise), custom_call_target="tpu_custom_call" | custom-call | tf_op jit(solution)/shard_map/neighbour/pallas_call | solution.py:606
  18.5 0.1 collective-permute-start.3
  18.6 0.4 collective-permute-done.6.rest_1_
  19.0 0.6 %middle.1 = (bf16[288,1024]{1,0:T(8,128)(2,1)S(1)}, bf16[288,1024]{1,0:T(8,128)(2,1)S(1)}, bf16[32,512]{1,0:T(8,128)(2,1)S(1)}, bf16[32,512]{1,0:T(8,128)(2,1)S(...) custom-call(f32[104,1536]{1,0:T(8,128)S(1)} %neighbour.1.wait.a_1_, ...), custom_call_target="tpu_custom_call" | custom-call | flops 16000000000 | tf_op jit(solution)/shard_map/middle/pallas_call | solution.py:618
  19.5 2.9 %scores.2 = (f32[9,32,192]{2,1,0:T(8,128)S(1)}, f32[9,32,192]{2,1,0:T(8,128)S(1)}, f32[9,32,192]{2,1,0:T(8,128)S(1)}, f32[9,32,192]{2,1,0:T(8,128)S(1)}, bf16[38...) custom-call(f32[104,1536]{1,0:T(8,128)S(1)} %get-tuple-element.45.a_0_, ...), custom_call_target="tpu_custom_call" | custom-call | flops 16000000000 | tf_op jit(solution)/shard_map/scores/pallas_call | solution.py:633
  22.4 0.0 collective-permute-done.a_0_
  22.4 0.0 collective-permute-done.3.a_1_
  22.4 3.1 %scores.3 = (f32[9,32,192]{2,1,0:T(8,128)S(1)}, f32[9,32,192]{2,1,0:T(8,128)S(1)}, f32[9,32,192]{2,1,0:T(8,128)S(1)}, f32[9,32,192]{2,1,0:T(8,128)S(1)}, bf16[11...) custom-call(f32[104,1536]{1,0:T(8,128)S(1)} %collective-permute-done.a_0_,, ...), custom_call_target="tpu_custom_call" | custom-call | tf_op jit(solution)/shard_map/scores/pallas_call | solution.py:633
  25.5 0.2 collective-permute-start.9
  25.7 1.5 %collective-permute-start.8 = (f32[8,512]{1,0:T(8,128)S(1)}, f32[8,512]{1,0:T(8,128)S(1)}, u32[]{:S(2)}, u32[]{:S(2)}) collective-permute-start(f32[8,512]{1,0:T(8,128)S(1)} %get-tuple-element.68.a_0_), channel_id=1, source_target_pairs={{0,2},{1,3},{2,0},{3,1},{4,6},{5,7},{6,4},{7,5},{8,10},{9,11},{10,... | collective-permute-start | bytes 49160 | tf_op jit(solution)/shard_map/ppermute | solution.py:452
  27.2 0.2 collective-permute-start.7
  27.4 1.3 %collective-permute-done.9.a_3_ = f32[8,512]{1,0:T(8,128)S(1)} collective-permute-done((f32[8,512]{1,0:T(8,128)S(1)}, f32[8,512]{1,0:T(8,128)S(1)}, u32[]{:S(2)}, u32[]{:S(2)}) %collective-permute-start.9) | collective-permute-done | bytes 16416 | tf_op jit(solution)/shard_map/ppermute | solution.py:452
  28.7 0.8 %collective-permute-done.8.a_2_ = f32[8,512]{1,0:T(8,128)S(1)} collective-permute-done((f32[8,512]{1,0:T(8,128)S(1)}, f32[8,512]{1,0:T(8,128)S(1)}, u32[]{:S(2)}, u32[]{:S(2)}) %collective-permute-start.8) | collective-permute-done | bytes 16416 | tf_op jit(solution)/shard_map/ppermute | solution.py:452
  29.4 0.0 collective-permute-done.7.a_1_
  29.4 1.2 %sums.4 = (f32[16,1536]{1,0:T(8,128)S(1)}, f32[16,1536]{1,0:T(8,128)S(1)}) custom-call(f32[8,512]{1,0:T(8,128)S(1)} %get-tuple-element.68.a_0_, f32[8,512]{1,0:T(8,128)S(1)} %collective-permute-done.7.a_1_, f32[8,512]{1,0:T(8,128)S(1)} %collective-permute-done.8.a_2_, f32[8,512]{1,0:T(8,128)S(1)} %collective-permute-done.9.a_3_, ...), custom_call_target="tpu_custom_call" | custom-call | tf_op jit(solution)/shard_map/sums/pallas_call | solution.py:660
  30.7 1.8 %collective-permute-start.11 = (f32[16,1536]{1,0:T(8,128)S(1)}, f32[16,1536]{1,0:T(8,128)S(1)}, u32[]{:S(2)}, u32[]{:S(2)}) collective-permute-start(f32[16,1536]{1,0:T(8,128)S(1)} %get-tuple-element.79), channel_id=1, source_target_pairs={{0,4},{1,5},{2,6},{3,7},{4,0},{5,1},{6,2},{7,3},{8,12},{9,13},{10,... | collective-permute-start | bytes 294920 | tf_op jit(solution)/shard_map/ppermute | solution.py:452
  32.5 0.2 collective-permute-start.10
  32.7 1.2 %sums.5 = (f32[16,1536]{1,0:T(8,128)S(1)}, f32[16,1536]{1,0:T(8,128)S(1)}) custom-call(f32[8,512]{1,0:T(8,128)S(1)} %get-tuple-element.68.a_0_, f32[8,512]{1,0:T(8,128)S(1)} %collective-permute-done.7.a_1_, f32[8,512]{1,0:T(8,128)S(1)} %collective-permute-done.8.a_2_, f32[8,512]{1,0:T(8,128)S(1)} %collective-permute-done.9.a_3_, ...), custom_call_target="tpu_custom_call" | custom-call | tf_op jit(solution)/shard_map/sums/pallas_call | solution.py:660
  33.9 1.3 %sums.7 = (f32[16,1536]{1,0:T(8,128)S(1)}, f32[16,1536]{1,0:T(8,128)S(1)}) custom-call(f32[8,512]{1,0:T(8,128)S(1)} %get-tuple-element.68.a_0_, f32[8,512]{1,0:T(8,128)S(1)} %collective-permute-done.7.a_1_, f32[8,512]{1,0:T(8,128)S(1)} %collective-permute-done.8.a_2_, f32[8,512]{1,0:T(8,128)S(1)} %collective-permute-done.9.a_3_, ...), custom_call_target="tpu_custom_call" | custom-call | tf_op jit(solution)/shard_map/sums/pallas_call | solution.py:660
  35.2 1.8 %collective-permute-start.12 = (f32[16,1536]{1,0:T(8,128)S(1)}, f32[16,1536]{1,0:T(8,128)S(1)}, u32[]{:S(2)}, u32[]{:S(2)}) collective-permute-start(f32[16,1536]{1,0:T(8,128)S(1)} %get-tuple-element.86), channel_id=1, source_target_pairs={{0,4},{1,5},{2,6},{3,7},{4,0},{5,1},{6,2},{7,3},{8,12},{9,13},{10,... | collective-permute-start | bytes 294920 | tf_op jit(solution)/shard_map/ppermute | solution.py:452
  37.0 0.2 collective-permute-start.13
  37.2 0.0 collective-permute-done.11.rest_0_
  37.3 2.7 %collective-permute-start.15 = (f32[16,1536]{1,0:T(8,128)S(1)}, f32[16,1536]{1,0:T(8,128)S(1)}, u32[]{:S(2)}, u32[]{:S(2)}) collective-permute-start(f32[16,1536]{1,0:T(8,128)S(1)} %combined.4.a_6_), channel_id=1, source_target_pairs={{0,8},{1,9},{2,10},{3,11},{4,12},{5,13},{6,14},{7,15},{8,0},{9,1},... | collective-permute-start | bytes 294920 | tf_op jit(solution)/shard_map/ppermute | solution.py:452
  40.0 0.0 collective-permute-done.10.rest_0_
  40.0 0.3 collective-permute-start.14
  40.3 1.7 %sums.6 = (f32[32,1536]{1,0:T(8,128)S(1)}, f32[2,96]{1,0:T(2,128)}) custom-call(f32[8,512]{1,0:T(8,128)S(1)} %get-tuple-element.68.a_0_, f32[8,512]{1,0:T(8,128)S(1)} %collective-permute-done.7.a_1_, f32[8,512]{1,0:T(8,128)S(1)} %collective-permute-done.8.a_2_, f32[8,512]{1,0:T(8,128)S(1)} %collective-permute-done.9.a_3_, ...), custom_call_target="tpu_custom_call" | custom-call | tf_op jit(solution)/shard_map/sums/pallas_call | solution.py:660
  42.1 0.0 collective-permute-done.12.rest_0_
  42.1 1.5 %collective-permute-done.13.rest_1_ = f32[16,1536]{1,0:T(8,128)S(1)} collective-permute-done((f32[16,1536]{1,0:T(8,128)S(1)}, f32[16,1536]{1,0:T(8,128)S(1)}, u32[]{:S(2)}, u32[]{:S(2)}) %collective-permute-start.13) | collective-permute-done | bytes 98336 | tf_op jit(solution)/shard_map/ppermute | solution.py:452
  43.5 0.0 copy-start
  43.6 4.1 %collective-permute-done.15.a_2_ = f32[16,1536]{1,0:T(8,128)S(1)} collective-permute-done((f32[16,1536]{1,0:T(8,128)S(1)}, f32[16,1536]{1,0:T(8,128)S(1)}, u32[]{:S(2)}, u32[]{:S(2)}) %collective-permute-start.15) | collective-permute-done | bytes 98336 | tf_op jit(solution)/shard_map/ppermute | solution.py:452
  47.6 1.1 %collective-permute-done.14.a_1_ = f32[16,1536]{1,0:T(8,128)S(1)} collective-permute-done((f32[16,1536]{1,0:T(8,128)S(1)}, f32[16,1536]{1,0:T(8,128)S(1)}, u32[]{:S(2)}, u32[]{:S(2)}) %collective-permute-start.14) | collective-permute-done | bytes 98336 | tf_op jit(solution)/shard_map/ppermute | solution.py:452
  48.7 0.0 copy-done
  48.7 0.7 %update.1 = f32[32,1024]{1,0:T(8,128)} custom-call(f32[32,1536]{1,0:T(8,128)S(1)} %combined.5.a_0_, f32[16,1536]{1,0:T(8,128)S(1)} %collective-permute-done.14.a_1_, f32[16,1536]{1,0:T(8,128)S(1)} %collective-permute-done.15.a_2_, f32[1,512]{1,0:T(1,128)S(1)} %bitcast.8), custom_call_target="tpu_custom_call" | custom-call | tf_op jit(solution)/shard_map/update/pallas_call | solution.py:695
  (4 shorter events, 0.0 us)
Async XLA Ops:
  0.6 17.2 %collective-permute-start.1 = (f32[96,1024]{1,0:T(8,128)}, f32[96,1024]{1,0:T(8,128)S(1)}, u32[]{:S(2)}, u32[]{:S(2)}) collective-permute-start(f32[96,1024]{1,0:T(8,128)} %src_at.1), channel_id=1, source_target_pairs={{0,2},{1,3},{2,0},{3,1},{4,6},{5,7},{6,4},{7,5},{8,10},{9,11},{10,... | collective-permute-start | bytes 1179656 | tf_op jit(solution)/shard_map/ppermute | solution.py:452
  3.7 6.8 %collective-permute-start.4 = (f32[32,1024]{1,0:T(8,128)}, f32[32,1024]{1,0:T(8,128)S(1)}, u32[]{:S(2)}, u32[]{:S(2)}) collective-permute-start(f32[32,1024]{1,0:T(8,128)} %bitcast.9), channel_id=1, source_target_pairs={{0,4},{1,5},{2,6},{3,7},{4,0},{5,1},{6,2},{7,3},{8,12},{9,13},{10,... | collective-permute-start | bytes 393224 | tf_op jit(solution)/shard_map/ppermute | solution.py:452
  5.2 8.8 %collective-permute-start.5 = (f32[32,1024]{1,0:T(8,128)}, f32[32,1024]{1,0:T(8,128)S(1)}, u32[]{:S(2)}, u32[]{:S(2)}) collective-permute-start(f32[32,1024]{1,0:T(8,128)} %bitcast.10), channel_id=1, source_target_pairs={{0,8},{1,9},{2,10},{3,11},{4,12},{5,13},{6,14},{7,15},{8,0},{9,1},... | collective-permute-start | bytes 393224 | tf_op jit(solution)/shard_map/ppermute | solution.py:452
  14.0 5.0 %collective-permute-start.6 = (f32[32,1024]{1,0:T(8,128)S(1)}, f32[32,1024]{1,0:T(8,128)S(1)}, u32[]{:S(2)}, u32[]{:S(2)}) collective-permute-start(f32[32,1024]{1,0:T(8,128)S(1)} %gate.1.rest_0_), channel_id=1, source_target_pairs={{0,4},{1,5},{2,6},{3,7},{4,0},{5,1},{6,2},{7,3},{8,12},{9,13},{10,... | collective-permute-start | bytes 393224 | tf_op jit(solution)/shard_map/ppermute | solution.py:452
  14.2 3.6 %collective-permute-start.2 = (f32[8,128]{1,0:T(8,128)S(1)}, f32[8,128]{1,0:T(8,128)S(1)}, u32[]{:S(2)}, u32[]{:S(2)}) collective-permute-start(f32[8,128]{1,0:T(8,128)S(1)} %get-tuple-element.46.a_1_), channel_id=1, source_target_pairs={{0,2},{1,3},{2,0},{3,1},{4,6},{5,7},{6,4},{7,5},{8,10},{9,11},{10,... | collective-permute-start | bytes 12296 | tf_op jit(solution)/shard_map/ppermute | solution.py:452
  14.7 7.7 %collective-permute-start = (f32[104,1536]{1,0:T(8,128)S(1)}, f32[104,1536]{1,0:T(8,128)S(1)}, u32[]{:S(2)}, u32[]{:S(2)}) collective-permute-start(f32[104,1536]{1,0:T(8,128)S(1)} %get-tuple-element.45.a_0_), channel_id=1, source_target_pairs={{0,1},{1,0},{2,3},{3,2},{4,5},{5,4},{6,7},{7,6},{8,9},{9,8},{10,11... | collective-permute-start | bytes 1916936 | tf_op jit(solution)/shard_map/ppermute | solution.py:452
  18.5 3.9 %collective-permute-start.3 = (f32[104,1536]{1,0:T(8,128)S(1)}, f32[104,1536]{1,0:T(8,128)S(1)}, u32[]{:S(2)}, u32[]{:S(2)}) collective-permute-start(f32[104,1536]{1,0:T(8,128)S(1)} %neighbour.1.wait.a_1_), channel_id=1, source_target_pairs={{0,1},{1,0},{2,3},{3,2},{4,5},{5,4},{6,7},{7,6},{8,9},{9,8},{10,11... | collective-permute-start | bytes 1916936 | tf_op jit(solution)/shard_map/ppermute | solution.py:452
  25.5 3.2 %collective-permute-start.9 = (f32[8,512]{1,0:T(8,128)S(1)}, f32[8,512]{1,0:T(8,128)S(1)}, u32[]{:S(2)}, u32[]{:S(2)}) collective-permute-start(f32[8,512]{1,0:T(8,128)S(1)} %get-tuple-element.68.a_0_), channel_id=1, source_target_pairs={{0,3},{1,2},{2,1},{3,0},{4,7},{5,6},{6,5},{7,4},{8,11},{9,10},{10,... | collective-permute-start | bytes 49160 | tf_op jit(solution)/shard_map/ppermute | solution.py:452
  25.7 3.7 %collective-permute-start.8 = (f32[8,512]{1,0:T(8,128)S(1)}, f32[8,512]{1,0:T(8,128)S(1)}, u32[]{:S(2)}, u32[]{:S(2)}) collective-permute-start(f32[8,512]{1,0:T(8,128)S(1)} %get-tuple-element.68.a_0_), channel_id=1, source_target_pairs={{0,2},{1,3},{2,0},{3,1},{4,6},{5,7},{6,4},{7,5},{8,10},{9,11},{10,... | collective-permute-start | bytes 49160 | tf_op jit(solution)/shard_map/ppermute | solution.py:452
  27.2 2.2 %collective-permute-start.7 = (f32[8,512]{1,0:T(8,128)S(1)}, f32[8,512]{1,0:T(8,128)S(1)}, u32[]{:S(2)}, u32[]{:S(2)}) collective-permute-start(f32[8,512]{1,0:T(8,128)S(1)} %get-tuple-element.68.a_0_), channel_id=1, source_target_pairs={{0,1},{1,0},{2,3},{3,2},{4,5},{5,4},{6,7},{7,6},{8,9},{9,8},{10,11... | collective-permute-start | bytes 49160 | tf_op jit(solution)/shard_map/ppermute | solution.py:452
  30.7 6.6 %collective-permute-start.11 = (f32[16,1536]{1,0:T(8,128)S(1)}, f32[16,1536]{1,0:T(8,128)S(1)}, u32[]{:S(2)}, u32[]{:S(2)}) collective-permute-start(f32[16,1536]{1,0:T(8,128)S(1)} %get-tuple-element.79), channel_id=1, source_target_pairs={{0,4},{1,5},{2,6},{3,7},{4,0},{5,1},{6,2},{7,3},{8,12},{9,13},{10,... | collective-permute-start | bytes 294920 | tf_op jit(solution)/shard_map/ppermute | solution.py:452
  32.5 7.5 %collective-permute-start.10 = (f32[16,1536]{1,0:T(8,128)S(1)}, f32[16,1536]{1,0:T(8,128)S(1)}, u32[]{:S(2)}, u32[]{:S(2)}) collective-permute-start(f32[16,1536]{1,0:T(8,128)S(1)} %get-tuple-element.74.a_5_), channel_id=1, source_target_pairs={{0,4},{1,5},{2,6},{3,7},{4,0},{5,1},{6,2},{7,3},{8,12},{9,13},{10,... | collective-permute-start | bytes 294920 | tf_op jit(solution)/shard_map/ppermute | solution.py:452
  35.2 6.9 %collective-permute-start.12 = (f32[16,1536]{1,0:T(8,128)S(1)}, f32[16,1536]{1,0:T(8,128)S(1)}, u32[]{:S(2)}, u32[]{:S(2)}) collective-permute-start(f32[16,1536]{1,0:T(8,128)S(1)} %get-tuple-element.86), channel_id=1, source_target_pairs={{0,4},{1,5},{2,6},{3,7},{4,0},{5,1},{6,2},{7,3},{8,12},{9,13},{10,... | collective-permute-start | bytes 294920 | tf_op jit(solution)/shard_map/ppermute | solution.py:452
  37.0 6.5 %collective-permute-start.13 = (f32[16,1536]{1,0:T(8,128)S(1)}, f32[16,1536]{1,0:T(8,128)S(1)}, u32[]{:S(2)}, u32[]{:S(2)}) collective-permute-start(f32[16,1536]{1,0:T(8,128)S(1)} %get-tuple-element.87), channel_id=1, source_target_pairs={{0,4},{1,5},{2,6},{3,7},{4,0},{5,1},{6,2},{7,3},{8,12},{9,13},{10,... | collective-permute-start | bytes 294920 | tf_op jit(solution)/shard_map/ppermute | solution.py:452
  37.3 10.4 %collective-permute-start.15 = (f32[16,1536]{1,0:T(8,128)S(1)}, f32[16,1536]{1,0:T(8,128)S(1)}, u32[]{:S(2)}, u32[]{:S(2)}) collective-permute-start(f32[16,1536]{1,0:T(8,128)S(1)} %combined.4.a_6_), channel_id=1, source_target_pairs={{0,8},{1,9},{2,10},{3,11},{4,12},{5,13},{6,14},{7,15},{8,0},{9,1},... | collective-permute-start | bytes 294920 | tf_op jit(solution)/shard_map/ppermute | solution.py:452
  40.0 8.7 %collective-permute-start.14 = (f32[16,1536]{1,0:T(8,128)S(1)}, f32[16,1536]{1,0:T(8,128)S(1)}, u32[]{:S(2)}, u32[]{:S(2)}) collective-permute-start(f32[16,1536]{1,0:T(8,128)S(1)} %combined.3.a_5_), channel_id=1, source_target_pairs={{0,8},{1,9},{2,10},{3,11},{4,12},{5,13},{6,14},{7,15},{8,0},{9,1},... | collective-permute-start | bytes 294920 | tf_op jit(solution)/shard_map/ppermute | solution.py:452
  43.5 5.2 %copy-start = (f32[512]{0:T(512)S(1)}, f32[512]{0:T(512)}, u32[]{:S(2)}) copy-start(f32[512]{0:T(512)} %param.16) | copy-start | bytes 6148

commit v11 on v8

--- a/solution.py
+++ b/solution.py
@@ -78,27 +78,21 @@
     return high, (x - high.astype(jnp.float32)).astype(jnp.bfloat16)
 
 
-def main_rows(half, part):
-    return 256 * part + 128 * half
-
-
-def left_rows(half, part, left):
-    return 768 + 2 * left * part + left * half
-
-
-def deep_lanes(a, b):
-    rows, lanes = a.shape
-    left = lanes - 128
-    high, low = halves(jnp.concatenate([a[:, :128], b[:, :128]], axis=1))
-    empty = jnp.zeros((rows, 128 - left), jnp.float32)
-    tail = jnp.concatenate([a[:, 128:], empty], axis=1) + pltpu.roll(
-        jnp.concatenate([b[:, 128:], empty], axis=1), left, 1
-    )
+MAIN = 256
+
+
+def deep_at(part, row):
+    return MAIN * part + row if row < MAIN else 3 * MAIN + 32 * part + row - MAIN
+
+
+def deep_lanes(x):
+    rows, lanes = x.shape
+    left = lanes - MAIN
+    high, low = halves(x[:, :MAIN])
+    tail = jnp.concatenate([x[:, MAIN:], jnp.zeros((rows, 128 - left), jnp.float32)], axis=1)
     tail_high = tail.astype(jnp.bfloat16).astype(jnp.float32)
     tail_low = tail - tail_high
-    mixed = (
-        tail_high + pltpu.roll(tail_high, 2 * left, 1) + pltpu.roll(tail_low, 4 * left, 1)
-    )
+    mixed = tail_high + pltpu.roll(tail_high, left, 1) + pltpu.roll(tail_low, 2 * left, 1)
     return jnp.concatenate([high, high, low, mixed.astype(jnp.bfloat16)], axis=1)
 
 
@@ -195,54 +189,74 @@
     prepared_rows(src, facts[...], inverse_noise[...], out)
 
 
-def even_core():
-    return lax.axis_index("dom") % 2 == 0
-
-
-def place_half(half, mine, other, y_out, power_out):
+def team_order(own, cnb, ynb, cynb):
+    for even in (True, False):
+        for first in (True, False):
+            heavy, light = ((own, ynb), (cnb, cynb)) if even else ((cnb, cynb), (own, ynb))
+            if not first:
+                heavy, light = heavy[::-1], light[::-1]
+            yield even, first, heavy, light
+
+
+def place_rows(even, first, parts, y_out, power_out):
     width = y_out.shape[1]
-    slots = mine.shape[0] - 8
-    left = slots + slots // 2 - 128
-
-    def place(src, rows, to):
+    slots = parts[0].shape[0] - 8
+    half = slots // 2
+    cut = MAIN - 2 * slots - half
+
+    def place(src, start, stop, to):
         for cols, out in ((slice(0, width), y_out), (slice(width, None), power_out)):
-            high, low = halves(src[rows, cols])
-            for part, value in enumerate((high, low, high)):
-                if to < 128:
-                    at = main_rows(half, part) + to
-                else:
-                    at = left_rows(half, part, left) + to - 128
-                out[at : at + value.shape[0]] = value
-
-    def place_both(heavy, light):
-        place(heavy, slice(0, slots), 0)
-        place(light, slice(0, 128 - slots), slots)
-        place(light, slice(128 - slots, slots // 2), 128)
-
-    even = even_core()
-
-    @pl.when(even)
-    def _():
-        place_both(mine, other)
-
-    @pl.when(jnp.logical_not(even))
-    def _():
-        place_both(other, mine)
-
-
-def placed(half, part, left, out):
-    main, tail = main_rows(half, part), left_rows(half, part, left)
-    return jnp.concatenate([out[main : main + 128], out[tail : tail + left]], axis=0)
-
-
-def half_facts(mine, other):
-    slots = mine.shape[0] - 8
-    even = even_core()
-    x, y = mine[slots:, :128], other[slots:, :128]
-    heavy = jnp.where(even, x, y)
-    light = pltpu.roll(jnp.where(even, y, x), 96, 1)
-    lane = lax.broadcasted_iota(jnp.int32, (8, 128), 1)
-    return jnp.concatenate([jnp.where(lane < 96, heavy, light), light], axis=1)
+            pair = halves(src[start:stop, cols])
+            for part in range(3):
+                row = deep_at(part, to)
+                out[row : row + stop - start] = pair[part % 2]
+
+    for is_even, is_first, heavy, light in team_order(*parts):
+
+        @pl.when(jnp.logical_and(even == is_even, first == is_first))
+        def _(heavy=heavy, light=light):
+            place(heavy[0], 0, slots, 0)
+            place(heavy[1], 0, slots, slots)
+            place(light[0], 0, half, 2 * slots)
+            place(light[1], 0, cut, 2 * slots + half)
+            place(light[1], cut, half, MAIN)
+
+
+def placed(out, part, rows):
+    main, left = deep_at(part, 0), deep_at(part, MAIN)
+    return jnp.concatenate([out[main : main + MAIN], out[left : left + rows - MAIN]], axis=0)
+
+
+def lane_index():
+    return lax.broadcasted_iota(jnp.int32, (8, 128), 1)
+
+
+def row_facts(even, first, parts):
+    lane = lane_index()
+    own, cnb, ynb, cynb = (x[x.shape[0] - 8 :, :128] for x in parts)
+    heavy = (jnp.where(even, own, cnb), jnp.where(even, ynb, cynb))
+    light = (jnp.where(even, cnb, own), jnp.where(even, cynb, ynb))
+    a0, b0 = (jnp.where(first, x[0], x[1]) for x in (heavy, light))
+    a1, b1 = (jnp.where(first, x[1], x[0]) for x in (heavy, light))
+    a1 = pltpu.roll(a1, 96, 1)
+    b1 = pltpu.roll(b1, 112, 1)
+    middle = jnp.where(lane < 64, a1, jnp.where(lane < 112, pltpu.roll(b0, 64, 1), b1))
+    return jnp.concatenate([jnp.where(lane < 96, a0, a1), middle, b1], axis=1)
+
+
+def own_lanes(even, first, x):
+    lane = lane_index()
+    a, b, c = x[:, :128], x[:, 128:256], x[:, 256:]
+    heavy_far = jnp.where(lane < 32, pltpu.roll(a, 32, 1), pltpu.roll(b, 32, 1))
+    light_far = jnp.where(lane < 16, pltpu.roll(b, 16, 1), pltpu.roll(c, 16, 1))
+    light = jnp.where(first, pltpu.roll(b, 64, 1), light_far)
+    heavy = jnp.where(first, a, heavy_far)
+    return jnp.where(even, heavy, jnp.where(lane < 48, light, 0.0))
+
+
+def place_of_device():
+    me = lax.axis_index("dom")
+    return me % 2 == 0, (me // 2) % 2 == 0
 
 
 def prior_rows(facts, per, lanes):
@@ -270,11 +284,10 @@
     q_high[...], q_low[...] = halves(rr * rr + ri * ri)
 
 
-def block_scores(prepared, particles, prior):
+def block_scores(prepared, y_terms, power_terms, prior):
     r_high, r_low, q_high, q_low = (x[...] for x in prepared)
-    y_high, y_low, p_high, p_low = particles
-    quad = dot_nt(q_high, p_high) + dot_nt(q_low, p_high) + dot_nt(q_high, p_low)
-    score = dot_nt(r_high, y_high) + dot_nt(r_low, y_high) + dot_nt(r_high, y_low)
+    quad = dot_nt(jnp.concatenate([q_high, q_low, q_high], axis=1), power_terms)
+    score = dot_nt(jnp.concatenate([r_high, r_low, r_high], axis=1), y_terms)
     per, lanes = prior.shape
     return score.reshape(SHIFTS, per, lanes) + (prior - 0.5 * quad)[None]
 
@@ -320,78 +333,54 @@
 
 def late_kernel(blocks, own, cnb, ynb, cynb, *rest):
     prepared, rest = rest[: 4 * blocks], rest[4 * blocks :]
-    e_outs, rest = (rest[:blocks], rest[blocks : 2 * blocks]), rest[2 * blocks :]
-    y_out, power_out, stats_out, tops_out, *half_out = rest
-    half_stats, half_tops = half_out[:2], half_out[2:]
-    per, lanes = e_outs[0][0].shape[1:]
-    left = lanes - 128
-    pairs = ((own, cnb), (ynb, cynb))
-    facts = [half_facts(*pair) for pair in pairs]
-    for half, pair in enumerate(pairs):
-        place_half(half, *pair, y_out, power_out)
+    e_outs, (y_out, power_out, stats_out, tops_out) = rest[:blocks], rest[blocks:]
+    per, lanes = e_outs[0].shape[1:]
+    parts = (own, cnb, ynb, cynb)
+    even, first = place_of_device()
+    place_rows(even, first, parts, y_out, power_out)
+    facts = row_facts(even, first, parts)
+    empty = deep_at(2, lanes)
     for out in (y_out, power_out):
-        empty = 768 + 6 * left
         out[empty:] = jnp.zeros_like(out[empty:])
-    for out in half_out:
-        out[...] = jnp.zeros_like(out)
-    for half in range(2):
-        particles = [placed(half, part, left, out) for out in (y_out, power_out) for part in (0, 1)]
-        prior = prior_rows(facts[half], per, lanes)
-        tops, sums = [], []
-        for n in range(blocks):
-            score = block_scores(prepared[4 * n : 4 * n + 4], particles, prior)
-            top, sums_here = weigh(score, e_outs[half][n])
-            half_tops[half][n : n + 1, :lanes] = top
-            tops.append(top)
-            sums.append(sums_here)
-        top, sums = joined_sums(tops, sums)
-        for k, row in enumerate((top, *sums, facts[half][5:6, :lanes])):
-            half_stats[half][k : k + 1, :lanes] = row
-    first = (lax.axis_index("dom") // 2) % 2 == 0
-    for out, (mine, others) in ((stats_out, half_stats), (tops_out, half_tops)):
-        mine, others = mine[...], others[...]
-        out[:, :256] = jnp.where(first, mine, others)
-        out[:, 256:] = jnp.where(first, others, mine)
-
-
-def chip_kernel(mine, other, out):
-    pair = (mine[...], other[...])
-    top, sums = joined_sums([x[0:1] for x in pair], [[x[k : k + 1] for k in (1, 2, 3)] for x in pair])
-    out[...] = pair[0]
-    for k, row in enumerate((top, *sums)):
-        out[k : k + 1] = row
-
-
-def sum_kernel(n, cuts, last, waits, here, there, tops, *rest):
-    ea_ref, eb_ref, y_ref, power_ref, *outs = rest[waits:]
-    per, lanes = ea_ref.shape[1:]
+    stats_out[...] = jnp.zeros_like(stats_out)
+    tops_out[...] = jnp.zeros_like(tops_out)
+    terms = []
+    for out in (y_out, power_out):
+        high, low = (placed(out, part, lanes) for part in (0, 1))
+        terms.append(jnp.concatenate([high, high, low], axis=1))
+    prior = prior_rows(facts, per, lanes)
+    tops, sums = [], []
+    for n in range(blocks):
+        score = block_scores(prepared[4 * n : 4 * n + 4], *terms, prior)
+        top, sums_here = weigh(score, e_outs[n])
+        tops_out[n : n + 1, :lanes] = top
+        tops.append(top)
+        sums.append(sums_here)
+    top, sums = joined_sums(tops, sums)
+    for k, row in enumerate((top, *sums, facts[5:6, :lanes])):
+        stats_out[k : k + 1, :lanes] = row
+
+
+def sum_kernel(n, cuts, last, waits, *rest):
+    team, tops, rest = rest[:TEAM], rest[TEAM], rest[TEAM + 1 + waits :]
+    e_ref, y_ref, power_ref, *outs = rest
+    per, lanes = e_ref.shape[1:]
     width = y_ref.shape[1]
     freq = width // 2
-    first = (lax.axis_index("dom") // 2) % 2 == 0
-    pair = (here[...], there[...])
+    team = [x[...] for x in team]
     top, (mass, *move) = joined_sums(
-        [x[0:1] for x in pair], [[x[k : k + 1] for k in (1, 2, 3)] for x in pair]
-    )
-    live = pair[0][4:5] / mass
-    gain = jnp.exp(tops[n : n + 1] - top) * live
-    gain_a = jnp.where(first, gain[:, :256], gain[:, 256:])[:, :lanes]
-    gain_b = jnp.where(first, gain[:, 256:], gain[:, :256])[:, :lanes]
+        [x[0:1] for x in team], [[x[k : k + 1] for k in (1, 2, 3)] for x in team]
+    )
+    live = team[0][4:5] / mass
+    gain = (jnp.exp(tops[n : n + 1] - top) * live)[:, :lanes]
     if last:
-        move = jnp.concatenate([x * live for x in move], axis=0)
-        move = jnp.concatenate([move, jnp.zeros((6, 512), jnp.float32)], axis=0)
-        move = jnp.where(first, move[:, :256], move[:, 256:])
-        lane = lax.broadcasted_iota(jnp.int32, (8, 128), 1)
-        light = jnp.where(
-            lane < 32, pltpu.roll(move[:, :128], 32, 1), pltpu.roll(move[:, 128:], 32, 1)
-        )
-        light = jnp.where(lane < 48, light, 0.0)
         shift_out = outs.pop()
-        slots = shift_out.shape[1]
-        shift_out[...] = jnp.where(even_core(), move[:, :128], light)[:2, :slots]
-    wa = ea_ref[...] * gain_a[None]
-    wb = eb_ref[...] * gain_b[None]
-    rows = SHIFTS * per
-    flat = dot_nn(deep_lanes(wa.reshape(rows, lanes), wb.reshape(rows, lanes)), y_ref[...])
+        move = [x * live for x in move] + [jnp.zeros((6, live.shape[1]), jnp.float32)]
+        move = own_lanes(*place_of_device(), jnp.concatenate(move, axis=0))
+        shift_out[...] = move[:2, : shift_out.shape[1]]
+    w = e_ref[...] * gain[None]
+    flat = dot_nn(deep_lanes(w.reshape(SHIFTS * per, lanes)), y_ref[...])
+    weight = dot_nn(deep_lanes(jnp.sum(w, axis=0)), power_ref[...])
     phases = grid_phases(freq)
     mid = SHIFTS // 2
 
@@ -405,7 +394,6 @@
         br, bi = block(SHIFTS - 1 - t)
         re = re + (ar + br) * c - (ai - bi) * s
         im = im + (ar - br) * s + (ai + bi) * c
-    weight = dot_nn(deep_lanes(jnp.sum(wa, axis=0), jnp.sum(wb, axis=0)), power_ref[...])
     for start, stop, out in zip(cuts, cuts[1:], outs):
         part = slice(start, stop)
         out[:, :freq] = re[part]
@@ -516,7 +504,7 @@
         name="own",
     )(*(pltpu.with_memory_space_constraint(x, pltpu.HBM) for x in own_facts), live_count)
     cnb = crossed(own, 1)
-    half = slots + slots // 2
+    lanes = 3 * slots
     bf16 = jnp.bfloat16
     early = 2
 
@@ -524,7 +512,7 @@
         return jax.ShapeDtypeStruct((rows, cols), dtype)
 
     block_shapes = [shaped(SHIFTS * per, width, bf16)] * 2 + [shaped(per, freq, bf16)] * 2
-    score_shape = jax.ShapeDtypeStruct((SHIFTS, per, half), f32)
+    score_shape = jax.ShapeDtypeStruct((SHIFTS, per, lanes), f32)
 
     def call(kernel, operands, out_shape, name, mib, cost=None, scratch=()):
         return pl.pallas_call(
@@ -568,23 +556,20 @@
         much,
     )
     prepared = (*prepared, *outs)
-    deep = 3 * 256 + 128
+    deep = 3 * MAIN + 128
     top_rows = -(-blocks // 8) * 8
     outs = call(
         lambda *a: late_kernel(blocks, *a),
         (own, cnb, ynb_prepared, cynb, *prepared),
-        [score_shape] * (2 * blocks)
-        + [shaped(deep, width, bf16), shaped(deep, freq, bf16), shaped(8, 512)]
-        + [shaped(top_rows, 512)],
+        [score_shape] * blocks
+        + [shaped(deep, width, bf16), shaped(deep, freq, bf16)]
+        + [shaped(8, 384), shaped(top_rows, 384)],
         "late",
         8 + 2 * blocks,
-        scratch=[pltpu.VMEM((8, 256), f32)] * 2 + [pltpu.VMEM((top_rows, 256), f32)] * 2,
-    )
-    e_own, e_other = outs[:blocks], outs[blocks : 2 * blocks]
-    y, power, stats, tops = outs[2 * blocks :]
-
-    (here,) = call(chip_kernel, (stats, crossed(stats, 1)), [shaped(8, 512)], "chip", 1)
-    there = crossed(here, 2)
+    )
+    weights, (y, power, stats, tops) = outs[:blocks], outs[blocks:]
+
+    team = [stats] + [crossed(stats, n) for n in range(1, TEAM)]
 
     def sums(n, cuts, last=False, waits=()):
         out_shape = [shaped(b - a, width + freq) for a, b in zip(cuts, cuts[1:])]
@@ -593,11 +578,11 @@
         return pl.pallas_call(
             lambda *a: sum_kernel(n, cuts, last, len(waits), *a),
             out_shape=tuple(out_shape),
-            in_specs=[vmem] * 3 + [anywhere] * len(waits) + [vmem] * 4,
+            in_specs=[vmem] * (TEAM + 1) + [anywhere] * len(waits) + [vmem] * 3,
             out_specs=(vmem,) * len(out_shape),
             compiler_params=params(8),
             name="sums",
-        )(here, there, tops, *waits, e_own[n], e_other[n], y, power)
+        )(*team, tops, *waits, weights[n], y, power)
 
     def combined(mine, others, cost=None):
         return pl.pallas_call(
@@ -614,10 +599,11 @@
     far = []
     waits = []
     for n in range(2, blocks, 2):
-        handed = [crossed(x, TEAM) for x in sums(n + 1, cut)]
+        handed = sums(n + 1, cut)
+        mine = sums(n, cut, waits=handed[:1])
         if n == 2:
-            near = sums(1, cut)
-        joined = [combined(x, [y]) for x, y in zip(sums(n, cut, waits=near[:1]), handed)]
+            near = sums(1, cut, waits=mine[:1])
+        joined = [combined(x, [crossed(y, TEAM)]) for x, y in zip(mine, handed)]
         far.extend(crossed(x, TEAM * n) for x in joined)
         waits.extend(joined)
     own_part, shift = sums(0, whole, last=True, waits=waits)

time: 49.1 us -> 47.9 us (0.976)
  waiting for transfers between devices: 18.4 us -> 14.8 us
  starting transfers between devices: 14.3 us -> 16.9 us
    ppermute x15 -> x16, waiting for transfers between devices: 18.4 us -> 14.8 us  [crossed(): return lax.ppermute(block, 'dom', [(i, i ^ mask) for i in range(size)])]
    ppermute x15 -> x16, starting transfers between devices: 14.3 us -> 16.9 us  [crossed(): return lax.ppermute(block, 'dom', [(i, i ^ mask) for i in range(size)])]
    pallas_call x3 -> x2, Pallas kernels: 6.11 us -> 5.93 us  [call(): pl.pallas_call(kernel, cost_estimate=cost, out_shape=tuple(out_shape), in...]
  transfers between devices with their start and end apart: 15 -> 16, of which waited for: 9 -> 8; matrix products, arithmetic and copies ran while one was open for 0% -> 0% of each run, Pallas kernels for 16% -> 16%
where the time goes in v11:
time: 47.9 us; the launch traced here: 47.8 us
  starting transfers between devices  16.9 us (35%)
  waiting for transfers between devices  14.8 us (31%)
  Pallas kernels  14.7 us (31%)
  between operations  1.39 us (3%)
    ppermute x16, starting transfers between devices, crossed(): return lax.ppermute(block, 'dom', [(i, i ^ mask) for i in range(size)])  16.9 us
    ppermute x16, waiting for transfers between devices, crossed(): return lax.ppermute(block, 'dom', [(i, i ^ mask) for i in range(size)])  14.8 us
    pallas_call x2, Pallas kernels, call(): pl.pallas_call(kernel, cost_estimate=cost, out_shape=tuple(out_shape), in...  5.93 us
    pallas_call x4, Pallas kernels, sums(): pl.pallas_call(lambda *a: sum_kernel(n, cuts, last, len(waits), *a), out_...  4.4 us
    pallas_call x1, Pallas kernels, on_device(): pl.pallas_call(own_kernel, out_shape=(jax.ShapeDtypeStruct((slots + 8, wi...  1.83 us
    pallas_call x1, Pallas kernels, on_device(): pl.pallas_call(early_kernel, out_shape=tuple(block_shapes * early), in_sp...  1.16 us
  transfers between devices with their start and end apart: 16, of which 8 were waited for; matrix products, arithmetic and copies ran while one was open for 0% of the time, Pallas kernels for 16%

profile of v11, /device:TPU:0, one launch (start us, length us, event | category | flops | bytes accessed | tf_op | source)
XLA Modules:
  0.0 47.8 jit_solution(3469523389196664879)
XLA Ops:
  0.6 3.0 %collective-permute-start.1 = (f32[96,1024]{1,0:T(8,128)}, f32[96,1024]{1,0:T(8,128)S(1)}, u32[]{:S(2)}, u32[]{:S(2)}) collective-permute-start(f32[96,1024]{1,0:T(8,128)} %src_at.1), channel_id=1, source_target_pairs={{0,2},{1,3},{2,0},{3,1},{4,6},{5,7},{6,4},{7,5},{8,10},{9,11},{10,... | collective-permute-start | bytes 1179656 | tf_op jit(solution)/shard_map/ppermute | solution.py:438
  3.7 1.6 %collective-permute-start.3 = (f32[32,1024]{1,0:T(8,128)}, f32[32,1024]{1,0:T(8,128)S(1)}, u32[]{:S(2)}, u32[]{:S(2)}) collective-permute-start(f32[32,1024]{1,0:T(8,128)} %bitcast.9), channel_id=1, source_target_pairs={{0,4},{1,5},{2,6},{3,7},{4,0},{5,1},{6,2},{7,3},{8,12},{9,13},{10,... | collective-permute-start | bytes 393224 | tf_op jit(solution)/shard_map/ppermute | solution.py:438
  5.2 2.5 %collective-permute-start.6 = (f32[32,1024]{1,0:T(8,128)}, f32[32,1024]{1,0:T(8,128)S(1)}, u32[]{:S(2)}, u32[]{:S(2)}) collective-permute-start(f32[32,1024]{1,0:T(8,128)} %bitcast.10), channel_id=1, source_target_pairs={{0,12},{1,13},{2,14},{3,15},{4,8},{5,9},{6,10},{7,11},{8,4},{9,5},... | collective-permute-start | bytes 393224 | tf_op jit(solution)/shard_map/ppermute | solution.py:438
  7.7 0.1 collective-permute-start.5
  8.5 1.8 %own.1 = (f32[104,1536]{1,0:T(8,128)S(1)}, f32[8,128]{1,0:T(8,128)S(1)}, f32[128,512]{1,0:T(8,128)S(1)}) custom-call(f32[96,1024]{1,0:T(8,128)} %src_at.1, f32[1,96]{1,0:T(1,128)} %bitcast.15, s32[2,96]{1,0:T(2,128)} %bitcast.14, s32[1,96]{1,0:T(1,128)} %bitcast.16, s32[1,96]{1,0:T(1,128)} %bitcast.17, f32[128,512]{1,0:T(8,128)} %noise_at.1, ...), custom_call_target="tpu_custom_call" | custom-call | tf_op jit(solution)/shard_map/own/pallas_call | solution.py:491
  10.3 0.6 %collective-permute-start.2 = (f32[8,128]{1,0:T(8,128)S(1)}, f32[8,128]{1,0:T(8,128)S(1)}, u32[]{:S(2)}, u32[]{:S(2)}) collective-permute-start(f32[8,128]{1,0:T(8,128)S(1)} %get-tuple-element.38), channel_id=1, source_target_pairs={{0,2},{1,3},{2,0},{3,1},{4,6},{5,7},{6,4},{7,5},{8,10},{9,11},{10,... | collective-permute-start | bytes 12296 | tf_op jit(solution)/shard_map/ppermute | solution.py:438
  10.9 0.0 collective-permute-done.3.near
  10.9 0.0 collective-permute-start
  10.9 1.2 %early.1 = (bf16[288,1024]{1,0:T(8,128)(2,1)S(1)}, bf16[288,1024]{1,0:T(8,128)(2,1)S(1)}, bf16[32,512]{1,0:T(8,128)(2,1)S(1)}, bf16[32,512]{1,0:T(8,128)(2,1)S(1...) custom-call(f32[32,1024]{1,0:T(8,128)} %bitcast.12, ...), custom_call_target="tpu_custom_call" | custom-call | tf_op jit(solution)/shard_map/early/pallas_call | solution.py:529
  12.1 1.9 %collective-permute-done.2.facts = f32[8,128]{1,0:T(8,128)S(1)} collective-permute-done((f32[8,128]{1,0:T(8,128)S(1)}, f32[8,128]{1,0:T(8,128)S(1)}, u32[]{:S(2)}, u32[]{:S(2)}) %collective-permute-start.2) | collective-permute-done | bytes 4128 | tf_op jit(solution)/shard_map/ppermute | solution.py:438
  14.0 0.0 collective-permute-done.1.src
  14.0 0.6 %neighbour.1.a_2_ = f32[104,1536]{1,0:T(8,128)S(1)} custom-call(f32[96,1024]{1,0:T(8,128)S(1)} %collective-permute-done.1.src, f32[8,128]{1,0:T(8,128)S(1)} %collective-permute-done.2.facts, f32[128,512]{1,0:T(8,128)S(1)} %get-tuple-element.39.inverse_noise, bf16[32,512]{1,0:T(8,128)(2,1)S(1)} %get-tuple-element.40.wait.a_6_), custom_call_target="tpu_custom_call" | custom-call | tf_op jit(solution)/shard_map/neighbour/pallas_call | solution.py:538
  14.6 0.1 collective-permute-start.4
  14.7 0.4 collective-permute-done.6.rest_1_
  15.1 4.4 %collective-permute-done.5.rest_0_ = f32[32,1024]{1,0:T(8,128)S(1)} collective-permute-done((f32[32,1024]{1,0:T(8,128)}, f32[32,1024]{1,0:T(8,128)S(1)}, u32[]{:S(2)}, u32[]{:S(2)}) %collective-permute-start.5) | collective-permute-done | bytes 131104 | tf_op jit(solution)/shard_map/ppermute | solution.py:438
  19.4 0.6 %middle.1 = (bf16[288,1024]{1,0:T(8,128)(2,1)S(1)}, bf16[288,1024]{1,0:T(8,128)(2,1)S(1)}, bf16[32,512]{1,0:T(8,128)(2,1)S(1)}, bf16[32,512]{1,0:T(8,128)(2,1)S(...) custom-call(f32[32,1024]{1,0:T(8,128)S(1)} %collective-permute-done., ...), custom_call_target="tpu_custom_call" | custom-call | flops 16000000000 | tf_op jit(solution)/shard_map/middle/pallas_call | solution.py:518
  20.0 0.0 collective-permute-done.a_1_
  20.0 0.0 collective-permute-done.4.a_3_
  20.0 5.4 %late.1 = (f32[9,32,288]{2,1,0:T(8,128)S(1)}, f32[9,32,288]{2,1,0:T(8,128)S(1)}, f32[9,32,288]{2,1,0:T(8,128)S(1)}, f32[9,32,288]{2,1,0:T(8,128)S(1)}, bf16[896,...) custom-call(f32[104,1536]{1,0:T(8,128)S(1)} %get-tuple-element.37.a_0_, ...), custom_call_target="tpu_custom_call" | custom-call | tf_op jit(solution)/shard_map/late/pallas_call | solution.py:518
  25.4 0.1 collective-permute-start.9
  25.5 0.6 %collective-permute-start.8 = (f32[8,384]{1,0:T(8,128)S(1)}, f32[8,384]{1,0:T(8,128)S(1)}, u32[]{:S(2)}, u32[]{:S(2)}) collective-permute-start(f32[8,384]{1,0:T(8,128)S(1)} %get-tuple-element.56.a_0_), channel_id=1, source_target_pairs={{0,2},{1,3},{2,0},{3,1},{4,6},{5,7},{6,4},{7,5},{8,10},{9,11},{10,... | collective-permute-start | bytes 36872 | tf_op jit(solution)/shard_map/ppermute | solution.py:438
  26.1 1.2 %collective-permute-start.7 = (f32[8,384]{1,0:T(8,128)S(1)}, f32[8,384]{1,0:T(8,128)S(1)}, u32[]{:S(2)}, u32[]{:S(2)}) collective-permute-start(f32[8,384]{1,0:T(8,128)S(1)} %get-tuple-element.56.a_0_), channel_id=1, source_target_pairs={{0,1},{1,0},{2,3},{3,2},{4,5},{5,4},{6,7},{7,6},{8,9},{9,8},{10,11... | collective-permute-start | bytes 36872 | tf_op jit(solution)/shard_map/ppermute | solution.py:438
  27.3 1.3 %collective-permute-done.9.a_3_ = f32[8,384]{1,0:T(8,128)S(1)} collective-permute-done((f32[8,384]{1,0:T(8,128)S(1)}, f32[8,384]{1,0:T(8,128)S(1)}, u32[]{:S(2)}, u32[]{:S(2)}) %collective-permute-start.9) | collective-permute-done | bytes 12320 | tf_op jit(solution)/shard_map/ppermute | solution.py:438
  28.6 0.7 %collective-permute-done.8.a_2_ = f32[8,384]{1,0:T(8,128)S(1)} collective-permute-done((f32[8,384]{1,0:T(8,128)S(1)}, f32[8,384]{1,0:T(8,128)S(1)}, u32[]{:S(2)}, u32[]{:S(2)}) %collective-permute-start.8) | collective-permute-done | bytes 12320 | tf_op jit(solution)/shard_map/ppermute | solution.py:438
  29.2 0.0 collective-permute-done.7.a_1_
  29.2 0.9 %sums.4 = (f32[16,1536]{1,0:T(8,128)S(1)}, f32[16,1536]{1,0:T(8,128)S(1)}) custom-call(f32[8,384]{1,0:T(8,128)S(1)} %get-tuple-element.56.a_0_, f32[8,384]{1,0:T(8,128)S(1)} %collective-permute-done.7.a_1_, f32[8,384]{1,0:T(8,128)S(1)} %collective-permute-done.8.a_2_, f32[8,384]{1,0:T(8,128)S(1)} %collective-permute-done.9.a_3_, ...), custom_call_target="tpu_custom_call" | custom-call | tf_op jit(solution)/shard_map/sums/pallas_call | solution.py:578
  30.2 0.0 collective-permute-start.11
  30.2 2.0 %collective-permute-start.10 = (f32[16,1536]{1,0:T(8,128)S(1)}, f32[16,1536]{1,0:T(8,128)S(1)}, u32[]{:S(2)}, u32[]{:S(2)}) collective-permute-start(f32[16,1536]{1,0:T(8,128)S(1)} %get-tuple-element.61.a_5_), channel_id=1, source_target_pairs={{0,4},{1,5},{2,6},{3,7},{4,0},{5,1},{6,2},{7,3},{8,12},{9,13},{10,... | collective-permute-start | bytes 294920 | tf_op jit(solution)/shard_map/ppermute | solution.py:438
  32.3 0.9 %sums.5 = (f32[16,1536]{1,0:T(8,128)S(1)}, f32[16,1536]{1,0:T(8,128)S(1)}) custom-call(f32[8,384]{1,0:T(8,128)S(1)} %get-tuple-element.56.a_0_, f32[8,384]{1,0:T(8,128)S(1)} %collective-permute-done.7.a_1_, f32[8,384]{1,0:T(8,128)S(1)} %collective-permute-done.8.a_2_, f32[8,384]{1,0:T(8,128)S(1)} %collective-permute-done.9.a_3_, ...), custom_call_target="tpu_custom_call" | custom-call | tf_op jit(solution)/shard_map/sums/pallas_call | solution.py:578
  33.2 1.0 %sums.7 = (f32[16,1536]{1,0:T(8,128)S(1)}, f32[16,1536]{1,0:T(8,128)S(1)}) custom-call(f32[8,384]{1,0:T(8,128)S(1)} %get-tuple-element.56.a_0_, f32[8,384]{1,0:T(8,128)S(1)} %collective-permute-done.7.a_1_, f32[8,384]{1,0:T(8,128)S(1)} %collective-permute-done.8.a_2_, f32[8,384]{1,0:T(8,128)S(1)} %collective-permute-done.9.a_3_, ...), custom_call_target="tpu_custom_call" | custom-call | tf_op jit(solution)/shard_map/sums/pallas_call | solution.py:578
  34.2 0.1 collective-permute-start.12
  34.3 1.9 %collective-permute-start.13 = (f32[16,1536]{1,0:T(8,128)S(1)}, f32[16,1536]{1,0:T(8,128)S(1)}, u32[]{:S(2)}, u32[]{:S(2)}) collective-permute-start(f32[16,1536]{1,0:T(8,128)S(1)} %get-tuple-element.71), channel_id=1, source_target_pairs={{0,4},{1,5},{2,6},{3,7},{4,0},{5,1},{6,2},{7,3},{8,12},{9,13},{10,... | collective-permute-start | bytes 294920 | tf_op jit(solution)/shard_map/ppermute | solution.py:438
  36.2 0.0 collective-permute-done.11.rest_0_
  36.2 1.3 %collective-permute-start.15 = (f32[16,1536]{1,0:T(8,128)S(1)}, f32[16,1536]{1,0:T(8,128)S(1)}, u32[]{:S(2)}, u32[]{:S(2)}) collective-permute-start(f32[16,1536]{1,0:T(8,128)S(1)} %combined.4.a_6_), channel_id=1, source_target_pairs={{0,8},{1,9},{2,10},{3,11},{4,12},{5,13},{6,14},{7,15},{8,0},{9,1},... | collective-permute-start | bytes 294920 | tf_op jit(solution)/shard_map/ppermute | solution.py:438
  37.5 0.0 collective-permute-done.10.rest_0_
  37.5 1.8 %collective-permute-start.14 = (f32[16,1536]{1,0:T(8,128)S(1)}, f32[16,1536]{1,0:T(8,128)S(1)}, u32[]{:S(2)}, u32[]{:S(2)}) collective-permute-start(f32[16,1536]{1,0:T(8,128)S(1)} %combined.3.a_5_), channel_id=1, source_target_pairs={{0,8},{1,9},{2,10},{3,11},{4,12},{5,13},{6,14},{7,15},{8,0},{9,1},... | collective-permute-start | bytes 294920 | tf_op jit(solution)/shard_map/ppermute | solution.py:438
  39.3 1.6 %sums.6 = (f32[32,1536]{1,0:T(8,128)S(1)}, f32[2,96]{1,0:T(2,128)}) custom-call(f32[8,384]{1,0:T(8,128)S(1)} %get-tuple-element.56.a_0_, f32[8,384]{1,0:T(8,128)S(1)} %collective-permute-done.7.a_1_, f32[8,384]{1,0:T(8,128)S(1)} %collective-permute-done.8.a_2_, f32[8,384]{1,0:T(8,128)S(1)} %collective-permute-done.9.a_3_, ...), custom_call_target="tpu_custom_call" | custom-call | tf_op jit(solution)/shard_map/sums/pallas_call | solution.py:578
  40.9 2.0 %collective-permute-done.12.rest_0_ = f32[16,1536]{1,0:T(8,128)S(1)} collective-permute-done((f32[16,1536]{1,0:T(8,128)S(1)}, f32[16,1536]{1,0:T(8,128)S(1)}, u32[]{:S(2)}, u32[]{:S(2)}) %collective-permute-start.12) | collective-permute-done | bytes 98336 | tf_op jit(solution)/shard_map/ppermute | solution.py:438
  42.9 1.1 %collective-permute-done.13.rest_1_ = f32[16,1536]{1,0:T(8,128)S(1)} collective-permute-done((f32[16,1536]{1,0:T(8,128)S(1)}, f32[16,1536]{1,0:T(8,128)S(1)}, u32[]{:S(2)}, u32[]{:S(2)}) %collective-permute-start.13) | collective-permute-done | bytes 98336 | tf_op jit(solution)/shard_map/ppermute | solution.py:438
  43.9 0.0 copy-start
  43.9 0.0 collective-permute-done.15.a_2_
  43.9 3.1 %collective-permute-done.14.a_1_ = f32[16,1536]{1,0:T(8,128)S(1)} collective-permute-done((f32[16,1536]{1,0:T(8,128)S(1)}, f32[16,1536]{1,0:T(8,128)S(1)}, u32[]{:S(2)}, u32[]{:S(2)}) %collective-permute-start.14) | collective-permute-done | bytes 98336 | tf_op jit(solution)/shard_map/ppermute | solution.py:438
  47.1 0.0 copy-done
  47.1 0.7 %update.1 = f32[32,1024]{1,0:T(8,128)} custom-call(f32[32,1536]{1,0:T(8,128)S(1)} %combined.5.a_0_, f32[16,1536]{1,0:T(8,128)S(1)} %collective-permute-done.14.a_1_, f32[16,1536]{1,0:T(8,128)S(1)} %collective-permute-done.15.a_2_, f32[1,512]{1,0:T(1,128)S(1)} %bitcast.8), custom_call_target="tpu_custom_call" | custom-call | tf_op jit(solution)/shard_map/update/pallas_call | solution.py:613
  (3 shorter events, 0.0 us)
Async XLA Ops:
  0.6 13.4 %collective-permute-start.1 = (f32[96,1024]{1,0:T(8,128)}, f32[96,1024]{1,0:T(8,128)S(1)}, u32[]{:S(2)}, u32[]{:S(2)}) collective-permute-start(f32[96,1024]{1,0:T(8,128)} %src_at.1), channel_id=1, source_target_pairs={{0,2},{1,3},{2,0},{3,1},{4,6},{5,7},{6,4},{7,5},{8,10},{9,11},{10,... | collective-permute-start | bytes 1179656 | tf_op jit(solution)/shard_map/ppermute | solution.py:438
  3.7 7.2 %collective-permute-start.3 = (f32[32,1024]{1,0:T(8,128)}, f32[32,1024]{1,0:T(8,128)S(1)}, u32[]{:S(2)}, u32[]{:S(2)}) collective-permute-start(f32[32,1024]{1,0:T(8,128)} %bitcast.9), channel_id=1, source_target_pairs={{0,4},{1,5},{2,6},{3,7},{4,0},{5,1},{6,2},{7,3},{8,12},{9,13},{10,... | collective-permute-start | bytes 393224 | tf_op jit(solution)/shard_map/ppermute | solution.py:438
  5.2 9.8 %collective-permute-start.6 = (f32[32,1024]{1,0:T(8,128)}, f32[32,1024]{1,0:T(8,128)S(1)}, u32[]{:S(2)}, u32[]{:S(2)}) collective-permute-start(f32[32,1024]{1,0:T(8,128)} %bitcast.10), channel_id=1, source_target_pairs={{0,12},{1,13},{2,14},{3,15},{4,8},{5,9},{6,10},{7,11},{8,4},{9,5},... | collective-permute-start | bytes 393224 | tf_op jit(solution)/shard_map/ppermute | solution.py:438
  7.7 11.7 %collective-permute-start.5 = (f32[32,1024]{1,0:T(8,128)}, f32[32,1024]{1,0:T(8,128)S(1)}, u32[]{:S(2)}, u32[]{:S(2)}) collective-permute-start(f32[32,1024]{1,0:T(8,128)} %bitcast.11), channel_id=1, source_target_pairs={{0,8},{1,9},{2,10},{3,11},{4,12},{5,13},{6,14},{7,15},{8,0},{9,1},... | collective-permute-start | bytes 393224 | tf_op jit(solution)/shard_map/ppermute | solution.py:438
  10.3 3.7 %collective-permute-start.2 = (f32[8,128]{1,0:T(8,128)S(1)}, f32[8,128]{1,0:T(8,128)S(1)}, u32[]{:S(2)}, u32[]{:S(2)}) collective-permute-start(f32[8,128]{1,0:T(8,128)S(1)} %get-tuple-element.38), channel_id=1, source_target_pairs={{0,2},{1,3},{2,0},{3,1},{4,6},{5,7},{6,4},{7,5},{8,10},{9,11},{10,... | collective-permute-start | bytes 12296 | tf_op jit(solution)/shard_map/ppermute | solution.py:438
  10.9 9.1 %collective-permute-start = (f32[104,1536]{1,0:T(8,128)S(1)}, f32[104,1536]{1,0:T(8,128)S(1)}, u32[]{:S(2)}, u32[]{:S(2)}) collective-permute-start(f32[104,1536]{1,0:T(8,128)S(1)} %get-tuple-element.37.a_0_), channel_id=1, source_target_pairs={{0,1},{1,0},{2,3},{3,2},{4,5},{5,4},{6,7},{7,6},{8,9},{9,8},{10,11... | collective-permute-start | bytes 1916936 | tf_op jit(solution)/shard_map/ppermute | solution.py:438
  14.6 5.4 %collective-permute-start.4 = (f32[104,1536]{1,0:T(8,128)S(1)}, f32[104,1536]{1,0:T(8,128)S(1)}, u32[]{:S(2)}, u32[]{:S(2)}) collective-permute-start(f32[104,1536]{1,0:T(8,128)S(1)} %neighbour.1.a_2_), channel_id=1, source_target_pairs={{0,1},{1,0},{2,3},{3,2},{4,5},{5,4},{6,7},{7,6},{8,9},{9,8},{10,11... | collective-permute-start | bytes 1916936 | tf_op jit(solution)/shard_map/ppermute | solution.py:438
  25.4 3.2 %collective-permute-start.9 = (f32[8,384]{1,0:T(8,128)S(1)}, f32[8,384]{1,0:T(8,128)S(1)}, u32[]{:S(2)}, u32[]{:S(2)}) collective-permute-start(f32[8,384]{1,0:T(8,128)S(1)} %get-tuple-element.56.a_0_), channel_id=1, source_target_pairs={{0,3},{1,2},{2,1},{3,0},{4,7},{5,6},{6,5},{7,4},{8,11},{9,10},{10,... | collective-permute-start | bytes 36872 | tf_op jit(solution)/shard_map/ppermute | solution.py:438
  25.5 3.8 %collective-permute-start.8 = (f32[8,384]{1,0:T(8,128)S(1)}, f32[8,384]{1,0:T(8,128)S(1)}, u32[]{:S(2)}, u32[]{:S(2)}) collective-permute-start(f32[8,384]{1,0:T(8,128)S(1)} %get-tuple-element.56.a_0_), channel_id=1, source_target_pairs={{0,2},{1,3},{2,0},{3,1},{4,6},{5,7},{6,4},{7,5},{8,10},{9,11},{10,... | collective-permute-start | bytes 36872 | tf_op jit(solution)/shard_map/ppermute | solution.py:438
  26.1 3.1 %collective-permute-start.7 = (f32[8,384]{1,0:T(8,128)S(1)}, f32[8,384]{1,0:T(8,128)S(1)}, u32[]{:S(2)}, u32[]{:S(2)}) collective-permute-start(f32[8,384]{1,0:T(8,128)S(1)} %get-tuple-element.56.a_0_), channel_id=1, source_target_pairs={{0,1},{1,0},{2,3},{3,2},{4,5},{5,4},{6,7},{7,6},{8,9},{9,8},{10,11... | collective-permute-start | bytes 36872 | tf_op jit(solution)/shard_map/ppermute | solution.py:438
  30.2 6.0 %collective-permute-start.11 = (f32[16,1536]{1,0:T(8,128)S(1)}, f32[16,1536]{1,0:T(8,128)S(1)}, u32[]{:S(2)}, u32[]{:S(2)}) collective-permute-start(f32[16,1536]{1,0:T(8,128)S(1)} %get-tuple-element.65), channel_id=1, source_target_pairs={{0,4},{1,5},{2,6},{3,7},{4,0},{5,1},{6,2},{7,3},{8,12},{9,13},{10,... | collective-permute-start | bytes 294920 | tf_op jit(solution)/shard_map/ppermute | solution.py:438
  30.2 7.3 %collective-permute-start.10 = (f32[16,1536]{1,0:T(8,128)S(1)}, f32[16,1536]{1,0:T(8,128)S(1)}, u32[]{:S(2)}, u32[]{:S(2)}) collective-permute-start(f32[16,1536]{1,0:T(8,128)S(1)} %get-tuple-element.61.a_5_), channel_id=1, source_target_pairs={{0,4},{1,5},{2,6},{3,7},{4,0},{5,1},{6,2},{7,3},{8,12},{9,13},{10,... | collective-permute-start | bytes 294920 | tf_op jit(solution)/shard_map/ppermute | solution.py:438
  34.2 8.7 %collective-permute-start.12 = (f32[16,1536]{1,0:T(8,128)S(1)}, f32[16,1536]{1,0:T(8,128)S(1)}, u32[]{:S(2)}, u32[]{:S(2)}) collective-permute-start(f32[16,1536]{1,0:T(8,128)S(1)} %get-tuple-element.70), channel_id=1, source_target_pairs={{0,4},{1,5},{2,6},{3,7},{4,0},{5,1},{6,2},{7,3},{8,12},{9,13},{10,... | collective-permute-start | bytes 294920 | tf_op jit(solution)/shard_map/ppermute | solution.py:438
  34.3 9.6 %collective-permute-start.13 = (f32[16,1536]{1,0:T(8,128)S(1)}, f32[16,1536]{1,0:T(8,128)S(1)}, u32[]{:S(2)}, u32[]{:S(2)}) collective-permute-start(f32[16,1536]{1,0:T(8,128)S(1)} %get-tuple-element.71), channel_id=1, source_target_pairs={{0,4},{1,5},{2,6},{3,7},{4,0},{5,1},{6,2},{7,3},{8,12},{9,13},{10,... | collective-permute-start | bytes 294920 | tf_op jit(solution)/shard_map/ppermute | solution.py:438
  36.2 7.7 %collective-permute-start.15 = (f32[16,1536]{1,0:T(8,128)S(1)}, f32[16,1536]{1,0:T(8,128)S(1)}, u32[]{:S(2)}, u32[]{:S(2)}) collective-permute-start(f32[16,1536]{1,0:T(8,128)S(1)} %combined.4.a_6_), channel_id=1, source_target_pairs={{0,8},{1,9},{2,10},{3,11},{4,12},{5,13},{6,14},{7,15},{8,0},{9,1},... | collective-permute-start | bytes 294920 | tf_op jit(solution)/shard_map/ppermute | solution.py:438
  37.5 9.5 %collective-permute-start.14 = (f32[16,1536]{1,0:T(8,128)S(1)}, f32[16,1536]{1,0:T(8,128)S(1)}, u32[]{:S(2)}, u32[]{:S(2)}) collective-permute-start(f32[16,1536]{1,0:T(8,128)S(1)} %combined.3.a_5_), channel_id=1, source_target_pairs={{0,8},{1,9},{2,10},{3,11},{4,12},{5,13},{6,14},{7,15},{8,0},{9,1},... | collective-permute-start | bytes 294920 | tf_op jit(solution)/shard_map/ppermute | solution.py:438
  43.9 3.2 %copy-start = (f32[512]{0:T(512)S(1)}, f32[512]{0:T(512)}, u32[]{:S(2)}) copy-start(f32[512]{0:T(512)} %param.16) | copy-start | bytes 6148

commit v12 on v11

--- a/solution.py
+++ b/solution.py
@@ -198,7 +198,7 @@
             yield even, first, heavy, light
 
 
-def place_rows(even, first, parts, y_out, power_out):
+def place_rows(even, first, parts, y_out, power_out, left_out):
     width = y_out.shape[1]
     slots = parts[0].shape[0] - 8
     half = slots // 2
@@ -220,11 +220,7 @@
             place(light[0], 0, half, 2 * slots)
             place(light[1], 0, cut, 2 * slots + half)
             place(light[1], cut, half, MAIN)
-
-
-def placed(out, part, rows):
-    main, left = deep_at(part, 0), deep_at(part, MAIN)
-    return jnp.concatenate([out[main : main + MAIN], out[left : left + rows - MAIN]], axis=0)
+            left_out[...] = light[1][cut:half, :width]
 
 
 def lane_index():
@@ -284,12 +280,26 @@
     q_high[...], q_low[...] = halves(rr * rr + ri * ri)
 
 
-def block_scores(prepared, y_terms, power_terms, prior):
-    r_high, r_low, q_high, q_low = (x[...] for x in prepared)
-    quad = dot_nt(jnp.concatenate([q_high, q_low, q_high], axis=1), power_terms)
-    score = dot_nt(jnp.concatenate([r_high, r_low, r_high], axis=1), y_terms)
-    per, lanes = prior.shape
-    return score.reshape(SHIFTS, per, lanes) + (prior - 0.5 * quad)[None]
+def terms(high, low):
+    return jnp.concatenate([high, high, low], axis=1)
+
+
+def terms_left(high, low):
+    return jnp.concatenate([high, low, high], axis=1)
+
+
+def shifted_rows(rows, phases):
+    freq = rows.shape[1] // 2
+    re, im = rows[:, :freq], rows[:, freq:]
+    mid = SHIFTS // 2
+    out = [None] * SHIFTS
+    out[mid] = rows
+    for t in range(mid):
+        c, s = phases[t]
+        a, b, d, e = re * c, im * s, im * c, re * s
+        out[t] = jnp.concatenate([a - b, e + d], axis=1)
+        out[SHIFTS - 1 - t] = jnp.concatenate([a + b, d - e], axis=1)
+    return jnp.concatenate(out, axis=0)
 
 
 def weigh(score, e_out):
@@ -333,25 +343,51 @@
 
 def late_kernel(blocks, own, cnb, ynb, cynb, *rest):
     prepared, rest = rest[: 4 * blocks], rest[4 * blocks :]
-    e_outs, (y_out, power_out, stats_out, tops_out) = rest[:blocks], rest[blocks:]
+    e_outs, rest = rest[:blocks], rest[blocks:]
+    y_out, power_out, stats_out, tops_out, left_rows = rest
     per, lanes = e_outs[0].shape[1:]
+    freq = power_out.shape[1]
+    left = lanes - MAIN
     parts = (own, cnb, ynb, cynb)
     even, first = place_of_device()
-    place_rows(even, first, parts, y_out, power_out)
+    place_rows(even, first, parts, y_out, power_out, left_rows)
     facts = row_facts(even, first, parts)
     empty = deep_at(2, lanes)
     for out in (y_out, power_out):
         out[empty:] = jnp.zeros_like(out[empty:])
     stats_out[...] = jnp.zeros_like(stats_out)
     tops_out[...] = jnp.zeros_like(tops_out)
-    terms = []
-    for out in (y_out, power_out):
-        high, low = (placed(out, part, lanes) for part in (0, 1))
-        terms.append(jnp.concatenate([high, high, low], axis=1))
+
+    def rows(out, part, size):
+        at = deep_at(part, 0)
+        main = out[at : at + MAIN]
+        at = deep_at(part, MAIN)
+        return jnp.concatenate([main, out[at : at + left]], axis=0)[:size]
+
+    q_terms = [terms_left(prepared[4 * n + 2][...], prepared[4 * n + 3][...]) for n in range(blocks)]
+    quad = dot_nt(
+        jnp.concatenate(q_terms, axis=0), terms(*(rows(power_out, k, lanes) for k in (0, 1)))
+    )
     prior = prior_rows(facts, per, lanes)
+    mid = slice(SHIFTS // 2 * per, (SHIFTS // 2 + 1) * per)
+    r_terms = [terms_left(prepared[4 * n][mid], prepared[4 * n + 1][mid]) for n in range(blocks)]
+    moved = terms(*halves(shifted_rows(left_rows[...], grid_phases(freq))))
+    far = dot_nt(jnp.concatenate(r_terms, axis=0), moved)
+    far = jnp.concatenate([far, jnp.zeros((blocks * per, 384 - SHIFTS * left), jnp.float32)], axis=1)
+    step = 128 // left
+    far = [
+        pltpu.roll(far[:, 128 * (t // step) : 128 * (t // step + 1)], -left * (t % step) % 128, 1)
+        for t in range(SHIFTS)
+    ]
+    main_terms = terms(*(rows(y_out, k, MAIN) for k in (0, 1)))
     tops, sums = [], []
     for n in range(blocks):
-        score = block_scores(prepared[4 * n : 4 * n + 4], *terms, prior)
+        part = slice(n * per, (n + 1) * per)
+        base = prior - 0.5 * quad[part]
+        score = dot_nt(terms_left(prepared[4 * n][...], prepared[4 * n + 1][...]), main_terms)
+        score = score.reshape(SHIFTS, per, MAIN)
+        tail = jnp.stack([x[part, :left] for x in far])
+        score = jnp.concatenate([score, tail], axis=2) + base[None]
         top, sums_here = weigh(score, e_outs[n])
         tops_out[n : n + 1, :lanes] = top
         tops.append(top)
@@ -401,13 +437,8 @@
         out[:, width:] = weight[part]
 
 
-def add_kernel(a, *rest):
-    *parts, out = rest
-    at = 0
-    for part in parts:
-        rows = slice(at, at + part.shape[0])
-        out[rows] = a[rows] + part[...]
-        at += part.shape[0]
+def add_kernel(a, b, wait, out):
+    out[...] = a[...] + b[...]
 
 
 def final_kernel(row_cuts, *refs):
@@ -566,6 +597,7 @@
         + [shaped(8, 384), shaped(top_rows, 384)],
         "late",
         8 + 2 * blocks,
+        scratch=[pltpu.VMEM((lanes - MAIN, width), f32)],
     )
     weights, (y, power, stats, tops) = outs[:blocks], outs[blocks:]
 
@@ -584,16 +616,27 @@
             name="sums",
         )(*team, tops, *waits, weights[n], y, power)
 
-    def combined(mine, others, cost=None):
+    def combined(mine, other, wait):
         return pl.pallas_call(
             add_kernel,
             out_shape=jax.ShapeDtypeStruct(mine.shape, f32),
-            in_specs=[vmem] * (1 + len(others)),
+            in_specs=[vmem] * 2 + [anywhere],
             out_specs=vmem,
             compiler_params=params(4),
+            name="combined",
+        )(mine, other, wait)
+
+    def gated(arrays, cost):
+        return pl.pallas_call(
+            lambda *a: None,
+            out_shape=tuple(jax.ShapeDtypeStruct(x.shape, x.dtype) for x in arrays),
+            in_specs=[anywhere] * len(arrays),
+            out_specs=(anywhere,) * len(arrays),
+            input_output_aliases={n: n for n in range(len(arrays))},
+            compiler_params=params(1),
             cost_estimate=cost,
-            name="combined",
-        )(mine, *others)
+            name="gate",
+        )(*arrays)
 
     whole, cut = (0, per), (0, per // 2, per)
     far = []
@@ -602,13 +645,13 @@
         handed = sums(n + 1, cut)
         mine = sums(n, cut, waits=handed[:1])
         if n == 2:
-            near = sums(1, cut, waits=mine[:1])
-        joined = [combined(x, [crossed(y, TEAM)]) for x, y in zip(mine, handed)]
+            (near,) = sums(1, whole, waits=mine[:1])
+        joined = [combined(x, crossed(y, TEAM), near) for x, y in zip(mine, handed)]
         far.extend(crossed(x, TEAM * n) for x in joined)
         waits.extend(joined)
     own_part, shift = sums(0, whole, last=True, waits=waits)
-    own_part = combined(own_part, [crossed(x, TEAM) for x in near], much)
-    row_cuts = [cut] * (len(far) // 2)
+    far = [crossed(near, TEAM), *gated(far, much)]
+    row_cuts = [whole] + [cut] * (len(far) // 2)
 
     refs_new = pl.pallas_call(
         lambda *a: final_kernel(row_cuts, *a),

time: 47.9 us -> 45.6 us (0.952)
  Pallas kernels: 14.7 us -> 12.9 us
  starting transfers between devices: 16.9 us -> 16.1 us
    pallas_call x2, Pallas kernels: 5.93 us -> 4.18 us  [call(): pl.pallas_call(kernel, cost_estimate=cost, out_shape=tuple(out_shape), in...]
    ppermute x16 -> x15, starting transfers between devices: 16.9 us -> 16.1 us  [crossed(): return lax.ppermute(block, 'dom', [(i, i ^ mask) for i in range(size)])]
    ppermute x16 -> x15, waiting for transfers between devices: 14.8 us -> 15.1 us  [crossed(): return lax.ppermute(block, 'dom', [(i, i ^ mask) for i in range(size)])]
  transfers between devices with their start and end apart: 16 -> 15, of which waited for: 8 -> 9; matrix products, arithmetic and copies ran while one was open for 0% -> 0% of each run, Pallas kernels for 16% -> 17%
where the time goes in v12:
time: 45.6 us; the launch traced here: 45.5 us
  starting transfers between devices  16.1 us (35%)
  waiting for transfers between devices  15.1 us (33%)
  Pallas kernels  12.9 us (28%)
  between operations  1.38 us (3%)
    ppermute x15, starting transfers between devices, crossed(): return lax.ppermute(block, 'dom', [(i, i ^ mask) for i in range(size)])  16.1 us
    ppermute x15, waiting for transfers between devices, crossed(): return lax.ppermute(block, 'dom', [(i, i ^ mask) for i in range(size)])  15.1 us
    pallas_call x4, Pallas kernels, sums(): pl.pallas_call(lambda *a: sum_kernel(n, cuts, last, len(waits), *a), out_...  4.4 us
    pallas_call x2, Pallas kernels, call(): pl.pallas_call(kernel, cost_estimate=cost, out_shape=tuple(out_shape), in...  4.18 us
    pallas_call x1, Pallas kernels, on_device(): pl.pallas_call(own_kernel, out_shape=(jax.ShapeDtypeStruct((slots + 8, wi...  1.83 us
    pallas_call x1, Pallas kernels, on_device(): pl.pallas_call(early_kernel, out_shape=tuple(block_shapes * early), in_sp...  1.16 us
  transfers between devices with their start and end apart: 15, of which 9 were waited for; matrix products, arithmetic and copies ran while one was open for 0% of the time, Pallas kernels for 17%

profile of v12, /device:TPU:0, one launch (start us, length us, event | category | flops | bytes accessed | tf_op | source)
XLA Modules:
  0.0 45.5 jit_solution(6058854485670010734)
XLA Ops:
  0.6 3.0 %collective-permute-start.1 = (f32[96,1024]{1,0:T(8,128)}, f32[96,1024]{1,0:T(8,128)S(1)}, u32[]{:S(2)}, u32[]{:S(2)}) collective-permute-start(f32[96,1024]{1,0:T(8,128)} %src_at.1), channel_id=1, source_target_pairs={{0,2},{1,3},{2,0},{3,1},{4,6},{5,7},{6,4},{7,5},{8,10},{9,11},{10,... | collective-permute-start | bytes 1179656 | tf_op jit(solution)/shard_map/ppermute | solution.py:469
  3.7 1.6 %collective-permute-start.3 = (f32[32,1024]{1,0:T(8,128)}, f32[32,1024]{1,0:T(8,128)S(1)}, u32[]{:S(2)}, u32[]{:S(2)}) collective-permute-start(f32[32,1024]{1,0:T(8,128)} %bitcast.9), channel_id=1, source_target_pairs={{0,4},{1,5},{2,6},{3,7},{4,0},{5,1},{6,2},{7,3},{8,12},{9,13},{10,... | collective-permute-start | bytes 393224 | tf_op jit(solution)/shard_map/ppermute | solution.py:469
  5.2 2.5 %collective-permute-start.6 = (f32[32,1024]{1,0:T(8,128)}, f32[32,1024]{1,0:T(8,128)S(1)}, u32[]{:S(2)}, u32[]{:S(2)}) collective-permute-start(f32[32,1024]{1,0:T(8,128)} %bitcast.10), channel_id=1, source_target_pairs={{0,12},{1,13},{2,14},{3,15},{4,8},{5,9},{6,10},{7,11},{8,4},{9,5},... | collective-permute-start | bytes 393224 | tf_op jit(solution)/shard_map/ppermute | solution.py:469
  7.7 0.1 collective-permute-start.5
  8.5 1.8 %own.1 = (f32[104,1536]{1,0:T(8,128)S(1)}, f32[8,128]{1,0:T(8,128)S(1)}, f32[128,512]{1,0:T(8,128)S(1)}) custom-call(f32[96,1024]{1,0:T(8,128)} %src_at.1, f32[1,96]{1,0:T(1,128)} %bitcast.15, s32[2,96]{1,0:T(2,128)} %bitcast.14, s32[1,96]{1,0:T(1,128)} %bitcast.16, s32[1,96]{1,0:T(1,128)} %bitcast.17, f32[128,512]{1,0:T(8,128)} %noise_at.1, ...), custom_call_target="tpu_custom_call" | custom-call | tf_op jit(solution)/shard_map/own/pallas_call | solution.py:522
  10.3 0.6 %collective-permute-start.2 = (f32[8,128]{1,0:T(8,128)S(1)}, f32[8,128]{1,0:T(8,128)S(1)}, u32[]{:S(2)}, u32[]{:S(2)}) collective-permute-start(f32[8,128]{1,0:T(8,128)S(1)} %get-tuple-element.38), channel_id=1, source_target_pairs={{0,2},{1,3},{2,0},{3,1},{4,6},{5,7},{6,4},{7,5},{8,10},{9,11},{10,... | collective-permute-start | bytes 12296 | tf_op jit(solution)/shard_map/ppermute | solution.py:469
  10.9 0.0 collective-permute-done.3.near
  10.9 0.0 collective-permute-start
  10.9 1.2 %early.1 = (bf16[288,1024]{1,0:T(8,128)(2,1)S(1)}, bf16[288,1024]{1,0:T(8,128)(2,1)S(1)}, bf16[32,512]{1,0:T(8,128)(2,1)S(1)}, bf16[32,512]{1,0:T(8,128)(2,1)S(1...) custom-call(f32[32,1024]{1,0:T(8,128)} %bitcast.12, ...), custom_call_target="tpu_custom_call" | custom-call | tf_op jit(solution)/shard_map/early/pallas_call | solution.py:560
  12.1 1.9 %collective-permute-done.2.facts = f32[8,128]{1,0:T(8,128)S(1)} collective-permute-done((f32[8,128]{1,0:T(8,128)S(1)}, f32[8,128]{1,0:T(8,128)S(1)}, u32[]{:S(2)}, u32[]{:S(2)}) %collective-permute-start.2) | collective-permute-done | bytes 4128 | tf_op jit(solution)/shard_map/ppermute | solution.py:469
  14.0 0.0 collective-permute-done.1.src
  14.0 0.6 %neighbour.1.a_2_ = f32[104,1536]{1,0:T(8,128)S(1)} custom-call(f32[96,1024]{1,0:T(8,128)S(1)} %collective-permute-done.1.src, f32[8,128]{1,0:T(8,128)S(1)} %collective-permute-done.2.facts, f32[128,512]{1,0:T(8,128)S(1)} %get-tuple-element.39.inverse_noise, bf16[32,512]{1,0:T(8,128)(2,1)S(1)} %get-tuple-element.40.wait.a_6_), custom_call_target="tpu_custom_call" | custom-call | tf_op jit(solution)/shard_map/neighbour/pallas_call | solution.py:569
  14.6 0.1 collective-permute-start.4
  14.7 0.4 collective-permute-done.6.rest_1_
  15.1 4.4 %collective-permute-done.5.rest_0_ = f32[32,1024]{1,0:T(8,128)S(1)} collective-permute-done((f32[32,1024]{1,0:T(8,128)}, f32[32,1024]{1,0:T(8,128)S(1)}, u32[]{:S(2)}, u32[]{:S(2)}) %collective-permute-start.5) | collective-permute-done | bytes 131104 | tf_op jit(solution)/shard_map/ppermute | solution.py:469
  19.4 0.6 %middle.1 = (bf16[288,1024]{1,0:T(8,128)(2,1)S(1)}, bf16[288,1024]{1,0:T(8,128)(2,1)S(1)}, bf16[32,512]{1,0:T(8,128)(2,1)S(1)}, bf16[32,512]{1,0:T(8,128)(2,1)S(...) custom-call(f32[32,1024]{1,0:T(8,128)S(1)} %collective-permute-done., ...), custom_call_target="tpu_custom_call" | custom-call | flops 16000000000 | tf_op jit(solution)/shard_map/middle/pallas_call | solution.py:549
  20.0 0.0 collective-permute-done.a_1_
  20.0 0.0 collective-permute-done.4.a_3_
  20.0 3.6 %late.1 = (f32[9,32,288]{2,1,0:T(8,128)S(1)}, f32[9,32,288]{2,1,0:T(8,128)S(1)}, f32[9,32,288]{2,1,0:T(8,128)S(1)}, f32[9,32,288]{2,1,0:T(8,128)S(1)}, bf16[896,...) custom-call(f32[104,1536]{1,0:T(8,128)S(1)} %get-tuple-element.37.a_0_, ...), custom_call_target="tpu_custom_call" | custom-call | tf_op jit(solution)/shard_map/late/pallas_call | solution.py:549
  23.6 0.1 collective-permute-start.9
  23.7 0.6 %collective-permute-start.8 = (f32[8,384]{1,0:T(8,128)S(1)}, f32[8,384]{1,0:T(8,128)S(1)}, u32[]{:S(2)}, u32[]{:S(2)}) collective-permute-start(f32[8,384]{1,0:T(8,128)S(1)} %get-tuple-element.56.a_0_), channel_id=1, source_target_pairs={{0,2},{1,3},{2,0},{3,1},{4,6},{5,7},{6,4},{7,5},{8,10},{9,11},{10,... | collective-permute-start | bytes 36872 | tf_op jit(solution)/shard_map/ppermute | solution.py:469
  24.3 1.2 %collective-permute-start.7 = (f32[8,384]{1,0:T(8,128)S(1)}, f32[8,384]{1,0:T(8,128)S(1)}, u32[]{:S(2)}, u32[]{:S(2)}) collective-permute-start(f32[8,384]{1,0:T(8,128)S(1)} %get-tuple-element.56.a_0_), channel_id=1, source_target_pairs={{0,1},{1,0},{2,3},{3,2},{4,5},{5,4},{6,7},{7,6},{8,9},{9,8},{10,11... | collective-permute-start | bytes 36872 | tf_op jit(solution)/shard_map/ppermute | solution.py:469
  25.6 1.3 %collective-permute-done.9.a_3_ = f32[8,384]{1,0:T(8,128)S(1)} collective-permute-done((f32[8,384]{1,0:T(8,128)S(1)}, f32[8,384]{1,0:T(8,128)S(1)}, u32[]{:S(2)}, u32[]{:S(2)}) %collective-permute-start.9) | collective-permute-done | bytes 12320 | tf_op jit(solution)/shard_map/ppermute | solution.py:469
  26.8 0.7 %collective-permute-done.8.a_2_ = f32[8,384]{1,0:T(8,128)S(1)} collective-permute-done((f32[8,384]{1,0:T(8,128)S(1)}, f32[8,384]{1,0:T(8,128)S(1)}, u32[]{:S(2)}, u32[]{:S(2)}) %collective-permute-start.8) | collective-permute-done | bytes 12320 | tf_op jit(solution)/shard_map/ppermute | solution.py:469
  27.5 0.0 collective-permute-done.7.a_1_
  27.5 0.9 %sums.4 = (f32[16,1536]{1,0:T(8,128)S(1)}, f32[16,1536]{1,0:T(8,128)S(1)}) custom-call(f32[8,384]{1,0:T(8,128)S(1)} %get-tuple-element.56.a_0_, f32[8,384]{1,0:T(8,128)S(1)} %collective-permute-done.7.a_1_, f32[8,384]{1,0:T(8,128)S(1)} %collective-permute-done.8.a_2_, f32[8,384]{1,0:T(8,128)S(1)} %collective-permute-done.9.a_3_, ...), custom_call_target="tpu_custom_call" | custom-call | tf_op jit(solution)/shard_map/sums/pallas_call | solution.py:610
  28.4 0.0 collective-permute-start.11
  28.5 2.0 %collective-permute-start.10 = (f32[16,1536]{1,0:T(8,128)S(1)}, f32[16,1536]{1,0:T(8,128)S(1)}, u32[]{:S(2)}, u32[]{:S(2)}) collective-permute-start(f32[16,1536]{1,0:T(8,128)S(1)} %get-tuple-element.61.a_5_), channel_id=1, source_target_pairs={{0,4},{1,5},{2,6},{3,7},{4,0},{5,1},{6,2},{7,3},{8,12},{9,13},{10,... | collective-permute-start | bytes 294920 | tf_op jit(solution)/shard_map/ppermute | solution.py:469
  30.5 0.9 %sums.5 = (f32[16,1536]{1,0:T(8,128)S(1)}, f32[16,1536]{1,0:T(8,128)S(1)}) custom-call(f32[8,384]{1,0:T(8,128)S(1)} %get-tuple-element.56.a_0_, f32[8,384]{1,0:T(8,128)S(1)} %collective-permute-done.7.a_1_, f32[8,384]{1,0:T(8,128)S(1)} %collective-permute-done.8.a_2_, f32[8,384]{1,0:T(8,128)S(1)} %collective-permute-done.9.a_3_, ...), custom_call_target="tpu_custom_call" | custom-call | tf_op jit(solution)/shard_map/sums/pallas_call | solution.py:610
  31.4 1.0 %sums.6.wait = f32[32,1536]{1,0:T(8,128)S(1)} custom-call(f32[8,384]{1,0:T(8,128)S(1)} %get-tuple-element.56.a_0_, f32[8,384]{1,0:T(8,128)S(1)} %collective-permute-done.7.a_1_, f32[8,384]{1,0:T(8,128)S(1)} %collective-permute-done.8.a_2_, f32[8,384]{1,0:T(8,128)S(1)} %collective-permute-done.9.a_3_, f32[8,384]{1,0:T(8,128)S(1)} %get-tuple-element.57.a_4_, ...), custom_call_target="tpu_custom_call" | custom-call | tf_op jit(solution)/shard_map/sums/pallas_call | solution.py:610
  32.4 1.3 %collective-permute-done.11.b = f32[16,1536]{1,0:T(8,128)S(1)} collective-permute-done((f32[16,1536]{1,0:T(8,128)S(1)}, f32[16,1536]{1,0:T(8,128)S(1)}, u32[]{:S(2)}, u32[]{:S(2)}) %collective-permute-start.11) | collective-permute-done | bytes 98336 | tf_op jit(solution)/shard_map/ppermute | solution.py:469
  33.7 1.5 %collective-permute-start.14 = (f32[16,1536]{1,0:T(8,128)S(1)}, f32[16,1536]{1,0:T(8,128)S(1)}, u32[]{:S(2)}, u32[]{:S(2)}) collective-permute-start(f32[16,1536]{1,0:T(8,128)S(1)} %combined.3.a_6_), channel_id=1, source_target_pairs={{0,8},{1,9},{2,10},{3,11},{4,12},{5,13},{6,14},{7,15},{8,0},{9,1},... | collective-permute-start | bytes 294920 | tf_op jit(solution)/shard_map/ppermute | solution.py:469
  35.2 0.0 collective-permute-done.10.b
  35.2 2.1 %collective-permute-start.13 = (f32[16,1536]{1,0:T(8,128)S(1)}, f32[16,1536]{1,0:T(8,128)S(1)}, u32[]{:S(2)}, u32[]{:S(2)}) collective-permute-start(f32[16,1536]{1,0:T(8,128)S(1)} %combined.2.a_5_), channel_id=1, source_target_pairs={{0,8},{1,9},{2,10},{3,11},{4,12},{5,13},{6,14},{7,15},{8,0},{9,1},... | collective-permute-start | bytes 294920 | tf_op jit(solution)/shard_map/ppermute | solution.py:469
  37.3 0.7 %collective-permute-start.12 = (f32[32,1536]{1,0:T(8,128)S(1)}, f32[32,1536]{1,0:T(8,128)S(1)}, u32[]{:S(2)}, u32[]{:S(2)}) collective-permute-start(f32[32,1536]{1,0:T(8,128)S(1)} %sums.6.wait), channel_id=1, source_target_pairs={{0,4},{1,5},{2,6},{3,7},{4,0},{5,1},{6,2},{7,3},{8,12},{9,13},{10,... | collective-permute-start | bytes 589832 | tf_op jit(solution)/shard_map/ppermute | solution.py:469
  38.0 1.6 %sums.7 = (f32[32,1536]{1,0:T(8,128)S(1)}, f32[2,96]{1,0:T(2,128)}) custom-call(f32[8,384]{1,0:T(8,128)S(1)} %get-tuple-element.56.a_0_, f32[8,384]{1,0:T(8,128)S(1)} %collective-permute-done.7.a_1_, f32[8,384]{1,0:T(8,128)S(1)} %collective-permute-done.8.a_2_, f32[8,384]{1,0:T(8,128)S(1)} %collective-permute-done.9.a_3_, ...), custom_call_target="tpu_custom_call" | custom-call | tf_op jit(solution)/shard_map/sums/pallas_call | solution.py:610
  39.6 0.0 copy-start
  39.6 2.1 %collective-permute-done.14.a_1_ = f32[16,1536]{1,0:T(8,128)S(1)} collective-permute-done((f32[16,1536]{1,0:T(8,128)S(1)}, f32[16,1536]{1,0:T(8,128)S(1)}, u32[]{:S(2)}, u32[]{:S(2)}) %collective-permute-start.14) | collective-permute-done | bytes 98336 | tf_op jit(solution)/shard_map/ppermute | solution.py:469
  41.6 1.8 %collective-permute-done.13.a_0_ = f32[16,1536]{1,0:T(8,128)S(1)} collective-permute-done((f32[16,1536]{1,0:T(8,128)S(1)}, f32[16,1536]{1,0:T(8,128)S(1)}, u32[]{:S(2)}, u32[]{:S(2)}) %collective-permute-start.13) | collective-permute-done | bytes 98336 | tf_op jit(solution)/shard_map/ppermute | solution.py:469
  43.5 1.3 %collective-permute-done.12.a_1_ = f32[32,1536]{1,0:T(8,128)S(1)} collective-permute-done((f32[32,1536]{1,0:T(8,128)S(1)}, f32[32,1536]{1,0:T(8,128)S(1)}, u32[]{:S(2)}, u32[]{:S(2)}) %collective-permute-start.12) | collective-permute-done | bytes 196640 | tf_op jit(solution)/shard_map/ppermute | solution.py:469
  44.8 0.0 copy-done
  44.8 0.7 %update.1 = f32[32,1024]{1,0:T(8,128)} custom-call(f32[32,1536]{1,0:T(8,128)S(1)} %get-tuple-element.69.a_0_, f32[32,1536]{1,0:T(8,128)S(1)} %collective-permute-done.12.a_1_, f32[16,1536]{1,0:T(8,128)S(1)} %get-tuple-element.70.a_2_, f32[16,1536]{1,0:T(8,128)S(1)} %get-tuple-element.71.a_3_, f32[1,512]{1,0:T(1,128)S(1)} %bitcast.8), custom_call_target="tpu_custom_call" | custom-call | tf_op jit(solution)/shard_map/update/pallas_call | solution.py:656
  (3 shorter events, 0.0 us)
Async XLA Ops:
  0.6 13.4 %collective-permute-start.1 = (f32[96,1024]{1,0:T(8,128)}, f32[96,1024]{1,0:T(8,128)S(1)}, u32[]{:S(2)}, u32[]{:S(2)}) collective-permute-start(f32[96,1024]{1,0:T(8,128)} %src_at.1), channel_id=1, source_target_pairs={{0,2},{1,3},{2,0},{3,1},{4,6},{5,7},{6,4},{7,5},{8,10},{9,11},{10,... | collective-permute-start | bytes 1179656 | tf_op jit(solution)/shard_map/ppermute | solution.py:469
  3.7 7.2 %collective-permute-start.3 = (f32[32,1024]{1,0:T(8,128)}, f32[32,1024]{1,0:T(8,128)S(1)}, u32[]{:S(2)}, u32[]{:S(2)}) collective-permute-start(f32[32,1024]{1,0:T(8,128)} %bitcast.9), channel_id=1, source_target_pairs={{0,4},{1,5},{2,6},{3,7},{4,0},{5,1},{6,2},{7,3},{8,12},{9,13},{10,... | collective-permute-start | bytes 393224 | tf_op jit(solution)/shard_map/ppermute | solution.py:469
  5.2 9.8 %collective-permute-start.6 = (f32[32,1024]{1,0:T(8,128)}, f32[32,1024]{1,0:T(8,128)S(1)}, u32[]{:S(2)}, u32[]{:S(2)}) collective-permute-start(f32[32,1024]{1,0:T(8,128)} %bitcast.10), channel_id=1, source_target_pairs={{0,12},{1,13},{2,14},{3,15},{4,8},{5,9},{6,10},{7,11},{8,4},{9,5},... | collective-permute-start | bytes 393224 | tf_op jit(solution)/shard_map/ppermute | solution.py:469
  7.7 11.7 %collective-permute-start.5 = (f32[32,1024]{1,0:T(8,128)}, f32[32,1024]{1,0:T(8,128)S(1)}, u32[]{:S(2)}, u32[]{:S(2)}) collective-permute-start(f32[32,1024]{1,0:T(8,128)} %bitcast.11), channel_id=1, source_target_pairs={{0,8},{1,9},{2,10},{3,11},{4,12},{5,13},{6,14},{7,15},{8,0},{9,1},... | collective-permute-start | bytes 393224 | tf_op jit(solution)/shard_map/ppermute | solution.py:469
  10.3 3.7 %collective-permute-start.2 = (f32[8,128]{1,0:T(8,128)S(1)}, f32[8,128]{1,0:T(8,128)S(1)}, u32[]{:S(2)}, u32[]{:S(2)}) collective-permute-start(f32[8,128]{1,0:T(8,128)S(1)} %get-tuple-element.38), channel_id=1, source_target_pairs={{0,2},{1,3},{2,0},{3,1},{4,6},{5,7},{6,4},{7,5},{8,10},{9,11},{10,... | collective-permute-start | bytes 12296 | tf_op jit(solution)/shard_map/ppermute | solution.py:469
  10.9 9.1 %collective-permute-start = (f32[104,1536]{1,0:T(8,128)S(1)}, f32[104,1536]{1,0:T(8,128)S(1)}, u32[]{:S(2)}, u32[]{:S(2)}) collective-permute-start(f32[104,1536]{1,0:T(8,128)S(1)} %get-tuple-element.37.a_0_), channel_id=1, source_target_pairs={{0,1},{1,0},{2,3},{3,2},{4,5},{5,4},{6,7},{7,6},{8,9},{9,8},{10,11... | collective-permute-start | bytes 1916936 | tf_op jit(solution)/shard_map/ppermute | solution.py:469
  14.6 5.4 %collective-permute-start.4 = (f32[104,1536]{1,0:T(8,128)S(1)}, f32[104,1536]{1,0:T(8,128)S(1)}, u32[]{:S(2)}, u32[]{:S(2)}) collective-permute-start(f32[104,1536]{1,0:T(8,128)S(1)} %neighbour.1.a_2_), channel_id=1, source_target_pairs={{0,1},{1,0},{2,3},{3,2},{4,5},{5,4},{6,7},{7,6},{8,9},{9,8},{10,11... | collective-permute-start | bytes 1916936 | tf_op jit(solution)/shard_map/ppermute | solution.py:469
  23.6 3.2 %collective-permute-start.9 = (f32[8,384]{1,0:T(8,128)S(1)}, f32[8,384]{1,0:T(8,128)S(1)}, u32[]{:S(2)}, u32[]{:S(2)}) collective-permute-start(f32[8,384]{1,0:T(8,128)S(1)} %get-tuple-element.56.a_0_), channel_id=1, source_target_pairs={{0,3},{1,2},{2,1},{3,0},{4,7},{5,6},{6,5},{7,4},{8,11},{9,10},{10,... | collective-permute-start | bytes 36872 | tf_op jit(solution)/shard_map/ppermute | solution.py:469
  23.7 3.8 %collective-permute-start.8 = (f32[8,384]{1,0:T(8,128)S(1)}, f32[8,384]{1,0:T(8,128)S(1)}, u32[]{:S(2)}, u32[]{:S(2)}) collective-permute-start(f32[8,384]{1,0:T(8,128)S(1)} %get-tuple-element.56.a_0_), channel_id=1, source_target_pairs={{0,2},{1,3},{2,0},{3,1},{4,6},{5,7},{6,4},{7,5},{8,10},{9,11},{10,... | collective-permute-start | bytes 36872 | tf_op jit(solution)/shard_map/ppermute | solution.py:469
  24.3 3.1 %collective-permute-start.7 = (f32[8,384]{1,0:T(8,128)S(1)}, f32[8,384]{1,0:T(8,128)S(1)}, u32[]{:S(2)}, u32[]{:S(2)}) collective-permute-start(f32[8,384]{1,0:T(8,128)S(1)} %get-tuple-element.56.a_0_), channel_id=1, source_target_pairs={{0,1},{1,0},{2,3},{3,2},{4,5},{5,4},{6,7},{7,6},{8,9},{9,8},{10,11... | collective-permute-start | bytes 36872 | tf_op jit(solution)/shard_map/ppermute | solution.py:469
  28.4 5.3 %collective-permute-start.11 = (f32[16,1536]{1,0:T(8,128)S(1)}, f32[16,1536]{1,0:T(8,128)S(1)}, u32[]{:S(2)}, u32[]{:S(2)}) collective-permute-start(f32[16,1536]{1,0:T(8,128)S(1)} %get-tuple-element.66), channel_id=1, source_target_pairs={{0,4},{1,5},{2,6},{3,7},{4,0},{5,1},{6,2},{7,3},{8,12},{9,13},{10,... | collective-permute-start | bytes 294920 | tf_op jit(solution)/shard_map/ppermute | solution.py:469
  28.5 6.7 %collective-permute-start.10 = (f32[16,1536]{1,0:T(8,128)S(1)}, f32[16,1536]{1,0:T(8,128)S(1)}, u32[]{:S(2)}, u32[]{:S(2)}) collective-permute-start(f32[16,1536]{1,0:T(8,128)S(1)} %get-tuple-element.61.a_5_), channel_id=1, source_target_pairs={{0,4},{1,5},{2,6},{3,7},{4,0},{5,1},{6,2},{7,3},{8,12},{9,13},{10,... | collective-permute-start | bytes 294920 | tf_op jit(solution)/shard_map/ppermute | solution.py:469
  33.7 7.9 %collective-permute-start.14 = (f32[16,1536]{1,0:T(8,128)S(1)}, f32[16,1536]{1,0:T(8,128)S(1)}, u32[]{:S(2)}, u32[]{:S(2)}) collective-permute-start(f32[16,1536]{1,0:T(8,128)S(1)} %combined.3.a_6_), channel_id=1, source_target_pairs={{0,8},{1,9},{2,10},{3,11},{4,12},{5,13},{6,14},{7,15},{8,0},{9,1},... | collective-permute-start | bytes 294920 | tf_op jit(solution)/shard_map/ppermute | solution.py:469
  35.2 8.3 %collective-permute-start.13 = (f32[16,1536]{1,0:T(8,128)S(1)}, f32[16,1536]{1,0:T(8,128)S(1)}, u32[]{:S(2)}, u32[]{:S(2)}) collective-permute-start(f32[16,1536]{1,0:T(8,128)S(1)} %combined.2.a_5_), channel_id=1, source_target_pairs={{0,8},{1,9},{2,10},{3,11},{4,12},{5,13},{6,14},{7,15},{8,0},{9,1},... | collective-permute-start | bytes 294920 | tf_op jit(solution)/shard_map/ppermute | solution.py:469
  37.3 7.5 %collective-permute-start.12 = (f32[32,1536]{1,0:T(8,128)S(1)}, f32[32,1536]{1,0:T(8,128)S(1)}, u32[]{:S(2)}, u32[]{:S(2)}) collective-permute-start(f32[32,1536]{1,0:T(8,128)S(1)} %sums.6.wait), channel_id=1, source_target_pairs={{0,4},{1,5},{2,6},{3,7},{4,0},{5,1},{6,2},{7,3},{8,12},{9,13},{10,... | collective-permute-start | bytes 589832 | tf_op jit(solution)/shard_map/ppermute | solution.py:469
  39.6 5.2 %copy-start = (f32[512]{0:T(512)S(1)}, f32[512]{0:T(512)}, u32[]{:S(2)}) copy-start(f32[512]{0:T(512)} %param.16) | copy-start | bytes 6148

commit v13 on v12

--- a/solution.py
+++ b/solution.py
@@ -491,11 +491,7 @@
     no_cost = pl.CostEstimate(flops=0, bytes_accessed=0, transcendentals=0)
     much = pl.CostEstimate(flops=16 * 10**9, bytes_accessed=0, transcendentals=0)
 
-    ynb = crossed(particle_fourier, 2)
-    anywhere = pl.BlockSpec(memory_space=pl.ANY)
-    ynb = crossed(particle_fourier, 2)
-    anywhere = pl.BlockSpec(memory_space=pl.ANY)
-    def gated(arrays, waits, cost):
+    def gated(arrays, cost, waits=()):
         return pl.pallas_call(
             lambda *a: None,
             out_shape=tuple(jax.ShapeDtypeStruct(x.shape, x.dtype) for x in arrays),
@@ -510,7 +506,13 @@
     ynb = crossed(particle_fourier, 2)
     anywhere = pl.BlockSpec(memory_space=pl.ANY)
     ynb = crossed(particle_fourier, 2)
-    refs = [refs_own] + [crossed(refs_own, TEAM * n) for n in range(1, blocks)]
+    anywhere = pl.BlockSpec(memory_space=pl.ANY)
+    ynb = crossed(particle_fourier, 2)
+    anywhere = pl.BlockSpec(memory_space=pl.ANY)
+    ynb = crossed(particle_fourier, 2)
+    refs = {0: refs_own, 1: crossed(refs_own, TEAM)}
+    for n in range(2, blocks, 2):
+        refs[n] = crossed(refs_own, TEAM * n)
     own_facts = (
         particle_fourier,
         defocus.reshape(1, slots),
@@ -535,6 +537,7 @@
         name="own",
     )(*(pltpu.with_memory_space_constraint(x, pltpu.HBM) for x in own_facts), live_count)
     cnb = crossed(own, 1)
+    ynb_facts = crossed(facts, 2)
     lanes = 3 * slots
     bf16 = jnp.bfloat16
     early = 2
@@ -566,6 +569,10 @@
         compiler_params=params(8),
         name="early",
     )(pltpu.with_memory_space_constraint(refs_own, pltpu.HBM), refs[1])
+    for n in range(2, blocks, 2):
+        (refs[n],) = gated([refs[n]], no_cost, [ynb_facts, prepared[2]])
+        refs[n + 1] = crossed(refs[n], TEAM)
+    refs = [refs[n] for n in range(blocks)]
     ynb_prepared = pl.pallas_call(
         neighbour_kernel,
         out_shape=jax.ShapeDtypeStruct((slots + 8, width + freq), f32),
@@ -574,18 +581,14 @@
         compiler_params=params(6),
         cost_estimate=no_cost,
         name="neighbour",
-    )(ynb, crossed(facts, 2), inverse_noise, prepared[2])
+    )(ynb, ynb_facts, inverse_noise, prepared[2])
     cynb = crossed(ynb_prepared, 1)
 
-    late = blocks - early
-    outs = call(
-        middle_kernel,
-        refs[early:],
-        block_shapes * late,
-        "middle",
-        4 + 2 * blocks,
-        much,
-    )
+    outs = []
+    for n in range(early, blocks):
+        outs += call(
+            middle_kernel, [refs[n]], block_shapes, "middle", 6, much if n == blocks - 1 else None
+        )
     prepared = (*prepared, *outs)
     deep = 3 * MAIN + 128
     top_rows = -(-blocks // 8) * 8
@@ -625,18 +628,6 @@
             compiler_params=params(4),
             name="combined",
         )(mine, other, wait)
-
-    def gated(arrays, cost):
-        return pl.pallas_call(
-            lambda *a: None,
-            out_shape=tuple(jax.ShapeDtypeStruct(x.shape, x.dtype) for x in arrays),
-            in_specs=[anywhere] * len(arrays),
-            out_specs=(anywhere,) * len(arrays),
-            input_output_aliases={n: n for n in range(len(arrays))},
-            compiler_params=params(1),
-            cost_estimate=cost,
-            name="gate",
-        )(*arrays)
 
     whole, cut = (0, per), (0, per // 2, per)
     far = []

time: 45.6 us -> 46.3 us (1.015)
  starting transfers between devices: 16.1 us -> 18.2 us
  waiting for transfers between devices: 15.1 us -> 13.5 us
    ppermute x15, starting transfers between devices: 16.1 us -> 18.2 us  [crossed(): return lax.ppermute(block, 'dom', [(i, i ^ mask) for i in range(size)])]
    ppermute x15, waiting for transfers between devices: 15.1 us -> 13.5 us  [crossed(): return lax.ppermute(block, 'dom', [(i, i ^ mask) for i in range(size)])]
    pallas_call x2 -> x3, Pallas kernels: 4.18 us -> 4.24 us  [call(): pl.pallas_call(kernel, cost_estimate=cost, out_shape=tuple(out_shape), in...]
  transfers between devices with their start and end apart: 15 -> 15, of which waited for: 9 -> 8; matrix products, arithmetic and copies ran while one was open for 0% -> 0% of each run, Pallas kernels for 17% -> 17%
where the time goes in v13:
time: 46.3 us; the launch traced here: 46.1 us
  starting transfers between devices  18.2 us (39%)
  waiting for transfers between devices  13.5 us (29%)
  Pallas kernels  13 us (28%)
  between operations  1.37 us (3%)
    ppermute x15, starting transfers between devices, crossed(): return lax.ppermute(block, 'dom', [(i, i ^ mask) for i in range(size)])  18.2 us
    ppermute x15, waiting for transfers between devices, crossed(): return lax.ppermute(block, 'dom', [(i, i ^ mask) for i in range(size)])  13.5 us
    pallas_call x4, Pallas kernels, sums(): pl.pallas_call(lambda *a: sum_kernel(n, cuts, last, len(waits), *a), out_...  4.39 us
    pallas_call x3, Pallas kernels, call(): pl.pallas_call(kernel, cost_estimate=cost, out_shape=tuple(out_shape), in...  4.24 us
    pallas_call x1, Pallas kernels, on_device(): pl.pallas_call(own_kernel, out_shape=(jax.ShapeDtypeStruct((slots + 8, wi...  1.83 us
    pallas_call x1, Pallas kernels, on_device(): pl.pallas_call(early_kernel, out_shape=tuple(block_shapes * early), in_sp...  1.16 us
  transfers between devices with their start and end apart: 15, of which 8 were waited for; matrix products, arithmetic and copies ran while one was open for 0% of the time, Pallas kernels for 17%

profile of v13, /device:TPU:0, one launch (start us, length us, event | category | flops | bytes accessed | tf_op | source)
XLA Modules:
  0.0 46.1 jit_solution(13407492057361063797)
XLA Ops:
  0.6 3.0 %collective-permute-start.1 = (f32[96,1024]{1,0:T(8,128)}, f32[96,1024]{1,0:T(8,128)S(1)}, u32[]{:S(2)}, u32[]{:S(2)}) collective-permute-start(f32[96,1024]{1,0:T(8,128)} %src_at.1), channel_id=1, source_target_pairs={{0,2},{1,3},{2,0},{3,1},{4,6},{5,7},{6,4},{7,5},{8,10},{9,11},{10,... | collective-permute-start | bytes 1179656 | tf_op jit(solution)/shard_map/ppermute | solution.py:469
  3.7 1.6 %collective-permute-start.3 = (f32[32,1024]{1,0:T(8,128)}, f32[32,1024]{1,0:T(8,128)S(1)}, u32[]{:S(2)}, u32[]{:S(2)}) collective-permute-start(f32[32,1024]{1,0:T(8,128)} %bitcast.9), channel_id=1, source_target_pairs={{0,4},{1,5},{2,6},{3,7},{4,0},{5,1},{6,2},{7,3},{8,12},{9,13},{10,... | collective-permute-start | bytes 393224 | tf_op jit(solution)/shard_map/ppermute | solution.py:469
  5.2 2.6 %collective-permute-start.5 = (f32[32,1024]{1,0:T(8,128)}, f32[32,1024]{1,0:T(8,128)S(1)}, u32[]{:S(2)}, u32[]{:S(2)}) collective-permute-start(f32[32,1024]{1,0:T(8,128)} %bitcast.10), channel_id=1, source_target_pairs={{0,8},{1,9},{2,10},{3,11},{4,12},{5,13},{6,14},{7,15},{8,0},{9,1},... | collective-permute-start | bytes 393224 | tf_op jit(solution)/shard_map/ppermute | solution.py:469
  8.5 1.8 %own.1 = (f32[104,1536]{1,0:T(8,128)S(1)}, f32[8,128]{1,0:T(8,128)S(1)}, f32[128,512]{1,0:T(8,128)S(1)}) custom-call(f32[96,1024]{1,0:T(8,128)} %src_at.1, f32[1,96]{1,0:T(1,128)} %bitcast.14, s32[2,96]{1,0:T(2,128)} %bitcast.13, s32[1,96]{1,0:T(1,128)} %bitcast.15, s32[1,96]{1,0:T(1,128)} %bitcast.16, f32[128,512]{1,0:T(8,128)} %noise_at.1, ...), custom_call_target="tpu_custom_call" | custom-call | tf_op jit(solution)/shard_map/own/pallas_call | solution.py:524
  10.3 0.6 %collective-permute-start.2 = (f32[8,128]{1,0:T(8,128)S(1)}, f32[8,128]{1,0:T(8,128)S(1)}, u32[]{:S(2)}, u32[]{:S(2)}) collective-permute-start(f32[8,128]{1,0:T(8,128)S(1)} %get-tuple-element.38), channel_id=1, source_target_pairs={{0,2},{1,3},{2,0},{3,1},{4,6},{5,7},{6,4},{7,5},{8,10},{9,11},{10,... | collective-permute-start | bytes 12296 | tf_op jit(solution)/shard_map/ppermute | solution.py:469
  10.9 0.0 collective-permute-done.3.near
  10.9 1.2 %early.1 = (bf16[288,1024]{1,0:T(8,128)(2,1)S(1)}, bf16[288,1024]{1,0:T(8,128)(2,1)S(1)}, bf16[32,512]{1,0:T(8,128)(2,1)S(1)}, bf16[32,512]{1,0:T(8,128)(2,1)S(1...) custom-call(f32[32,1024]{1,0:T(8,128)} %bitcast.11, ...), custom_call_target="tpu_custom_call" | custom-call | tf_op jit(solution)/shard_map/early/pallas_call | solution.py:563
  12.1 1.9 %collective-permute-done.2.facts.a_1_ = f32[8,128]{1,0:T(8,128)S(1)} collective-permute-done((f32[8,128]{1,0:T(8,128)S(1)}, f32[8,128]{1,0:T(8,128)S(1)}, u32[]{:S(2)}, u32[]{:S(2)}) %collective-permute-start.2) | collective-permute-done | bytes 4128 | tf_op jit(solution)/shard_map/ppermute | solution.py:469
  14.0 0.0 collective-permute-done.5.a_0_
  14.0 0.9 %collective-permute-start.6 = (f32[32,1024]{1,0:T(8,128)S(1)}, f32[32,1024]{1,0:T(8,128)S(1)}, u32[]{:S(2)}, u32[]{:S(2)}) collective-permute-start(f32[32,1024]{1,0:T(8,128)S(1)} %gate.2.rest_0_), channel_id=1, source_target_pairs={{0,4},{1,5},{2,6},{3,7},{4,0},{5,1},{6,2},{7,3},{8,12},{9,13},{10,... | collective-permute-start | bytes 393224 | tf_op jit(solution)/shard_map/ppermute | solution.py:469
  14.9 0.0 collective-permute-start
  14.9 0.3 middle.2
  15.2 0.0 collective-permute-done.1.src
  15.2 0.6 %neighbour.1.a_2_ = f32[104,1536]{1,0:T(8,128)S(1)} custom-call(f32[96,1024]{1,0:T(8,128)S(1)} %collective-permute-done.1.src, f32[8,128]{1,0:T(8,128)S(1)} %collective-permute-done.2.facts.a_1_, f32[128,512]{1,0:T(8,128)S(1)} %get-tuple-element.39.inverse_noise, bf16[32,512]{1,0:T(8,128)(2,1)S(1)} %get-tuple-element.40.wait.a_2_.a_6_), custom_call_target="tpu_custom_call" | custom-call | tf_op jit(solution)/shard_map/neighbour/pallas_call | solution.py:576
  15.9 0.6 %collective-permute-start.4 = (f32[104,1536]{1,0:T(8,128)S(1)}, f32[104,1536]{1,0:T(8,128)S(1)}, u32[]{:S(2)}, u32[]{:S(2)}) collective-permute-start(f32[104,1536]{1,0:T(8,128)S(1)} %neighbour.1.a_2_), channel_id=1, source_target_pairs={{0,1},{1,0},{2,3},{3,2},{4,5},{5,4},{6,7},{7,6},{8,9},{9,8},{10,11... | collective-permute-start | bytes 1916936 | tf_op jit(solution)/shard_map/ppermute | solution.py:469
  16.4 2.5 %collective-permute-done.6.rest_0_ = f32[32,1024]{1,0:T(8,128)S(1)} collective-permute-done((f32[32,1024]{1,0:T(8,128)S(1)}, f32[32,1024]{1,0:T(8,128)S(1)}, u32[]{:S(2)}, u32[]{:S(2)}) %collective-permute-start.6) | collective-permute-done | bytes 131104 | tf_op jit(solution)/shard_map/ppermute | solution.py:469
  19.0 0.3 middle.3
  19.3 0.0 collective-permute-done.a_1_
  19.3 0.0 collective-permute-done.4.a_3_
  19.3 3.6 %late.1 = (f32[9,32,288]{2,1,0:T(8,128)S(1)}, f32[9,32,288]{2,1,0:T(8,128)S(1)}, f32[9,32,288]{2,1,0:T(8,128)S(1)}, f32[9,32,288]{2,1,0:T(8,128)S(1)}, bf16[896,...) custom-call(f32[104,1536]{1,0:T(8,128)S(1)} %get-tuple-element.37.a_0_, ...), custom_call_target="tpu_custom_call" | custom-call | tf_op jit(solution)/shard_map/late/pallas_call | solution.py:552
  22.9 0.3 collective-permute-start.9
  23.3 0.6 %collective-permute-start.8 = (f32[8,384]{1,0:T(8,128)S(1)}, f32[8,384]{1,0:T(8,128)S(1)}, u32[]{:S(2)}, u32[]{:S(2)}) collective-permute-start(f32[8,384]{1,0:T(8,128)S(1)} %get-tuple-element.56.a_0_), channel_id=1, source_target_pairs={{0,2},{1,3},{2,0},{3,1},{4,6},{5,7},{6,4},{7,5},{8,10},{9,11},{10,... | collective-permute-start | bytes 36872 | tf_op jit(solution)/shard_map/ppermute | solution.py:469
  23.9 1.0 %collective-permute-start.7 = (f32[8,384]{1,0:T(8,128)S(1)}, f32[8,384]{1,0:T(8,128)S(1)}, u32[]{:S(2)}, u32[]{:S(2)}) collective-permute-start(f32[8,384]{1,0:T(8,128)S(1)} %get-tuple-element.56.a_0_), channel_id=1, source_target_pairs={{0,1},{1,0},{2,3},{3,2},{4,5},{5,4},{6,7},{7,6},{8,9},{9,8},{10,11... | collective-permute-start | bytes 36872 | tf_op jit(solution)/shard_map/ppermute | solution.py:469
  24.9 1.3 %collective-permute-done.9.a_3_ = f32[8,384]{1,0:T(8,128)S(1)} collective-permute-done((f32[8,384]{1,0:T(8,128)S(1)}, f32[8,384]{1,0:T(8,128)S(1)}, u32[]{:S(2)}, u32[]{:S(2)}) %collective-permute-start.9) | collective-permute-done | bytes 12320 | tf_op jit(solution)/shard_map/ppermute | solution.py:469
  26.1 0.9 %collective-permute-done.8.a_2_ = f32[8,384]{1,0:T(8,128)S(1)} collective-permute-done((f32[8,384]{1,0:T(8,128)S(1)}, f32[8,384]{1,0:T(8,128)S(1)}, u32[]{:S(2)}, u32[]{:S(2)}) %collective-permute-start.8) | collective-permute-done | bytes 12320 | tf_op jit(solution)/shard_map/ppermute | solution.py:469
  27.0 0.0 collective-permute-done.7.a_1_
  27.0 0.9 %sums.4 = (f32[16,1536]{1,0:T(8,128)S(1)}, f32[16,1536]{1,0:T(8,128)S(1)}) custom-call(f32[8,384]{1,0:T(8,128)S(1)} %get-tuple-element.56.a_0_, f32[8,384]{1,0:T(8,128)S(1)} %collective-permute-done.7.a_1_, f32[8,384]{1,0:T(8,128)S(1)} %collective-permute-done.8.a_2_, f32[8,384]{1,0:T(8,128)S(1)} %collective-permute-done.9.a_3_, ...), custom_call_target="tpu_custom_call" | custom-call | tf_op jit(solution)/shard_map/sums/pallas_call | solution.py:613
  27.9 0.7 %collective-permute-start.11 = (f32[16,1536]{1,0:T(8,128)S(1)}, f32[16,1536]{1,0:T(8,128)S(1)}, u32[]{:S(2)}, u32[]{:S(2)}) collective-permute-start(f32[16,1536]{1,0:T(8,128)S(1)} %get-tuple-element.66), channel_id=1, source_target_pairs={{0,4},{1,5},{2,6},{3,7},{4,0},{5,1},{6,2},{7,3},{8,12},{9,13},{10,... | collective-permute-start | bytes 294920 | tf_op jit(solution)/shard_map/ppermute | solution.py:469
  28.6 1.3 %collective-permute-start.10 = (f32[16,1536]{1,0:T(8,128)S(1)}, f32[16,1536]{1,0:T(8,128)S(1)}, u32[]{:S(2)}, u32[]{:S(2)}) collective-permute-start(f32[16,1536]{1,0:T(8,128)S(1)} %get-tuple-element.61.a_5_), channel_id=1, source_target_pairs={{0,4},{1,5},{2,6},{3,7},{4,0},{5,1},{6,2},{7,3},{8,12},{9,13},{10,... | collective-permute-start | bytes 294920 | tf_op jit(solution)/shard_map/ppermute | solution.py:469
  30.0 0.9 %sums.5 = (f32[16,1536]{1,0:T(8,128)S(1)}, f32[16,1536]{1,0:T(8,128)S(1)}) custom-call(f32[8,384]{1,0:T(8,128)S(1)} %get-tuple-element.56.a_0_, f32[8,384]{1,0:T(8,128)S(1)} %collective-permute-done.7.a_1_, f32[8,384]{1,0:T(8,128)S(1)} %collective-permute-done.8.a_2_, f32[8,384]{1,0:T(8,128)S(1)} %collective-permute-done.9.a_3_, ...), custom_call_target="tpu_custom_call" | custom-call | tf_op jit(solution)/shard_map/sums/pallas_call | solution.py:613
  30.9 1.0 %sums.6.wait = f32[32,1536]{1,0:T(8,128)S(1)} custom-call(f32[8,384]{1,0:T(8,128)S(1)} %get-tuple-element.56.a_0_, f32[8,384]{1,0:T(8,128)S(1)} %collective-permute-done.7.a_1_, f32[8,384]{1,0:T(8,128)S(1)} %collective-permute-done.8.a_2_, f32[8,384]{1,0:T(8,128)S(1)} %collective-permute-done.9.a_3_, f32[8,384]{1,0:T(8,128)S(1)} %get-tuple-element.57.a_4_, ...), custom_call_target="tpu_custom_call" | custom-call | tf_op jit(solution)/shard_map/sums/pallas_call | solution.py:613
  31.9 1.6 %collective-permute-done.11.b = f32[16,1536]{1,0:T(8,128)S(1)} collective-permute-done((f32[16,1536]{1,0:T(8,128)S(1)}, f32[16,1536]{1,0:T(8,128)S(1)}, u32[]{:S(2)}, u32[]{:S(2)}) %collective-permute-start.11) | collective-permute-done | bytes 98336 | tf_op jit(solution)/shard_map/ppermute | solution.py:469
  33.5 2.7 %collective-permute-start.14 = (f32[16,1536]{1,0:T(8,128)S(1)}, f32[16,1536]{1,0:T(8,128)S(1)}, u32[]{:S(2)}, u32[]{:S(2)}) collective-permute-start(f32[16,1536]{1,0:T(8,128)S(1)} %combined.3.a_6_), channel_id=1, source_target_pairs={{0,8},{1,9},{2,10},{3,11},{4,12},{5,13},{6,14},{7,15},{8,0},{9,1},... | collective-permute-start | bytes 294920 | tf_op jit(solution)/shard_map/ppermute | solution.py:469
  36.2 0.0 collective-permute-done.10.b
  36.2 1.1 %collective-permute-start.13 = (f32[16,1536]{1,0:T(8,128)S(1)}, f32[16,1536]{1,0:T(8,128)S(1)}, u32[]{:S(2)}, u32[]{:S(2)}) collective-permute-start(f32[16,1536]{1,0:T(8,128)S(1)} %combined.2.a_5_), channel_id=1, source_target_pairs={{0,8},{1,9},{2,10},{3,11},{4,12},{5,13},{6,14},{7,15},{8,0},{9,1},... | collective-permute-start | bytes 294920 | tf_op jit(solution)/shard_map/ppermute | solution.py:469
  37.3 1.3 %collective-permute-start.12 = (f32[32,1536]{1,0:T(8,128)S(1)}, f32[32,1536]{1,0:T(8,128)S(1)}, u32[]{:S(2)}, u32[]{:S(2)}) collective-permute-start(f32[32,1536]{1,0:T(8,128)S(1)} %sums.6.wait), channel_id=1, source_target_pairs={{0,4},{1,5},{2,6},{3,7},{4,0},{5,1},{6,2},{7,3},{8,12},{9,13},{10,... | collective-permute-start | bytes 589832 | tf_op jit(solution)/shard_map/ppermute | solution.py:469
  38.5 1.6 %sums.7 = (f32[32,1536]{1,0:T(8,128)S(1)}, f32[2,96]{1,0:T(2,128)}) custom-call(f32[8,384]{1,0:T(8,128)S(1)} %get-tuple-element.56.a_0_, f32[8,384]{1,0:T(8,128)S(1)} %collective-permute-done.7.a_1_, f32[8,384]{1,0:T(8,128)S(1)} %collective-permute-done.8.a_2_, f32[8,384]{1,0:T(8,128)S(1)} %collective-permute-done.9.a_3_, ...), custom_call_target="tpu_custom_call" | custom-call | tf_op jit(solution)/shard_map/sums/pallas_call | solution.py:613
  40.1 0.0 copy-start
  40.1 2.6 %collective-permute-done.14.a_1_ = f32[16,1536]{1,0:T(8,128)S(1)} collective-permute-done((f32[16,1536]{1,0:T(8,128)S(1)}, f32[16,1536]{1,0:T(8,128)S(1)}, u32[]{:S(2)}, u32[]{:S(2)}) %collective-permute-start.14) | collective-permute-done | bytes 98336 | tf_op jit(solution)/shard_map/ppermute | solution.py:469
  42.7 1.3 %collective-permute-done.13.a_0_ = f32[16,1536]{1,0:T(8,128)S(1)} collective-permute-done((f32[16,1536]{1,0:T(8,128)S(1)}, f32[16,1536]{1,0:T(8,128)S(1)}, u32[]{:S(2)}, u32[]{:S(2)}) %collective-permute-start.13) | collective-permute-done | bytes 98336 | tf_op jit(solution)/shard_map/ppermute | solution.py:469
  44.0 1.4 %collective-permute-done.12.a_1_ = f32[32,1536]{1,0:T(8,128)S(1)} collective-permute-done((f32[32,1536]{1,0:T(8,128)S(1)}, f32[32,1536]{1,0:T(8,128)S(1)}, u32[]{:S(2)}, u32[]{:S(2)}) %collective-permute-start.12) | collective-permute-done | bytes 196640 | tf_op jit(solution)/shard_map/ppermute | solution.py:469
  45.4 0.0 copy-done
  45.4 0.7 %update.1 = f32[32,1024]{1,0:T(8,128)} custom-call(f32[32,1536]{1,0:T(8,128)S(1)} %get-tuple-element.69.a_0_, f32[32,1536]{1,0:T(8,128)S(1)} %collective-permute-done.12.a_1_, f32[16,1536]{1,0:T(8,128)S(1)} %get-tuple-element.70.a_2_, f32[16,1536]{1,0:T(8,128)S(1)} %get-tuple-element.71.a_3_, f32[1,512]{1,0:T(1,128)S(1)} %bitcast.8), custom_call_target="tpu_custom_call" | custom-call | tf_op jit(solution)/shard_map/update/pallas_call | solution.py:647
  (4 shorter events, 0.0 us)
Async XLA Ops:
  0.6 14.6 %collective-permute-start.1 = (f32[96,1024]{1,0:T(8,128)}, f32[96,1024]{1,0:T(8,128)S(1)}, u32[]{:S(2)}, u32[]{:S(2)}) collective-permute-start(f32[96,1024]{1,0:T(8,128)} %src_at.1), channel_id=1, source_target_pairs={{0,2},{1,3},{2,0},{3,1},{4,6},{5,7},{6,4},{7,5},{8,10},{9,11},{10,... | collective-permute-start | bytes 1179656 | tf_op jit(solution)/shard_map/ppermute | solution.py:469
  3.7 7.2 %collective-permute-start.3 = (f32[32,1024]{1,0:T(8,128)}, f32[32,1024]{1,0:T(8,128)S(1)}, u32[]{:S(2)}, u32[]{:S(2)}) collective-permute-start(f32[32,1024]{1,0:T(8,128)} %bitcast.9), channel_id=1, source_target_pairs={{0,4},{1,5},{2,6},{3,7},{4,0},{5,1},{6,2},{7,3},{8,12},{9,13},{10,... | collective-permute-start | bytes 393224 | tf_op jit(solution)/shard_map/ppermute | solution.py:469
  5.2 8.8 %collective-permute-start.5 = (f32[32,1024]{1,0:T(8,128)}, f32[32,1024]{1,0:T(8,128)S(1)}, u32[]{:S(2)}, u32[]{:S(2)}) collective-permute-start(f32[32,1024]{1,0:T(8,128)} %bitcast.10), channel_id=1, source_target_pairs={{0,8},{1,9},{2,10},{3,11},{4,12},{5,13},{6,14},{7,15},{8,0},{9,1},... | collective-permute-start | bytes 393224 | tf_op jit(solution)/shard_map/ppermute | solution.py:469
  10.3 3.7 %collective-permute-start.2 = (f32[8,128]{1,0:T(8,128)S(1)}, f32[8,128]{1,0:T(8,128)S(1)}, u32[]{:S(2)}, u32[]{:S(2)}) collective-permute-start(f32[8,128]{1,0:T(8,128)S(1)} %get-tuple-element.38), channel_id=1, source_target_pairs={{0,2},{1,3},{2,0},{3,1},{4,6},{5,7},{6,4},{7,5},{8,10},{9,11},{10,... | collective-permute-start | bytes 12296 | tf_op jit(solution)/shard_map/ppermute | solution.py:469
  14.0 5.0 %collective-permute-start.6 = (f32[32,1024]{1,0:T(8,128)S(1)}, f32[32,1024]{1,0:T(8,128)S(1)}, u32[]{:S(2)}, u32[]{:S(2)}) collective-permute-start(f32[32,1024]{1,0:T(8,128)S(1)} %gate.2.rest_0_), channel_id=1, source_target_pairs={{0,4},{1,5},{2,6},{3,7},{4,0},{5,1},{6,2},{7,3},{8,12},{9,13},{10,... | collective-permute-start | bytes 393224 | tf_op jit(solution)/shard_map/ppermute | solution.py:469
  14.9 4.4 %collective-permute-start = (f32[104,1536]{1,0:T(8,128)S(1)}, f32[104,1536]{1,0:T(8,128)S(1)}, u32[]{:S(2)}, u32[]{:S(2)}) collective-permute-start(f32[104,1536]{1,0:T(8,128)S(1)} %get-tuple-element.37.a_0_), channel_id=1, source_target_pairs={{0,1},{1,0},{2,3},{3,2},{4,5},{5,4},{6,7},{7,6},{8,9},{9,8},{10,11... | collective-permute-start | bytes 1916936 | tf_op jit(solution)/shard_map/ppermute | solution.py:469
  15.9 3.4 %collective-permute-start.4 = (f32[104,1536]{1,0:T(8,128)S(1)}, f32[104,1536]{1,0:T(8,128)S(1)}, u32[]{:S(2)}, u32[]{:S(2)}) collective-permute-start(f32[104,1536]{1,0:T(8,128)S(1)} %neighbour.1.a_2_), channel_id=1, source_target_pairs={{0,1},{1,0},{2,3},{3,2},{4,5},{5,4},{6,7},{7,6},{8,9},{9,8},{10,11... | collective-permute-start | bytes 1916936 | tf_op jit(solution)/shard_map/ppermute | solution.py:469
  22.9 3.2 %collective-permute-start.9 = (f32[8,384]{1,0:T(8,128)S(1)}, f32[8,384]{1,0:T(8,128)S(1)}, u32[]{:S(2)}, u32[]{:S(2)}) collective-permute-start(f32[8,384]{1,0:T(8,128)S(1)} %get-tuple-element.56.a_0_), channel_id=1, source_target_pairs={{0,3},{1,2},{2,1},{3,0},{4,7},{5,6},{6,5},{7,4},{8,11},{9,10},{10,... | collective-permute-start | bytes 36872 | tf_op jit(solution)/shard_map/ppermute | solution.py:469
  23.3 3.7 %collective-permute-start.8 = (f32[8,384]{1,0:T(8,128)S(1)}, f32[8,384]{1,0:T(8,128)S(1)}, u32[]{:S(2)}, u32[]{:S(2)}) collective-permute-start(f32[8,384]{1,0:T(8,128)S(1)} %get-tuple-element.56.a_0_), channel_id=1, source_target_pairs={{0,2},{1,3},{2,0},{3,1},{4,6},{5,7},{6,4},{7,5},{8,10},{9,11},{10,... | collective-permute-start | bytes 36872 | tf_op jit(solution)/shard_map/ppermute | solution.py:469
  23.9 3.1 %collective-permute-start.7 = (f32[8,384]{1,0:T(8,128)S(1)}, f32[8,384]{1,0:T(8,128)S(1)}, u32[]{:S(2)}, u32[]{:S(2)}) collective-permute-start(f32[8,384]{1,0:T(8,128)S(1)} %get-tuple-element.56.a_0_), channel_id=1, source_target_pairs={{0,1},{1,0},{2,3},{3,2},{4,5},{5,4},{6,7},{7,6},{8,9},{9,8},{10,11... | collective-permute-start | bytes 36872 | tf_op jit(solution)/shard_map/ppermute | solution.py:469
  27.9 5.6 %collective-permute-start.11 = (f32[16,1536]{1,0:T(8,128)S(1)}, f32[16,1536]{1,0:T(8,128)S(1)}, u32[]{:S(2)}, u32[]{:S(2)}) collective-permute-start(f32[16,1536]{1,0:T(8,128)S(1)} %get-tuple-element.66), channel_id=1, source_target_pairs={{0,4},{1,5},{2,6},{3,7},{4,0},{5,1},{6,2},{7,3},{8,12},{9,13},{10,... | collective-permute-start | bytes 294920 | tf_op jit(solution)/shard_map/ppermute | solution.py:469
  28.6 7.5 %collective-permute-start.10 = (f32[16,1536]{1,0:T(8,128)S(1)}, f32[16,1536]{1,0:T(8,128)S(1)}, u32[]{:S(2)}, u32[]{:S(2)}) collective-permute-start(f32[16,1536]{1,0:T(8,128)S(1)} %get-tuple-element.61.a_5_), channel_id=1, source_target_pairs={{0,4},{1,5},{2,6},{3,7},{4,0},{5,1},{6,2},{7,3},{8,12},{9,13},{10,... | collective-permute-start | bytes 294920 | tf_op jit(solution)/shard_map/ppermute | solution.py:469
  33.5 9.2 %collective-permute-start.14 = (f32[16,1536]{1,0:T(8,128)S(1)}, f32[16,1536]{1,0:T(8,128)S(1)}, u32[]{:S(2)}, u32[]{:S(2)}) collective-permute-start(f32[16,1536]{1,0:T(8,128)S(1)} %combined.3.a_6_), channel_id=1, source_target_pairs={{0,8},{1,9},{2,10},{3,11},{4,12},{5,13},{6,14},{7,15},{8,0},{9,1},... | collective-permute-start | bytes 294920 | tf_op jit(solution)/shard_map/ppermute | solution.py:469
  36.2 7.8 %collective-permute-start.13 = (f32[16,1536]{1,0:T(8,128)S(1)}, f32[16,1536]{1,0:T(8,128)S(1)}, u32[]{:S(2)}, u32[]{:S(2)}) collective-permute-start(f32[16,1536]{1,0:T(8,128)S(1)} %combined.2.a_5_), channel_id=1, source_target_pairs={{0,8},{1,9},{2,10},{3,11},{4,12},{5,13},{6,14},{7,15},{8,0},{9,1},... | collective-permute-start | bytes 294920 | tf_op jit(solution)/shard_map/ppermute | solution.py:469
  37.3 8.1 %collective-permute-start.12 = (f32[32,1536]{1,0:T(8,128)S(1)}, f32[32,1536]{1,0:T(8,128)S(1)}, u32[]{:S(2)}, u32[]{:S(2)}) collective-permute-start(f32[32,1536]{1,0:T(8,128)S(1)} %sums.6.wait), channel_id=1, source_target_pairs={{0,4},{1,5},{2,6},{3,7},{4,0},{5,1},{6,2},{7,3},{8,12},{9,13},{10,... | collective-permute-start | bytes 589832 | tf_op jit(solution)/shard_map/ppermute | solution.py:469
  40.1 5.3 %copy-start = (f32[512]{0:T(512)S(1)}, f32[512]{0:T(512)}, u32[]{:S(2)}) copy-start(f32[512]{0:T(512)} %param.16) | copy-start | bytes 6148

commit v14 on v13

--- a/solution.py
+++ b/solution.py
@@ -636,13 +636,14 @@
         handed = sums(n + 1, cut)
         mine = sums(n, cut, waits=handed[:1])
         if n == 2:
-            (near,) = sums(1, whole, waits=mine[:1])
-        joined = [combined(x, crossed(y, TEAM), near) for x, y in zip(mine, handed)]
+            near = sums(1, cut, waits=mine[:1])
+        joined = [combined(x, crossed(y, TEAM), near[0]) for x, y in zip(mine, handed)]
         far.extend(crossed(x, TEAM * n) for x in joined)
         waits.extend(joined)
     own_part, shift = sums(0, whole, last=True, waits=waits)
-    far = [crossed(near, TEAM), *gated(far, much)]
-    row_cuts = [whole] + [cut] * (len(far) // 2)
+    near = gated([crossed(x, TEAM) for x in near], much, [shift])
+    far = [*near, *far]
+    row_cuts = [cut] * (len(far) // 2)
 
     refs_new = pl.pallas_call(
         lambda *a: final_kernel(row_cuts, *a),

time: 46.3 us -> 46.6 us (level)
  waiting for transfers between devices: 13.5 us -> 11.9 us
  starting transfers between devices: 18.2 us -> 19.5 us
  local copies, waits for them, and re-layouts: 0.01 us -> 0.68 us
    ppermute x15 -> x16, waiting for transfers between devices: 13.5 us -> 11.9 us  [crossed(): return lax.ppermute(block, 'dom', [(i, i ^ mask) for i in range(size)])]
    ppermute x15 -> x16, starting transfers between devices: 18.2 us -> 19.5 us  [crossed(): return lax.ppermute(block, 'dom', [(i, i ^ mask) for i in range(size)])]
    unnamed x2 -> x4, local copies, waits for them, and re-layouts: 0.01 us -> 0.68 us
  transfers between devices with their start and end apart: 15 -> 16, of which waited for: 8 -> 7; matrix products, arithmetic and copies ran while one was open for 0% -> 0% of each run, Pallas kernels for 17% -> 17%
where the time goes in v14:
time: 46.6 us; the launch traced here: 46.4 us
  starting transfers between devices  19.5 us (42%)
  Pallas kernels  13 us (28%)
  waiting for transfers between devices  11.9 us (26%)
  between operations  1.37 us (3%)
  local copies, waits for them, and re-layouts  0.68 us (1%)
    ppermute x16, starting transfers between devices, crossed(): return lax.ppermute(block, 'dom', [(i, i ^ mask) for i in range(size)])  19.5 us
    ppermute x16, waiting for transfers between devices, crossed(): return lax.ppermute(block, 'dom', [(i, i ^ mask) for i in range(size)])  11.9 us
    pallas_call x4, Pallas kernels, sums(): pl.pallas_call(lambda *a: sum_kernel(n, cuts, last, len(waits), *a), out_...  4.39 us
    pallas_call x3, Pallas kernels, call(): pl.pallas_call(kernel, cost_estimate=cost, out_shape=tuple(out_shape), in...  4.24 us
    pallas_call x1, Pallas kernels, on_device(): pl.pallas_call(own_kernel, out_shape=(jax.ShapeDtypeStruct((slots + 8, wi...  1.83 us
    pallas_call x1, Pallas kernels, on_device(): pl.pallas_call(early_kernel, out_shape=tuple(block_shapes * early), in_sp...  1.16 us
  transfers between devices with their start and end apart: 16, of which 7 were waited for; matrix products, arithmetic and copies ran while one was open for 0% of the time, Pallas kernels for 17%

profile of v14, /device:TPU:0, one launch (start us, length us, event | category | flops | bytes accessed | tf_op | source)
XLA Modules:
  0.0 46.4 jit_solution(10939808545193841046)
XLA Ops:
  0.6 3.0 %collective-permute-start.1 = (f32[96,1024]{1,0:T(8,128)}, f32[96,1024]{1,0:T(8,128)S(1)}, u32[]{:S(2)}, u32[]{:S(2)}) collective-permute-start(f32[96,1024]{1,0:T(8,128)} %src_at.1), channel_id=1, source_target_pairs={{0,2},{1,3},{2,0},{3,1},{4,6},{5,7},{6,4},{7,5},{8,10},{9,11},{10,... | collective-permute-start | bytes 1179656 | tf_op jit(solution)/shard_map/ppermute | solution.py:469
  3.7 1.6 %collective-permute-start.3 = (f32[32,1024]{1,0:T(8,128)}, f32[32,1024]{1,0:T(8,128)S(1)}, u32[]{:S(2)}, u32[]{:S(2)}) collective-permute-start(f32[32,1024]{1,0:T(8,128)} %bitcast.10), channel_id=1, source_target_pairs={{0,4},{1,5},{2,6},{3,7},{4,0},{5,1},{6,2},{7,3},{8,12},{9,13},{10,... | collective-permute-start | bytes 393224 | tf_op jit(solution)/shard_map/ppermute | solution.py:469
  5.2 2.6 %collective-permute-start.5 = (f32[32,1024]{1,0:T(8,128)}, f32[32,1024]{1,0:T(8,128)S(1)}, u32[]{:S(2)}, u32[]{:S(2)}) collective-permute-start(f32[32,1024]{1,0:T(8,128)} %bitcast.11), channel_id=1, source_target_pairs={{0,8},{1,9},{2,10},{3,11},{4,12},{5,13},{6,14},{7,15},{8,0},{9,1},... | collective-permute-start | bytes 393224 | tf_op jit(solution)/shard_map/ppermute | solution.py:469
  8.5 1.8 %own.1 = (f32[104,1536]{1,0:T(8,128)S(1)}, f32[8,128]{1,0:T(8,128)S(1)}, f32[128,512]{1,0:T(8,128)S(1)}) custom-call(f32[96,1024]{1,0:T(8,128)} %src_at.1, f32[1,96]{1,0:T(1,128)} %bitcast.15, s32[2,96]{1,0:T(2,128)} %bitcast.14, s32[1,96]{1,0:T(1,128)} %bitcast.16, s32[1,96]{1,0:T(1,128)} %bitcast.17, f32[128,512]{1,0:T(8,128)} %noise_at.1, ...), custom_call_target="tpu_custom_call" | custom-call | tf_op jit(solution)/shard_map/own/pallas_call | solution.py:524
  10.3 0.6 %collective-permute-start.2 = (f32[8,128]{1,0:T(8,128)S(1)}, f32[8,128]{1,0:T(8,128)S(1)}, u32[]{:S(2)}, u32[]{:S(2)}) collective-permute-start(f32[8,128]{1,0:T(8,128)S(1)} %get-tuple-element.40), channel_id=1, source_target_pairs={{0,2},{1,3},{2,0},{3,1},{4,6},{5,7},{6,4},{7,5},{8,10},{9,11},{10,... | collective-permute-start | bytes 12296 | tf_op jit(solution)/shard_map/ppermute | solution.py:469
  10.9 0.0 collective-permute-done.3.near
  10.9 1.2 %early.1 = (bf16[288,1024]{1,0:T(8,128)(2,1)S(1)}, bf16[288,1024]{1,0:T(8,128)(2,1)S(1)}, bf16[32,512]{1,0:T(8,128)(2,1)S(1)}, bf16[32,512]{1,0:T(8,128)(2,1)S(1...) custom-call(f32[32,1024]{1,0:T(8,128)} %bitcast.12, ...), custom_call_target="tpu_custom_call" | custom-call | tf_op jit(solution)/shard_map/early/pallas_call | solution.py:563
  12.1 1.9 %collective-permute-done.2.facts.a_1_ = f32[8,128]{1,0:T(8,128)S(1)} collective-permute-done((f32[8,128]{1,0:T(8,128)S(1)}, f32[8,128]{1,0:T(8,128)S(1)}, u32[]{:S(2)}, u32[]{:S(2)}) %collective-permute-start.2) | collective-permute-done | bytes 4128 | tf_op jit(solution)/shard_map/ppermute | solution.py:469
  14.0 0.0 collective-permute-done.5.a_0_
  14.0 0.9 %collective-permute-start.6 = (f32[32,1024]{1,0:T(8,128)S(1)}, f32[32,1024]{1,0:T(8,128)S(1)}, u32[]{:S(2)}, u32[]{:S(2)}) collective-permute-start(f32[32,1024]{1,0:T(8,128)S(1)} %gate.2.rest_0_), channel_id=1, source_target_pairs={{0,4},{1,5},{2,6},{3,7},{4,0},{5,1},{6,2},{7,3},{8,12},{9,13},{10,... | collective-permute-start | bytes 393224 | tf_op jit(solution)/shard_map/ppermute | solution.py:469
  14.9 0.0 collective-permute-start
  14.9 0.3 middle.2
  15.2 0.0 collective-permute-done.1.src
  15.2 0.6 %neighbour.1.a_2_ = f32[104,1536]{1,0:T(8,128)S(1)} custom-call(f32[96,1024]{1,0:T(8,128)S(1)} %collective-permute-done.1.src, f32[8,128]{1,0:T(8,128)S(1)} %collective-permute-done.2.facts.a_1_, f32[128,512]{1,0:T(8,128)S(1)} %get-tuple-element.41.inverse_noise, bf16[32,512]{1,0:T(8,128)(2,1)S(1)} %get-tuple-element.42.wait.a_2_.a_6_), custom_call_target="tpu_custom_call" | custom-call | tf_op jit(solution)/shard_map/neighbour/pallas_call | solution.py:576
  15.9 0.6 %collective-permute-start.4 = (f32[104,1536]{1,0:T(8,128)S(1)}, f32[104,1536]{1,0:T(8,128)S(1)}, u32[]{:S(2)}, u32[]{:S(2)}) collective-permute-start(f32[104,1536]{1,0:T(8,128)S(1)} %neighbour.1.a_2_), channel_id=1, source_target_pairs={{0,1},{1,0},{2,3},{3,2},{4,5},{5,4},{6,7},{7,6},{8,9},{9,8},{10,11... | collective-permute-start | bytes 1916936 | tf_op jit(solution)/shard_map/ppermute | solution.py:469
  16.4 2.5 %collective-permute-done.6.rest_0_ = f32[32,1024]{1,0:T(8,128)S(1)} collective-permute-done((f32[32,1024]{1,0:T(8,128)S(1)}, f32[32,1024]{1,0:T(8,128)S(1)}, u32[]{:S(2)}, u32[]{:S(2)}) %collective-permute-start.6) | collective-permute-done | bytes 131104 | tf_op jit(solution)/shard_map/ppermute | solution.py:469
  19.0 0.3 middle.3
  19.3 0.0 collective-permute-done.a_1_
  19.3 0.0 collective-permute-done.4.a_3_
  19.3 3.6 %late.1 = (f32[9,32,288]{2,1,0:T(8,128)S(1)}, f32[9,32,288]{2,1,0:T(8,128)S(1)}, f32[9,32,288]{2,1,0:T(8,128)S(1)}, f32[9,32,288]{2,1,0:T(8,128)S(1)}, bf16[896,...) custom-call(f32[104,1536]{1,0:T(8,128)S(1)} %get-tuple-element.39.a_0_, ...), custom_call_target="tpu_custom_call" | custom-call | tf_op jit(solution)/shard_map/late/pallas_call | solution.py:552
  22.9 0.3 collective-permute-start.9
  23.3 0.6 %collective-permute-start.8 = (f32[8,384]{1,0:T(8,128)S(1)}, f32[8,384]{1,0:T(8,128)S(1)}, u32[]{:S(2)}, u32[]{:S(2)}) collective-permute-start(f32[8,384]{1,0:T(8,128)S(1)} %get-tuple-element.58.a_0_), channel_id=1, source_target_pairs={{0,2},{1,3},{2,0},{3,1},{4,6},{5,7},{6,4},{7,5},{8,10},{9,11},{10,... | collective-permute-start | bytes 36872 | tf_op jit(solution)/shard_map/ppermute | solution.py:469
  23.9 1.0 %collective-permute-start.7 = (f32[8,384]{1,0:T(8,128)S(1)}, f32[8,384]{1,0:T(8,128)S(1)}, u32[]{:S(2)}, u32[]{:S(2)}) collective-permute-start(f32[8,384]{1,0:T(8,128)S(1)} %get-tuple-element.58.a_0_), channel_id=1, source_target_pairs={{0,1},{1,0},{2,3},{3,2},{4,5},{5,4},{6,7},{7,6},{8,9},{9,8},{10,11... | collective-permute-start | bytes 36872 | tf_op jit(solution)/shard_map/ppermute | solution.py:469
  24.9 1.3 %collective-permute-done.9.a_3_ = f32[8,384]{1,0:T(8,128)S(1)} collective-permute-done((f32[8,384]{1,0:T(8,128)S(1)}, f32[8,384]{1,0:T(8,128)S(1)}, u32[]{:S(2)}, u32[]{:S(2)}) %collective-permute-start.9) | collective-permute-done | bytes 12320 | tf_op jit(solution)/shard_map/ppermute | solution.py:469
  26.1 0.9 %collective-permute-done.8.a_2_ = f32[8,384]{1,0:T(8,128)S(1)} collective-permute-done((f32[8,384]{1,0:T(8,128)S(1)}, f32[8,384]{1,0:T(8,128)S(1)}, u32[]{:S(2)}, u32[]{:S(2)}) %collective-permute-start.8) | collective-permute-done | bytes 12320 | tf_op jit(solution)/shard_map/ppermute | solution.py:469
  27.0 0.0 collective-permute-done.7.a_1_
  27.0 0.9 %sums.4 = (f32[16,1536]{1,0:T(8,128)S(1)}, f32[16,1536]{1,0:T(8,128)S(1)}) custom-call(f32[8,384]{1,0:T(8,128)S(1)} %get-tuple-element.58.a_0_, f32[8,384]{1,0:T(8,128)S(1)} %collective-permute-done.7.a_1_, f32[8,384]{1,0:T(8,128)S(1)} %collective-permute-done.8.a_2_, f32[8,384]{1,0:T(8,128)S(1)} %collective-permute-done.9.a_3_, ...), custom_call_target="tpu_custom_call" | custom-call | tf_op jit(solution)/shard_map/sums/pallas_call | solution.py:613
  27.9 0.7 %collective-permute-start.11 = (f32[16,1536]{1,0:T(8,128)S(1)}, f32[16,1536]{1,0:T(8,128)S(1)}, u32[]{:S(2)}, u32[]{:S(2)}) collective-permute-start(f32[16,1536]{1,0:T(8,128)S(1)} %get-tuple-element.69), channel_id=1, source_target_pairs={{0,4},{1,5},{2,6},{3,7},{4,0},{5,1},{6,2},{7,3},{8,12},{9,13},{10,... | collective-permute-start | bytes 294920 | tf_op jit(solution)/shard_map/ppermute | solution.py:469
  28.6 1.3 %collective-permute-start.10 = (f32[16,1536]{1,0:T(8,128)S(1)}, f32[16,1536]{1,0:T(8,128)S(1)}, u32[]{:S(2)}, u32[]{:S(2)}) collective-permute-start(f32[16,1536]{1,0:T(8,128)S(1)} %get-tuple-element.63.a_5_), channel_id=1, source_target_pairs={{0,4},{1,5},{2,6},{3,7},{4,0},{5,1},{6,2},{7,3},{8,12},{9,13},{10,... | collective-permute-start | bytes 294920 | tf_op jit(solution)/shard_map/ppermute | solution.py:469
  30.0 0.9 %sums.5 = (f32[16,1536]{1,0:T(8,128)S(1)}, f32[16,1536]{1,0:T(8,128)S(1)}) custom-call(f32[8,384]{1,0:T(8,128)S(1)} %get-tuple-element.58.a_0_, f32[8,384]{1,0:T(8,128)S(1)} %collective-permute-done.7.a_1_, f32[8,384]{1,0:T(8,128)S(1)} %collective-permute-done.8.a_2_, f32[8,384]{1,0:T(8,128)S(1)} %collective-permute-done.9.a_3_, ...), custom_call_target="tpu_custom_call" | custom-call | tf_op jit(solution)/shard_map/sums/pallas_call | solution.py:613
  30.9 1.0 %sums.6 = (f32[16,1536]{1,0:T(8,128)S(1)}, f32[16,1536]{1,0:T(8,128)S(1)}) custom-call(f32[8,384]{1,0:T(8,128)S(1)} %get-tuple-element.58.a_0_, f32[8,384]{1,0:T(8,128)S(1)} %collective-permute-done.7.a_1_, f32[8,384]{1,0:T(8,128)S(1)} %collective-permute-done.8.a_2_, f32[8,384]{1,0:T(8,128)S(1)} %collective-permute-done.9.a_3_, ...), custom_call_target="tpu_custom_call" | custom-call | tf_op jit(solution)/shard_map/sums/pallas_call | solution.py:613
  31.9 0.7 %collective-permute-start.13 = (f32[16,1536]{1,0:T(8,128)S(1)}, f32[16,1536]{1,0:T(8,128)S(1)}, u32[]{:S(2)}, u32[]{:S(2)}) collective-permute-start(f32[16,1536]{1,0:T(8,128)S(1)} %get-tuple-element.73), channel_id=1, source_target_pairs={{0,4},{1,5},{2,6},{3,7},{4,0},{5,1},{6,2},{7,3},{8,12},{9,13},{10,... | collective-permute-start | bytes 294920 | tf_op jit(solution)/shard_map/ppermute | solution.py:469
  32.6 1.3 %collective-permute-start.12 = (f32[16,1536]{1,0:T(8,128)S(1)}, f32[16,1536]{1,0:T(8,128)S(1)}, u32[]{:S(2)}, u32[]{:S(2)}) collective-permute-start(f32[16,1536]{1,0:T(8,128)S(1)} %get-tuple-element.67.wait), channel_id=1, source_target_pairs={{0,4},{1,5},{2,6},{3,7},{4,0},{5,1},{6,2},{7,3},{8,12},{9,13},{10,... | collective-permute-start | bytes 294920 | tf_op jit(solution)/shard_map/ppermute | solution.py:469
  33.9 0.0 collective-permute-done.11.b
  34.0 2.6 %collective-permute-start.15 = (f32[16,1536]{1,0:T(8,128)S(1)}, f32[16,1536]{1,0:T(8,128)S(1)}, u32[]{:S(2)}, u32[]{:S(2)}) collective-permute-start(f32[16,1536]{1,0:T(8,128)S(1)} %combined.3.a_6_), channel_id=1, source_target_pairs={{0,8},{1,9},{2,10},{3,11},{4,12},{5,13},{6,14},{7,15},{8,0},{9,1},... | collective-permute-start | bytes 294920 | tf_op jit(solution)/shard_map/ppermute | solution.py:469
  36.6 0.0 collective-permute-done.10.b
  36.6 1.6 %collective-permute-start.14 = (f32[16,1536]{1,0:T(8,128)S(1)}, f32[16,1536]{1,0:T(8,128)S(1)}, u32[]{:S(2)}, u32[]{:S(2)}) collective-permute-start(f32[16,1536]{1,0:T(8,128)S(1)} %combined.2.a_5_), channel_id=1, source_target_pairs={{0,8},{1,9},{2,10},{3,11},{4,12},{5,13},{6,14},{7,15},{8,0},{9,1},... | collective-permute-start | bytes 294920 | tf_op jit(solution)/shard_map/ppermute | solution.py:469
  38.2 1.6 %sums.7 = (f32[32,1536]{1,0:T(8,128)S(1)}, f32[2,96]{1,0:T(2,128)}) custom-call(f32[8,384]{1,0:T(8,128)S(1)} %get-tuple-element.58.a_0_, f32[8,384]{1,0:T(8,128)S(1)} %collective-permute-done.7.a_1_, f32[8,384]{1,0:T(8,128)S(1)} %collective-permute-done.8.a_2_, f32[8,384]{1,0:T(8,128)S(1)} %collective-permute-done.9.a_3_, ...), custom_call_target="tpu_custom_call" | custom-call | tf_op jit(solution)/shard_map/sums/pallas_call | solution.py:613
  39.8 0.7 %collective-permute-done.13.a_1_ = f32[16,1536]{1,0:T(8,128)S(1)} collective-permute-done((f32[16,1536]{1,0:T(8,128)S(1)}, f32[16,1536]{1,0:T(8,128)S(1)}, u32[]{:S(2)}, u32[]{:S(2)}) %collective-permute-start.13) | collective-permute-done | bytes 98336 | tf_op jit(solution)/shard_map/ppermute | solution.py:469
  40.5 1.9 %collective-permute-done.12.a_0_ = f32[16,1536]{1,0:T(8,128)S(1)} collective-permute-done((f32[16,1536]{1,0:T(8,128)S(1)}, f32[16,1536]{1,0:T(8,128)S(1)}, u32[]{:S(2)}, u32[]{:S(2)}) %collective-permute-start.12) | collective-permute-done | bytes 98336 | tf_op jit(solution)/shard_map/ppermute | solution.py:469
  42.3 0.0 copy-start.1
  42.3 0.7 %copy-done.1 = f32[2,96]{1,0:T(2,128)S(1)} copy-done((f32[2,96]{1,0:T(2,128)S(1)}, f32[2,96]{1,0:T(2,128)}, u32[]{:S(2)}) %copy-start.1) | copy-done | bytes 792
  43.0 0.0 copy-start
  43.0 0.0 collective-permute-done.15.a_4_
  43.0 2.7 %collective-permute-done.14.a_3_ = f32[16,1536]{1,0:T(8,128)S(1)} collective-permute-done((f32[16,1536]{1,0:T(8,128)S(1)}, f32[16,1536]{1,0:T(8,128)S(1)}, u32[]{:S(2)}, u32[]{:S(2)}) %collective-permute-start.14) | collective-permute-done | bytes 98336 | tf_op jit(solution)/shard_map/ppermute | solution.py:469
  45.7 0.0 copy-done
  45.7 0.7 %update.1 = f32[32,1024]{1,0:T(8,128)} custom-call(f32[32,1536]{1,0:T(8,128)S(1)} %get-tuple-element.72.a_0_, f32[16,1536]{1,0:T(8,128)S(1)} %get-tuple-element.74.a_1_, f32[16,1536]{1,0:T(8,128)S(1)} %get-tuple-element.75.a_2_, f32[16,1536]{1,0:T(8,128)S(1)} %collective-permute-done.14.a_3_, f32[16,1536]{1,0:T(8,128)S(1)} %collective-permute-done.15.a_4_, ...), custom_call_target="tpu_custom_call" | custom-call | tf_op jit(solution)/shard_map/update/pallas_call | solution.py:648
  (4 shorter events, 0.0 us)
Async XLA Ops:
  0.6 14.6 %collective-permute-start.1 = (f32[96,1024]{1,0:T(8,128)}, f32[96,1024]{1,0:T(8,128)S(1)}, u32[]{:S(2)}, u32[]{:S(2)}) collective-permute-start(f32[96,1024]{1,0:T(8,128)} %src_at.1), channel_id=1, source_target_pairs={{0,2},{1,3},{2,0},{3,1},{4,6},{5,7},{6,4},{7,5},{8,10},{9,11},{10,... | collective-permute-start | bytes 1179656 | tf_op jit(solution)/shard_map/ppermute | solution.py:469
  3.7 7.2 %collective-permute-start.3 = (f32[32,1024]{1,0:T(8,128)}, f32[32,1024]{1,0:T(8,128)S(1)}, u32[]{:S(2)}, u32[]{:S(2)}) collective-permute-start(f32[32,1024]{1,0:T(8,128)} %bitcast.10), channel_id=1, source_target_pairs={{0,4},{1,5},{2,6},{3,7},{4,0},{5,1},{6,2},{7,3},{8,12},{9,13},{10,... | collective-permute-start | bytes 393224 | tf_op jit(solution)/shard_map/ppermute | solution.py:469
  5.2 8.8 %collective-permute-start.5 = (f32[32,1024]{1,0:T(8,128)}, f32[32,1024]{1,0:T(8,128)S(1)}, u32[]{:S(2)}, u32[]{:S(2)}) collective-permute-start(f32[32,1024]{1,0:T(8,128)} %bitcast.11), channel_id=1, source_target_pairs={{0,8},{1,9},{2,10},{3,11},{4,12},{5,13},{6,14},{7,15},{8,0},{9,1},... | collective-permute-start | bytes 393224 | tf_op jit(solution)/shard_map/ppermute | solution.py:469
  10.3 3.7 %collective-permute-start.2 = (f32[8,128]{1,0:T(8,128)S(1)}, f32[8,128]{1,0:T(8,128)S(1)}, u32[]{:S(2)}, u32[]{:S(2)}) collective-permute-start(f32[8,128]{1,0:T(8,128)S(1)} %get-tuple-element.40), channel_id=1, source_target_pairs={{0,2},{1,3},{2,0},{3,1},{4,6},{5,7},{6,4},{7,5},{8,10},{9,11},{10,... | collective-permute-start | bytes 12296 | tf_op jit(solution)/shard_map/ppermute | solution.py:469
  14.0 5.0 %collective-permute-start.6 = (f32[32,1024]{1,0:T(8,128)S(1)}, f32[32,1024]{1,0:T(8,128)S(1)}, u32[]{:S(2)}, u32[]{:S(2)}) collective-permute-start(f32[32,1024]{1,0:T(8,128)S(1)} %gate.2.rest_0_), channel_id=1, source_target_pairs={{0,4},{1,5},{2,6},{3,7},{4,0},{5,1},{6,2},{7,3},{8,12},{9,13},{10,... | collective-permute-start | bytes 393224 | tf_op jit(solution)/shard_map/ppermute | solution.py:469
  14.9 4.4 %collective-permute-start = (f32[104,1536]{1,0:T(8,128)S(1)}, f32[104,1536]{1,0:T(8,128)S(1)}, u32[]{:S(2)}, u32[]{:S(2)}) collective-permute-start(f32[104,1536]{1,0:T(8,128)S(1)} %get-tuple-element.39.a_0_), channel_id=1, source_target_pairs={{0,1},{1,0},{2,3},{3,2},{4,5},{5,4},{6,7},{7,6},{8,9},{9,8},{10,11... | collective-permute-start | bytes 1916936 | tf_op jit(solution)/shard_map/ppermute | solution.py:469
  15.9 3.4 %collective-permute-start.4 = (f32[104,1536]{1,0:T(8,128)S(1)}, f32[104,1536]{1,0:T(8,128)S(1)}, u32[]{:S(2)}, u32[]{:S(2)}) collective-permute-start(f32[104,1536]{1,0:T(8,128)S(1)} %neighbour.1.a_2_), channel_id=1, source_target_pairs={{0,1},{1,0},{2,3},{3,2},{4,5},{5,4},{6,7},{7,6},{8,9},{9,8},{10,11... | collective-permute-start | bytes 1916936 | tf_op jit(solution)/shard_map/ppermute | solution.py:469
  22.9 3.2 %collective-permute-start.9 = (f32[8,384]{1,0:T(8,128)S(1)}, f32[8,384]{1,0:T(8,128)S(1)}, u32[]{:S(2)}, u32[]{:S(2)}) collective-permute-start(f32[8,384]{1,0:T(8,128)S(1)} %get-tuple-element.58.a_0_), channel_id=1, source_target_pairs={{0,3},{1,2},{2,1},{3,0},{4,7},{5,6},{6,5},{7,4},{8,11},{9,10},{10,... | collective-permute-start | bytes 36872 | tf_op jit(solution)/shard_map/ppermute | solution.py:469
  23.3 3.7 %collective-permute-start.8 = (f32[8,384]{1,0:T(8,128)S(1)}, f32[8,384]{1,0:T(8,128)S(1)}, u32[]{:S(2)}, u32[]{:S(2)}) collective-permute-start(f32[8,384]{1,0:T(8,128)S(1)} %get-tuple-element.58.a_0_), channel_id=1, source_target_pairs={{0,2},{1,3},{2,0},{3,1},{4,6},{5,7},{6,4},{7,5},{8,10},{9,11},{10,... | collective-permute-start | bytes 36872 | tf_op jit(solution)/shard_map/ppermute | solution.py:469
  23.9 3.1 %collective-permute-start.7 = (f32[8,384]{1,0:T(8,128)S(1)}, f32[8,384]{1,0:T(8,128)S(1)}, u32[]{:S(2)}, u32[]{:S(2)}) collective-permute-start(f32[8,384]{1,0:T(8,128)S(1)} %get-tuple-element.58.a_0_), channel_id=1, source_target_pairs={{0,1},{1,0},{2,3},{3,2},{4,5},{5,4},{6,7},{7,6},{8,9},{9,8},{10,11... | collective-permute-start | bytes 36872 | tf_op jit(solution)/shard_map/ppermute | solution.py:469
  27.9 6.0 %collective-permute-start.11 = (f32[16,1536]{1,0:T(8,128)S(1)}, f32[16,1536]{1,0:T(8,128)S(1)}, u32[]{:S(2)}, u32[]{:S(2)}) collective-permute-start(f32[16,1536]{1,0:T(8,128)S(1)} %get-tuple-element.69), channel_id=1, source_target_pairs={{0,4},{1,5},{2,6},{3,7},{4,0},{5,1},{6,2},{7,3},{8,12},{9,13},{10,... | collective-permute-start | bytes 294920 | tf_op jit(solution)/shard_map/ppermute | solution.py:469
  28.6 8.0 %collective-permute-start.10 = (f32[16,1536]{1,0:T(8,128)S(1)}, f32[16,1536]{1,0:T(8,128)S(1)}, u32[]{:S(2)}, u32[]{:S(2)}) collective-permute-start(f32[16,1536]{1,0:T(8,128)S(1)} %get-tuple-element.63.a_5_), channel_id=1, source_target_pairs={{0,4},{1,5},{2,6},{3,7},{4,0},{5,1},{6,2},{7,3},{8,12},{9,13},{10,... | collective-permute-start | bytes 294920 | tf_op jit(solution)/shard_map/ppermute | solution.py:469
  31.9 8.6 %collective-permute-start.13 = (f32[16,1536]{1,0:T(8,128)S(1)}, f32[16,1536]{1,0:T(8,128)S(1)}, u32[]{:S(2)}, u32[]{:S(2)}) collective-permute-start(f32[16,1536]{1,0:T(8,128)S(1)} %get-tuple-element.73), channel_id=1, source_target_pairs={{0,4},{1,5},{2,6},{3,7},{4,0},{5,1},{6,2},{7,3},{8,12},{9,13},{10,... | collective-permute-start | bytes 294920 | tf_op jit(solution)/shard_map/ppermute | solution.py:469
  32.6 9.7 %collective-permute-start.12 = (f32[16,1536]{1,0:T(8,128)S(1)}, f32[16,1536]{1,0:T(8,128)S(1)}, u32[]{:S(2)}, u32[]{:S(2)}) collective-permute-start(f32[16,1536]{1,0:T(8,128)S(1)} %get-tuple-element.67.wait), channel_id=1, source_target_pairs={{0,4},{1,5},{2,6},{3,7},{4,0},{5,1},{6,2},{7,3},{8,12},{9,13},{10,... | collective-permute-start | bytes 294920 | tf_op jit(solution)/shard_map/ppermute | solution.py:469
  34.0 9.1 %collective-permute-start.15 = (f32[16,1536]{1,0:T(8,128)S(1)}, f32[16,1536]{1,0:T(8,128)S(1)}, u32[]{:S(2)}, u32[]{:S(2)}) collective-permute-start(f32[16,1536]{1,0:T(8,128)S(1)} %combined.3.a_6_), channel_id=1, source_target_pairs={{0,8},{1,9},{2,10},{3,11},{4,12},{5,13},{6,14},{7,15},{8,0},{9,1},... | collective-permute-start | bytes 294920 | tf_op jit(solution)/shard_map/ppermute | solution.py:469
  36.6 9.1 %collective-permute-start.14 = (f32[16,1536]{1,0:T(8,128)S(1)}, f32[16,1536]{1,0:T(8,128)S(1)}, u32[]{:S(2)}, u32[]{:S(2)}) collective-permute-start(f32[16,1536]{1,0:T(8,128)S(1)} %combined.2.a_5_), channel_id=1, source_target_pairs={{0,8},{1,9},{2,10},{3,11},{4,12},{5,13},{6,14},{7,15},{8,0},{9,1},... | collective-permute-start | bytes 294920 | tf_op jit(solution)/shard_map/ppermute | solution.py:469
  42.3 0.7 %copy-start.1 = (f32[2,96]{1,0:T(2,128)S(1)}, f32[2,96]{1,0:T(2,128)}, u32[]{:S(2)}) copy-start(f32[2,96]{1,0:T(2,128)} %get-tuple-element.71.a_2_) | copy-start | bytes 2308
  43.0 2.7 %copy-start = (f32[512]{0:T(512)S(1)}, f32[512]{0:T(512)}, u32[]{:S(2)}) copy-start(f32[512]{0:T(512)} %param.16) | copy-start | bytes 6148

commit v15 on v13

--- a/solution.py
+++ b/solution.py
@@ -185,7 +185,19 @@
     prepared_rows(src, facts_out[...], inverse, out)
 
 
-def neighbour_kernel(src, facts, inverse_noise, wait, out):
+def neighbour_kernel(src_even, src_odd, facts, inverse_noise, wait, out, src):
+    half = src_odd.shape[0]
+    even, _ = place_of_device()
+
+    @pl.when(even)
+    def _():
+        src[...] = src_even[...]
+
+    @pl.when(jnp.logical_not(even))
+    def _():
+        src[:half] = src_odd[...]
+        src[half:] = jnp.zeros_like(src[half:])
+
     prepared_rows(src, facts[...], inverse_noise[...], out)
 
 
@@ -464,9 +476,9 @@
     return pltpu.CompilerParams(vmem_limit_bytes=mib * 1024 * 1024)
 
 
-def crossed(block, mask):
-    size = lax.axis_size("dom")
-    return lax.ppermute(block, "dom", [(i, i ^ mask) for i in range(size)])
+def crossed(block, mask, core=None):
+    devices = [i for i in range(lax.axis_size("dom")) if core is None or i % 2 == core]
+    return lax.ppermute(block, "dom", [(i, i ^ mask) for i in devices])
 
 
 def on_device(
@@ -503,13 +515,17 @@
             name="gate",
         )(*arrays, *waits)
 
-    ynb = crossed(particle_fourier, 2)
+    ynb_even = crossed(particle_fourier, 2, 0)
+    ynb_odd = crossed(particle_fourier[: slots // 2], 2, 1)
     anywhere = pl.BlockSpec(memory_space=pl.ANY)
-    ynb = crossed(particle_fourier, 2)
+    ynb_even = crossed(particle_fourier, 2, 0)
+    ynb_odd = crossed(particle_fourier[: slots // 2], 2, 1)
     anywhere = pl.BlockSpec(memory_space=pl.ANY)
-    ynb = crossed(particle_fourier, 2)
+    ynb_even = crossed(particle_fourier, 2, 0)
+    ynb_odd = crossed(particle_fourier[: slots // 2], 2, 1)
     anywhere = pl.BlockSpec(memory_space=pl.ANY)
-    ynb = crossed(particle_fourier, 2)
+    ynb_even = crossed(particle_fourier, 2, 0)
+    ynb_odd = crossed(particle_fourier[: slots // 2], 2, 1)
     refs = {0: refs_own, 1: crossed(refs_own, TEAM)}
     for n in range(2, blocks, 2):
         refs[n] = crossed(refs_own, TEAM * n)
@@ -576,12 +592,13 @@
     ynb_prepared = pl.pallas_call(
         neighbour_kernel,
         out_shape=jax.ShapeDtypeStruct((slots + 8, width + freq), f32),
-        in_specs=[vmem] * 3 + [anywhere],
+        in_specs=[vmem] * 4 + [anywhere],
         out_specs=vmem,
+        scratch_shapes=[pltpu.VMEM((slots, width), f32)],
         compiler_params=params(6),
         cost_estimate=no_cost,
         name="neighbour",
-    )(ynb, ynb_facts, inverse_noise, prepared[2])
+    )(ynb_even, ynb_odd, ynb_facts, inverse_noise, prepared[2])
     cynb = crossed(ynb_prepared, 1)
 
     outs = []

time: 46.3 us -> 48.1 us (1.039)
  local copies, waits for them, and re-layouts: 0.01 us -> 0.94 us
  waiting for transfers between devices: 13.5 us -> 14 us
    slice x0 -> x1, local copies, waits for them, and re-layouts: none -> 0.94 us  [on_device(): ynb_odd = crossed(particle_fourier[:slots // 2], 2, 1)]
    ppermute x15 -> x16, waiting for transfers between devices: 13.5 us -> 14 us  [crossed(): return lax.ppermute(block, 'dom', [(i, i ^ mask) for i in devices])]
    ppermute x15 -> x16, starting transfers between devices: 18.2 us -> 18.6 us  [crossed(): return lax.ppermute(block, 'dom', [(i, i ^ mask) for i in devices])]
  transfers between devices with their start and end apart: 15 -> 16, of which waited for: 8 -> 9; matrix products, arithmetic and copies ran while one was open for 0% -> 2% of each run, Pallas kernels for 17% -> 16%
where the time goes in v15:
time: 48.1 us; the launch traced here: 47.9 us
  starting transfers between devices  18.6 us (39%)
  waiting for transfers between devices  14 us (29%)
  Pallas kernels  13 us (27%)
  between operations  1.39 us (3%)
  local copies, waits for them, and re-layouts  0.94 us (2%)
    ppermute x16, starting transfers between devices, crossed(): return lax.ppermute(block, 'dom', [(i, i ^ mask) for i in devices])  18.6 us
    ppermute x16, waiting for transfers between devices, crossed(): return lax.ppermute(block, 'dom', [(i, i ^ mask) for i in devices])  14 us
    pallas_call x4, Pallas kernels, sums(): pl.pallas_call(lambda *a: sum_kernel(n, cuts, last, len(waits), *a), out_...  4.39 us
    pallas_call x3, Pallas kernels, call(): pl.pallas_call(kernel, cost_estimate=cost, out_shape=tuple(out_shape), in...  4.24 us
    pallas_call x1, Pallas kernels, on_device(): pl.pallas_call(own_kernel, out_shape=(jax.ShapeDtypeStruct((slots + 8, wi...  1.83 us
    pallas_call x1, Pallas kernels, on_device(): pl.pallas_call(early_kernel, out_shape=tuple(block_shapes * early), in_sp...  1.16 us
  transfers between devices with their start and end apart: 16, of which 9 were waited for; matrix products, arithmetic and copies ran while one was open for 2% of the time, Pallas kernels for 16%

profile of v15, /device:TPU:0, one launch (start us, length us, event | category | flops | bytes accessed | tf_op | source)
XLA Modules:
  0.0 47.9 jit_solution(14424085457787988341)
XLA Ops:
  0.6 4.9 %collective-permute-start.1 = (f32[96,1024]{1,0:T(8,128)}, f32[96,1024]{1,0:T(8,128)S(1)}, u32[]{:S(2)}, u32[]{:S(2)}) collective-permute-start(f32[96,1024]{1,0:T(8,128)} %src_at.1), channel_id=1, source_target_pairs={{0,2},{2,0},{4,6},{6,4},{8,10},{10,8},{12,14},{14,12},{16,18},{18,... | collective-permute-start | bytes 1179656 | tf_op jit(solution)/shard_map/ppermute | solution.py:481
  5.5 1.6 %collective-permute-start.4 = (f32[32,1024]{1,0:T(8,128)}, f32[32,1024]{1,0:T(8,128)S(1)}, u32[]{:S(2)}, u32[]{:S(2)}) collective-permute-start(f32[32,1024]{1,0:T(8,128)} %bitcast.9), channel_id=1, source_target_pairs={{0,4},{1,5},{2,6},{3,7},{4,0},{5,1},{6,2},{7,3},{8,12},{9,13},{10,... | collective-permute-start | bytes 393224 | tf_op jit(solution)/shard_map/ppermute | solution.py:481
  7.2 2.6 %collective-permute-start.6 = (f32[32,1024]{1,0:T(8,128)}, f32[32,1024]{1,0:T(8,128)S(1)}, u32[]{:S(2)}, u32[]{:S(2)}) collective-permute-start(f32[32,1024]{1,0:T(8,128)} %bitcast.10), channel_id=1, source_target_pairs={{0,8},{1,9},{2,10},{3,11},{4,12},{5,13},{6,14},{7,15},{8,0},{9,1},... | collective-permute-start | bytes 393224 | tf_op jit(solution)/shard_map/ppermute | solution.py:481
  9.7 0.9 %slice.3 = f32[48,1024]{1,0:T(8,128)S(1)} slice(f32[96,1024]{1,0:T(8,128)} %src_at.1), slice={[0:48], [0:1024]} | slice | bytes 393216 | tf_op jit(solution)/shard_map/slice | solution.py:528
  10.7 0.7 %collective-permute-start.2 = (f32[48,1024]{1,0:T(8,128)S(1)}, f32[48,1024]{1,0:T(8,128)S(1)}, u32[]{:S(2)}, u32[]{:S(2)}) collective-permute-start(f32[48,1024]{1,0:T(8,128)S(1)} %slice.3), channel_id=1, source_target_pairs={{1,3},{3,1},{5,7},{7,5},{9,11},{11,9},{13,15},{15,13},{17,19},{19,... | collective-permute-start | bytes 589832 | tf_op jit(solution)/shard_map/ppermute | solution.py:481
  12.0 1.8 %own.1 = (f32[104,1536]{1,0:T(8,128)S(1)}, f32[8,128]{1,0:T(8,128)S(1)}, f32[128,512]{1,0:T(8,128)S(1)}) custom-call(f32[96,1024]{1,0:T(8,128)} %src_at.1, f32[1,96]{1,0:T(1,128)} %bitcast.14, s32[2,96]{1,0:T(2,128)} %bitcast.13, s32[1,96]{1,0:T(1,128)} %bitcast.15, s32[1,96]{1,0:T(1,128)} %bitcast.16, f32[128,512]{1,0:T(8,128)} %noise_at.1, ...), custom_call_target="tpu_custom_call" | custom-call | tf_op jit(solution)/shard_map/own/pallas_call | solution.py:540
  13.9 0.6 %collective-permute-start.3 = (f32[8,128]{1,0:T(8,128)S(1)}, f32[8,128]{1,0:T(8,128)S(1)}, u32[]{:S(2)}, u32[]{:S(2)}) collective-permute-start(f32[8,128]{1,0:T(8,128)S(1)} %get-tuple-element.38), channel_id=1, source_target_pairs={{0,2},{1,3},{2,0},{3,1},{4,6},{5,7},{6,4},{7,5},{8,10},{9,11},{10,... | collective-permute-start | bytes 12296 | tf_op jit(solution)/shard_map/ppermute | solution.py:481
  14.4 0.0 collective-permute-done.4.near
  14.4 1.2 %early.1 = (bf16[288,1024]{1,0:T(8,128)(2,1)S(1)}, bf16[288,1024]{1,0:T(8,128)(2,1)S(1)}, bf16[32,512]{1,0:T(8,128)(2,1)S(1)}, bf16[32,512]{1,0:T(8,128)(2,1)S(1...) custom-call(f32[32,1024]{1,0:T(8,128)} %bitcast.11, ...), custom_call_target="tpu_custom_call" | custom-call | tf_op jit(solution)/shard_map/early/pallas_call | solution.py:579
  15.6 1.9 %collective-permute-done.3.facts.a_1_ = f32[8,128]{1,0:T(8,128)S(1)} collective-permute-done((f32[8,128]{1,0:T(8,128)S(1)}, f32[8,128]{1,0:T(8,128)S(1)}, u32[]{:S(2)}, u32[]{:S(2)}) %collective-permute-start.3) | collective-permute-done | bytes 4128 | tf_op jit(solution)/shard_map/ppermute | solution.py:481
  17.5 0.0 collective-permute-done.6.a_0_
  17.5 0.5 collective-permute-start.7
  18.0 0.0 collective-permute-start
  18.0 0.3 middle.2
  18.3 0.0 collective-permute-done.2.src_odd
  18.3 0.0 collective-permute-done.1.src_even
  18.3 0.7 %neighbour.1.a_2_ = f32[104,1536]{1,0:T(8,128)S(1)} custom-call(f32[96,1024]{1,0:T(8,128)S(1)} %collective-permute-done.1.src_even, f32[48,1024]{1,0:T(8,128)S(1)} %collective-permute-done.2.src_odd, f32[8,128]{1,0:T(8,128)S(1)} %collective-permute-done.3.facts.a_1_, f32[128,512]{1,0:T(8,128)S(1)} %get-tuple-element.39.inverse_noise, ...), custom_call_target="tpu_custom_call" | custom-call | tf_op jit(solution)/shard_map/neighbour/pallas_call | solution.py:592
  19.0 0.6 %collective-permute-start.5 = (f32[104,1536]{1,0:T(8,128)S(1)}, f32[104,1536]{1,0:T(8,128)S(1)}, u32[]{:S(2)}, u32[]{:S(2)}) collective-permute-start(f32[104,1536]{1,0:T(8,128)S(1)} %neighbour.1.a_2_), channel_id=1, source_target_pairs={{0,1},{1,0},{2,3},{3,2},{4,5},{5,4},{6,7},{7,6},{8,9},{9,8},{10,11... | collective-permute-start | bytes 1916936 | tf_op jit(solution)/shard_map/ppermute | solution.py:481
  19.6 2.9 %collective-permute-done.7.rest_0_ = f32[32,1024]{1,0:T(8,128)S(1)} collective-permute-done((f32[32,1024]{1,0:T(8,128)S(1)}, f32[32,1024]{1,0:T(8,128)S(1)}, u32[]{:S(2)}, u32[]{:S(2)}) %collective-permute-start.7) | collective-permute-done | bytes 131104 | tf_op jit(solution)/shard_map/ppermute | solution.py:481
  22.5 0.3 middle.3
  22.8 0.0 collective-permute-done.a_1_
  22.8 0.0 collective-permute-done.5.a_3_
  22.8 3.6 %late.1 = (f32[9,32,288]{2,1,0:T(8,128)S(1)}, f32[9,32,288]{2,1,0:T(8,128)S(1)}, f32[9,32,288]{2,1,0:T(8,128)S(1)}, f32[9,32,288]{2,1,0:T(8,128)S(1)}, bf16[896,...) custom-call(f32[104,1536]{1,0:T(8,128)S(1)} %get-tuple-element.37.a_0_, ...), custom_call_target="tpu_custom_call" | custom-call | tf_op jit(solution)/shard_map/late/pallas_call | solution.py:568
  26.5 0.1 collective-permute-start.10
  26.5 0.6 %collective-permute-start.9 = (f32[8,384]{1,0:T(8,128)S(1)}, f32[8,384]{1,0:T(8,128)S(1)}, u32[]{:S(2)}, u32[]{:S(2)}) collective-permute-start(f32[8,384]{1,0:T(8,128)S(1)} %get-tuple-element.56.a_0_), channel_id=1, source_target_pairs={{0,2},{1,3},{2,0},{3,1},{4,6},{5,7},{6,4},{7,5},{8,10},{9,11},{10,... | collective-permute-start | bytes 36872 | tf_op jit(solution)/shard_map/ppermute | solution.py:481
  27.1 1.3 %collective-permute-start.8 = (f32[8,384]{1,0:T(8,128)S(1)}, f32[8,384]{1,0:T(8,128)S(1)}, u32[]{:S(2)}, u32[]{:S(2)}) collective-permute-start(f32[8,384]{1,0:T(8,128)S(1)} %get-tuple-element.56.a_0_), channel_id=1, source_target_pairs={{0,1},{1,0},{2,3},{3,2},{4,5},{5,4},{6,7},{7,6},{8,9},{9,8},{10,11... | collective-permute-start | bytes 36872 | tf_op jit(solution)/shard_map/ppermute | solution.py:481
  28.4 1.3 %collective-permute-done.10.a_3_ = f32[8,384]{1,0:T(8,128)S(1)} collective-permute-done((f32[8,384]{1,0:T(8,128)S(1)}, f32[8,384]{1,0:T(8,128)S(1)}, u32[]{:S(2)}, u32[]{:S(2)}) %collective-permute-start.10) | collective-permute-done | bytes 12320 | tf_op jit(solution)/shard_map/ppermute | solution.py:481
  29.7 0.7 %collective-permute-done.9.a_2_ = f32[8,384]{1,0:T(8,128)S(1)} collective-permute-done((f32[8,384]{1,0:T(8,128)S(1)}, f32[8,384]{1,0:T(8,128)S(1)}, u32[]{:S(2)}, u32[]{:S(2)}) %collective-permute-start.9) | collective-permute-done | bytes 12320 | tf_op jit(solution)/shard_map/ppermute | solution.py:481
  30.3 0.0 collective-permute-done.8.a_1_
  30.3 0.9 %sums.4 = (f32[16,1536]{1,0:T(8,128)S(1)}, f32[16,1536]{1,0:T(8,128)S(1)}) custom-call(f32[8,384]{1,0:T(8,128)S(1)} %get-tuple-element.56.a_0_, f32[8,384]{1,0:T(8,128)S(1)} %collective-permute-done.8.a_1_, f32[8,384]{1,0:T(8,128)S(1)} %collective-permute-done.9.a_2_, f32[8,384]{1,0:T(8,128)S(1)} %collective-permute-done.10.a_3_, ...), custom_call_target="tpu_custom_call" | custom-call | tf_op jit(solution)/shard_map/sums/pallas_call | solution.py:630
  31.3 0.5 %collective-permute-start.12 = (f32[16,1536]{1,0:T(8,128)S(1)}, f32[16,1536]{1,0:T(8,128)S(1)}, u32[]{:S(2)}, u32[]{:S(2)}) collective-permute-start(f32[16,1536]{1,0:T(8,128)S(1)} %get-tuple-element.66), channel_id=1, source_target_pairs={{0,4},{1,5},{2,6},{3,7},{4,0},{5,1},{6,2},{7,3},{8,12},{9,13},{10,... | collective-permute-start | bytes 294920 | tf_op jit(solution)/shard_map/ppermute | solution.py:481
  31.7 1.6 %collective-permute-start.11 = (f32[16,1536]{1,0:T(8,128)S(1)}, f32[16,1536]{1,0:T(8,128)S(1)}, u32[]{:S(2)}, u32[]{:S(2)}) collective-permute-start(f32[16,1536]{1,0:T(8,128)S(1)} %get-tuple-element.61.a_5_), channel_id=1, source_target_pairs={{0,4},{1,5},{2,6},{3,7},{4,0},{5,1},{6,2},{7,3},{8,12},{9,13},{10,... | collective-permute-start | bytes 294920 | tf_op jit(solution)/shard_map/ppermute | solution.py:481
  33.3 0.9 %sums.5 = (f32[16,1536]{1,0:T(8,128)S(1)}, f32[16,1536]{1,0:T(8,128)S(1)}) custom-call(f32[8,384]{1,0:T(8,128)S(1)} %get-tuple-element.56.a_0_, f32[8,384]{1,0:T(8,128)S(1)} %collective-permute-done.8.a_1_, f32[8,384]{1,0:T(8,128)S(1)} %collective-permute-done.9.a_2_, f32[8,384]{1,0:T(8,128)S(1)} %collective-permute-done.10.a_3_, ...), custom_call_target="tpu_custom_call" | custom-call | tf_op jit(solution)/shard_map/sums/pallas_call | solution.py:630
  34.3 1.0 %sums.6.wait = f32[32,1536]{1,0:T(8,128)S(1)} custom-call(f32[8,384]{1,0:T(8,128)S(1)} %get-tuple-element.56.a_0_, f32[8,384]{1,0:T(8,128)S(1)} %collective-permute-done.8.a_1_, f32[8,384]{1,0:T(8,128)S(1)} %collective-permute-done.9.a_2_, f32[8,384]{1,0:T(8,128)S(1)} %collective-permute-done.10.a_3_, f32[8,384]{1,0:T(8,128)S(1)} %get-tuple-element.57.a_4_, ...), custom_call_target="tpu_custom_call" | custom-call | tf_op jit(solution)/shard_map/sums/pallas_call | solution.py:630
  35.2 1.3 %collective-permute-done.12.b = f32[16,1536]{1,0:T(8,128)S(1)} collective-permute-done((f32[16,1536]{1,0:T(8,128)S(1)}, f32[16,1536]{1,0:T(8,128)S(1)}, u32[]{:S(2)}, u32[]{:S(2)}) %collective-permute-start.12) | collective-permute-done | bytes 98336 | tf_op jit(solution)/shard_map/ppermute | solution.py:481
  36.5 0.5 %collective-permute-start.15 = (f32[16,1536]{1,0:T(8,128)S(1)}, f32[16,1536]{1,0:T(8,128)S(1)}, u32[]{:S(2)}, u32[]{:S(2)}) collective-permute-start(f32[16,1536]{1,0:T(8,128)S(1)} %combined.3.a_6_), channel_id=1, source_target_pairs={{0,8},{1,9},{2,10},{3,11},{4,12},{5,13},{6,14},{7,15},{8,0},{9,1},... | collective-permute-start | bytes 294920 | tf_op jit(solution)/shard_map/ppermute | solution.py:481
  37.0 0.5 %collective-permute-done.11.b = f32[16,1536]{1,0:T(8,128)S(1)} collective-permute-done((f32[16,1536]{1,0:T(8,128)S(1)}, f32[16,1536]{1,0:T(8,128)S(1)}, u32[]{:S(2)}, u32[]{:S(2)}) %collective-permute-start.11) | collective-permute-done | bytes 98336 | tf_op jit(solution)/shard_map/ppermute | solution.py:481
  37.6 2.0 %collective-permute-start.14 = (f32[16,1536]{1,0:T(8,128)S(1)}, f32[16,1536]{1,0:T(8,128)S(1)}, u32[]{:S(2)}, u32[]{:S(2)}) collective-permute-start(f32[16,1536]{1,0:T(8,128)S(1)} %combined.2.a_5_), channel_id=1, source_target_pairs={{0,8},{1,9},{2,10},{3,11},{4,12},{5,13},{6,14},{7,15},{8,0},{9,1},... | collective-permute-start | bytes 294920 | tf_op jit(solution)/shard_map/ppermute | solution.py:481
  39.6 0.7 %collective-permute-start.13 = (f32[32,1536]{1,0:T(8,128)S(1)}, f32[32,1536]{1,0:T(8,128)S(1)}, u32[]{:S(2)}, u32[]{:S(2)}) collective-permute-start(f32[32,1536]{1,0:T(8,128)S(1)} %sums.6.wait), channel_id=1, source_target_pairs={{0,4},{1,5},{2,6},{3,7},{4,0},{5,1},{6,2},{7,3},{8,12},{9,13},{10,... | collective-permute-start | bytes 589832 | tf_op jit(solution)/shard_map/ppermute | solution.py:481
  40.3 1.6 %sums.7 = (f32[32,1536]{1,0:T(8,128)S(1)}, f32[2,96]{1,0:T(2,128)}) custom-call(f32[8,384]{1,0:T(8,128)S(1)} %get-tuple-element.56.a_0_, f32[8,384]{1,0:T(8,128)S(1)} %collective-permute-done.8.a_1_, f32[8,384]{1,0:T(8,128)S(1)} %collective-permute-done.9.a_2_, f32[8,384]{1,0:T(8,128)S(1)} %collective-permute-done.10.a_3_, ...), custom_call_target="tpu_custom_call" | custom-call | tf_op jit(solution)/shard_map/sums/pallas_call | solution.py:630
  41.8 0.0 copy-start
  41.8 3.0 %collective-permute-done.15.a_1_ = f32[16,1536]{1,0:T(8,128)S(1)} collective-permute-done((f32[16,1536]{1,0:T(8,128)S(1)}, f32[16,1536]{1,0:T(8,128)S(1)}, u32[]{:S(2)}, u32[]{:S(2)}) %collective-permute-start.15) | collective-permute-done | bytes 98336 | tf_op jit(solution)/shard_map/ppermute | solution.py:481
  44.8 1.5 %collective-permute-done.14.a_0_ = f32[16,1536]{1,0:T(8,128)S(1)} collective-permute-done((f32[16,1536]{1,0:T(8,128)S(1)}, f32[16,1536]{1,0:T(8,128)S(1)}, u32[]{:S(2)}, u32[]{:S(2)}) %collective-permute-start.14) | collective-permute-done | bytes 98336 | tf_op jit(solution)/shard_map/ppermute | solution.py:481
  46.3 0.9 %collective-permute-done.13.a_1_ = f32[32,1536]{1,0:T(8,128)S(1)} collective-permute-done((f32[32,1536]{1,0:T(8,128)S(1)}, f32[32,1536]{1,0:T(8,128)S(1)}, u32[]{:S(2)}, u32[]{:S(2)}) %collective-permute-start.13) | collective-permute-done | bytes 196640 | tf_op jit(solution)/shard_map/ppermute | solution.py:481
  47.2 0.0 copy-done
  47.2 0.7 %update.1 = f32[32,1024]{1,0:T(8,128)} custom-call(f32[32,1536]{1,0:T(8,128)S(1)} %get-tuple-element.69.a_0_, f32[32,1536]{1,0:T(8,128)S(1)} %collective-permute-done.13.a_1_, f32[16,1536]{1,0:T(8,128)S(1)} %get-tuple-element.70.a_2_, f32[16,1536]{1,0:T(8,128)S(1)} %get-tuple-element.71.a_3_, f32[1,512]{1,0:T(1,128)S(1)} %bitcast.8), custom_call_target="tpu_custom_call" | custom-call | tf_op jit(solution)/shard_map/update/pallas_call | solution.py:664
  (4 shorter events, 0.0 us)
Async XLA Ops:
  0.6 17.7 %collective-permute-start.1 = (f32[96,1024]{1,0:T(8,128)}, f32[96,1024]{1,0:T(8,128)S(1)}, u32[]{:S(2)}, u32[]{:S(2)}) collective-permute-start(f32[96,1024]{1,0:T(8,128)} %src_at.1), channel_id=1, source_target_pairs={{0,2},{2,0},{4,6},{6,4},{8,10},{10,8},{12,14},{14,12},{16,18},{18,... | collective-permute-start | bytes 1179656 | tf_op jit(solution)/shard_map/ppermute | solution.py:481
  5.5 8.9 %collective-permute-start.4 = (f32[32,1024]{1,0:T(8,128)}, f32[32,1024]{1,0:T(8,128)S(1)}, u32[]{:S(2)}, u32[]{:S(2)}) collective-permute-start(f32[32,1024]{1,0:T(8,128)} %bitcast.9), channel_id=1, source_target_pairs={{0,4},{1,5},{2,6},{3,7},{4,0},{5,1},{6,2},{7,3},{8,12},{9,13},{10,... | collective-permute-start | bytes 393224 | tf_op jit(solution)/shard_map/ppermute | solution.py:481
  7.2 10.4 %collective-permute-start.6 = (f32[32,1024]{1,0:T(8,128)}, f32[32,1024]{1,0:T(8,128)S(1)}, u32[]{:S(2)}, u32[]{:S(2)}) collective-permute-start(f32[32,1024]{1,0:T(8,128)} %bitcast.10), channel_id=1, source_target_pairs={{0,8},{1,9},{2,10},{3,11},{4,12},{5,13},{6,14},{7,15},{8,0},{9,1},... | collective-permute-start | bytes 393224 | tf_op jit(solution)/shard_map/ppermute | solution.py:481
  10.7 7.6 %collective-permute-start.2 = (f32[48,1024]{1,0:T(8,128)S(1)}, f32[48,1024]{1,0:T(8,128)S(1)}, u32[]{:S(2)}, u32[]{:S(2)}) collective-permute-start(f32[48,1024]{1,0:T(8,128)S(1)} %slice.3), channel_id=1, source_target_pairs={{1,3},{3,1},{5,7},{7,5},{9,11},{11,9},{13,15},{15,13},{17,19},{19,... | collective-permute-start | bytes 589832 | tf_op jit(solution)/shard_map/ppermute | solution.py:481
  13.9 3.7 %collective-permute-start.3 = (f32[8,128]{1,0:T(8,128)S(1)}, f32[8,128]{1,0:T(8,128)S(1)}, u32[]{:S(2)}, u32[]{:S(2)}) collective-permute-start(f32[8,128]{1,0:T(8,128)S(1)} %get-tuple-element.38), channel_id=1, source_target_pairs={{0,2},{1,3},{2,0},{3,1},{4,6},{5,7},{6,4},{7,5},{8,10},{9,11},{10,... | collective-permute-start | bytes 12296 | tf_op jit(solution)/shard_map/ppermute | solution.py:481
  17.5 5.0 %collective-permute-start.7 = (f32[32,1024]{1,0:T(8,128)S(1)}, f32[32,1024]{1,0:T(8,128)S(1)}, u32[]{:S(2)}, u32[]{:S(2)}) collective-permute-start(f32[32,1024]{1,0:T(8,128)S(1)} %gate.2.rest_0_), channel_id=1, source_target_pairs={{0,4},{1,5},{2,6},{3,7},{4,0},{5,1},{6,2},{7,3},{8,12},{9,13},{10,... | collective-permute-start | bytes 393224 | tf_op jit(solution)/shard_map/ppermute | solution.py:481
  18.0 4.8 %collective-permute-start = (f32[104,1536]{1,0:T(8,128)S(1)}, f32[104,1536]{1,0:T(8,128)S(1)}, u32[]{:S(2)}, u32[]{:S(2)}) collective-permute-start(f32[104,1536]{1,0:T(8,128)S(1)} %get-tuple-element.37.a_0_), channel_id=1, source_target_pairs={{0,1},{1,0},{2,3},{3,2},{4,5},{5,4},{6,7},{7,6},{8,9},{9,8},{10,11... | collective-permute-start | bytes 1916936 | tf_op jit(solution)/shard_map/ppermute | solution.py:481
  19.0 3.8 %collective-permute-start.5 = (f32[104,1536]{1,0:T(8,128)S(1)}, f32[104,1536]{1,0:T(8,128)S(1)}, u32[]{:S(2)}, u32[]{:S(2)}) collective-permute-start(f32[104,1536]{1,0:T(8,128)S(1)} %neighbour.1.a_2_), channel_id=1, source_target_pairs={{0,1},{1,0},{2,3},{3,2},{4,5},{5,4},{6,7},{7,6},{8,9},{9,8},{10,11... | collective-permute-start | bytes 1916936 | tf_op jit(solution)/shard_map/ppermute | solution.py:481
  26.5 3.2 %collective-permute-start.10 = (f32[8,384]{1,0:T(8,128)S(1)}, f32[8,384]{1,0:T(8,128)S(1)}, u32[]{:S(2)}, u32[]{:S(2)}) collective-permute-start(f32[8,384]{1,0:T(8,128)S(1)} %get-tuple-element.56.a_0_), channel_id=1, source_target_pairs={{0,3},{1,2},{2,1},{3,0},{4,7},{5,6},{6,5},{7,4},{8,11},{9,10},{10,... | collective-permute-start | bytes 36872 | tf_op jit(solution)/shard_map/ppermute | solution.py:481
  26.5 3.8 %collective-permute-start.9 = (f32[8,384]{1,0:T(8,128)S(1)}, f32[8,384]{1,0:T(8,128)S(1)}, u32[]{:S(2)}, u32[]{:S(2)}) collective-permute-start(f32[8,384]{1,0:T(8,128)S(1)} %get-tuple-element.56.a_0_), channel_id=1, source_target_pairs={{0,2},{1,3},{2,0},{3,1},{4,6},{5,7},{6,4},{7,5},{8,10},{9,11},{10,... | collective-permute-start | bytes 36872 | tf_op jit(solution)/shard_map/ppermute | solution.py:481
  27.1 3.2 %collective-permute-start.8 = (f32[8,384]{1,0:T(8,128)S(1)}, f32[8,384]{1,0:T(8,128)S(1)}, u32[]{:S(2)}, u32[]{:S(2)}) collective-permute-start(f32[8,384]{1,0:T(8,128)S(1)} %get-tuple-element.56.a_0_), channel_id=1, source_target_pairs={{0,1},{1,0},{2,3},{3,2},{4,5},{5,4},{6,7},{7,6},{8,9},{9,8},{10,11... | collective-permute-start | bytes 36872 | tf_op jit(solution)/shard_map/ppermute | solution.py:481
  31.3 5.3 %collective-permute-start.12 = (f32[16,1536]{1,0:T(8,128)S(1)}, f32[16,1536]{1,0:T(8,128)S(1)}, u32[]{:S(2)}, u32[]{:S(2)}) collective-permute-start(f32[16,1536]{1,0:T(8,128)S(1)} %get-tuple-element.66), channel_id=1, source_target_pairs={{0,4},{1,5},{2,6},{3,7},{4,0},{5,1},{6,2},{7,3},{8,12},{9,13},{10,... | collective-permute-start | bytes 294920 | tf_op jit(solution)/shard_map/ppermute | solution.py:481
  31.7 5.8 %collective-permute-start.11 = (f32[16,1536]{1,0:T(8,128)S(1)}, f32[16,1536]{1,0:T(8,128)S(1)}, u32[]{:S(2)}, u32[]{:S(2)}) collective-permute-start(f32[16,1536]{1,0:T(8,128)S(1)} %get-tuple-element.61.a_5_), channel_id=1, source_target_pairs={{0,4},{1,5},{2,6},{3,7},{4,0},{5,1},{6,2},{7,3},{8,12},{9,13},{10,... | collective-permute-start | bytes 294920 | tf_op jit(solution)/shard_map/ppermute | solution.py:481
  36.5 8.3 %collective-permute-start.15 = (f32[16,1536]{1,0:T(8,128)S(1)}, f32[16,1536]{1,0:T(8,128)S(1)}, u32[]{:S(2)}, u32[]{:S(2)}) collective-permute-start(f32[16,1536]{1,0:T(8,128)S(1)} %combined.3.a_6_), channel_id=1, source_target_pairs={{0,8},{1,9},{2,10},{3,11},{4,12},{5,13},{6,14},{7,15},{8,0},{9,1},... | collective-permute-start | bytes 294920 | tf_op jit(solution)/shard_map/ppermute | solution.py:481
  37.6 8.7 %collective-permute-start.14 = (f32[16,1536]{1,0:T(8,128)S(1)}, f32[16,1536]{1,0:T(8,128)S(1)}, u32[]{:S(2)}, u32[]{:S(2)}) collective-permute-start(f32[16,1536]{1,0:T(8,128)S(1)} %combined.2.a_5_), channel_id=1, source_target_pairs={{0,8},{1,9},{2,10},{3,11},{4,12},{5,13},{6,14},{7,15},{8,0},{9,1},... | collective-permute-start | bytes 294920 | tf_op jit(solution)/shard_map/ppermute | solution.py:481
  39.6 7.6 %collective-permute-start.13 = (f32[32,1536]{1,0:T(8,128)S(1)}, f32[32,1536]{1,0:T(8,128)S(1)}, u32[]{:S(2)}, u32[]{:S(2)}) collective-permute-start(f32[32,1536]{1,0:T(8,128)S(1)} %sums.6.wait), channel_id=1, source_target_pairs={{0,4},{1,5},{2,6},{3,7},{4,0},{5,1},{6,2},{7,3},{8,12},{9,13},{10,... | collective-permute-start | bytes 589832 | tf_op jit(solution)/shard_map/ppermute | solution.py:481
  41.8 5.4 %copy-start = (f32[512]{0:T(512)S(1)}, f32[512]{0:T(512)}, u32[]{:S(2)}) copy-start(f32[512]{0:T(512)} %param.16) | copy-start | bytes 6148

commit v16 on v12

--- a/solution.py
+++ b/solution.py
@@ -323,22 +323,17 @@
     return top, [sum(f * x for f, x in zip(factors, column)) for column in zip(*sums)]
 
 
-def early_kernel(own_at, near, *rest):
+def own_refs_kernel(own_at, wait, *rest):
     *prepared, own, sem = rest
     copy = pltpu.make_async_copy(own_at, own, sem)
     copy.start()
     phases = grid_phases(own.shape[1] // 2)
-    prepare_refs(near, phases, *prepared[4:])
     copy.wait()
-    prepare_refs(own, phases, *prepared[:4])
-
-
-def middle_kernel(*rest):
-    count = len(rest) // 5
-    refs, prepared = rest[:count], rest[count:]
-    phases = grid_phases(refs[0].shape[1] // 2)
-    for n in range(count):
-        prepare_refs(refs[n], phases, *prepared[4 * n : 4 * n + 4])
+    prepare_refs(own, phases, *prepared)
+
+
+def refs_kernel(ref, wait, *prepared):
+    prepare_refs(ref, grid_phases(ref.shape[1] // 2), *prepared)
 
 
 def late_kernel(blocks, own, cnb, ynb, cynb, *rest):
@@ -495,18 +490,6 @@
     anywhere = pl.BlockSpec(memory_space=pl.ANY)
     ynb = crossed(particle_fourier, 2)
     anywhere = pl.BlockSpec(memory_space=pl.ANY)
-    def gated(arrays, waits, cost):
-        return pl.pallas_call(
-            lambda *a: None,
-            out_shape=tuple(jax.ShapeDtypeStruct(x.shape, x.dtype) for x in arrays),
-            in_specs=[anywhere] * (len(arrays) + len(waits)),
-            out_specs=(anywhere,) * len(arrays),
-            input_output_aliases={n: n for n in range(len(arrays))},
-            compiler_params=params(1),
-            cost_estimate=cost,
-            name="gate",
-        )(*arrays, *waits)
-
     ynb = crossed(particle_fourier, 2)
     anywhere = pl.BlockSpec(memory_space=pl.ANY)
     ynb = crossed(particle_fourier, 2)
@@ -537,7 +520,6 @@
     cnb = crossed(own, 1)
     lanes = 3 * slots
     bf16 = jnp.bfloat16
-    early = 2
 
     def shaped(rows, cols, dtype=f32):
         return jax.ShapeDtypeStruct((rows, cols), dtype)
@@ -558,14 +540,14 @@
         )(*operands)
 
     prepared = pl.pallas_call(
-        early_kernel,
-        out_shape=tuple(block_shapes * early),
-        in_specs=[anywhere, vmem],
-        out_specs=(vmem,) * (4 * early),
+        own_refs_kernel,
+        out_shape=tuple(block_shapes),
+        in_specs=[anywhere] * 2,
+        out_specs=(vmem,) * 4,
         scratch_shapes=[pltpu.VMEM(refs_own.shape, f32), pltpu.SemaphoreType.DMA],
         compiler_params=params(8),
-        name="early",
-    )(pltpu.with_memory_space_constraint(refs_own, pltpu.HBM), refs[1])
+        name="own_refs",
+    )(pltpu.with_memory_space_constraint(refs_own, pltpu.HBM), facts)
     ynb_prepared = pl.pallas_call(
         neighbour_kernel,
         out_shape=jax.ShapeDtypeStruct((slots + 8, width + freq), f32),
@@ -577,16 +559,21 @@
     )(ynb, crossed(facts, 2), inverse_noise, prepared[2])
     cynb = crossed(ynb_prepared, 1)
 
-    late = blocks - early
-    outs = call(
-        middle_kernel,
-        refs[early:],
-        block_shapes * late,
-        "middle",
-        4 + 2 * blocks,
-        much,
-    )
-    prepared = (*prepared, *outs)
+    order = [*range(blocks - 1, 2, -1), 1, 2]
+    wait = ynb_prepared
+    by_block = {0: prepared}
+    for n in order:
+        by_block[n] = pl.pallas_call(
+            refs_kernel,
+            out_shape=tuple(block_shapes),
+            in_specs=[vmem, anywhere],
+            out_specs=(vmem,) * 4,
+            compiler_params=params(6),
+            cost_estimate=much if n == order[-1] else None,
+            name="refs",
+        )(refs[n], wait)
+        wait = by_block[n][2]
+    prepared = [x for n in range(blocks) for x in by_block[n]]
     deep = 3 * MAIN + 128
     top_rows = -(-blocks // 8) * 8
     outs = call(

time: 45.6 us -> 44.2 us (0.969)
  waiting for transfers between devices: 15.1 us -> 12.9 us
    ppermute x15, waiting for transfers between devices: 15.1 us -> 12.9 us  [crossed(): return lax.ppermute(block, 'dom', [(i, i ^ mask) for i in range(size)])]
    pallas_call x1 -> x4, Pallas kernels: 1.16 us -> 2.1 us  [the longest x1 1.15 us: on_device(): pl.pallas_call(own_refs_kernel, out_shape=tuple(block_shapes), in_specs=[...]
    pallas_call x2 -> x1, Pallas kernels: 4.18 us -> 3.61 us  [call(): pl.pallas_call(kernel, cost_estimate=cost, out_shape=tuple(out_shape), in...]
  transfers between devices with their start and end apart: 15 -> 15, of which waited for: 9 -> 8; matrix products, arithmetic and copies ran while one was open for 0% -> 0% of each run, Pallas kernels for 17% -> 18%
where the time goes in v16:
time: 44.2 us; the launch traced here: 44 us
  starting transfers between devices  16.5 us (37%)
  Pallas kernels  13.3 us (30%)
  waiting for transfers between devices  12.9 us (29%)
  between operations  1.38 us (3%)
    ppermute x15, starting transfers between devices, crossed(): return lax.ppermute(block, 'dom', [(i, i ^ mask) for i in range(size)])  16.5 us
    ppermute x15, waiting for transfers between devices, crossed(): return lax.ppermute(block, 'dom', [(i, i ^ mask) for i in range(size)])  12.9 us
    pallas_call x4, Pallas kernels, sums(): pl.pallas_call(lambda *a: sum_kernel(n, cuts, last, len(waits), *a), out_...  4.39 us
    pallas_call x1, Pallas kernels, call(): pl.pallas_call(kernel, cost_estimate=cost, out_shape=tuple(out_shape), in...  3.61 us
    pallas_call x1, Pallas kernels, on_device(): pl.pallas_call(own_kernel, out_shape=(jax.ShapeDtypeStruct((slots + 8, wi...  1.83 us
    pallas_call x1, Pallas kernels, on_device(): pl.pallas_call(own_refs_kernel, out_shape=tuple(block_shapes), in_specs=[...  1.15 us
    pallas_call x3, Pallas kernels, on_device(): pl.pallas_call(refs_kernel, out_shape=tuple(block_shapes), in_specs=[vmem...  0.94 us
  transfers between devices with their start and end apart: 15, of which 8 were waited for; matrix products, arithmetic and copies ran while one was open for 0% of the time, Pallas kernels for 18%

profile of v16, /device:TPU:0, one launch (start us, length us, event | category | flops | bytes accessed | tf_op | source)
XLA Modules:
  0.0 44.0 jit_solution(15024988259284250745)
XLA Ops:
  0.6 3.0 %collective-permute-start.1 = (f32[96,1024]{1,0:T(8,128)}, f32[96,1024]{1,0:T(8,128)S(1)}, u32[]{:S(2)}, u32[]{:S(2)}) collective-permute-start(f32[96,1024]{1,0:T(8,128)} %src_at.1), channel_id=1, source_target_pairs={{0,2},{1,3},{2,0},{3,1},{4,6},{5,7},{6,4},{7,5},{8,10},{9,11},{10,... | collective-permute-start | bytes 1179656 | tf_op jit(solution)/shard_map/ppermute | solution.py:464
  3.7 3.6 %collective-permute-start.5 = (f32[32,1024]{1,0:T(8,128)}, f32[32,1024]{1,0:T(8,128)S(1)}, u32[]{:S(2)}, u32[]{:S(2)}) collective-permute-start(f32[32,1024]{1,0:T(8,128)} %bitcast.9), channel_id=1, source_target_pairs={{0,12},{1,13},{2,14},{3,15},{4,8},{5,9},{6,10},{7,11},{8,4},{9,5},... | collective-permute-start | bytes 393224 | tf_op jit(solution)/shard_map/ppermute | solution.py:464
  7.3 0.0 collective-permute-start.4
  7.3 0.8 %collective-permute-start.6 = (f32[32,1024]{1,0:T(8,128)}, f32[32,1024]{1,0:T(8,128)S(1)}, u32[]{:S(2)}, u32[]{:S(2)}) collective-permute-start(f32[32,1024]{1,0:T(8,128)} %bitcast.11), channel_id=1, source_target_pairs={{0,8},{1,9},{2,10},{3,11},{4,12},{5,13},{6,14},{7,15},{8,0},{9,1},... | collective-permute-start | bytes 393224 | tf_op jit(solution)/shard_map/ppermute | solution.py:464
  8.7 1.8 %own.1 = (f32[104,1536]{1,0:T(8,128)S(1)}, f32[8,128]{1,0:T(8,128)S(1)}, f32[128,512]{1,0:T(8,128)S(1)}) custom-call(f32[96,1024]{1,0:T(8,128)} %src_at.1, f32[1,96]{1,0:T(1,128)} %bitcast.15, s32[2,96]{1,0:T(2,128)} %bitcast.14, s32[1,96]{1,0:T(1,128)} %bitcast.16, s32[1,96]{1,0:T(1,128)} %bitcast.17, f32[128,512]{1,0:T(8,128)} %noise_at.1, ...), custom_call_target="tpu_custom_call" | custom-call | tf_op jit(solution)/shard_map/own/pallas_call | solution.py:505
  10.5 0.4 collective-permute-start.2
  10.9 1.2 %own_refs.1 = (bf16[288,1024]{1,0:T(8,128)(2,1)S(1)}, bf16[288,1024]{1,0:T(8,128)(2,1)S(1)}, bf16[32,512]{1,0:T(8,128)(2,1)S(1)}, bf16[32,512]{1,0:T(8,128)(2,1)S(1)}) custom-call(f32[32,1024]{1,0:T(8,128)} %bitcast.12, f32[8,128]{1,0:T(8,128)S(1)} %get-tuple-element.38.wait), custom_call_target="tpu_custom_call" | custom-call | tf_op jit(solution)/shard_map/own_refs/pallas_call | solution.py:542
  12.1 2.2 %collective-permute-done.2.facts = f32[8,128]{1,0:T(8,128)S(1)} collective-permute-done((f32[8,128]{1,0:T(8,128)S(1)}, f32[8,128]{1,0:T(8,128)S(1)}, u32[]{:S(2)}, u32[]{:S(2)}) %collective-permute-start.2) | collective-permute-done | bytes 4128 | tf_op jit(solution)/shard_map/ppermute | solution.py:464
  14.2 0.0 collective-permute-start
  14.2 0.0 collective-permute-done.1.src
  14.2 0.6 %neighbour.1.wait.a_2_ = f32[104,1536]{1,0:T(8,128)S(1)} custom-call(f32[96,1024]{1,0:T(8,128)S(1)} %collective-permute-done.1.src, f32[8,128]{1,0:T(8,128)S(1)} %collective-permute-done.2.facts, f32[128,512]{1,0:T(8,128)S(1)} %get-tuple-element.39.inverse_noise, bf16[32,512]{1,0:T(8,128)(2,1)S(1)} %get-tuple-element.40.wait.a_6_), custom_call_target="tpu_custom_call" | custom-call | tf_op jit(solution)/shard_map/neighbour/pallas_call | solution.py:551
  14.9 0.6 %collective-permute-start.3 = (f32[104,1536]{1,0:T(8,128)S(1)}, f32[104,1536]{1,0:T(8,128)S(1)}, u32[]{:S(2)}, u32[]{:S(2)}) collective-permute-start(f32[104,1536]{1,0:T(8,128)S(1)} %neighbour.1.wait.a_2_), channel_id=1, source_target_pairs={{0,1},{1,0},{2,3},{3,2},{4,5},{5,4},{6,7},{7,6},{8,9},{9,8},{10,11... | collective-permute-start | bytes 1916936 | tf_op jit(solution)/shard_map/ppermute | solution.py:464
  15.4 0.0 collective-permute-done.5.ref
  15.4 0.3 refs.3
  15.8 0.0 collective-permute-done.4.ref
  15.8 0.3 refs.4
  16.1 2.2 %collective-permute-done.6.ref = f32[32,1024]{1,0:T(8,128)S(1)} collective-permute-done((f32[32,1024]{1,0:T(8,128)}, f32[32,1024]{1,0:T(8,128)S(1)}, u32[]{:S(2)}, u32[]{:S(2)}) %collective-permute-start.6) | collective-permute-done | bytes 131104 | tf_op jit(solution)/shard_map/ppermute | solution.py:464
  18.3 0.3 refs.5
  18.6 0.0 collective-permute-done.a_1_
  18.6 0.0 collective-permute-done.3.a_3_
  18.6 3.6 %late.1 = (f32[9,32,288]{2,1,0:T(8,128)S(1)}, f32[9,32,288]{2,1,0:T(8,128)S(1)}, f32[9,32,288]{2,1,0:T(8,128)S(1)}, f32[9,32,288]{2,1,0:T(8,128)S(1)}, bf16[896,...) custom-call(f32[104,1536]{1,0:T(8,128)S(1)} %get-tuple-element.37.a_0_, ...), custom_call_target="tpu_custom_call" | custom-call | tf_op jit(solution)/shard_map/late/pallas_call | solution.py:531
  22.2 0.1 collective-permute-start.9
  22.3 0.7 %collective-permute-start.8 = (f32[8,384]{1,0:T(8,128)S(1)}, f32[8,384]{1,0:T(8,128)S(1)}, u32[]{:S(2)}, u32[]{:S(2)}) collective-permute-start(f32[8,384]{1,0:T(8,128)S(1)} %get-tuple-element.56.a_0_), channel_id=1, source_target_pairs={{0,2},{1,3},{2,0},{3,1},{4,6},{5,7},{6,4},{7,5},{8,10},{9,11},{10,... | collective-permute-start | bytes 36872 | tf_op jit(solution)/shard_map/ppermute | solution.py:464
  23.0 1.1 %collective-permute-start.7 = (f32[8,384]{1,0:T(8,128)S(1)}, f32[8,384]{1,0:T(8,128)S(1)}, u32[]{:S(2)}, u32[]{:S(2)}) collective-permute-start(f32[8,384]{1,0:T(8,128)S(1)} %get-tuple-element.56.a_0_), channel_id=1, source_target_pairs={{0,1},{1,0},{2,3},{3,2},{4,5},{5,4},{6,7},{7,6},{8,9},{9,8},{10,11... | collective-permute-start | bytes 36872 | tf_op jit(solution)/shard_map/ppermute | solution.py:464
  24.2 1.3 %collective-permute-done.9.a_3_ = f32[8,384]{1,0:T(8,128)S(1)} collective-permute-done((f32[8,384]{1,0:T(8,128)S(1)}, f32[8,384]{1,0:T(8,128)S(1)}, u32[]{:S(2)}, u32[]{:S(2)}) %collective-permute-start.9) | collective-permute-done | bytes 12320 | tf_op jit(solution)/shard_map/ppermute | solution.py:464
  25.4 0.7 %collective-permute-done.8.a_2_ = f32[8,384]{1,0:T(8,128)S(1)} collective-permute-done((f32[8,384]{1,0:T(8,128)S(1)}, f32[8,384]{1,0:T(8,128)S(1)}, u32[]{:S(2)}, u32[]{:S(2)}) %collective-permute-start.8) | collective-permute-done | bytes 12320 | tf_op jit(solution)/shard_map/ppermute | solution.py:464
  26.1 0.0 collective-permute-done.7.a_1_
  26.1 0.9 %sums.4 = (f32[16,1536]{1,0:T(8,128)S(1)}, f32[16,1536]{1,0:T(8,128)S(1)}) custom-call(f32[8,384]{1,0:T(8,128)S(1)} %get-tuple-element.56.a_0_, f32[8,384]{1,0:T(8,128)S(1)} %collective-permute-done.7.a_1_, f32[8,384]{1,0:T(8,128)S(1)} %collective-permute-done.8.a_2_, f32[8,384]{1,0:T(8,128)S(1)} %collective-permute-done.9.a_3_, ...), custom_call_target="tpu_custom_call" | custom-call | tf_op jit(solution)/shard_map/sums/pallas_call | solution.py:597
  27.0 0.6 %collective-permute-start.11 = (f32[16,1536]{1,0:T(8,128)S(1)}, f32[16,1536]{1,0:T(8,128)S(1)}, u32[]{:S(2)}, u32[]{:S(2)}) collective-permute-start(f32[16,1536]{1,0:T(8,128)S(1)} %get-tuple-element.66), channel_id=1, source_target_pairs={{0,4},{1,5},{2,6},{3,7},{4,0},{5,1},{6,2},{7,3},{8,12},{9,13},{10,... | collective-permute-start | bytes 294920 | tf_op jit(solution)/shard_map/ppermute | solution.py:464
  27.6 1.5 %collective-permute-start.10 = (f32[16,1536]{1,0:T(8,128)S(1)}, f32[16,1536]{1,0:T(8,128)S(1)}, u32[]{:S(2)}, u32[]{:S(2)}) collective-permute-start(f32[16,1536]{1,0:T(8,128)S(1)} %get-tuple-element.61.a_5_), channel_id=1, source_target_pairs={{0,4},{1,5},{2,6},{3,7},{4,0},{5,1},{6,2},{7,3},{8,12},{9,13},{10,... | collective-permute-start | bytes 294920 | tf_op jit(solution)/shard_map/ppermute | solution.py:464
  29.1 0.9 %sums.5 = (f32[16,1536]{1,0:T(8,128)S(1)}, f32[16,1536]{1,0:T(8,128)S(1)}) custom-call(f32[8,384]{1,0:T(8,128)S(1)} %get-tuple-element.56.a_0_, f32[8,384]{1,0:T(8,128)S(1)} %collective-permute-done.7.a_1_, f32[8,384]{1,0:T(8,128)S(1)} %collective-permute-done.8.a_2_, f32[8,384]{1,0:T(8,128)S(1)} %collective-permute-done.9.a_3_, ...), custom_call_target="tpu_custom_call" | custom-call | tf_op jit(solution)/shard_map/sums/pallas_call | solution.py:597
  30.0 1.0 %sums.6.wait = f32[32,1536]{1,0:T(8,128)S(1)} custom-call(f32[8,384]{1,0:T(8,128)S(1)} %get-tuple-element.56.a_0_, f32[8,384]{1,0:T(8,128)S(1)} %collective-permute-done.7.a_1_, f32[8,384]{1,0:T(8,128)S(1)} %collective-permute-done.8.a_2_, f32[8,384]{1,0:T(8,128)S(1)} %collective-permute-done.9.a_3_, f32[8,384]{1,0:T(8,128)S(1)} %get-tuple-element.57.a_4_, ...), custom_call_target="tpu_custom_call" | custom-call | tf_op jit(solution)/shard_map/sums/pallas_call | solution.py:597
  31.0 1.3 %collective-permute-done.11.b = f32[16,1536]{1,0:T(8,128)S(1)} collective-permute-done((f32[16,1536]{1,0:T(8,128)S(1)}, f32[16,1536]{1,0:T(8,128)S(1)}, u32[]{:S(2)}, u32[]{:S(2)}) %collective-permute-start.11) | collective-permute-done | bytes 98336 | tf_op jit(solution)/shard_map/ppermute | solution.py:464
  32.3 1.8 %collective-permute-start.14 = (f32[16,1536]{1,0:T(8,128)S(1)}, f32[16,1536]{1,0:T(8,128)S(1)}, u32[]{:S(2)}, u32[]{:S(2)}) collective-permute-start(f32[16,1536]{1,0:T(8,128)S(1)} %combined.3.a_6_), channel_id=1, source_target_pairs={{0,8},{1,9},{2,10},{3,11},{4,12},{5,13},{6,14},{7,15},{8,0},{9,1},... | collective-permute-start | bytes 294920 | tf_op jit(solution)/shard_map/ppermute | solution.py:464
  34.1 0.0 collective-permute-done.10.b
  34.1 2.0 %collective-permute-start.13 = (f32[16,1536]{1,0:T(8,128)S(1)}, f32[16,1536]{1,0:T(8,128)S(1)}, u32[]{:S(2)}, u32[]{:S(2)}) collective-permute-start(f32[16,1536]{1,0:T(8,128)S(1)} %combined.2.a_5_), channel_id=1, source_target_pairs={{0,8},{1,9},{2,10},{3,11},{4,12},{5,13},{6,14},{7,15},{8,0},{9,1},... | collective-permute-start | bytes 294920 | tf_op jit(solution)/shard_map/ppermute | solution.py:464
  36.1 0.3 collective-permute-start.12
  36.5 1.6 %sums.7 = (f32[32,1536]{1,0:T(8,128)S(1)}, f32[2,96]{1,0:T(2,128)}) custom-call(f32[8,384]{1,0:T(8,128)S(1)} %get-tuple-element.56.a_0_, f32[8,384]{1,0:T(8,128)S(1)} %collective-permute-done.7.a_1_, f32[8,384]{1,0:T(8,128)S(1)} %collective-permute-done.8.a_2_, f32[8,384]{1,0:T(8,128)S(1)} %collective-permute-done.9.a_3_, ...), custom_call_target="tpu_custom_call" | custom-call | tf_op jit(solution)/shard_map/sums/pallas_call | solution.py:597
  38.0 0.0 copy-start
  38.0 2.2 %collective-permute-done.14.a_1_ = f32[16,1536]{1,0:T(8,128)S(1)} collective-permute-done((f32[16,1536]{1,0:T(8,128)S(1)}, f32[16,1536]{1,0:T(8,128)S(1)}, u32[]{:S(2)}, u32[]{:S(2)}) %collective-permute-start.14) | collective-permute-done | bytes 98336 | tf_op jit(solution)/shard_map/ppermute | solution.py:464
  40.2 1.8 %collective-permute-done.13.a_0_ = f32[16,1536]{1,0:T(8,128)S(1)} collective-permute-done((f32[16,1536]{1,0:T(8,128)S(1)}, f32[16,1536]{1,0:T(8,128)S(1)}, u32[]{:S(2)}, u32[]{:S(2)}) %collective-permute-start.13) | collective-permute-done | bytes 98336 | tf_op jit(solution)/shard_map/ppermute | solution.py:464
  42.0 1.3 %collective-permute-done.12.a_1_ = f32[32,1536]{1,0:T(8,128)S(1)} collective-permute-done((f32[32,1536]{1,0:T(8,128)S(1)}, f32[32,1536]{1,0:T(8,128)S(1)}, u32[]{:S(2)}, u32[]{:S(2)}) %collective-permute-start.12) | collective-permute-done | bytes 196640 | tf_op jit(solution)/shard_map/ppermute | solution.py:464
  43.3 0.0 copy-done
  43.3 0.7 %update.1 = f32[32,1024]{1,0:T(8,128)} custom-call(f32[32,1536]{1,0:T(8,128)S(1)} %get-tuple-element.69.a_0_, f32[32,1536]{1,0:T(8,128)S(1)} %collective-permute-done.12.a_1_, f32[16,1536]{1,0:T(8,128)S(1)} %get-tuple-element.70.a_2_, f32[16,1536]{1,0:T(8,128)S(1)} %get-tuple-element.71.a_3_, f32[1,512]{1,0:T(1,128)S(1)} %bitcast.8), custom_call_target="tpu_custom_call" | custom-call | tf_op jit(solution)/shard_map/update/pallas_call | solution.py:643
  (3 shorter events, 0.0 us)
Async XLA Ops:
  0.6 13.6 %collective-permute-start.1 = (f32[96,1024]{1,0:T(8,128)}, f32[96,1024]{1,0:T(8,128)S(1)}, u32[]{:S(2)}, u32[]{:S(2)}) collective-permute-start(f32[96,1024]{1,0:T(8,128)} %src_at.1), channel_id=1, source_target_pairs={{0,2},{1,3},{2,0},{3,1},{4,6},{5,7},{6,4},{7,5},{8,10},{9,11},{10,... | collective-permute-start | bytes 1179656 | tf_op jit(solution)/shard_map/ppermute | solution.py:464
  3.7 11.8 %collective-permute-start.5 = (f32[32,1024]{1,0:T(8,128)}, f32[32,1024]{1,0:T(8,128)S(1)}, u32[]{:S(2)}, u32[]{:S(2)}) collective-permute-start(f32[32,1024]{1,0:T(8,128)} %bitcast.9), channel_id=1, source_target_pairs={{0,12},{1,13},{2,14},{3,15},{4,8},{5,9},{6,10},{7,11},{8,4},{9,5},... | collective-permute-start | bytes 393224 | tf_op jit(solution)/shard_map/ppermute | solution.py:464
  7.3 8.5 %collective-permute-start.4 = (f32[32,1024]{1,0:T(8,128)}, f32[32,1024]{1,0:T(8,128)S(1)}, u32[]{:S(2)}, u32[]{:S(2)}) collective-permute-start(f32[32,1024]{1,0:T(8,128)} %bitcast.10), channel_id=1, source_target_pairs={{0,4},{1,5},{2,6},{3,7},{4,0},{5,1},{6,2},{7,3},{8,12},{9,13},{10,... | collective-permute-start | bytes 393224 | tf_op jit(solution)/shard_map/ppermute | solution.py:464
  7.3 11.0 %collective-permute-start.6 = (f32[32,1024]{1,0:T(8,128)}, f32[32,1024]{1,0:T(8,128)S(1)}, u32[]{:S(2)}, u32[]{:S(2)}) collective-permute-start(f32[32,1024]{1,0:T(8,128)} %bitcast.11), channel_id=1, source_target_pairs={{0,8},{1,9},{2,10},{3,11},{4,12},{5,13},{6,14},{7,15},{8,0},{9,1},... | collective-permute-start | bytes 393224 | tf_op jit(solution)/shard_map/ppermute | solution.py:464
  10.5 3.7 %collective-permute-start.2 = (f32[8,128]{1,0:T(8,128)S(1)}, f32[8,128]{1,0:T(8,128)S(1)}, u32[]{:S(2)}, u32[]{:S(2)}) collective-permute-start(f32[8,128]{1,0:T(8,128)S(1)} %get-tuple-element.38.wait), channel_id=1, source_target_pairs={{0,2},{1,3},{2,0},{3,1},{4,6},{5,7},{6,4},{7,5},{8,10},{9,11},{10,... | collective-permute-start | bytes 12296 | tf_op jit(solution)/shard_map/ppermute | solution.py:464
  14.2 4.4 %collective-permute-start = (f32[104,1536]{1,0:T(8,128)S(1)}, f32[104,1536]{1,0:T(8,128)S(1)}, u32[]{:S(2)}, u32[]{:S(2)}) collective-permute-start(f32[104,1536]{1,0:T(8,128)S(1)} %get-tuple-element.37.a_0_), channel_id=1, source_target_pairs={{0,1},{1,0},{2,3},{3,2},{4,5},{5,4},{6,7},{7,6},{8,9},{9,8},{10,11... | collective-permute-start | bytes 1916936 | tf_op jit(solution)/shard_map/ppermute | solution.py:464
  14.9 3.7 %collective-permute-start.3 = (f32[104,1536]{1,0:T(8,128)S(1)}, f32[104,1536]{1,0:T(8,128)S(1)}, u32[]{:S(2)}, u32[]{:S(2)}) collective-permute-start(f32[104,1536]{1,0:T(8,128)S(1)} %neighbour.1.wait.a_2_), channel_id=1, source_target_pairs={{0,1},{1,0},{2,3},{3,2},{4,5},{5,4},{6,7},{7,6},{8,9},{9,8},{10,11... | collective-permute-start | bytes 1916936 | tf_op jit(solution)/shard_map/ppermute | solution.py:464
  22.2 3.2 %collective-permute-start.9 = (f32[8,384]{1,0:T(8,128)S(1)}, f32[8,384]{1,0:T(8,128)S(1)}, u32[]{:S(2)}, u32[]{:S(2)}) collective-permute-start(f32[8,384]{1,0:T(8,128)S(1)} %get-tuple-element.56.a_0_), channel_id=1, source_target_pairs={{0,3},{1,2},{2,1},{3,0},{4,7},{5,6},{6,5},{7,4},{8,11},{9,10},{10,... | collective-permute-start | bytes 36872 | tf_op jit(solution)/shard_map/ppermute | solution.py:464
  22.3 3.8 %collective-permute-start.8 = (f32[8,384]{1,0:T(8,128)S(1)}, f32[8,384]{1,0:T(8,128)S(1)}, u32[]{:S(2)}, u32[]{:S(2)}) collective-permute-start(f32[8,384]{1,0:T(8,128)S(1)} %get-tuple-element.56.a_0_), channel_id=1, source_target_pairs={{0,2},{1,3},{2,0},{3,1},{4,6},{5,7},{6,4},{7,5},{8,10},{9,11},{10,... | collective-permute-start | bytes 36872 | tf_op jit(solution)/shard_map/ppermute | solution.py:464
  23.0 3.0 %collective-permute-start.7 = (f32[8,384]{1,0:T(8,128)S(1)}, f32[8,384]{1,0:T(8,128)S(1)}, u32[]{:S(2)}, u32[]{:S(2)}) collective-permute-start(f32[8,384]{1,0:T(8,128)S(1)} %get-tuple-element.56.a_0_), channel_id=1, source_target_pairs={{0,1},{1,0},{2,3},{3,2},{4,5},{5,4},{6,7},{7,6},{8,9},{9,8},{10,11... | collective-permute-start | bytes 36872 | tf_op jit(solution)/shard_map/ppermute | solution.py:464
  27.0 5.3 %collective-permute-start.11 = (f32[16,1536]{1,0:T(8,128)S(1)}, f32[16,1536]{1,0:T(8,128)S(1)}, u32[]{:S(2)}, u32[]{:S(2)}) collective-permute-start(f32[16,1536]{1,0:T(8,128)S(1)} %get-tuple-element.66), channel_id=1, source_target_pairs={{0,4},{1,5},{2,6},{3,7},{4,0},{5,1},{6,2},{7,3},{8,12},{9,13},{10,... | collective-permute-start | bytes 294920 | tf_op jit(solution)/shard_map/ppermute | solution.py:464
  27.6 6.5 %collective-permute-start.10 = (f32[16,1536]{1,0:T(8,128)S(1)}, f32[16,1536]{1,0:T(8,128)S(1)}, u32[]{:S(2)}, u32[]{:S(2)}) collective-permute-start(f32[16,1536]{1,0:T(8,128)S(1)} %get-tuple-element.61.a_5_), channel_id=1, source_target_pairs={{0,4},{1,5},{2,6},{3,7},{4,0},{5,1},{6,2},{7,3},{8,12},{9,13},{10,... | collective-permute-start | bytes 294920 | tf_op jit(solution)/shard_map/ppermute | solution.py:464
  32.3 7.9 %collective-permute-start.14 = (f32[16,1536]{1,0:T(8,128)S(1)}, f32[16,1536]{1,0:T(8,128)S(1)}, u32[]{:S(2)}, u32[]{:S(2)}) collective-permute-start(f32[16,1536]{1,0:T(8,128)S(1)} %combined.3.a_6_), channel_id=1, source_target_pairs={{0,8},{1,9},{2,10},{3,11},{4,12},{5,13},{6,14},{7,15},{8,0},{9,1},... | collective-permute-start | bytes 294920 | tf_op jit(solution)/shard_map/ppermute | solution.py:464
  34.1 7.9 %collective-permute-start.13 = (f32[16,1536]{1,0:T(8,128)S(1)}, f32[16,1536]{1,0:T(8,128)S(1)}, u32[]{:S(2)}, u32[]{:S(2)}) collective-permute-start(f32[16,1536]{1,0:T(8,128)S(1)} %combined.2.a_5_), channel_id=1, source_target_pairs={{0,8},{1,9},{2,10},{3,11},{4,12},{5,13},{6,14},{7,15},{8,0},{9,1},... | collective-permute-start | bytes 294920 | tf_op jit(solution)/shard_map/ppermute | solution.py:464
  36.1 7.2 %collective-permute-start.12 = (f32[32,1536]{1,0:T(8,128)S(1)}, f32[32,1536]{1,0:T(8,128)S(1)}, u32[]{:S(2)}, u32[]{:S(2)}) collective-permute-start(f32[32,1536]{1,0:T(8,128)S(1)} %sums.6.wait), channel_id=1, source_target_pairs={{0,4},{1,5},{2,6},{3,7},{4,0},{5,1},{6,2},{7,3},{8,12},{9,13},{10,... | collective-permute-start | bytes 589832 | tf_op jit(solution)/shard_map/ppermute | solution.py:464
  38.0 5.3 %copy-start = (f32[512]{0:T(512)S(1)}, f32[512]{0:T(512)}, u32[]{:S(2)}) copy-start(f32[512]{0:T(512)} %param.16) | copy-start | bytes 6148

commit v17 on v16

--- a/solution.py
+++ b/solution.py
@@ -559,7 +559,7 @@
     )(ynb, crossed(facts, 2), inverse_noise, prepared[2])
     cynb = crossed(ynb_prepared, 1)
 
-    order = [*range(blocks - 1, 2, -1), 1, 2]
+    order = [*range(2, blocks - 1), 1, blocks - 1]
     wait = ynb_prepared
     by_block = {0: prepared}
     for n in order:

time: 44.2 us -> 44.8 us (1.014)
  starting transfers between devices: 16.5 us -> 18.1 us
  waiting for transfers between devices: 12.9 us -> 11.8 us
    ppermute x15, starting transfers between devices: 16.5 us -> 18.1 us  [crossed(): return lax.ppermute(block, 'dom', [(i, i ^ mask) for i in range(size)])]
    ppermute x15, waiting for transfers between devices: 12.9 us -> 11.8 us  [crossed(): return lax.ppermute(block, 'dom', [(i, i ^ mask) for i in range(size)])]
where the time goes in v17:
time: 44.8 us; the launch traced here: 44.6 us
  starting transfers between devices  18.1 us (40%)
  Pallas kernels  13.3 us (30%)
  waiting for transfers between devices  11.8 us (26%)
  between operations  1.39 us (3%)
    ppermute x15, starting transfers between devices, crossed(): return lax.ppermute(block, 'dom', [(i, i ^ mask) for i in range(size)])  18.1 us
    ppermute x15, waiting for transfers between devices, crossed(): return lax.ppermute(block, 'dom', [(i, i ^ mask) for i in range(size)])  11.8 us
    pallas_call x4, Pallas kernels, sums(): pl.pallas_call(lambda *a: sum_kernel(n, cuts, last, len(waits), *a), out_...  4.39 us
    pallas_call x1, Pallas kernels, call(): pl.pallas_call(kernel, cost_estimate=cost, out_shape=tuple(out_shape), in...  3.62 us
    pallas_call x1, Pallas kernels, on_device(): pl.pallas_call(own_kernel, out_shape=(jax.ShapeDtypeStruct((slots + 8, wi...  1.83 us
    pallas_call x1, Pallas kernels, on_device(): pl.pallas_call(own_refs_kernel, out_shape=tuple(block_shapes), in_specs=[...  1.15 us
    pallas_call x3, Pallas kernels, on_device(): pl.pallas_call(refs_kernel, out_shape=tuple(block_shapes), in_specs=[vmem...  0.94 us
  transfers between devices with their start and end apart: 15, of which 8 were waited for; matrix products, arithmetic and copies ran while one was open for 0% of the time, Pallas kernels for 18%

profile of v17, /device:TPU:0, one launch (start us, length us, event | category | flops | bytes accessed | tf_op | source)
XLA Modules:
  0.0 44.6 jit_solution(15827036356097913084)
XLA Ops:
  0.6 3.0 %collective-permute-start.1 = (f32[96,1024]{1,0:T(8,128)}, f32[96,1024]{1,0:T(8,128)S(1)}, u32[]{:S(2)}, u32[]{:S(2)}) collective-permute-start(f32[96,1024]{1,0:T(8,128)} %src_at.1), channel_id=1, source_target_pairs={{0,2},{1,3},{2,0},{3,1},{4,6},{5,7},{6,4},{7,5},{8,10},{9,11},{10,... | collective-permute-start | bytes 1179656 | tf_op jit(solution)/shard_map/ppermute | solution.py:464
  3.7 2.6 %collective-permute-start.5 = (f32[32,1024]{1,0:T(8,128)}, f32[32,1024]{1,0:T(8,128)S(1)}, u32[]{:S(2)}, u32[]{:S(2)}) collective-permute-start(f32[32,1024]{1,0:T(8,128)} %bitcast.9), channel_id=1, source_target_pairs={{0,8},{1,9},{2,10},{3,11},{4,12},{5,13},{6,14},{7,15},{8,0},{9,1},... | collective-permute-start | bytes 393224 | tf_op jit(solution)/shard_map/ppermute | solution.py:464
  6.3 1.6 %collective-permute-start.4 = (f32[32,1024]{1,0:T(8,128)}, f32[32,1024]{1,0:T(8,128)S(1)}, u32[]{:S(2)}, u32[]{:S(2)}) collective-permute-start(f32[32,1024]{1,0:T(8,128)} %bitcast.10), channel_id=1, source_target_pairs={{0,4},{1,5},{2,6},{3,7},{4,0},{5,1},{6,2},{7,3},{8,12},{9,13},{10,... | collective-permute-start | bytes 393224 | tf_op jit(solution)/shard_map/ppermute | solution.py:464
  7.8 0.2 collective-permute-start.6
  8.7 1.8 %own.1 = (f32[104,1536]{1,0:T(8,128)S(1)}, f32[8,128]{1,0:T(8,128)S(1)}, f32[128,512]{1,0:T(8,128)S(1)}) custom-call(f32[96,1024]{1,0:T(8,128)} %src_at.1, f32[1,96]{1,0:T(1,128)} %bitcast.15, s32[2,96]{1,0:T(2,128)} %bitcast.14, s32[1,96]{1,0:T(1,128)} %bitcast.16, s32[1,96]{1,0:T(1,128)} %bitcast.17, f32[128,512]{1,0:T(8,128)} %noise_at.1, ...), custom_call_target="tpu_custom_call" | custom-call | tf_op jit(solution)/shard_map/own/pallas_call | solution.py:505
  10.5 0.4 collective-permute-start.2
  10.9 1.2 %own_refs.1 = (bf16[288,1024]{1,0:T(8,128)(2,1)S(1)}, bf16[288,1024]{1,0:T(8,128)(2,1)S(1)}, bf16[32,512]{1,0:T(8,128)(2,1)S(1)}, bf16[32,512]{1,0:T(8,128)(2,1)S(1)}) custom-call(f32[32,1024]{1,0:T(8,128)} %bitcast.12, f32[8,128]{1,0:T(8,128)S(1)} %get-tuple-element.38.wait), custom_call_target="tpu_custom_call" | custom-call | tf_op jit(solution)/shard_map/own_refs/pallas_call | solution.py:542
  12.1 2.2 %collective-permute-done.2.facts = f32[8,128]{1,0:T(8,128)S(1)} collective-permute-done((f32[8,128]{1,0:T(8,128)S(1)}, f32[8,128]{1,0:T(8,128)S(1)}, u32[]{:S(2)}, u32[]{:S(2)}) %collective-permute-start.2) | collective-permute-done | bytes 4128 | tf_op jit(solution)/shard_map/ppermute | solution.py:464
  14.2 0.0 collective-permute-start
  14.2 0.0 collective-permute-done.1.src
  14.2 0.6 %neighbour.1.wait.a_2_ = f32[104,1536]{1,0:T(8,128)S(1)} custom-call(f32[96,1024]{1,0:T(8,128)S(1)} %collective-permute-done.1.src, f32[8,128]{1,0:T(8,128)S(1)} %collective-permute-done.2.facts, f32[128,512]{1,0:T(8,128)S(1)} %get-tuple-element.39.inverse_noise, bf16[32,512]{1,0:T(8,128)(2,1)S(1)} %get-tuple-element.40.wait.a_6_), custom_call_target="tpu_custom_call" | custom-call | tf_op jit(solution)/shard_map/neighbour/pallas_call | solution.py:551
  14.9 0.6 %collective-permute-start.3 = (f32[104,1536]{1,0:T(8,128)S(1)}, f32[104,1536]{1,0:T(8,128)S(1)}, u32[]{:S(2)}, u32[]{:S(2)}) collective-permute-start(f32[104,1536]{1,0:T(8,128)S(1)} %neighbour.1.wait.a_2_), channel_id=1, source_target_pairs={{0,1},{1,0},{2,3},{3,2},{4,5},{5,4},{6,7},{7,6},{8,9},{9,8},{10,11... | collective-permute-start | bytes 1916936 | tf_op jit(solution)/shard_map/ppermute | solution.py:464
  15.4 1.1 %collective-permute-done.5.ref = f32[32,1024]{1,0:T(8,128)S(1)} collective-permute-done((f32[32,1024]{1,0:T(8,128)}, f32[32,1024]{1,0:T(8,128)S(1)}, u32[]{:S(2)}, u32[]{:S(2)}) %collective-permute-start.5) | collective-permute-done | bytes 131104 | tf_op jit(solution)/shard_map/ppermute | solution.py:464
  16.5 0.3 refs.3
  16.8 0.0 collective-permute-done.4.ref
  16.8 0.3 refs.4
  17.2 0.0 collective-permute-done.6.ref
  17.2 0.3 refs.5
  17.5 0.0 collective-permute-done.a_1_
  17.5 0.0 collective-permute-done.3.a_3_
  17.5 3.6 %late.1 = (f32[9,32,288]{2,1,0:T(8,128)S(1)}, f32[9,32,288]{2,1,0:T(8,128)S(1)}, f32[9,32,288]{2,1,0:T(8,128)S(1)}, f32[9,32,288]{2,1,0:T(8,128)S(1)}, bf16[896,...) custom-call(f32[104,1536]{1,0:T(8,128)S(1)} %get-tuple-element.37.a_0_, ...), custom_call_target="tpu_custom_call" | custom-call | tf_op jit(solution)/shard_map/late/pallas_call | solution.py:531
  21.1 0.2 collective-permute-start.9
  21.4 1.4 %collective-permute-start.8 = (f32[8,384]{1,0:T(8,128)S(1)}, f32[8,384]{1,0:T(8,128)S(1)}, u32[]{:S(2)}, u32[]{:S(2)}) collective-permute-start(f32[8,384]{1,0:T(8,128)S(1)} %get-tuple-element.56.a_0_), channel_id=1, source_target_pairs={{0,2},{1,3},{2,0},{3,1},{4,6},{5,7},{6,4},{7,5},{8,10},{9,11},{10,... | collective-permute-start | bytes 36872 | tf_op jit(solution)/shard_map/ppermute | solution.py:464
  22.8 0.3 collective-permute-start.7
  23.1 1.3 %collective-permute-done.9.a_3_ = f32[8,384]{1,0:T(8,128)S(1)} collective-permute-done((f32[8,384]{1,0:T(8,128)S(1)}, f32[8,384]{1,0:T(8,128)S(1)}, u32[]{:S(2)}, u32[]{:S(2)}) %collective-permute-start.9) | collective-permute-done | bytes 12320 | tf_op jit(solution)/shard_map/ppermute | solution.py:464
  24.3 0.7 %collective-permute-done.8.a_2_ = f32[8,384]{1,0:T(8,128)S(1)} collective-permute-done((f32[8,384]{1,0:T(8,128)S(1)}, f32[8,384]{1,0:T(8,128)S(1)}, u32[]{:S(2)}, u32[]{:S(2)}) %collective-permute-start.8) | collective-permute-done | bytes 12320 | tf_op jit(solution)/shard_map/ppermute | solution.py:464
  25.1 0.0 collective-permute-done.7.a_1_
  25.1 0.9 %sums.4 = (f32[16,1536]{1,0:T(8,128)S(1)}, f32[16,1536]{1,0:T(8,128)S(1)}) custom-call(f32[8,384]{1,0:T(8,128)S(1)} %get-tuple-element.56.a_0_, f32[8,384]{1,0:T(8,128)S(1)} %collective-permute-done.7.a_1_, f32[8,384]{1,0:T(8,128)S(1)} %collective-permute-done.8.a_2_, f32[8,384]{1,0:T(8,128)S(1)} %collective-permute-done.9.a_3_, ...), custom_call_target="tpu_custom_call" | custom-call | tf_op jit(solution)/shard_map/sums/pallas_call | solution.py:597
  26.0 1.7 %collective-permute-start.11 = (f32[16,1536]{1,0:T(8,128)S(1)}, f32[16,1536]{1,0:T(8,128)S(1)}, u32[]{:S(2)}, u32[]{:S(2)}) collective-permute-start(f32[16,1536]{1,0:T(8,128)S(1)} %get-tuple-element.66), channel_id=1, source_target_pairs={{0,4},{1,5},{2,6},{3,7},{4,0},{5,1},{6,2},{7,3},{8,12},{9,13},{10,... | collective-permute-start | bytes 294920 | tf_op jit(solution)/shard_map/ppermute | solution.py:464
  27.8 0.3 collective-permute-start.10
  28.1 0.9 %sums.5 = (f32[16,1536]{1,0:T(8,128)S(1)}, f32[16,1536]{1,0:T(8,128)S(1)}) custom-call(f32[8,384]{1,0:T(8,128)S(1)} %get-tuple-element.56.a_0_, f32[8,384]{1,0:T(8,128)S(1)} %collective-permute-done.7.a_1_, f32[8,384]{1,0:T(8,128)S(1)} %collective-permute-done.8.a_2_, f32[8,384]{1,0:T(8,128)S(1)} %collective-permute-done.9.a_3_, ...), custom_call_target="tpu_custom_call" | custom-call | tf_op jit(solution)/shard_map/sums/pallas_call | solution.py:597
  29.0 0.9 %sums.6.wait = f32[32,1536]{1,0:T(8,128)S(1)} custom-call(f32[8,384]{1,0:T(8,128)S(1)} %get-tuple-element.56.a_0_, f32[8,384]{1,0:T(8,128)S(1)} %collective-permute-done.7.a_1_, f32[8,384]{1,0:T(8,128)S(1)} %collective-permute-done.8.a_2_, f32[8,384]{1,0:T(8,128)S(1)} %collective-permute-done.9.a_3_, f32[8,384]{1,0:T(8,128)S(1)} %get-tuple-element.57.a_4_, ...), custom_call_target="tpu_custom_call" | custom-call | tf_op jit(solution)/shard_map/sums/pallas_call | solution.py:597
  30.0 1.6 %collective-permute-done.11.b = f32[16,1536]{1,0:T(8,128)S(1)} collective-permute-done((f32[16,1536]{1,0:T(8,128)S(1)}, f32[16,1536]{1,0:T(8,128)S(1)}, u32[]{:S(2)}, u32[]{:S(2)}) %collective-permute-start.11) | collective-permute-done | bytes 98336 | tf_op jit(solution)/shard_map/ppermute | solution.py:464
  31.7 3.7 %collective-permute-start.14 = (f32[16,1536]{1,0:T(8,128)S(1)}, f32[16,1536]{1,0:T(8,128)S(1)}, u32[]{:S(2)}, u32[]{:S(2)}) collective-permute-start(f32[16,1536]{1,0:T(8,128)S(1)} %combined.3.a_6_), channel_id=1, source_target_pairs={{0,8},{1,9},{2,10},{3,11},{4,12},{5,13},{6,14},{7,15},{8,0},{9,1},... | collective-permute-start | bytes 294920 | tf_op jit(solution)/shard_map/ppermute | solution.py:464
  35.4 0.0 collective-permute-done.10.b
  35.4 2.1 %collective-permute-start.13 = (f32[16,1536]{1,0:T(8,128)S(1)}, f32[16,1536]{1,0:T(8,128)S(1)}, u32[]{:S(2)}, u32[]{:S(2)}) collective-permute-start(f32[16,1536]{1,0:T(8,128)S(1)} %combined.2.a_5_), channel_id=1, source_target_pairs={{0,8},{1,9},{2,10},{3,11},{4,12},{5,13},{6,14},{7,15},{8,0},{9,1},... | collective-permute-start | bytes 294920 | tf_op jit(solution)/shard_map/ppermute | solution.py:464
  37.5 0.0 collective-permute-start.12
  37.5 1.6 %sums.7 = (f32[32,1536]{1,0:T(8,128)S(1)}, f32[2,96]{1,0:T(2,128)}) custom-call(f32[8,384]{1,0:T(8,128)S(1)} %get-tuple-element.56.a_0_, f32[8,384]{1,0:T(8,128)S(1)} %collective-permute-done.7.a_1_, f32[8,384]{1,0:T(8,128)S(1)} %collective-permute-done.8.a_2_, f32[8,384]{1,0:T(8,128)S(1)} %collective-permute-done.9.a_3_, ...), custom_call_target="tpu_custom_call" | custom-call | tf_op jit(solution)/shard_map/sums/pallas_call | solution.py:597
  39.0 0.0 copy-start
  39.0 1.5 %collective-permute-done.14.a_1_ = f32[16,1536]{1,0:T(8,128)S(1)} collective-permute-done((f32[16,1536]{1,0:T(8,128)S(1)}, f32[16,1536]{1,0:T(8,128)S(1)}, u32[]{:S(2)}, u32[]{:S(2)}) %collective-permute-start.14) | collective-permute-done | bytes 98336 | tf_op jit(solution)/shard_map/ppermute | solution.py:464
  40.5 1.7 %collective-permute-done.13.a_0_ = f32[16,1536]{1,0:T(8,128)S(1)} collective-permute-done((f32[16,1536]{1,0:T(8,128)S(1)}, f32[16,1536]{1,0:T(8,128)S(1)}, u32[]{:S(2)}, u32[]{:S(2)}) %collective-permute-start.13) | collective-permute-done | bytes 98336 | tf_op jit(solution)/shard_map/ppermute | solution.py:464
  42.2 1.7 %collective-permute-done.12.a_1_ = f32[32,1536]{1,0:T(8,128)S(1)} collective-permute-done((f32[32,1536]{1,0:T(8,128)S(1)}, f32[32,1536]{1,0:T(8,128)S(1)}, u32[]{:S(2)}, u32[]{:S(2)}) %collective-permute-start.12) | collective-permute-done | bytes 196640 | tf_op jit(solution)/shard_map/ppermute | solution.py:464
  43.9 0.0 copy-done
  43.9 0.7 %update.1 = f32[32,1024]{1,0:T(8,128)} custom-call(f32[32,1536]{1,0:T(8,128)S(1)} %get-tuple-element.69.a_0_, f32[32,1536]{1,0:T(8,128)S(1)} %collective-permute-done.12.a_1_, f32[16,1536]{1,0:T(8,128)S(1)} %get-tuple-element.70.a_2_, f32[16,1536]{1,0:T(8,128)S(1)} %get-tuple-element.71.a_3_, f32[1,512]{1,0:T(1,128)S(1)} %bitcast.8), custom_call_target="tpu_custom_call" | custom-call | tf_op jit(solution)/shard_map/update/pallas_call | solution.py:643
  (3 shorter events, 0.0 us)
Async XLA Ops:
  0.6 13.6 %collective-permute-start.1 = (f32[96,1024]{1,0:T(8,128)}, f32[96,1024]{1,0:T(8,128)S(1)}, u32[]{:S(2)}, u32[]{:S(2)}) collective-permute-start(f32[96,1024]{1,0:T(8,128)} %src_at.1), channel_id=1, source_target_pairs={{0,2},{1,3},{2,0},{3,1},{4,6},{5,7},{6,4},{7,5},{8,10},{9,11},{10,... | collective-permute-start | bytes 1179656 | tf_op jit(solution)/shard_map/ppermute | solution.py:464
  3.7 12.8 %collective-permute-start.5 = (f32[32,1024]{1,0:T(8,128)}, f32[32,1024]{1,0:T(8,128)S(1)}, u32[]{:S(2)}, u32[]{:S(2)}) collective-permute-start(f32[32,1024]{1,0:T(8,128)} %bitcast.9), channel_id=1, source_target_pairs={{0,8},{1,9},{2,10},{3,11},{4,12},{5,13},{6,14},{7,15},{8,0},{9,1},... | collective-permute-start | bytes 393224 | tf_op jit(solution)/shard_map/ppermute | solution.py:464
  6.3 10.6 %collective-permute-start.4 = (f32[32,1024]{1,0:T(8,128)}, f32[32,1024]{1,0:T(8,128)S(1)}, u32[]{:S(2)}, u32[]{:S(2)}) collective-permute-start(f32[32,1024]{1,0:T(8,128)} %bitcast.10), channel_id=1, source_target_pairs={{0,4},{1,5},{2,6},{3,7},{4,0},{5,1},{6,2},{7,3},{8,12},{9,13},{10,... | collective-permute-start | bytes 393224 | tf_op jit(solution)/shard_map/ppermute | solution.py:464
  7.8 9.3 %collective-permute-start.6 = (f32[32,1024]{1,0:T(8,128)}, f32[32,1024]{1,0:T(8,128)S(1)}, u32[]{:S(2)}, u32[]{:S(2)}) collective-permute-start(f32[32,1024]{1,0:T(8,128)} %bitcast.11), channel_id=1, source_target_pairs={{0,12},{1,13},{2,14},{3,15},{4,8},{5,9},{6,10},{7,11},{8,4},{9,5},... | collective-permute-start | bytes 393224 | tf_op jit(solution)/shard_map/ppermute | solution.py:464
  10.5 3.7 %collective-permute-start.2 = (f32[8,128]{1,0:T(8,128)S(1)}, f32[8,128]{1,0:T(8,128)S(1)}, u32[]{:S(2)}, u32[]{:S(2)}) collective-permute-start(f32[8,128]{1,0:T(8,128)S(1)} %get-tuple-element.38.wait), channel_id=1, source_target_pairs={{0,2},{1,3},{2,0},{3,1},{4,6},{5,7},{6,4},{7,5},{8,10},{9,11},{10,... | collective-permute-start | bytes 12296 | tf_op jit(solution)/shard_map/ppermute | solution.py:464
  14.2 3.3 %collective-permute-start = (f32[104,1536]{1,0:T(8,128)S(1)}, f32[104,1536]{1,0:T(8,128)S(1)}, u32[]{:S(2)}, u32[]{:S(2)}) collective-permute-start(f32[104,1536]{1,0:T(8,128)S(1)} %get-tuple-element.37.a_0_), channel_id=1, source_target_pairs={{0,1},{1,0},{2,3},{3,2},{4,5},{5,4},{6,7},{7,6},{8,9},{9,8},{10,11... | collective-permute-start | bytes 1916936 | tf_op jit(solution)/shard_map/ppermute | solution.py:464
  14.9 2.6 %collective-permute-start.3 = (f32[104,1536]{1,0:T(8,128)S(1)}, f32[104,1536]{1,0:T(8,128)S(1)}, u32[]{:S(2)}, u32[]{:S(2)}) collective-permute-start(f32[104,1536]{1,0:T(8,128)S(1)} %neighbour.1.wait.a_2_), channel_id=1, source_target_pairs={{0,1},{1,0},{2,3},{3,2},{4,5},{5,4},{6,7},{7,6},{8,9},{9,8},{10,11... | collective-permute-start | bytes 1916936 | tf_op jit(solution)/shard_map/ppermute | solution.py:464
  21.1 3.2 %collective-permute-start.9 = (f32[8,384]{1,0:T(8,128)S(1)}, f32[8,384]{1,0:T(8,128)S(1)}, u32[]{:S(2)}, u32[]{:S(2)}) collective-permute-start(f32[8,384]{1,0:T(8,128)S(1)} %get-tuple-element.56.a_0_), channel_id=1, source_target_pairs={{0,3},{1,2},{2,1},{3,0},{4,7},{5,6},{6,5},{7,4},{8,11},{9,10},{10,... | collective-permute-start | bytes 36872 | tf_op jit(solution)/shard_map/ppermute | solution.py:464
  21.4 3.7 %collective-permute-start.8 = (f32[8,384]{1,0:T(8,128)S(1)}, f32[8,384]{1,0:T(8,128)S(1)}, u32[]{:S(2)}, u32[]{:S(2)}) collective-permute-start(f32[8,384]{1,0:T(8,128)S(1)} %get-tuple-element.56.a_0_), channel_id=1, source_target_pairs={{0,2},{1,3},{2,0},{3,1},{4,6},{5,7},{6,4},{7,5},{8,10},{9,11},{10,... | collective-permute-start | bytes 36872 | tf_op jit(solution)/shard_map/ppermute | solution.py:464
  22.8 2.3 %collective-permute-start.7 = (f32[8,384]{1,0:T(8,128)S(1)}, f32[8,384]{1,0:T(8,128)S(1)}, u32[]{:S(2)}, u32[]{:S(2)}) collective-permute-start(f32[8,384]{1,0:T(8,128)S(1)} %get-tuple-element.56.a_0_), channel_id=1, source_target_pairs={{0,1},{1,0},{2,3},{3,2},{4,5},{5,4},{6,7},{7,6},{8,9},{9,8},{10,11... | collective-permute-start | bytes 36872 | tf_op jit(solution)/shard_map/ppermute | solution.py:464
  26.0 5.6 %collective-permute-start.11 = (f32[16,1536]{1,0:T(8,128)S(1)}, f32[16,1536]{1,0:T(8,128)S(1)}, u32[]{:S(2)}, u32[]{:S(2)}) collective-permute-start(f32[16,1536]{1,0:T(8,128)S(1)} %get-tuple-element.66), channel_id=1, source_target_pairs={{0,4},{1,5},{2,6},{3,7},{4,0},{5,1},{6,2},{7,3},{8,12},{9,13},{10,... | collective-permute-start | bytes 294920 | tf_op jit(solution)/shard_map/ppermute | solution.py:464
  27.8 7.6 %collective-permute-start.10 = (f32[16,1536]{1,0:T(8,128)S(1)}, f32[16,1536]{1,0:T(8,128)S(1)}, u32[]{:S(2)}, u32[]{:S(2)}) collective-permute-start(f32[16,1536]{1,0:T(8,128)S(1)} %get-tuple-element.61.a_5_), channel_id=1, source_target_pairs={{0,4},{1,5},{2,6},{3,7},{4,0},{5,1},{6,2},{7,3},{8,12},{9,13},{10,... | collective-permute-start | bytes 294920 | tf_op jit(solution)/shard_map/ppermute | solution.py:464
  31.7 8.9 %collective-permute-start.14 = (f32[16,1536]{1,0:T(8,128)S(1)}, f32[16,1536]{1,0:T(8,128)S(1)}, u32[]{:S(2)}, u32[]{:S(2)}) collective-permute-start(f32[16,1536]{1,0:T(8,128)S(1)} %combined.3.a_6_), channel_id=1, source_target_pairs={{0,8},{1,9},{2,10},{3,11},{4,12},{5,13},{6,14},{7,15},{8,0},{9,1},... | collective-permute-start | bytes 294920 | tf_op jit(solution)/shard_map/ppermute | solution.py:464
  35.4 6.8 %collective-permute-start.13 = (f32[16,1536]{1,0:T(8,128)S(1)}, f32[16,1536]{1,0:T(8,128)S(1)}, u32[]{:S(2)}, u32[]{:S(2)}) collective-permute-start(f32[16,1536]{1,0:T(8,128)S(1)} %combined.2.a_5_), channel_id=1, source_target_pairs={{0,8},{1,9},{2,10},{3,11},{4,12},{5,13},{6,14},{7,15},{8,0},{9,1},... | collective-permute-start | bytes 294920 | tf_op jit(solution)/shard_map/ppermute | solution.py:464
  37.5 6.5 %collective-permute-start.12 = (f32[32,1536]{1,0:T(8,128)S(1)}, f32[32,1536]{1,0:T(8,128)S(1)}, u32[]{:S(2)}, u32[]{:S(2)}) collective-permute-start(f32[32,1536]{1,0:T(8,128)S(1)} %sums.6.wait), channel_id=1, source_target_pairs={{0,4},{1,5},{2,6},{3,7},{4,0},{5,1},{6,2},{7,3},{8,12},{9,13},{10,... | collective-permute-start | bytes 589832 | tf_op jit(solution)/shard_map/ppermute | solution.py:464
  39.0 4.9 %copy-start = (f32[512]{0:T(512)S(1)}, f32[512]{0:T(512)}, u32[]{:S(2)}) copy-start(f32[512]{0:T(512)} %param.16) | copy-start | bytes 6148

commit v18 on v16

--- a/solution.py
+++ b/solution.py
@@ -625,12 +625,12 @@
             name="gate",
         )(*arrays)
 
-    whole, cut = (0, per), (0, per // 2, per)
+    whole = (0, per)
     far = []
     waits = []
     for n in range(2, blocks, 2):
-        handed = sums(n + 1, cut)
-        mine = sums(n, cut, waits=handed[:1])
+        handed = sums(n + 1, whole)
+        mine = sums(n, whole, waits=handed)
         if n == 2:
             (near,) = sums(1, whole, waits=mine[:1])
         joined = [combined(x, crossed(y, TEAM), near) for x, y in zip(mine, handed)]
@@ -638,7 +638,7 @@
         waits.extend(joined)
     own_part, shift = sums(0, whole, last=True, waits=waits)
     far = [crossed(near, TEAM), *gated(far, much)]
-    row_cuts = [whole] + [cut] * (len(far) // 2)
+    row_cuts = [whole] * len(far)
 
     refs_new = pl.pallas_call(
         lambda *a: final_kernel(row_cuts, *a),

time: 44.2 us -> 44.8 us (1.014)
  waiting for transfers between devices: 12.9 us -> 16 us
  starting transfers between devices: 16.5 us -> 14 us
    ppermute x15 -> x13, waiting for transfers between devices: 12.9 us -> 16 us  [crossed(): return lax.ppermute(block, 'dom', [(i, i ^ mask) for i in range(size)])]
    ppermute x15 -> x13, starting transfers between devices: 16.5 us -> 14 us  [crossed(): return lax.ppermute(block, 'dom', [(i, i ^ mask) for i in range(size)])]
  transfers between devices with their start and end apart: 15 -> 13, of which waited for: 8 -> 7; matrix products, arithmetic and copies ran while one was open for 0% -> 0% of each run, Pallas kernels for 18% -> 18%
where the time goes in v18:
time: 44.8 us; the launch traced here: 44.7 us
  waiting for transfers between devices  16 us (36%)
  starting transfers between devices  14 us (31%)
  Pallas kernels  13.3 us (30%)
  between operations  1.38 us (3%)
    ppermute x13, waiting for transfers between devices, crossed(): return lax.ppermute(block, 'dom', [(i, i ^ mask) for i in range(size)])  16 us
    ppermute x13, starting transfers between devices, crossed(): return lax.ppermute(block, 'dom', [(i, i ^ mask) for i in range(size)])  14 us
    pallas_call x4, Pallas kernels, sums(): pl.pallas_call(lambda *a: sum_kernel(n, cuts, last, len(waits), *a), out_...  4.39 us
    pallas_call x1, Pallas kernels, call(): pl.pallas_call(kernel, cost_estimate=cost, out_shape=tuple(out_shape), in...  3.61 us
    pallas_call x1, Pallas kernels, on_device(): pl.pallas_call(own_kernel, out_shape=(jax.ShapeDtypeStruct((slots + 8, wi...  1.83 us
    pallas_call x1, Pallas kernels, on_device(): pl.pallas_call(own_refs_kernel, out_shape=tuple(block_shapes), in_specs=[...  1.15 us
    pallas_call x3, Pallas kernels, on_device(): pl.pallas_call(refs_kernel, out_shape=tuple(block_shapes), in_specs=[vmem...  0.94 us
  transfers between devices with their start and end apart: 13, of which 7 were waited for; matrix products, arithmetic and copies ran while one was open for 0% of the time, Pallas kernels for 18%

profile of v18, /device:TPU:0, one launch (start us, length us, event | category | flops | bytes accessed | tf_op | source)
XLA Modules:
  0.0 44.7 jit_solution(11601356119914214243)
XLA Ops:
  0.6 3.0 %collective-permute-start.1 = (f32[96,1024]{1,0:T(8,128)}, f32[96,1024]{1,0:T(8,128)S(1)}, u32[]{:S(2)}, u32[]{:S(2)}) collective-permute-start(f32[96,1024]{1,0:T(8,128)} %src_at.1), channel_id=1, source_target_pairs={{0,2},{1,3},{2,0},{3,1},{4,6},{5,7},{6,4},{7,5},{8,10},{9,11},{10,... | collective-permute-start | bytes 1179656 | tf_op jit(solution)/shard_map/ppermute | solution.py:464
  3.7 3.6 %collective-permute-start.5 = (f32[32,1024]{1,0:T(8,128)}, f32[32,1024]{1,0:T(8,128)S(1)}, u32[]{:S(2)}, u32[]{:S(2)}) collective-permute-start(f32[32,1024]{1,0:T(8,128)} %bitcast.9), channel_id=1, source_target_pairs={{0,12},{1,13},{2,14},{3,15},{4,8},{5,9},{6,10},{7,11},{8,4},{9,5},... | collective-permute-start | bytes 393224 | tf_op jit(solution)/shard_map/ppermute | solution.py:464
  7.3 0.0 collective-permute-start.4
  7.3 0.8 %collective-permute-start.6 = (f32[32,1024]{1,0:T(8,128)}, f32[32,1024]{1,0:T(8,128)S(1)}, u32[]{:S(2)}, u32[]{:S(2)}) collective-permute-start(f32[32,1024]{1,0:T(8,128)} %bitcast.11), channel_id=1, source_target_pairs={{0,8},{1,9},{2,10},{3,11},{4,12},{5,13},{6,14},{7,15},{8,0},{9,1},... | collective-permute-start | bytes 393224 | tf_op jit(solution)/shard_map/ppermute | solution.py:464
  8.7 1.8 %own.1 = (f32[104,1536]{1,0:T(8,128)S(1)}, f32[8,128]{1,0:T(8,128)S(1)}, f32[128,512]{1,0:T(8,128)S(1)}) custom-call(f32[96,1024]{1,0:T(8,128)} %src_at.1, f32[1,96]{1,0:T(1,128)} %bitcast.15, s32[2,96]{1,0:T(2,128)} %bitcast.14, s32[1,96]{1,0:T(1,128)} %bitcast.16, s32[1,96]{1,0:T(1,128)} %bitcast.17, f32[128,512]{1,0:T(8,128)} %noise_at.1, ...), custom_call_target="tpu_custom_call" | custom-call | tf_op jit(solution)/shard_map/own/pallas_call | solution.py:505
  10.5 0.4 collective-permute-start.2
  10.9 1.2 %own_refs.1 = (bf16[288,1024]{1,0:T(8,128)(2,1)S(1)}, bf16[288,1024]{1,0:T(8,128)(2,1)S(1)}, bf16[32,512]{1,0:T(8,128)(2,1)S(1)}, bf16[32,512]{1,0:T(8,128)(2,1)S(1)}) custom-call(f32[32,1024]{1,0:T(8,128)} %bitcast.12, f32[8,128]{1,0:T(8,128)S(1)} %get-tuple-element.32.wait), custom_call_target="tpu_custom_call" | custom-call | tf_op jit(solution)/shard_map/own_refs/pallas_call | solution.py:542
  12.1 2.2 %collective-permute-done.2.facts = f32[8,128]{1,0:T(8,128)S(1)} collective-permute-done((f32[8,128]{1,0:T(8,128)S(1)}, f32[8,128]{1,0:T(8,128)S(1)}, u32[]{:S(2)}, u32[]{:S(2)}) %collective-permute-start.2) | collective-permute-done | bytes 4128 | tf_op jit(solution)/shard_map/ppermute | solution.py:464
  14.2 0.0 collective-permute-start
  14.2 0.0 collective-permute-done.1.src
  14.2 0.6 %neighbour.1.wait.a_2_ = f32[104,1536]{1,0:T(8,128)S(1)} custom-call(f32[96,1024]{1,0:T(8,128)S(1)} %collective-permute-done.1.src, f32[8,128]{1,0:T(8,128)S(1)} %collective-permute-done.2.facts, f32[128,512]{1,0:T(8,128)S(1)} %get-tuple-element.33.inverse_noise, bf16[32,512]{1,0:T(8,128)(2,1)S(1)} %get-tuple-element.34.wait.a_6_), custom_call_target="tpu_custom_call" | custom-call | tf_op jit(solution)/shard_map/neighbour/pallas_call | solution.py:551
  14.9 0.6 %collective-permute-start.3 = (f32[104,1536]{1,0:T(8,128)S(1)}, f32[104,1536]{1,0:T(8,128)S(1)}, u32[]{:S(2)}, u32[]{:S(2)}) collective-permute-start(f32[104,1536]{1,0:T(8,128)S(1)} %neighbour.1.wait.a_2_), channel_id=1, source_target_pairs={{0,1},{1,0},{2,3},{3,2},{4,5},{5,4},{6,7},{7,6},{8,9},{9,8},{10,11... | collective-permute-start | bytes 1916936 | tf_op jit(solution)/shard_map/ppermute | solution.py:464
  15.4 0.0 collective-permute-done.5.ref
  15.4 0.3 refs.3
  15.8 0.0 collective-permute-done.4.ref
  15.8 0.3 refs.4
  16.1 2.2 %collective-permute-done.6.ref = f32[32,1024]{1,0:T(8,128)S(1)} collective-permute-done((f32[32,1024]{1,0:T(8,128)}, f32[32,1024]{1,0:T(8,128)S(1)}, u32[]{:S(2)}, u32[]{:S(2)}) %collective-permute-start.6) | collective-permute-done | bytes 131104 | tf_op jit(solution)/shard_map/ppermute | solution.py:464
  18.3 0.3 refs.5
  18.6 0.0 collective-permute-done.a_1_
  18.6 0.0 collective-permute-done.3.a_3_
  18.6 3.6 %late.1 = (f32[9,32,288]{2,1,0:T(8,128)S(1)}, f32[9,32,288]{2,1,0:T(8,128)S(1)}, f32[9,32,288]{2,1,0:T(8,128)S(1)}, f32[9,32,288]{2,1,0:T(8,128)S(1)}, bf16[896,...) custom-call(f32[104,1536]{1,0:T(8,128)S(1)} %get-tuple-element.31.a_0_, ...), custom_call_target="tpu_custom_call" | custom-call | tf_op jit(solution)/shard_map/late/pallas_call | solution.py:531
  22.2 0.1 collective-permute-start.9
  22.3 0.7 %collective-permute-start.8 = (f32[8,384]{1,0:T(8,128)S(1)}, f32[8,384]{1,0:T(8,128)S(1)}, u32[]{:S(2)}, u32[]{:S(2)}) collective-permute-start(f32[8,384]{1,0:T(8,128)S(1)} %get-tuple-element.50.a_0_), channel_id=1, source_target_pairs={{0,2},{1,3},{2,0},{3,1},{4,6},{5,7},{6,4},{7,5},{8,10},{9,11},{10,... | collective-permute-start | bytes 36872 | tf_op jit(solution)/shard_map/ppermute | solution.py:464
  23.0 1.1 %collective-permute-start.7 = (f32[8,384]{1,0:T(8,128)S(1)}, f32[8,384]{1,0:T(8,128)S(1)}, u32[]{:S(2)}, u32[]{:S(2)}) collective-permute-start(f32[8,384]{1,0:T(8,128)S(1)} %get-tuple-element.50.a_0_), channel_id=1, source_target_pairs={{0,1},{1,0},{2,3},{3,2},{4,5},{5,4},{6,7},{7,6},{8,9},{9,8},{10,11... | collective-permute-start | bytes 36872 | tf_op jit(solution)/shard_map/ppermute | solution.py:464
  24.2 1.3 %collective-permute-done.9.a_3_ = f32[8,384]{1,0:T(8,128)S(1)} collective-permute-done((f32[8,384]{1,0:T(8,128)S(1)}, f32[8,384]{1,0:T(8,128)S(1)}, u32[]{:S(2)}, u32[]{:S(2)}) %collective-permute-start.9) | collective-permute-done | bytes 12320 | tf_op jit(solution)/shard_map/ppermute | solution.py:464
  25.4 0.7 %collective-permute-done.8.a_2_ = f32[8,384]{1,0:T(8,128)S(1)} collective-permute-done((f32[8,384]{1,0:T(8,128)S(1)}, f32[8,384]{1,0:T(8,128)S(1)}, u32[]{:S(2)}, u32[]{:S(2)}) %collective-permute-start.8) | collective-permute-done | bytes 12320 | tf_op jit(solution)/shard_map/ppermute | solution.py:464
  26.1 0.0 collective-permute-done.7.a_1_
  26.1 0.9 %sums.4.a_5_ = f32[32,1536]{1,0:T(8,128)S(1)} custom-call(f32[8,384]{1,0:T(8,128)S(1)} %get-tuple-element.50.a_0_, f32[8,384]{1,0:T(8,128)S(1)} %collective-permute-done.7.a_1_, f32[8,384]{1,0:T(8,128)S(1)} %collective-permute-done.8.a_2_, f32[8,384]{1,0:T(8,128)S(1)} %collective-permute-done.9.a_3_, f32[8,384]{1,0:T(8,128)S(1)} %get-tuple-element.51.a_4_, ...), custom_call_target="tpu_custom_call" | custom-call | tf_op jit(solution)/shard_map/sums/pallas_call | solution.py:597
  27.0 0.6 %collective-permute-start.10 = (f32[32,1536]{1,0:T(8,128)S(1)}, f32[32,1536]{1,0:T(8,128)S(1)}, u32[]{:S(2)}, u32[]{:S(2)}) collective-permute-start(f32[32,1536]{1,0:T(8,128)S(1)} %sums.4.a_5_), channel_id=1, source_target_pairs={{0,4},{1,5},{2,6},{3,7},{4,0},{5,1},{6,2},{7,3},{8,12},{9,13},{10,... | collective-permute-start | bytes 589832 | tf_op jit(solution)/shard_map/ppermute | solution.py:464
  27.6 0.9 %sums.5.a_5_.a = f32[32,1536]{1,0:T(8,128)S(1)} custom-call(f32[8,384]{1,0:T(8,128)S(1)} %get-tuple-element.50.a_0_, f32[8,384]{1,0:T(8,128)S(1)} %collective-permute-done.7.a_1_, f32[8,384]{1,0:T(8,128)S(1)} %collective-permute-done.8.a_2_, f32[8,384]{1,0:T(8,128)S(1)} %collective-permute-done.9.a_3_, f32[8,384]{1,0:T(8,128)S(1)} %get-tuple-element.51.a_4_, ...), custom_call_target="tpu_custom_call" | custom-call | tf_op jit(solution)/shard_map/sums/pallas_call | solution.py:597
  28.6 0.9 %sums.6.wait = f32[32,1536]{1,0:T(8,128)S(1)} custom-call(f32[8,384]{1,0:T(8,128)S(1)} %get-tuple-element.50.a_0_, f32[8,384]{1,0:T(8,128)S(1)} %collective-permute-done.7.a_1_, f32[8,384]{1,0:T(8,128)S(1)} %collective-permute-done.8.a_2_, f32[8,384]{1,0:T(8,128)S(1)} %collective-permute-done.9.a_3_, f32[8,384]{1,0:T(8,128)S(1)} %get-tuple-element.51.a_4_, ...), custom_call_target="tpu_custom_call" | custom-call | tf_op jit(solution)/shard_map/sums/pallas_call | solution.py:597
  29.5 3.8 %collective-permute-done.10.b = f32[32,1536]{1,0:T(8,128)S(1)} collective-permute-done((f32[32,1536]{1,0:T(8,128)S(1)}, f32[32,1536]{1,0:T(8,128)S(1)}, u32[]{:S(2)}, u32[]{:S(2)}) %collective-permute-start.10) | collective-permute-done | bytes 196640 | tf_op jit(solution)/shard_map/ppermute | solution.py:464
  33.4 1.4 %collective-permute-start.12 = (f32[32,1536]{1,0:T(8,128)S(1)}, f32[32,1536]{1,0:T(8,128)S(1)}, u32[]{:S(2)}, u32[]{:S(2)}) collective-permute-start(f32[32,1536]{1,0:T(8,128)S(1)} %combined.1.a_5_), channel_id=1, source_target_pairs={{0,8},{1,9},{2,10},{3,11},{4,12},{5,13},{6,14},{7,15},{8,0},{9,1},... | collective-permute-start | bytes 589832 | tf_op jit(solution)/shard_map/ppermute | solution.py:464
  34.7 1.7 %collective-permute-start.11 = (f32[32,1536]{1,0:T(8,128)S(1)}, f32[32,1536]{1,0:T(8,128)S(1)}, u32[]{:S(2)}, u32[]{:S(2)}) collective-permute-start(f32[32,1536]{1,0:T(8,128)S(1)} %sums.6.wait), channel_id=1, source_target_pairs={{0,4},{1,5},{2,6},{3,7},{4,0},{5,1},{6,2},{7,3},{8,12},{9,13},{10,... | collective-permute-start | bytes 589832 | tf_op jit(solution)/shard_map/ppermute | solution.py:464
  36.5 1.6 %sums.7 = (f32[32,1536]{1,0:T(8,128)S(1)}, f32[2,96]{1,0:T(2,128)}) custom-call(f32[8,384]{1,0:T(8,128)S(1)} %get-tuple-element.50.a_0_, f32[8,384]{1,0:T(8,128)S(1)} %collective-permute-done.7.a_1_, f32[8,384]{1,0:T(8,128)S(1)} %collective-permute-done.8.a_2_, f32[8,384]{1,0:T(8,128)S(1)} %collective-permute-done.9.a_3_, ...), custom_call_target="tpu_custom_call" | custom-call | tf_op jit(solution)/shard_map/sums/pallas_call | solution.py:597
  38.0 0.0 copy-start
  38.0 5.7 %collective-permute-done.12.a_0_ = f32[32,1536]{1,0:T(8,128)S(1)} collective-permute-done((f32[32,1536]{1,0:T(8,128)S(1)}, f32[32,1536]{1,0:T(8,128)S(1)}, u32[]{:S(2)}, u32[]{:S(2)}) %collective-permute-start.12) | collective-permute-done | bytes 196640 | tf_op jit(solution)/shard_map/ppermute | solution.py:464
  43.7 0.3 collective-permute-done.11.a_1_
  44.0 0.0 copy-done
  44.0 0.7 %update.1 = f32[32,1024]{1,0:T(8,128)} custom-call(f32[32,1536]{1,0:T(8,128)S(1)} %get-tuple-element.59.a_0_, f32[32,1536]{1,0:T(8,128)S(1)} %collective-permute-done.11.a_1_, f32[32,1536]{1,0:T(8,128)S(1)} %gate.1.a_2_, f32[1,512]{1,0:T(1,128)S(1)} %bitcast.8), custom_call_target="tpu_custom_call" | custom-call | tf_op jit(solution)/shard_map/update/pallas_call | solution.py:643
  (2 shorter events, 0.0 us)
Async XLA Ops:
  0.6 13.6 %collective-permute-start.1 = (f32[96,1024]{1,0:T(8,128)}, f32[96,1024]{1,0:T(8,128)S(1)}, u32[]{:S(2)}, u32[]{:S(2)}) collective-permute-start(f32[96,1024]{1,0:T(8,128)} %src_at.1), channel_id=1, source_target_pairs={{0,2},{1,3},{2,0},{3,1},{4,6},{5,7},{6,4},{7,5},{8,10},{9,11},{10,... | collective-permute-start | bytes 1179656 | tf_op jit(solution)/shard_map/ppermute | solution.py:464
  3.7 11.8 %collective-permute-start.5 = (f32[32,1024]{1,0:T(8,128)}, f32[32,1024]{1,0:T(8,128)S(1)}, u32[]{:S(2)}, u32[]{:S(2)}) collective-permute-start(f32[32,1024]{1,0:T(8,128)} %bitcast.9), channel_id=1, source_target_pairs={{0,12},{1,13},{2,14},{3,15},{4,8},{5,9},{6,10},{7,11},{8,4},{9,5},... | collective-permute-start | bytes 393224 | tf_op jit(solution)/shard_map/ppermute | solution.py:464
  7.3 8.5 %collective-permute-start.4 = (f32[32,1024]{1,0:T(8,128)}, f32[32,1024]{1,0:T(8,128)S(1)}, u32[]{:S(2)}, u32[]{:S(2)}) collective-permute-start(f32[32,1024]{1,0:T(8,128)} %bitcast.10), channel_id=1, source_target_pairs={{0,4},{1,5},{2,6},{3,7},{4,0},{5,1},{6,2},{7,3},{8,12},{9,13},{10,... | collective-permute-start | bytes 393224 | tf_op jit(solution)/shard_map/ppermute | solution.py:464
  7.3 11.0 %collective-permute-start.6 = (f32[32,1024]{1,0:T(8,128)}, f32[32,1024]{1,0:T(8,128)S(1)}, u32[]{:S(2)}, u32[]{:S(2)}) collective-permute-start(f32[32,1024]{1,0:T(8,128)} %bitcast.11), channel_id=1, source_target_pairs={{0,8},{1,9},{2,10},{3,11},{4,12},{5,13},{6,14},{7,15},{8,0},{9,1},... | collective-permute-start | bytes 393224 | tf_op jit(solution)/shard_map/ppermute | solution.py:464
  10.5 3.7 %collective-permute-start.2 = (f32[8,128]{1,0:T(8,128)S(1)}, f32[8,128]{1,0:T(8,128)S(1)}, u32[]{:S(2)}, u32[]{:S(2)}) collective-permute-start(f32[8,128]{1,0:T(8,128)S(1)} %get-tuple-element.32.wait), channel_id=1, source_target_pairs={{0,2},{1,3},{2,0},{3,1},{4,6},{5,7},{6,4},{7,5},{8,10},{9,11},{10,... | collective-permute-start | bytes 12296 | tf_op jit(solution)/shard_map/ppermute | solution.py:464
  14.2 4.4 %collective-permute-start = (f32[104,1536]{1,0:T(8,128)S(1)}, f32[104,1536]{1,0:T(8,128)S(1)}, u32[]{:S(2)}, u32[]{:S(2)}) collective-permute-start(f32[104,1536]{1,0:T(8,128)S(1)} %get-tuple-element.31.a_0_), channel_id=1, source_target_pairs={{0,1},{1,0},{2,3},{3,2},{4,5},{5,4},{6,7},{7,6},{8,9},{9,8},{10,11... | collective-permute-start | bytes 1916936 | tf_op jit(solution)/shard_map/ppermute | solution.py:464
  14.9 3.7 %collective-permute-start.3 = (f32[104,1536]{1,0:T(8,128)S(1)}, f32[104,1536]{1,0:T(8,128)S(1)}, u32[]{:S(2)}, u32[]{:S(2)}) collective-permute-start(f32[104,1536]{1,0:T(8,128)S(1)} %neighbour.1.wait.a_2_), channel_id=1, source_target_pairs={{0,1},{1,0},{2,3},{3,2},{4,5},{5,4},{6,7},{7,6},{8,9},{9,8},{10,11... | collective-permute-start | bytes 1916936 | tf_op jit(solution)/shard_map/ppermute | solution.py:464
  22.2 3.2 %collective-permute-start.9 = (f32[8,384]{1,0:T(8,128)S(1)}, f32[8,384]{1,0:T(8,128)S(1)}, u32[]{:S(2)}, u32[]{:S(2)}) collective-permute-start(f32[8,384]{1,0:T(8,128)S(1)} %get-tuple-element.50.a_0_), channel_id=1, source_target_pairs={{0,3},{1,2},{2,1},{3,0},{4,7},{5,6},{6,5},{7,4},{8,11},{9,10},{10,... | collective-permute-start | bytes 36872 | tf_op jit(solution)/shard_map/ppermute | solution.py:464
  22.3 3.8 %collective-permute-start.8 = (f32[8,384]{1,0:T(8,128)S(1)}, f32[8,384]{1,0:T(8,128)S(1)}, u32[]{:S(2)}, u32[]{:S(2)}) collective-permute-start(f32[8,384]{1,0:T(8,128)S(1)} %get-tuple-element.50.a_0_), channel_id=1, source_target_pairs={{0,2},{1,3},{2,0},{3,1},{4,6},{5,7},{6,4},{7,5},{8,10},{9,11},{10,... | collective-permute-start | bytes 36872 | tf_op jit(solution)/shard_map/ppermute | solution.py:464
  23.0 3.0 %collective-permute-start.7 = (f32[8,384]{1,0:T(8,128)S(1)}, f32[8,384]{1,0:T(8,128)S(1)}, u32[]{:S(2)}, u32[]{:S(2)}) collective-permute-start(f32[8,384]{1,0:T(8,128)S(1)} %get-tuple-element.50.a_0_), channel_id=1, source_target_pairs={{0,1},{1,0},{2,3},{3,2},{4,5},{5,4},{6,7},{7,6},{8,9},{9,8},{10,11... | collective-permute-start | bytes 36872 | tf_op jit(solution)/shard_map/ppermute | solution.py:464
  27.0 6.3 %collective-permute-start.10 = (f32[32,1536]{1,0:T(8,128)S(1)}, f32[32,1536]{1,0:T(8,128)S(1)}, u32[]{:S(2)}, u32[]{:S(2)}) collective-permute-start(f32[32,1536]{1,0:T(8,128)S(1)} %sums.4.a_5_), channel_id=1, source_target_pairs={{0,4},{1,5},{2,6},{3,7},{4,0},{5,1},{6,2},{7,3},{8,12},{9,13},{10,... | collective-permute-start | bytes 589832 | tf_op jit(solution)/shard_map/ppermute | solution.py:464
  33.4 10.3 %collective-permute-start.12 = (f32[32,1536]{1,0:T(8,128)S(1)}, f32[32,1536]{1,0:T(8,128)S(1)}, u32[]{:S(2)}, u32[]{:S(2)}) collective-permute-start(f32[32,1536]{1,0:T(8,128)S(1)} %combined.1.a_5_), channel_id=1, source_target_pairs={{0,8},{1,9},{2,10},{3,11},{4,12},{5,13},{6,14},{7,15},{8,0},{9,1},... | collective-permute-start | bytes 589832 | tf_op jit(solution)/shard_map/ppermute | solution.py:464
  34.7 9.2 %collective-permute-start.11 = (f32[32,1536]{1,0:T(8,128)S(1)}, f32[32,1536]{1,0:T(8,128)S(1)}, u32[]{:S(2)}, u32[]{:S(2)}) collective-permute-start(f32[32,1536]{1,0:T(8,128)S(1)} %sums.6.wait), channel_id=1, source_target_pairs={{0,4},{1,5},{2,6},{3,7},{4,0},{5,1},{6,2},{7,3},{8,12},{9,13},{10,... | collective-permute-start | bytes 589832 | tf_op jit(solution)/shard_map/ppermute | solution.py:464
  38.0 5.9 %copy-start = (f32[512]{0:T(512)S(1)}, f32[512]{0:T(512)}, u32[]{:S(2)}) copy-start(f32[512]{0:T(512)} %param.16) | copy-start | bytes 6148

commit v19 on v17

--- a/solution.py
+++ b/solution.py
@@ -559,7 +559,7 @@
     )(ynb, crossed(facts, 2), inverse_noise, prepared[2])
     cynb = crossed(ynb_prepared, 1)
 
-    order = [*range(2, blocks - 1), 1, blocks - 1]
+    order = [*range(2, blocks), 1]
     wait = ynb_prepared
     by_block = {0: prepared}
     for n in order:

time: 44.8 us -> 45.1 us (level)
  starting transfers between devices: 18.1 us -> 18.9 us
    ppermute x15, starting transfers between devices: 18.1 us -> 18.9 us  [crossed(): return lax.ppermute(block, 'dom', [(i, i ^ mask) for i in range(size)])]
where the time goes in v19:
time: 45.1 us; the launch traced here: 44.9 us
  starting transfers between devices  18.9 us (42%)
  Pallas kernels  13.3 us (29%)
  waiting for transfers between devices  11.4 us (25%)
  between operations  1.39 us (3%)
    ppermute x15, starting transfers between devices, crossed(): return lax.ppermute(block, 'dom', [(i, i ^ mask) for i in range(size)])  18.9 us
    ppermute x15, waiting for transfers between devices, crossed(): return lax.ppermute(block, 'dom', [(i, i ^ mask) for i in range(size)])  11.4 us
    pallas_call x4, Pallas kernels, sums(): pl.pallas_call(lambda *a: sum_kernel(n, cuts, last, len(waits), *a), out_...  4.39 us
    pallas_call x1, Pallas kernels, call(): pl.pallas_call(kernel, cost_estimate=cost, out_shape=tuple(out_shape), in...  3.61 us
    pallas_call x1, Pallas kernels, on_device(): pl.pallas_call(own_kernel, out_shape=(jax.ShapeDtypeStruct((slots + 8, wi...  1.83 us
    pallas_call x1, Pallas kernels, on_device(): pl.pallas_call(own_refs_kernel, out_shape=tuple(block_shapes), in_specs=[...  1.15 us
    pallas_call x3, Pallas kernels, on_device(): pl.pallas_call(refs_kernel, out_shape=tuple(block_shapes), in_specs=[vmem...  0.94 us
  transfers between devices with their start and end apart: 15, of which 8 were waited for; matrix products, arithmetic and copies ran while one was open for 0% of the time, Pallas kernels for 18%

profile of v19, /device:TPU:0, one launch (start us, length us, event | category | flops | bytes accessed | tf_op | source)
XLA Modules:
  0.0 44.9 jit_solution(4719880858834540298)
XLA Ops:
  0.6 3.0 %collective-permute-start.1 = (f32[96,1024]{1,0:T(8,128)}, f32[96,1024]{1,0:T(8,128)S(1)}, u32[]{:S(2)}, u32[]{:S(2)}) collective-permute-start(f32[96,1024]{1,0:T(8,128)} %src_at.1), channel_id=1, source_target_pairs={{0,2},{1,3},{2,0},{3,1},{4,6},{5,7},{6,4},{7,5},{8,10},{9,11},{10,... | collective-permute-start | bytes 1179656 | tf_op jit(solution)/shard_map/ppermute | solution.py:464
  3.7 2.6 %collective-permute-start.6 = (f32[32,1024]{1,0:T(8,128)}, f32[32,1024]{1,0:T(8,128)S(1)}, u32[]{:S(2)}, u32[]{:S(2)}) collective-permute-start(f32[32,1024]{1,0:T(8,128)} %bitcast.9), channel_id=1, source_target_pairs={{0,8},{1,9},{2,10},{3,11},{4,12},{5,13},{6,14},{7,15},{8,0},{9,1},... | collective-permute-start | bytes 393224 | tf_op jit(solution)/shard_map/ppermute | solution.py:464
  6.3 1.3 %collective-permute-start.5 = (f32[32,1024]{1,0:T(8,128)}, f32[32,1024]{1,0:T(8,128)S(1)}, u32[]{:S(2)}, u32[]{:S(2)}) collective-permute-start(f32[32,1024]{1,0:T(8,128)} %bitcast.10), channel_id=1, source_target_pairs={{0,12},{1,13},{2,14},{3,15},{4,8},{5,9},{6,10},{7,11},{8,4},{9,5},... | collective-permute-start | bytes 393224 | tf_op jit(solution)/shard_map/ppermute | solution.py:464
  7.6 0.2 collective-permute-start.4
  8.5 1.8 %own.1 = (f32[104,1536]{1,0:T(8,128)S(1)}, f32[8,128]{1,0:T(8,128)S(1)}, f32[128,512]{1,0:T(8,128)S(1)}) custom-call(f32[96,1024]{1,0:T(8,128)} %src_at.1, f32[1,96]{1,0:T(1,128)} %bitcast.15, s32[2,96]{1,0:T(2,128)} %bitcast.14, s32[1,96]{1,0:T(1,128)} %bitcast.16, s32[1,96]{1,0:T(1,128)} %bitcast.17, f32[128,512]{1,0:T(8,128)} %noise_at.1, ...), custom_call_target="tpu_custom_call" | custom-call | tf_op jit(solution)/shard_map/own/pallas_call | solution.py:505
  10.3 0.6 %collective-permute-start.2 = (f32[8,128]{1,0:T(8,128)S(1)}, f32[8,128]{1,0:T(8,128)S(1)}, u32[]{:S(2)}, u32[]{:S(2)}) collective-permute-start(f32[8,128]{1,0:T(8,128)S(1)} %get-tuple-element.38.wait), channel_id=1, source_target_pairs={{0,2},{1,3},{2,0},{3,1},{4,6},{5,7},{6,4},{7,5},{8,10},{9,11},{10,... | collective-permute-start | bytes 12296 | tf_op jit(solution)/shard_map/ppermute | solution.py:464
  10.9 1.2 %own_refs.1 = (bf16[288,1024]{1,0:T(8,128)(2,1)S(1)}, bf16[288,1024]{1,0:T(8,128)(2,1)S(1)}, bf16[32,512]{1,0:T(8,128)(2,1)S(1)}, bf16[32,512]{1,0:T(8,128)(2,1)S(1)}) custom-call(f32[32,1024]{1,0:T(8,128)} %bitcast.12, f32[8,128]{1,0:T(8,128)S(1)} %get-tuple-element.38.wait), custom_call_target="tpu_custom_call" | custom-call | tf_op jit(solution)/shard_map/own_refs/pallas_call | solution.py:542
  12.1 1.9 %collective-permute-done.2.facts = f32[8,128]{1,0:T(8,128)S(1)} collective-permute-done((f32[8,128]{1,0:T(8,128)S(1)}, f32[8,128]{1,0:T(8,128)S(1)}, u32[]{:S(2)}, u32[]{:S(2)}) %collective-permute-start.2) | collective-permute-done | bytes 4128 | tf_op jit(solution)/shard_map/ppermute | solution.py:464
  14.0 0.0 collective-permute-start
  14.0 0.0 collective-permute-done.1.src
  14.0 0.6 %neighbour.1.wait.a_2_ = f32[104,1536]{1,0:T(8,128)S(1)} custom-call(f32[96,1024]{1,0:T(8,128)S(1)} %collective-permute-done.1.src, f32[8,128]{1,0:T(8,128)S(1)} %collective-permute-done.2.facts, f32[128,512]{1,0:T(8,128)S(1)} %get-tuple-element.39.inverse_noise, bf16[32,512]{1,0:T(8,128)(2,1)S(1)} %get-tuple-element.40.wait.a_6_), custom_call_target="tpu_custom_call" | custom-call | tf_op jit(solution)/shard_map/neighbour/pallas_call | solution.py:551
  14.6 0.6 %collective-permute-start.3 = (f32[104,1536]{1,0:T(8,128)S(1)}, f32[104,1536]{1,0:T(8,128)S(1)}, u32[]{:S(2)}, u32[]{:S(2)}) collective-permute-start(f32[104,1536]{1,0:T(8,128)S(1)} %neighbour.1.wait.a_2_), channel_id=1, source_target_pairs={{0,1},{1,0},{2,3},{3,2},{4,5},{5,4},{6,7},{7,6},{8,9},{9,8},{10,11... | collective-permute-start | bytes 1916936 | tf_op jit(solution)/shard_map/ppermute | solution.py:464
  15.2 1.3 %collective-permute-done.6.ref = f32[32,1024]{1,0:T(8,128)S(1)} collective-permute-done((f32[32,1024]{1,0:T(8,128)}, f32[32,1024]{1,0:T(8,128)S(1)}, u32[]{:S(2)}, u32[]{:S(2)}) %collective-permute-start.6) | collective-permute-done | bytes 131104 | tf_op jit(solution)/shard_map/ppermute | solution.py:464
  16.5 0.3 refs.3
  16.8 0.0 collective-permute-done.5.ref
  16.8 0.3 refs.4
  17.2 0.0 collective-permute-done.4.ref
  17.2 0.3 refs.5
  17.5 0.0 collective-permute-done.a_1_
  17.5 0.0 collective-permute-done.3.a_3_
  17.5 3.6 %late.1 = (f32[9,32,288]{2,1,0:T(8,128)S(1)}, f32[9,32,288]{2,1,0:T(8,128)S(1)}, f32[9,32,288]{2,1,0:T(8,128)S(1)}, f32[9,32,288]{2,1,0:T(8,128)S(1)}, bf16[896,...) custom-call(f32[104,1536]{1,0:T(8,128)S(1)} %get-tuple-element.37.a_0_, ...), custom_call_target="tpu_custom_call" | custom-call | tf_op jit(solution)/shard_map/late/pallas_call | solution.py:531
  21.1 0.2 collective-permute-start.9
  21.4 1.2 %collective-permute-start.8 = (f32[8,384]{1,0:T(8,128)S(1)}, f32[8,384]{1,0:T(8,128)S(1)}, u32[]{:S(2)}, u32[]{:S(2)}) collective-permute-start(f32[8,384]{1,0:T(8,128)S(1)} %get-tuple-element.56.a_0_), channel_id=1, source_target_pairs={{0,2},{1,3},{2,0},{3,1},{4,6},{5,7},{6,4},{7,5},{8,10},{9,11},{10,... | collective-permute-start | bytes 36872 | tf_op jit(solution)/shard_map/ppermute | solution.py:464
  22.6 0.5 %collective-permute-start.7 = (f32[8,384]{1,0:T(8,128)S(1)}, f32[8,384]{1,0:T(8,128)S(1)}, u32[]{:S(2)}, u32[]{:S(2)}) collective-permute-start(f32[8,384]{1,0:T(8,128)S(1)} %get-tuple-element.56.a_0_), channel_id=1, source_target_pairs={{0,1},{1,0},{2,3},{3,2},{4,5},{5,4},{6,7},{7,6},{8,9},{9,8},{10,11... | collective-permute-start | bytes 36872 | tf_op jit(solution)/shard_map/ppermute | solution.py:464
  23.1 1.3 %collective-permute-done.9.a_3_ = f32[8,384]{1,0:T(8,128)S(1)} collective-permute-done((f32[8,384]{1,0:T(8,128)S(1)}, f32[8,384]{1,0:T(8,128)S(1)}, u32[]{:S(2)}, u32[]{:S(2)}) %collective-permute-start.9) | collective-permute-done | bytes 12320 | tf_op jit(solution)/shard_map/ppermute | solution.py:464
  24.4 0.7 %collective-permute-done.8.a_2_ = f32[8,384]{1,0:T(8,128)S(1)} collective-permute-done((f32[8,384]{1,0:T(8,128)S(1)}, f32[8,384]{1,0:T(8,128)S(1)}, u32[]{:S(2)}, u32[]{:S(2)}) %collective-permute-start.8) | collective-permute-done | bytes 12320 | tf_op jit(solution)/shard_map/ppermute | solution.py:464
  25.1 0.0 collective-permute-done.7.a_1_
  25.1 0.9 %sums.4 = (f32[16,1536]{1,0:T(8,128)S(1)}, f32[16,1536]{1,0:T(8,128)S(1)}) custom-call(f32[8,384]{1,0:T(8,128)S(1)} %get-tuple-element.56.a_0_, f32[8,384]{1,0:T(8,128)S(1)} %collective-permute-done.7.a_1_, f32[8,384]{1,0:T(8,128)S(1)} %collective-permute-done.8.a_2_, f32[8,384]{1,0:T(8,128)S(1)} %collective-permute-done.9.a_3_, ...), custom_call_target="tpu_custom_call" | custom-call | tf_op jit(solution)/shard_map/sums/pallas_call | solution.py:597
  26.0 2.1 %collective-permute-start.11 = (f32[16,1536]{1,0:T(8,128)S(1)}, f32[16,1536]{1,0:T(8,128)S(1)}, u32[]{:S(2)}, u32[]{:S(2)}) collective-permute-start(f32[16,1536]{1,0:T(8,128)S(1)} %get-tuple-element.66), channel_id=1, source_target_pairs={{0,4},{1,5},{2,6},{3,7},{4,0},{5,1},{6,2},{7,3},{8,12},{9,13},{10,... | collective-permute-start | bytes 294920 | tf_op jit(solution)/shard_map/ppermute | solution.py:464
  28.1 0.1 collective-permute-start.10
  28.2 0.9 %sums.5 = (f32[16,1536]{1,0:T(8,128)S(1)}, f32[16,1536]{1,0:T(8,128)S(1)}) custom-call(f32[8,384]{1,0:T(8,128)S(1)} %get-tuple-element.56.a_0_, f32[8,384]{1,0:T(8,128)S(1)} %collective-permute-done.7.a_1_, f32[8,384]{1,0:T(8,128)S(1)} %collective-permute-done.8.a_2_, f32[8,384]{1,0:T(8,128)S(1)} %collective-permute-done.9.a_3_, ...), custom_call_target="tpu_custom_call" | custom-call | tf_op jit(solution)/shard_map/sums/pallas_call | solution.py:597
  29.1 1.0 %sums.6.wait = f32[32,1536]{1,0:T(8,128)S(1)} custom-call(f32[8,384]{1,0:T(8,128)S(1)} %get-tuple-element.56.a_0_, f32[8,384]{1,0:T(8,128)S(1)} %collective-permute-done.7.a_1_, f32[8,384]{1,0:T(8,128)S(1)} %collective-permute-done.8.a_2_, f32[8,384]{1,0:T(8,128)S(1)} %collective-permute-done.9.a_3_, f32[8,384]{1,0:T(8,128)S(1)} %get-tuple-element.57.a_4_, ...), custom_call_target="tpu_custom_call" | custom-call | tf_op jit(solution)/shard_map/sums/pallas_call | solution.py:597
  30.1 1.5 %collective-permute-done.11.b = f32[16,1536]{1,0:T(8,128)S(1)} collective-permute-done((f32[16,1536]{1,0:T(8,128)S(1)}, f32[16,1536]{1,0:T(8,128)S(1)}, u32[]{:S(2)}, u32[]{:S(2)}) %collective-permute-start.11) | collective-permute-done | bytes 98336 | tf_op jit(solution)/shard_map/ppermute | solution.py:464
  31.6 4.2 %collective-permute-start.14 = (f32[16,1536]{1,0:T(8,128)S(1)}, f32[16,1536]{1,0:T(8,128)S(1)}, u32[]{:S(2)}, u32[]{:S(2)}) collective-permute-start(f32[16,1536]{1,0:T(8,128)S(1)} %combined.3.a_6_), channel_id=1, source_target_pairs={{0,8},{1,9},{2,10},{3,11},{4,12},{5,13},{6,14},{7,15},{8,0},{9,1},... | collective-permute-start | bytes 294920 | tf_op jit(solution)/shard_map/ppermute | solution.py:464
  35.7 0.0 collective-permute-done.10.b
  35.7 1.9 %collective-permute-start.13 = (f32[16,1536]{1,0:T(8,128)S(1)}, f32[16,1536]{1,0:T(8,128)S(1)}, u32[]{:S(2)}, u32[]{:S(2)}) collective-permute-start(f32[16,1536]{1,0:T(8,128)S(1)} %combined.2.a_5_), channel_id=1, source_target_pairs={{0,8},{1,9},{2,10},{3,11},{4,12},{5,13},{6,14},{7,15},{8,0},{9,1},... | collective-permute-start | bytes 294920 | tf_op jit(solution)/shard_map/ppermute | solution.py:464
  37.7 0.3 collective-permute-start.12
  38.0 1.6 %sums.7 = (f32[32,1536]{1,0:T(8,128)S(1)}, f32[2,96]{1,0:T(2,128)}) custom-call(f32[8,384]{1,0:T(8,128)S(1)} %get-tuple-element.56.a_0_, f32[8,384]{1,0:T(8,128)S(1)} %collective-permute-done.7.a_1_, f32[8,384]{1,0:T(8,128)S(1)} %collective-permute-done.8.a_2_, f32[8,384]{1,0:T(8,128)S(1)} %collective-permute-done.9.a_3_, ...), custom_call_target="tpu_custom_call" | custom-call | tf_op jit(solution)/shard_map/sums/pallas_call | solution.py:597
  39.6 0.0 copy-start
  39.6 1.3 %collective-permute-done.14.a_1_ = f32[16,1536]{1,0:T(8,128)S(1)} collective-permute-done((f32[16,1536]{1,0:T(8,128)S(1)}, f32[16,1536]{1,0:T(8,128)S(1)}, u32[]{:S(2)}, u32[]{:S(2)}) %collective-permute-start.14) | collective-permute-done | bytes 98336 | tf_op jit(solution)/shard_map/ppermute | solution.py:464
  40.9 1.7 %collective-permute-done.13.a_0_ = f32[16,1536]{1,0:T(8,128)S(1)} collective-permute-done((f32[16,1536]{1,0:T(8,128)S(1)}, f32[16,1536]{1,0:T(8,128)S(1)}, u32[]{:S(2)}, u32[]{:S(2)}) %collective-permute-start.13) | collective-permute-done | bytes 98336 | tf_op jit(solution)/shard_map/ppermute | solution.py:464
  42.6 1.6 %collective-permute-done.12.a_1_ = f32[32,1536]{1,0:T(8,128)S(1)} collective-permute-done((f32[32,1536]{1,0:T(8,128)S(1)}, f32[32,1536]{1,0:T(8,128)S(1)}, u32[]{:S(2)}, u32[]{:S(2)}) %collective-permute-start.12) | collective-permute-done | bytes 196640 | tf_op jit(solution)/shard_map/ppermute | solution.py:464
  44.2 0.0 copy-done
  44.2 0.7 %update.1 = f32[32,1024]{1,0:T(8,128)} custom-call(f32[32,1536]{1,0:T(8,128)S(1)} %get-tuple-element.69.a_0_, f32[32,1536]{1,0:T(8,128)S(1)} %collective-permute-done.12.a_1_, f32[16,1536]{1,0:T(8,128)S(1)} %get-tuple-element.70.a_2_, f32[16,1536]{1,0:T(8,128)S(1)} %get-tuple-element.71.a_3_, f32[1,512]{1,0:T(1,128)S(1)} %bitcast.8), custom_call_target="tpu_custom_call" | custom-call | tf_op jit(solution)/shard_map/update/pallas_call | solution.py:643
  (3 shorter events, 0.0 us)
Async XLA Ops:
  0.6 13.4 %collective-permute-start.1 = (f32[96,1024]{1,0:T(8,128)}, f32[96,1024]{1,0:T(8,128)S(1)}, u32[]{:S(2)}, u32[]{:S(2)}) collective-permute-start(f32[96,1024]{1,0:T(8,128)} %src_at.1), channel_id=1, source_target_pairs={{0,2},{1,3},{2,0},{3,1},{4,6},{5,7},{6,4},{7,5},{8,10},{9,11},{10,... | collective-permute-start | bytes 1179656 | tf_op jit(solution)/shard_map/ppermute | solution.py:464
  3.7 12.9 %collective-permute-start.6 = (f32[32,1024]{1,0:T(8,128)}, f32[32,1024]{1,0:T(8,128)S(1)}, u32[]{:S(2)}, u32[]{:S(2)}) collective-permute-start(f32[32,1024]{1,0:T(8,128)} %bitcast.9), channel_id=1, source_target_pairs={{0,8},{1,9},{2,10},{3,11},{4,12},{5,13},{6,14},{7,15},{8,0},{9,1},... | collective-permute-start | bytes 393224 | tf_op jit(solution)/shard_map/ppermute | solution.py:464
  6.3 10.6 %collective-permute-start.5 = (f32[32,1024]{1,0:T(8,128)}, f32[32,1024]{1,0:T(8,128)S(1)}, u32[]{:S(2)}, u32[]{:S(2)}) collective-permute-start(f32[32,1024]{1,0:T(8,128)} %bitcast.10), channel_id=1, source_target_pairs={{0,12},{1,13},{2,14},{3,15},{4,8},{5,9},{6,10},{7,11},{8,4},{9,5},... | collective-permute-start | bytes 393224 | tf_op jit(solution)/shard_map/ppermute | solution.py:464
  7.6 9.6 %collective-permute-start.4 = (f32[32,1024]{1,0:T(8,128)}, f32[32,1024]{1,0:T(8,128)S(1)}, u32[]{:S(2)}, u32[]{:S(2)}) collective-permute-start(f32[32,1024]{1,0:T(8,128)} %bitcast.11), channel_id=1, source_target_pairs={{0,4},{1,5},{2,6},{3,7},{4,0},{5,1},{6,2},{7,3},{8,12},{9,13},{10,... | collective-permute-start | bytes 393224 | tf_op jit(solution)/shard_map/ppermute | solution.py:464
  10.3 3.7 %collective-permute-start.2 = (f32[8,128]{1,0:T(8,128)S(1)}, f32[8,128]{1,0:T(8,128)S(1)}, u32[]{:S(2)}, u32[]{:S(2)}) collective-permute-start(f32[8,128]{1,0:T(8,128)S(1)} %get-tuple-element.38.wait), channel_id=1, source_target_pairs={{0,2},{1,3},{2,0},{3,1},{4,6},{5,7},{6,4},{7,5},{8,10},{9,11},{10,... | collective-permute-start | bytes 12296 | tf_op jit(solution)/shard_map/ppermute | solution.py:464
  14.0 3.5 %collective-permute-start = (f32[104,1536]{1,0:T(8,128)S(1)}, f32[104,1536]{1,0:T(8,128)S(1)}, u32[]{:S(2)}, u32[]{:S(2)}) collective-permute-start(f32[104,1536]{1,0:T(8,128)S(1)} %get-tuple-element.37.a_0_), channel_id=1, source_target_pairs={{0,1},{1,0},{2,3},{3,2},{4,5},{5,4},{6,7},{7,6},{8,9},{9,8},{10,11... | collective-permute-start | bytes 1916936 | tf_op jit(solution)/shard_map/ppermute | solution.py:464
  14.6 2.9 %collective-permute-start.3 = (f32[104,1536]{1,0:T(8,128)S(1)}, f32[104,1536]{1,0:T(8,128)S(1)}, u32[]{:S(2)}, u32[]{:S(2)}) collective-permute-start(f32[104,1536]{1,0:T(8,128)S(1)} %neighbour.1.wait.a_2_), channel_id=1, source_target_pairs={{0,1},{1,0},{2,3},{3,2},{4,5},{5,4},{6,7},{7,6},{8,9},{9,8},{10,11... | collective-permute-start | bytes 1916936 | tf_op jit(solution)/shard_map/ppermute | solution.py:464
  21.1 3.2 %collective-permute-start.9 = (f32[8,384]{1,0:T(8,128)S(1)}, f32[8,384]{1,0:T(8,128)S(1)}, u32[]{:S(2)}, u32[]{:S(2)}) collective-permute-start(f32[8,384]{1,0:T(8,128)S(1)} %get-tuple-element.56.a_0_), channel_id=1, source_target_pairs={{0,3},{1,2},{2,1},{3,0},{4,7},{5,6},{6,5},{7,4},{8,11},{9,10},{10,... | collective-permute-start | bytes 36872 | tf_op jit(solution)/shard_map/ppermute | solution.py:464
  21.4 3.7 %collective-permute-start.8 = (f32[8,384]{1,0:T(8,128)S(1)}, f32[8,384]{1,0:T(8,128)S(1)}, u32[]{:S(2)}, u32[]{:S(2)}) collective-permute-start(f32[8,384]{1,0:T(8,128)S(1)} %get-tuple-element.56.a_0_), channel_id=1, source_target_pairs={{0,2},{1,3},{2,0},{3,1},{4,6},{5,7},{6,4},{7,5},{8,10},{9,11},{10,... | collective-permute-start | bytes 36872 | tf_op jit(solution)/shard_map/ppermute | solution.py:464
  22.6 2.5 %collective-permute-start.7 = (f32[8,384]{1,0:T(8,128)S(1)}, f32[8,384]{1,0:T(8,128)S(1)}, u32[]{:S(2)}, u32[]{:S(2)}) collective-permute-start(f32[8,384]{1,0:T(8,128)S(1)} %get-tuple-element.56.a_0_), channel_id=1, source_target_pairs={{0,1},{1,0},{2,3},{3,2},{4,5},{5,4},{6,7},{7,6},{8,9},{9,8},{10,11... | collective-permute-start | bytes 36872 | tf_op jit(solution)/shard_map/ppermute | solution.py:464
  26.0 5.5 %collective-permute-start.11 = (f32[16,1536]{1,0:T(8,128)S(1)}, f32[16,1536]{1,0:T(8,128)S(1)}, u32[]{:S(2)}, u32[]{:S(2)}) collective-permute-start(f32[16,1536]{1,0:T(8,128)S(1)} %get-tuple-element.66), channel_id=1, source_target_pairs={{0,4},{1,5},{2,6},{3,7},{4,0},{5,1},{6,2},{7,3},{8,12},{9,13},{10,... | collective-permute-start | bytes 294920 | tf_op jit(solution)/shard_map/ppermute | solution.py:464
  28.1 7.6 %collective-permute-start.10 = (f32[16,1536]{1,0:T(8,128)S(1)}, f32[16,1536]{1,0:T(8,128)S(1)}, u32[]{:S(2)}, u32[]{:S(2)}) collective-permute-start(f32[16,1536]{1,0:T(8,128)S(1)} %get-tuple-element.61.a_5_), channel_id=1, source_target_pairs={{0,4},{1,5},{2,6},{3,7},{4,0},{5,1},{6,2},{7,3},{8,12},{9,13},{10,... | collective-permute-start | bytes 294920 | tf_op jit(solution)/shard_map/ppermute | solution.py:464
  31.6 9.3 %collective-permute-start.14 = (f32[16,1536]{1,0:T(8,128)S(1)}, f32[16,1536]{1,0:T(8,128)S(1)}, u32[]{:S(2)}, u32[]{:S(2)}) collective-permute-start(f32[16,1536]{1,0:T(8,128)S(1)} %combined.3.a_6_), channel_id=1, source_target_pairs={{0,8},{1,9},{2,10},{3,11},{4,12},{5,13},{6,14},{7,15},{8,0},{9,1},... | collective-permute-start | bytes 294920 | tf_op jit(solution)/shard_map/ppermute | solution.py:464
  35.7 6.9 %collective-permute-start.13 = (f32[16,1536]{1,0:T(8,128)S(1)}, f32[16,1536]{1,0:T(8,128)S(1)}, u32[]{:S(2)}, u32[]{:S(2)}) collective-permute-start(f32[16,1536]{1,0:T(8,128)S(1)} %combined.2.a_5_), channel_id=1, source_target_pairs={{0,8},{1,9},{2,10},{3,11},{4,12},{5,13},{6,14},{7,15},{8,0},{9,1},... | collective-permute-start | bytes 294920 | tf_op jit(solution)/shard_map/ppermute | solution.py:464
  37.7 6.6 %collective-permute-start.12 = (f32[32,1536]{1,0:T(8,128)S(1)}, f32[32,1536]{1,0:T(8,128)S(1)}, u32[]{:S(2)}, u32[]{:S(2)}) collective-permute-start(f32[32,1536]{1,0:T(8,128)S(1)} %sums.6.wait), channel_id=1, source_target_pairs={{0,4},{1,5},{2,6},{3,7},{4,0},{5,1},{6,2},{7,3},{8,12},{9,13},{10,... | collective-permute-start | bytes 589832 | tf_op jit(solution)/shard_map/ppermute | solution.py:464
  39.6 4.7 %copy-start = (f32[512]{0:T(512)S(1)}, f32[512]{0:T(512)}, u32[]{:S(2)}) copy-start(f32[512]{0:T(512)} %param.16) | copy-start | bytes 6148

commit v20 on v16

--- a/solution.py
+++ b/solution.py
@@ -379,8 +379,12 @@
     for n in range(blocks):
         part = slice(n * per, (n + 1) * per)
         base = prior - 0.5 * quad[part]
-        score = dot_nt(terms_left(prepared[4 * n][...], prepared[4 * n + 1][...]), main_terms)
-        score = score.reshape(SHIFTS, per, MAIN)
+        if n % 2 == 0:
+            pair = range(n, min(n + 2, blocks))
+            r_pair = [terms_left(prepared[4 * k][...], prepared[4 * k + 1][...]) for k in pair]
+            products = dot_nt(jnp.concatenate(r_pair, axis=0), main_terms)
+        at = n % 2 * SHIFTS * per
+        score = products[at : at + SHIFTS * per].reshape(SHIFTS, per, MAIN)
         tail = jnp.stack([x[part, :left] for x in far])
         score = jnp.concatenate([score, tail], axis=2) + base[None]
         top, sums_here = weigh(score, e_outs[n])

time: 44.2 us -> 44.1 us (level)
  no operation moved by 1% of the time
where the time goes in v20:
time: 44.1 us; the launch traced here: 44 us
  starting transfers between devices  16.5 us (37%)
  Pallas kernels  13.2 us (30%)
  waiting for transfers between devices  12.9 us (29%)
  between operations  1.38 us (3%)
    ppermute x15, starting transfers between devices, crossed(): return lax.ppermute(block, 'dom', [(i, i ^ mask) for i in range(size)])  16.5 us
    ppermute x15, waiting for transfers between devices, crossed(): return lax.ppermute(block, 'dom', [(i, i ^ mask) for i in range(size)])  12.9 us
    pallas_call x4, Pallas kernels, sums(): pl.pallas_call(lambda *a: sum_kernel(n, cuts, last, len(waits), *a), out_...  4.39 us
    pallas_call x1, Pallas kernels, call(): pl.pallas_call(kernel, cost_estimate=cost, out_shape=tuple(out_shape), in...  3.54 us
    pallas_call x1, Pallas kernels, on_device(): pl.pallas_call(own_kernel, out_shape=(jax.ShapeDtypeStruct((slots + 8, wi...  1.83 us
    pallas_call x1, Pallas kernels, on_device(): pl.pallas_call(own_refs_kernel, out_shape=tuple(block_shapes), in_specs=[...  1.15 us
    pallas_call x3, Pallas kernels, on_device(): pl.pallas_call(refs_kernel, out_shape=tuple(block_shapes), in_specs=[vmem...  0.94 us
  transfers between devices with their start and end apart: 15, of which 8 were waited for; matrix products, arithmetic and copies ran while one was open for 0% of the time, Pallas kernels for 18%

profile of v20, /device:TPU:0, one launch (start us, length us, event | category | flops | bytes accessed | tf_op | source)
XLA Modules:
  0.0 44.0 jit_solution(13821430086133735849)
XLA Ops:
  0.6 3.0 %collective-permute-start.1 = (f32[96,1024]{1,0:T(8,128)}, f32[96,1024]{1,0:T(8,128)S(1)}, u32[]{:S(2)}, u32[]{:S(2)}) collective-permute-start(f32[96,1024]{1,0:T(8,128)} %src_at.1), channel_id=1, source_target_pairs={{0,2},{1,3},{2,0},{3,1},{4,6},{5,7},{6,4},{7,5},{8,10},{9,11},{10,... | collective-permute-start | bytes 1179656 | tf_op jit(solution)/shard_map/ppermute | solution.py:468
  3.7 3.6 %collective-permute-start.5 = (f32[32,1024]{1,0:T(8,128)}, f32[32,1024]{1,0:T(8,128)S(1)}, u32[]{:S(2)}, u32[]{:S(2)}) collective-permute-start(f32[32,1024]{1,0:T(8,128)} %bitcast.9), channel_id=1, source_target_pairs={{0,12},{1,13},{2,14},{3,15},{4,8},{5,9},{6,10},{7,11},{8,4},{9,5},... | collective-permute-start | bytes 393224 | tf_op jit(solution)/shard_map/ppermute | solution.py:468
  7.3 0.0 collective-permute-start.4
  7.3 0.8 %collective-permute-start.6 = (f32[32,1024]{1,0:T(8,128)}, f32[32,1024]{1,0:T(8,128)S(1)}, u32[]{:S(2)}, u32[]{:S(2)}) collective-permute-start(f32[32,1024]{1,0:T(8,128)} %bitcast.11), channel_id=1, source_target_pairs={{0,8},{1,9},{2,10},{3,11},{4,12},{5,13},{6,14},{7,15},{8,0},{9,1},... | collective-permute-start | bytes 393224 | tf_op jit(solution)/shard_map/ppermute | solution.py:468
  8.7 1.8 %own.1 = (f32[104,1536]{1,0:T(8,128)S(1)}, f32[8,128]{1,0:T(8,128)S(1)}, f32[128,512]{1,0:T(8,128)S(1)}) custom-call(f32[96,1024]{1,0:T(8,128)} %src_at.1, f32[1,96]{1,0:T(1,128)} %bitcast.15, s32[2,96]{1,0:T(2,128)} %bitcast.14, s32[1,96]{1,0:T(1,128)} %bitcast.16, s32[1,96]{1,0:T(1,128)} %bitcast.17, f32[128,512]{1,0:T(8,128)} %noise_at.1, ...), custom_call_target="tpu_custom_call" | custom-call | tf_op jit(solution)/shard_map/own/pallas_call | solution.py:509
  10.5 0.4 collective-permute-start.2
  10.9 1.2 %own_refs.1 = (bf16[288,1024]{1,0:T(8,128)(2,1)S(1)}, bf16[288,1024]{1,0:T(8,128)(2,1)S(1)}, bf16[32,512]{1,0:T(8,128)(2,1)S(1)}, bf16[32,512]{1,0:T(8,128)(2,1)S(1)}) custom-call(f32[32,1024]{1,0:T(8,128)} %bitcast.12, f32[8,128]{1,0:T(8,128)S(1)} %get-tuple-element.38.wait), custom_call_target="tpu_custom_call" | custom-call | tf_op jit(solution)/shard_map/own_refs/pallas_call | solution.py:546
  12.1 2.2 %collective-permute-done.2.facts = f32[8,128]{1,0:T(8,128)S(1)} collective-permute-done((f32[8,128]{1,0:T(8,128)S(1)}, f32[8,128]{1,0:T(8,128)S(1)}, u32[]{:S(2)}, u32[]{:S(2)}) %collective-permute-start.2) | collective-permute-done | bytes 4128 | tf_op jit(solution)/shard_map/ppermute | solution.py:468
  14.2 0.0 collective-permute-start
  14.2 0.0 collective-permute-done.1.src
  14.2 0.6 %neighbour.1.wait.a_2_ = f32[104,1536]{1,0:T(8,128)S(1)} custom-call(f32[96,1024]{1,0:T(8,128)S(1)} %collective-permute-done.1.src, f32[8,128]{1,0:T(8,128)S(1)} %collective-permute-done.2.facts, f32[128,512]{1,0:T(8,128)S(1)} %get-tuple-element.39.inverse_noise, bf16[32,512]{1,0:T(8,128)(2,1)S(1)} %get-tuple-element.40.wait.a_6_), custom_call_target="tpu_custom_call" | custom-call | tf_op jit(solution)/shard_map/neighbour/pallas_call | solution.py:555
  14.9 0.6 %collective-permute-start.3 = (f32[104,1536]{1,0:T(8,128)S(1)}, f32[104,1536]{1,0:T(8,128)S(1)}, u32[]{:S(2)}, u32[]{:S(2)}) collective-permute-start(f32[104,1536]{1,0:T(8,128)S(1)} %neighbour.1.wait.a_2_), channel_id=1, source_target_pairs={{0,1},{1,0},{2,3},{3,2},{4,5},{5,4},{6,7},{7,6},{8,9},{9,8},{10,11... | collective-permute-start | bytes 1916936 | tf_op jit(solution)/shard_map/ppermute | solution.py:468
  15.4 0.0 collective-permute-done.5.ref
  15.4 0.3 refs.3
  15.8 0.0 collective-permute-done.4.ref
  15.8 0.3 refs.4
  16.1 2.2 %collective-permute-done.6.ref = f32[32,1024]{1,0:T(8,128)S(1)} collective-permute-done((f32[32,1024]{1,0:T(8,128)}, f32[32,1024]{1,0:T(8,128)S(1)}, u32[]{:S(2)}, u32[]{:S(2)}) %collective-permute-start.6) | collective-permute-done | bytes 131104 | tf_op jit(solution)/shard_map/ppermute | solution.py:468
  18.3 0.3 refs.5
  18.6 0.0 collective-permute-done.a_1_
  18.6 0.0 collective-permute-done.3.a_3_
  18.6 3.5 %late.1 = (f32[9,32,288]{2,1,0:T(8,128)S(1)}, f32[9,32,288]{2,1,0:T(8,128)S(1)}, f32[9,32,288]{2,1,0:T(8,128)S(1)}, f32[9,32,288]{2,1,0:T(8,128)S(1)}, bf16[896,...) custom-call(f32[104,1536]{1,0:T(8,128)S(1)} %get-tuple-element.37.a_0_, ...), custom_call_target="tpu_custom_call" | custom-call | tf_op jit(solution)/shard_map/late/pallas_call | solution.py:535
  22.2 0.1 collective-permute-start.9
  22.2 0.7 %collective-permute-start.8 = (f32[8,384]{1,0:T(8,128)S(1)}, f32[8,384]{1,0:T(8,128)S(1)}, u32[]{:S(2)}, u32[]{:S(2)}) collective-permute-start(f32[8,384]{1,0:T(8,128)S(1)} %get-tuple-element.56.a_0_), channel_id=1, source_target_pairs={{0,2},{1,3},{2,0},{3,1},{4,6},{5,7},{6,4},{7,5},{8,10},{9,11},{10,... | collective-permute-start | bytes 36872 | tf_op jit(solution)/shard_map/ppermute | solution.py:468
  23.0 1.1 %collective-permute-start.7 = (f32[8,384]{1,0:T(8,128)S(1)}, f32[8,384]{1,0:T(8,128)S(1)}, u32[]{:S(2)}, u32[]{:S(2)}) collective-permute-start(f32[8,384]{1,0:T(8,128)S(1)} %get-tuple-element.56.a_0_), channel_id=1, source_target_pairs={{0,1},{1,0},{2,3},{3,2},{4,5},{5,4},{6,7},{7,6},{8,9},{9,8},{10,11... | collective-permute-start | bytes 36872 | tf_op jit(solution)/shard_map/ppermute | solution.py:468
  24.1 1.3 %collective-permute-done.9.a_3_ = f32[8,384]{1,0:T(8,128)S(1)} collective-permute-done((f32[8,384]{1,0:T(8,128)S(1)}, f32[8,384]{1,0:T(8,128)S(1)}, u32[]{:S(2)}, u32[]{:S(2)}) %collective-permute-start.9) | collective-permute-done | bytes 12320 | tf_op jit(solution)/shard_map/ppermute | solution.py:468
  25.3 0.7 %collective-permute-done.8.a_2_ = f32[8,384]{1,0:T(8,128)S(1)} collective-permute-done((f32[8,384]{1,0:T(8,128)S(1)}, f32[8,384]{1,0:T(8,128)S(1)}, u32[]{:S(2)}, u32[]{:S(2)}) %collective-permute-start.8) | collective-permute-done | bytes 12320 | tf_op jit(solution)/shard_map/ppermute | solution.py:468
  26.0 0.0 collective-permute-done.7.a_1_
  26.0 0.9 %sums.4 = (f32[16,1536]{1,0:T(8,128)S(1)}, f32[16,1536]{1,0:T(8,128)S(1)}) custom-call(f32[8,384]{1,0:T(8,128)S(1)} %get-tuple-element.56.a_0_, f32[8,384]{1,0:T(8,128)S(1)} %collective-permute-done.7.a_1_, f32[8,384]{1,0:T(8,128)S(1)} %collective-permute-done.8.a_2_, f32[8,384]{1,0:T(8,128)S(1)} %collective-permute-done.9.a_3_, ...), custom_call_target="tpu_custom_call" | custom-call | tf_op jit(solution)/shard_map/sums/pallas_call | solution.py:601
  26.9 0.6 %collective-permute-start.11 = (f32[16,1536]{1,0:T(8,128)S(1)}, f32[16,1536]{1,0:T(8,128)S(1)}, u32[]{:S(2)}, u32[]{:S(2)}) collective-permute-start(f32[16,1536]{1,0:T(8,128)S(1)} %get-tuple-element.66), channel_id=1, source_target_pairs={{0,4},{1,5},{2,6},{3,7},{4,0},{5,1},{6,2},{7,3},{8,12},{9,13},{10,... | collective-permute-start | bytes 294920 | tf_op jit(solution)/shard_map/ppermute | solution.py:468
  27.5 1.5 %collective-permute-start.10 = (f32[16,1536]{1,0:T(8,128)S(1)}, f32[16,1536]{1,0:T(8,128)S(1)}, u32[]{:S(2)}, u32[]{:S(2)}) collective-permute-start(f32[16,1536]{1,0:T(8,128)S(1)} %get-tuple-element.61.a_5_), channel_id=1, source_target_pairs={{0,4},{1,5},{2,6},{3,7},{4,0},{5,1},{6,2},{7,3},{8,12},{9,13},{10,... | collective-permute-start | bytes 294920 | tf_op jit(solution)/shard_map/ppermute | solution.py:468
  29.0 0.9 %sums.5 = (f32[16,1536]{1,0:T(8,128)S(1)}, f32[16,1536]{1,0:T(8,128)S(1)}) custom-call(f32[8,384]{1,0:T(8,128)S(1)} %get-tuple-element.56.a_0_, f32[8,384]{1,0:T(8,128)S(1)} %collective-permute-done.7.a_1_, f32[8,384]{1,0:T(8,128)S(1)} %collective-permute-done.8.a_2_, f32[8,384]{1,0:T(8,128)S(1)} %collective-permute-done.9.a_3_, ...), custom_call_target="tpu_custom_call" | custom-call | tf_op jit(solution)/shard_map/sums/pallas_call | solution.py:601
  30.0 1.0 %sums.6.wait = f32[32,1536]{1,0:T(8,128)S(1)} custom-call(f32[8,384]{1,0:T(8,128)S(1)} %get-tuple-element.56.a_0_, f32[8,384]{1,0:T(8,128)S(1)} %collective-permute-done.7.a_1_, f32[8,384]{1,0:T(8,128)S(1)} %collective-permute-done.8.a_2_, f32[8,384]{1,0:T(8,128)S(1)} %collective-permute-done.9.a_3_, f32[8,384]{1,0:T(8,128)S(1)} %get-tuple-element.57.a_4_, ...), custom_call_target="tpu_custom_call" | custom-call | tf_op jit(solution)/shard_map/sums/pallas_call | solution.py:601
  30.9 1.3 %collective-permute-done.11.b = f32[16,1536]{1,0:T(8,128)S(1)} collective-permute-done((f32[16,1536]{1,0:T(8,128)S(1)}, f32[16,1536]{1,0:T(8,128)S(1)}, u32[]{:S(2)}, u32[]{:S(2)}) %collective-permute-start.11) | collective-permute-done | bytes 98336 | tf_op jit(solution)/shard_map/ppermute | solution.py:468
  32.2 1.8 %collective-permute-start.14 = (f32[16,1536]{1,0:T(8,128)S(1)}, f32[16,1536]{1,0:T(8,128)S(1)}, u32[]{:S(2)}, u32[]{:S(2)}) collective-permute-start(f32[16,1536]{1,0:T(8,128)S(1)} %combined.3.a_6_), channel_id=1, source_target_pairs={{0,8},{1,9},{2,10},{3,11},{4,12},{5,13},{6,14},{7,15},{8,0},{9,1},... | collective-permute-start | bytes 294920 | tf_op jit(solution)/shard_map/ppermute | solution.py:468
  34.0 0.0 collective-permute-done.10.b
  34.0 2.0 %collective-permute-start.13 = (f32[16,1536]{1,0:T(8,128)S(1)}, f32[16,1536]{1,0:T(8,128)S(1)}, u32[]{:S(2)}, u32[]{:S(2)}) collective-permute-start(f32[16,1536]{1,0:T(8,128)S(1)} %combined.2.a_5_), channel_id=1, source_target_pairs={{0,8},{1,9},{2,10},{3,11},{4,12},{5,13},{6,14},{7,15},{8,0},{9,1},... | collective-permute-start | bytes 294920 | tf_op jit(solution)/shard_map/ppermute | solution.py:468
  36.1 0.3 collective-permute-start.12
  36.4 1.6 %sums.7 = (f32[32,1536]{1,0:T(8,128)S(1)}, f32[2,96]{1,0:T(2,128)}) custom-call(f32[8,384]{1,0:T(8,128)S(1)} %get-tuple-element.56.a_0_, f32[8,384]{1,0:T(8,128)S(1)} %collective-permute-done.7.a_1_, f32[8,384]{1,0:T(8,128)S(1)} %collective-permute-done.8.a_2_, f32[8,384]{1,0:T(8,128)S(1)} %collective-permute-done.9.a_3_, ...), custom_call_target="tpu_custom_call" | custom-call | tf_op jit(solution)/shard_map/sums/pallas_call | solution.py:601
  37.9 0.0 copy-start
  37.9 2.2 %collective-permute-done.14.a_1_ = f32[16,1536]{1,0:T(8,128)S(1)} collective-permute-done((f32[16,1536]{1,0:T(8,128)S(1)}, f32[16,1536]{1,0:T(8,128)S(1)}, u32[]{:S(2)}, u32[]{:S(2)}) %collective-permute-start.14) | collective-permute-done | bytes 98336 | tf_op jit(solution)/shard_map/ppermute | solution.py:468
  40.1 1.8 %collective-permute-done.13.a_0_ = f32[16,1536]{1,0:T(8,128)S(1)} collective-permute-done((f32[16,1536]{1,0:T(8,128)S(1)}, f32[16,1536]{1,0:T(8,128)S(1)}, u32[]{:S(2)}, u32[]{:S(2)}) %collective-permute-start.13) | collective-permute-done | bytes 98336 | tf_op jit(solution)/shard_map/ppermute | solution.py:468
  41.9 1.3 %collective-permute-done.12.a_1_ = f32[32,1536]{1,0:T(8,128)S(1)} collective-permute-done((f32[32,1536]{1,0:T(8,128)S(1)}, f32[32,1536]{1,0:T(8,128)S(1)}, u32[]{:S(2)}, u32[]{:S(2)}) %collective-permute-start.12) | collective-permute-done | bytes 196640 | tf_op jit(solution)/shard_map/ppermute | solution.py:468
  43.3 0.0 copy-done
  43.3 0.7 %update.1 = f32[32,1024]{1,0:T(8,128)} custom-call(f32[32,1536]{1,0:T(8,128)S(1)} %get-tuple-element.69.a_0_, f32[32,1536]{1,0:T(8,128)S(1)} %collective-permute-done.12.a_1_, f32[16,1536]{1,0:T(8,128)S(1)} %get-tuple-element.70.a_2_, f32[16,1536]{1,0:T(8,128)S(1)} %get-tuple-element.71.a_3_, f32[1,512]{1,0:T(1,128)S(1)} %bitcast.8), custom_call_target="tpu_custom_call" | custom-call | tf_op jit(solution)/shard_map/update/pallas_call | solution.py:647
  (3 shorter events, 0.0 us)
Async XLA Ops:
  0.6 13.6 %collective-permute-start.1 = (f32[96,1024]{1,0:T(8,128)}, f32[96,1024]{1,0:T(8,128)S(1)}, u32[]{:S(2)}, u32[]{:S(2)}) collective-permute-start(f32[96,1024]{1,0:T(8,128)} %src_at.1), channel_id=1, source_target_pairs={{0,2},{1,3},{2,0},{3,1},{4,6},{5,7},{6,4},{7,5},{8,10},{9,11},{10,... | collective-permute-start | bytes 1179656 | tf_op jit(solution)/shard_map/ppermute | solution.py:468
  3.7 11.8 %collective-permute-start.5 = (f32[32,1024]{1,0:T(8,128)}, f32[32,1024]{1,0:T(8,128)S(1)}, u32[]{:S(2)}, u32[]{:S(2)}) collective-permute-start(f32[32,1024]{1,0:T(8,128)} %bitcast.9), channel_id=1, source_target_pairs={{0,12},{1,13},{2,14},{3,15},{4,8},{5,9},{6,10},{7,11},{8,4},{9,5},... | collective-permute-start | bytes 393224 | tf_op jit(solution)/shard_map/ppermute | solution.py:468
  7.3 8.5 %collective-permute-start.4 = (f32[32,1024]{1,0:T(8,128)}, f32[32,1024]{1,0:T(8,128)S(1)}, u32[]{:S(2)}, u32[]{:S(2)}) collective-permute-start(f32[32,1024]{1,0:T(8,128)} %bitcast.10), channel_id=1, source_target_pairs={{0,4},{1,5},{2,6},{3,7},{4,0},{5,1},{6,2},{7,3},{8,12},{9,13},{10,... | collective-permute-start | bytes 393224 | tf_op jit(solution)/shard_map/ppermute | solution.py:468
  7.3 11.0 %collective-permute-start.6 = (f32[32,1024]{1,0:T(8,128)}, f32[32,1024]{1,0:T(8,128)S(1)}, u32[]{:S(2)}, u32[]{:S(2)}) collective-permute-start(f32[32,1024]{1,0:T(8,128)} %bitcast.11), channel_id=1, source_target_pairs={{0,8},{1,9},{2,10},{3,11},{4,12},{5,13},{6,14},{7,15},{8,0},{9,1},... | collective-permute-start | bytes 393224 | tf_op jit(solution)/shard_map/ppermute | solution.py:468
  10.5 3.7 %collective-permute-start.2 = (f32[8,128]{1,0:T(8,128)S(1)}, f32[8,128]{1,0:T(8,128)S(1)}, u32[]{:S(2)}, u32[]{:S(2)}) collective-permute-start(f32[8,128]{1,0:T(8,128)S(1)} %get-tuple-element.38.wait), channel_id=1, source_target_pairs={{0,2},{1,3},{2,0},{3,1},{4,6},{5,7},{6,4},{7,5},{8,10},{9,11},{10,... | collective-permute-start | bytes 12296 | tf_op jit(solution)/shard_map/ppermute | solution.py:468
  14.2 4.4 %collective-permute-start = (f32[104,1536]{1,0:T(8,128)S(1)}, f32[104,1536]{1,0:T(8,128)S(1)}, u32[]{:S(2)}, u32[]{:S(2)}) collective-permute-start(f32[104,1536]{1,0:T(8,128)S(1)} %get-tuple-element.37.a_0_), channel_id=1, source_target_pairs={{0,1},{1,0},{2,3},{3,2},{4,5},{5,4},{6,7},{7,6},{8,9},{9,8},{10,11... | collective-permute-start | bytes 1916936 | tf_op jit(solution)/shard_map/ppermute | solution.py:468
  14.9 3.7 %collective-permute-start.3 = (f32[104,1536]{1,0:T(8,128)S(1)}, f32[104,1536]{1,0:T(8,128)S(1)}, u32[]{:S(2)}, u32[]{:S(2)}) collective-permute-start(f32[104,1536]{1,0:T(8,128)S(1)} %neighbour.1.wait.a_2_), channel_id=1, source_target_pairs={{0,1},{1,0},{2,3},{3,2},{4,5},{5,4},{6,7},{7,6},{8,9},{9,8},{10,11... | collective-permute-start | bytes 1916936 | tf_op jit(solution)/shard_map/ppermute | solution.py:468
  22.2 3.2 %collective-permute-start.9 = (f32[8,384]{1,0:T(8,128)S(1)}, f32[8,384]{1,0:T(8,128)S(1)}, u32[]{:S(2)}, u32[]{:S(2)}) collective-permute-start(f32[8,384]{1,0:T(8,128)S(1)} %get-tuple-element.56.a_0_), channel_id=1, source_target_pairs={{0,3},{1,2},{2,1},{3,0},{4,7},{5,6},{6,5},{7,4},{8,11},{9,10},{10,... | collective-permute-start | bytes 36872 | tf_op jit(solution)/shard_map/ppermute | solution.py:468
  22.2 3.8 %collective-permute-start.8 = (f32[8,384]{1,0:T(8,128)S(1)}, f32[8,384]{1,0:T(8,128)S(1)}, u32[]{:S(2)}, u32[]{:S(2)}) collective-permute-start(f32[8,384]{1,0:T(8,128)S(1)} %get-tuple-element.56.a_0_), channel_id=1, source_target_pairs={{0,2},{1,3},{2,0},{3,1},{4,6},{5,7},{6,4},{7,5},{8,10},{9,11},{10,... | collective-permute-start | bytes 36872 | tf_op jit(solution)/shard_map/ppermute | solution.py:468
  23.0 3.0 %collective-permute-start.7 = (f32[8,384]{1,0:T(8,128)S(1)}, f32[8,384]{1,0:T(8,128)S(1)}, u32[]{:S(2)}, u32[]{:S(2)}) collective-permute-start(f32[8,384]{1,0:T(8,128)S(1)} %get-tuple-element.56.a_0_), channel_id=1, source_target_pairs={{0,1},{1,0},{2,3},{3,2},{4,5},{5,4},{6,7},{7,6},{8,9},{9,8},{10,11... | collective-permute-start | bytes 36872 | tf_op jit(solution)/shard_map/ppermute | solution.py:468
  26.9 5.3 %collective-permute-start.11 = (f32[16,1536]{1,0:T(8,128)S(1)}, f32[16,1536]{1,0:T(8,128)S(1)}, u32[]{:S(2)}, u32[]{:S(2)}) collective-permute-start(f32[16,1536]{1,0:T(8,128)S(1)} %get-tuple-element.66), channel_id=1, source_target_pairs={{0,4},{1,5},{2,6},{3,7},{4,0},{5,1},{6,2},{7,3},{8,12},{9,13},{10,... | collective-permute-start | bytes 294920 | tf_op jit(solution)/shard_map/ppermute | solution.py:468
  27.5 6.5 %collective-permute-start.10 = (f32[16,1536]{1,0:T(8,128)S(1)}, f32[16,1536]{1,0:T(8,128)S(1)}, u32[]{:S(2)}, u32[]{:S(2)}) collective-permute-start(f32[16,1536]{1,0:T(8,128)S(1)} %get-tuple-element.61.a_5_), channel_id=1, source_target_pairs={{0,4},{1,5},{2,6},{3,7},{4,0},{5,1},{6,2},{7,3},{8,12},{9,13},{10,... | collective-permute-start | bytes 294920 | tf_op jit(solution)/shard_map/ppermute | solution.py:468
  32.2 7.9 %collective-permute-start.14 = (f32[16,1536]{1,0:T(8,128)S(1)}, f32[16,1536]{1,0:T(8,128)S(1)}, u32[]{:S(2)}, u32[]{:S(2)}) collective-permute-start(f32[16,1536]{1,0:T(8,128)S(1)} %combined.3.a_6_), channel_id=1, source_target_pairs={{0,8},{1,9},{2,10},{3,11},{4,12},{5,13},{6,14},{7,15},{8,0},{9,1},... | collective-permute-start | bytes 294920 | tf_op jit(solution)/shard_map/ppermute | solution.py:468
  34.0 7.9 %collective-permute-start.13 = (f32[16,1536]{1,0:T(8,128)S(1)}, f32[16,1536]{1,0:T(8,128)S(1)}, u32[]{:S(2)}, u32[]{:S(2)}) collective-permute-start(f32[16,1536]{1,0:T(8,128)S(1)} %combined.2.a_5_), channel_id=1, source_target_pairs={{0,8},{1,9},{2,10},{3,11},{4,12},{5,13},{6,14},{7,15},{8,0},{9,1},... | collective-permute-start | bytes 294920 | tf_op jit(solution)/shard_map/ppermute | solution.py:468
  36.1 7.2 %collective-permute-start.12 = (f32[32,1536]{1,0:T(8,128)S(1)}, f32[32,1536]{1,0:T(8,128)S(1)}, u32[]{:S(2)}, u32[]{:S(2)}) collective-permute-start(f32[32,1536]{1,0:T(8,128)S(1)} %sums.6.wait), channel_id=1, source_target_pairs={{0,4},{1,5},{2,6},{3,7},{4,0},{5,1},{6,2},{7,3},{8,12},{9,13},{10,... | collective-permute-start | bytes 589832 | tf_op jit(solution)/shard_map/ppermute | solution.py:468
  37.9 5.3 %copy-start = (f32[512]{0:T(512)S(1)}, f32[512]{0:T(512)}, u32[]{:S(2)}) copy-start(f32[512]{0:T(512)} %param.16) | copy-start | bytes 6148
